TPU v7x, 512 devices: a whole 4x8x8 slice. The times are simulated.
512 devices in a mesh: depth: 8 (over y_hi, core), height: 8 (over z), filt: 8 (over x, y_lo).
Axes of the slice: x: 4, y: 8 (y_hi: 4, y_lo: 2; y = y_hi * 2 + y_lo), z: 8, core: 2. Of those that a mesh axis runs over, the one named last changes fastest.
Arguments:
- activations: bfloat16 [64, 16, 64, 128], P('filt', 'depth', 'height'), may hold values from -6 to 6
- weights: bfloat16 [27, 64, 128], P(None, None, 'filt'), may hold values from -0.15625 to 0.15625
- bias: float32 [128], P('filt'), may hold values from -3 to 3
- cotangent: bfloat16 [128, 16, 64, 128], P('filt', 'depth', 'height'), may hold values from -6 to 6
Outputs:
- output: bfloat16 [128, 16, 64, 128], P('filt', 'depth', 'height')
- input_grad: bfloat16 [64, 16, 64, 128], P('filt', 'depth', 'height')
- weight_grad: float32 [27, 64, 128], P(None, None, 'filt')
- bias_grad: float32 [128], P('filt')
All inputs are finite; a program needn't handle non-finite values.
Results may differ from a plain program's by a relative error of at most 0.017.
Values may be sent and summed in bfloat16 or wider, within the bound.
No kernel may reach another device: no remote copies, remote signals or barrier semaphores. Data moves between devices by JAX's collectives and lax.ppermute only.
A program may use at most 64 MiB of HBM per device.

v0:
```python
import jax
import jax.numpy as jnp
from jax import lax
from jax.sharding import PartitionSpec as P


def padded_2(cells, sides, width):
    for axis, dim in sides:
        count = lax.axis_size(axis)
        ends = count - 1
        head = lax.slice_in_dim(cells, 0, width, axis=dim)
        tail = lax.slice_in_dim(cells, cells.shape[dim] - width, cells.shape[dim], axis=dim)
        cells = jnp.concatenate(
            [
                lax.ppermute(tail, axis, [(i, (i + 1) % count) for i in range(ends)]),
                cells,
                lax.ppermute(head, axis, [((i + 1) % count, i) for i in range(ends)]),
            ],
            axis=dim,
        )
    return cells


def widen(block):
    return jnp.pad(block, ((0, 0), (0, 0), (0, 0), (1, 1)))


def forward_stack(padded, first_d, first_h, planes, rows, width):
    return jnp.concatenate(
        [
            padded[:, first_d : first_d + planes, first_h : first_h + rows, kw : kw + width]
            for kw in range(3)
        ],
        axis=0,
    )


def input_term(grad_pad, w_part, planes, rows, width):
    total = jnp.zeros((w_part.shape[1], planes, rows, width), jnp.float32)
    for kd in range(3):
        for kh in range(3):
            stack = jnp.concatenate(
                [
                    grad_pad[
                        :, 2 - kd : 2 - kd + planes, 2 - kh : 2 - kh + rows, 2 - kw : 2 - kw + width
                    ]
                    for kw in range(3)
                ],
                axis=0,
            )
            block = jnp.concatenate([w_part[kd * 9 + kh * 3 + kw] for kw in range(3)], axis=1)
            total = total + jnp.einsum(
                "ik,kdhw->idhw", block, stack, preferred_element_type=jnp.float32
            )
    return total


def per_device(activations, weights, bias, cotangent):
    cin_dev, planes, rows, width = activations.shape
    cin_all = weights.shape[1]
    cout_dev = weights.shape[2]
    full = lax.all_gather(activations, "filt", axis=0, tiled=True)
    padded = padded_2(full, (("depth", 1), ("height", 2)), 1)
    padded = widen(padded)
    pre = jnp.zeros((cout_dev, planes, rows, width), jnp.float32) + bias[:, None, None, None]
    for kd in range(3):
        for kh in range(3):
            stack = forward_stack(padded, kd, kh, planes, rows, width)
            first = kd * 9 + kh * 3
            block = weights[first : first + 3].reshape(3 * cin_all, cout_dev)
            pre = pre + jnp.einsum(
                "kc,kdhw->cdhw", block, stack, preferred_element_type=jnp.float32
            )
    output = (0.2 * pre + 0.8 * jax.nn.softplus(pre)).astype(jnp.bfloat16)
    pre_grad = (cotangent.astype(jnp.float32) * (0.2 + 0.8 * jax.nn.sigmoid(pre))).astype(
        jnp.bfloat16
    )
    blocks = []
    for kd in range(3):
        for kh in range(3):
            stack = forward_stack(padded, kd, kh, planes, rows, width)
            blocks.append(
                jnp.einsum("kdhw,cdhw->kc", stack, pre_grad, preferred_element_type=jnp.float32)
            )
    weight_part = jnp.concatenate(blocks, axis=0).reshape(27, cin_all, cout_dev)
    bias_part = jnp.sum(pre_grad.astype(jnp.float32), axis=(1, 2, 3))
    weight_grad, bias_grad = lax.psum((weight_part, bias_part), ("depth", "height"))
    grad_rimmed = padded_2(pre_grad, (("depth", 1), ("height", 2)), 1)
    grad_pad = widen(grad_rimmed)
    summed = lax.psum_scatter(
        input_term(grad_pad, weights, planes, rows, width).astype(jnp.bfloat16),
        "filt",
        scatter_dimension=0,
        tiled=True,
    )
    return (output, summed, weight_grad, bias_grad)


def solution(mesh):
    placed = (
        P("filt", "depth", "height", None),
        P(None, None, "filt"),
        P("filt"),
        P("filt", "depth", "height", None),
    )
    return jax.shard_map(
        per_device,
        mesh=mesh,
        in_specs=placed,
        out_specs=(
            P("filt", "depth", "height", None),
            P("filt", "depth", "height", None),
            P(None, None, "filt"),
            P("filt"),
        ),
        check_vma=False,
    )
```

profile of v0, /device:TPU:8, one launch (start us, length us, event | category | flops | bytes accessed | tf_op | source)
XLA Modules:
  0.0 605.6 jit_solution(6888210761630406426)
XLA Ops:
  8.0 0.8 copy.36
  8.8 28.2 %all_gather.3 = bf16[64,2,8,128]{3,0,2,1:T(8,128)(2,1)S(1)} all-gather(bf16[8,2,8,128]{3,0,2,1:T(8,128)(2,1)S(1)} %copy.36), channel_id=1, replica_groups=mesh['depth'=8,'height'=8,'filt'=8] {'filt'}, dimensions={0}, use_global_device_ids=true | all-gather | bytes 294912 | tf_op jit(solution)/shard_map/all_gather | solution.py:62
  37.0 1.3 collective-permute-start
  38.3 1.3 collective-permute-start.1
  39.6 0.9 fusion.159
  40.5 0.9 slice_bitcast_fusion.2
  41.4 0.4 collective-permute-done.1
  41.8 4.3 collective-permute-start.2
  46.1 1.3 collective-permute-start.3
  47.4 0.8 slice_bitcast_fusion.1
  49.1 3.5 collective-permute-done.3
  52.6 0.7 fusion.5
  53.3 1.3 fusion.153
  54.7 0.6 copy-done.1
  57.1 0.6 copy-done
  57.7 0.4 convert_reduce_fusion
  58.1 0.3 convolution_bitcast_fusion.3
  58.4 0.3 convolution_bitcast_fusion.4
  58.8 0.3 convolution_bitcast_fusion.5
  59.1 5.3 collective-permute-start.4
  64.4 1.3 collective-permute-start.5
  65.7 0.3 convolution_bitcast_fusion
  66.0 0.3 convolution_bitcast_fusion.1
  66.4 0.3 convolution_bitcast_fusion.2
  66.7 0.3 convolution_bitcast_fusion.7
  67.0 0.3 convolution_bitcast_fusion.6
  67.3 0.6 collective-permute-done.5
  68.0 4.3 collective-permute-start.6
  72.2 1.3 collective-permute-start.7
  73.5 0.3 convolution_bitcast_fusion.8
  74.0 0.8 reshape.48
  74.9 4.6 collective-permute-done.7
  79.6 0.3 fusion.155
  80.0 0.3 fusion.34
  80.3 0.3 convolution_add_fusion.7
  80.6 0.3 convolution_add_fusion.6
  80.8 0.2 convolution_add_fusion.5
  81.1 0.3 convolution_add_fusion.4
  81.3 0.3 convolution_add_fusion.3
  81.6 0.3 convolution_add_fusion.2
  81.9 0.3 convolution_add_fusion.1
  82.1 0.3 fusion.6
  82.6 0.8 copy.83
  83.3 0.6 copy.47
  84.0 142.3 %psum.15 = f32[16]{0:T(128)} all-reduce(f32[16]{0:T(128)S(1)} %get-tuple-element.16), channel_id=1, replica_groups=mesh['depth'=8,'height'=8,'filt'=8] {'depth','height'}, use_global_device_ids=true, to_apply=%region_3.4 | all-reduce | flops 16 | bytes 128 | tf_op jit(solution)/shard_map/psum | solution.py:87
  226.3 368.8 %all-reduce.4.cloned.1.call-done = f32[27,64,16]{1,0,2:T(8,128)} async-done(((f32[27,64,16]{1,0,2:T(8,128)}), f32[27,64,16]{1,0,2:T(8,128)}) %all-reduce.4.cloned.1.call-update) | async-done | bytes 110608 | tf_op jit(solution)/shard_map/psum | solution.py:87
  595.1 1.8 copy.49
  596.8 1.4 copy.48
  (50 shorter events, 3.6 us)
Async XLA Ops:
  8.0 587.1 %all-reduce.4.cloned.1.call-start = ((), (), s32[]{:S(2)}) async-start(), calls=%async_computation.1 | async-start | bytes 524288 | tf_op jit(solution)/shard_map/psum | solution.py:87
  37.0 4.4 collective-permute-start
  38.3 3.5 collective-permute-start.1
  41.8 7.3 %collective-permute-start.2 = (bf16[64,4,1,128]{3,0,2,1:T(8,128)(2,1)S(1)}, bf16[64,4,1,128]{3,0,2,1:T(8,128)(2,1)S(1)}, u32[]{:S(2)}, u32[]{:S(2)}) collective-permute-start(bf16[64,4,1,128]{3,0,2,1:T(8,128)(2,1)S(1)} %get-tuple-element.42), channel_id=1, source_target_pairs={{0,8},{8,16},{16,24},{24,32},{32,40},{40,48},{48,56},{1,9},{9,17},... | collective-permute-start | bytes 196616 | tf_op jit(solution)/shard_map/ppermute | solution.py:15
  46.1 6.5 %collective-permute-start.3 = (bf16[64,4,1,128]{3,0,2,1:T(8,128)(2,1)S(1)}, bf16[64,4,1,128]{3,0,2,1:T(8,128)(2,1)S(1)}, u32[]{:S(2)}, u32[]{:S(2)}) collective-permute-start(bf16[64,4,1,128]{3,0,2,1:T(8,128)(2,1)S(1)} %get-tuple-element.43), channel_id=1, source_target_pairs={{8,0},{16,8},{24,16},{32,24},{40,32},{48,40},{56,48},{9,1},{17,9},... | collective-permute-start | bytes 196616 | tf_op jit(solution)/shard_map/ppermute | solution.py:17
  54.6 0.7 copy-start.1
  56.9 0.8 copy-start
  59.1 8.2 %collective-permute-start.4 = (bf16[16,1,8,128]{3,0,2,1:T(8,128)(2,1)S(1)}, bf16[16,1,8,128]{3,0,2,1:T(8,128)(2,1)S(1)}, u32[]{:S(2)}, u32[]{:S(2)}) collective-permute-start(bf16[16,1,8,128]{3,0,2,1:T(8,128)(2,1)S(1)} %get-tuple-element.111), channel_id=1, source_target_pairs={{0,64},{64,128},{128,192},{192,256},{256,320},{320,384},{384,448},... | collective-permute-start | bytes 98312 | tf_op jit(solution)/shard_map/ppermute | solution.py:15
  64.4 3.5 collective-permute-start.5
  68.0 6.9 %collective-permute-start.6 = (bf16[16,4,1,128]{3,0,2,1:T(8,128)(2,1)S(1)}, bf16[16,4,1,128]{3,0,2,1:T(8,128)(2,1)S(1)}, u32[]{:S(2)}, u32[]{:S(2)}) collective-permute-start(bf16[16,4,1,128]{3,0,2,1:T(8,128)(2,1)S(1)} %get-tuple-element.72), channel_id=1, source_target_pairs={{0,8},{8,16},{16,24},{24,32},{32,40},{40,48},{48,56},{1,9},{9,17},... | collective-permute-start | bytes 49160 | tf_op jit(solution)/shard_map/ppermute | solution.py:15
  72.2 7.2 %collective-permute-start.7 = (bf16[16,4,1,128]{3,0,2,1:T(8,128)(2,1)S(1)}, bf16[16,4,1,128]{3,0,2,1:T(8,128)(2,1)S(1)}, u32[]{:S(2)}, u32[]{:S(2)}) collective-permute-start(bf16[16,4,1,128]{3,0,2,1:T(8,128)(2,1)S(1)} %get-tuple-element.73), channel_id=1, source_target_pairs={{8,0},{16,8},{24,16},{32,24},{40,32},{48,40},{56,48},{9,1},{17,9},... | collective-permute-start | bytes 49160 | tf_op jit(solution)/shard_map/ppermute | solution.py:17
  74.8 522.0 %reduce-scatter.4.cloned.1.call-start = ((), (), s32[]{:S(2)}) async-start(), calls=%async_computation.2 | async-start | bytes 294912
Sparse Core Ops, SparseCore 0:
  74.9 520.0 all-reduce.3
Sparse Core Ops, SparseCore 1:
  83.4 43.9 reduce-scatter.3
where the time goes:
time: 607 us; the launch traced here: 606 us
  waiting for transfers between devices  378 us (62%)
  blocking collectives  170 us (28%)
  starting transfers between devices  20.4 us (3%)
  between operations  15.8 us (3%)
  local copies, waits for them, and re-layouts  12.7 us (2%)
  matrix products  7.4 us (1%)
    psum x1, waiting for transfers between devices, per_device(): lax.psum((weight_part, bias_part), ('depth', 'height'))  369 us
    psum x1, blocking collectives, per_device(): lax.psum((weight_part, bias_part), ('depth', 'height'))  142 us
    all_gather x1, blocking collectives, per_device(): full = lax.all_gather(activations, 'filt', axis=0, tiled=True)  28.2 us
    ppermute x4, starting transfers between devices, padded_2(): lax.ppermute(tail, axis, [(i, (i + 1) % count) for i in range(ends)])  15.1 us
  transfers between devices with their start and end apart: 10, of which 5 were waited for; matrix products, arithmetic and copies ran while one was open for 2% of the time, Pallas kernels for 0%

commit v1 on v0

v1 whole, which is shorter than its diff:
```python
import jax
import jax.numpy as jnp
from jax import lax
from jax.sharding import PartitionSpec as P

BF16 = jnp.bfloat16
F32 = jnp.float32


def padded_2(cells, sides, width):
    for axis, dim in sides:
        count = lax.axis_size(axis)
        ends = count - 1
        head = lax.slice_in_dim(cells, 0, width, axis=dim)
        tail = lax.slice_in_dim(cells, cells.shape[dim] - width, cells.shape[dim], axis=dim)
        cells = jnp.concatenate(
            [
                lax.ppermute(tail, axis, [(i, (i + 1) % count) for i in range(ends)]),
                cells,
                lax.ppermute(head, axis, [((i + 1) % count, i) for i in range(ends)]),
            ],
            axis=dim,
        )
    return cells


def spread(block, axis, groups=None):
    members = lax.axis_size(axis) if groups is None else len(groups[0])
    copies = jnp.broadcast_to(block[None], (members,) + block.shape)
    return lax.all_to_all(copies, axis, 0, 0, tiled=True, axis_index_groups=groups)


def widen(block):
    return jnp.pad(block, ((0, 0), (0, 0), (0, 0), (1, 1)))


def forward_stack(padded, first_d, first_h, planes, rows, width):
    return jnp.concatenate(
        [
            padded[:, first_d : first_d + planes, first_h : first_h + rows, kw : kw + width]
            for kw in range(3)
        ],
        axis=0,
    )


def input_term(grad_pad, w_part, planes, rows, width):
    total = jnp.zeros((w_part.shape[1], planes, rows, width), F32)
    for kd in range(3):
        for kh in range(3):
            stack = jnp.concatenate(
                [
                    grad_pad[
                        :, 2 - kd : 2 - kd + planes, 2 - kh : 2 - kh + rows, 2 - kw : 2 - kw + width
                    ]
                    for kw in range(3)
                ],
                axis=0,
            )
            block = jnp.concatenate([w_part[kd * 9 + kh * 3 + kw] for kw in range(3)], axis=1)
            total = total + jnp.einsum("ik,kdhw->idhw", block, stack, preferred_element_type=F32)
    return total


def sum_over_blocks(part):
    half = part.shape[1] // 2
    core = lax.axis_index("depth") % 2
    depth = lax.axis_size("depth")
    pairs = [(i, i ^ 1) for i in range(depth)]
    groups = [[i for i in range(depth) if i % 2 == c] for c in range(2)]
    low, high = part[:, :half], part[:, half:]
    sent = jnp.where(core == 0, high, low).astype(BF16)
    kept = jnp.where(core == 0, low, high)
    mine = (kept + lax.ppermute(sent, "depth", pairs).astype(F32)).astype(BF16)
    mine = jnp.sum(spread(mine, "depth", groups).astype(F32), axis=0).astype(BF16)
    mine = jnp.sum(spread(mine, "height").astype(F32), axis=0)
    other = lax.ppermute(mine, "depth", pairs)
    return jnp.concatenate(
        [jnp.where(core == 0, mine, other), jnp.where(core == 0, other, mine)], axis=1
    )


def per_device(activations, weights, bias, cotangent):
    cin_dev, planes, rows, width = activations.shape
    taps, cin_all, cout_dev = weights.shape
    sides = (("depth", 1), ("height", 2))
    rimmed = padded_2(activations, sides, 1)
    padded = widen(spread(rimmed, "filt").reshape((cin_all,) + rimmed.shape[1:]))
    pre = jnp.zeros((cout_dev, planes, rows, width), F32) + bias[:, None, None, None]
    for kd in range(3):
        for kh in range(3):
            stack = forward_stack(padded, kd, kh, planes, rows, width)
            first = kd * 9 + kh * 3
            block = weights[first : first + 3].reshape(3 * cin_all, cout_dev)
            pre = pre + jnp.einsum("kc,kdhw->cdhw", block, stack, preferred_element_type=F32)
    output = (0.2 * pre + 0.8 * jax.nn.softplus(pre)).astype(BF16)
    pre_grad = (cotangent.astype(F32) * (0.2 + 0.8 * jax.nn.sigmoid(pre))).astype(BF16)
    blocks = []
    for kd in range(3):
        for kh in range(3):
            stack = forward_stack(padded, kd, kh, planes, rows, width)
            blocks.append(jnp.einsum("kdhw,cdhw->ck", stack, pre_grad, preferred_element_type=F32))
    bias_part = jnp.sum(pre_grad.astype(F32), axis=(1, 2, 3))
    used = taps * cin_all
    blocks.append(jnp.pad(bias_part[:, None], ((0, 0), (0, -used % 256 - 1))))
    total = sum_over_blocks(jnp.concatenate(blocks, axis=1))
    weight_grad = total[:, :used].reshape(cout_dev, taps, cin_all).transpose(1, 2, 0)
    bias_grad = total[:, used]
    grad_pad = widen(padded_2(pre_grad, sides, 1))
    part = input_term(grad_pad, weights, planes, rows, width).astype(BF16)
    parts = lax.all_to_all(part, "filt", 0, 0, tiled=True)
    parts = parts.reshape((-1, cin_dev) + part.shape[1:])
    summed = jnp.sum(parts.astype(F32), axis=0).astype(BF16)
    return (output, summed, weight_grad, bias_grad)


def solution(mesh):
    placed = (
        P("filt", "depth", "height", None),
        P(None, None, "filt"),
        P("filt"),
        P("filt", "depth", "height", None),
    )
    return jax.shard_map(
        per_device,
        mesh=mesh,
        in_specs=placed,
        out_specs=(
            P("filt", "depth", "height", None),
            P("filt", "depth", "height", None),
            P(None, None, "filt"),
            P("filt"),
        ),
        check_vma=False,
    )
```

time: 607 us -> 111 us (0.18)
  waiting for transfers between devices: 378 us -> 36.7 us
  blocking collectives: 170 us -> 0 us
  starting transfers between devices: 20.4 us -> 52.6 us
  between operations: 15.8 us -> 0.99 us
    psum x1 -> x0, waiting for transfers between devices: 369 us -> none  [per_device(): lax.psum((weight_part, bias_part), ('depth', 'height'))]
    psum x1 -> x0, blocking collectives: 142 us -> none  [per_device(): lax.psum((weight_part, bias_part), ('depth', 'height'))]
    all_to_all x0 -> x4, waiting for transfers between devices: none -> 28.6 us  [the longest x3 25.1 us: spread(): lax.all_to_all(copies, axis, 0, 0, tiled=True, axis_index_groups=groups)]
    all_to_all x0 -> x4, starting transfers between devices: none -> 28.6 us  [the longest x3 24.2 us: spread(): lax.all_to_all(copies, axis, 0, 0, tiled=True, axis_index_groups=groups)]
    all_gather x1 -> x0, blocking collectives: 28.2 us -> none  [per_device(): full = lax.all_gather(activations, 'filt', axis=0, tiled=True)]
  transfers between devices with their start and end apart: 10 -> 14, of which waited for: 5 -> 7; matrix products, arithmetic and copies ran while one was open for 2% -> 7% of each run, Pallas kernels for 0% -> 0%
where the time goes in v1:
time: 111 us; the launch traced here: 110 us
  starting transfers between devices  52.6 us (47%)
  waiting for transfers between devices  36.7 us (33%)
  local copies, waits for them, and re-layouts  11.4 us (10%)
  matrix products  7.31 us (7%)
    all_to_all x3, waiting for transfers between devices, spread(): lax.all_to_all(copies, axis, 0, 0, tiled=True, axis_index_groups=groups)  25.1 us
    all_to_all x3, starting transfers between devices, spread(): lax.all_to_all(copies, axis, 0, 0, tiled=True, axis_index_groups=groups)  24.2 us
    ppermute x4, starting transfers between devices, padded_2(): lax.ppermute(tail, axis, [(i, (i + 1) % count) for i in range(ends)])  13.1 us
    ppermute x4, waiting for transfers between devices, padded_2(): lax.ppermute(head, axis, [((i + 1) % count, i) for i in range(ends)])  7.93 us
    ppermute x4, starting transfers between devices, padded_2(): lax.ppermute(head, axis, [((i + 1) % count, i) for i in range(ends)])  5.17 us
    all_to_all x1, starting transfers between devices, per_device(): parts = lax.all_to_all(part, 'filt', 0, 0, tiled=True)  4.35 us
    ppermute x1, starting transfers between devices, sum_over_blocks(): mine = (kept + lax.ppermute(sent, 'depth', pairs).astype(F32)).astype(BF16)  3.84 us
    all_to_all x1, waiting for transfers between devices, per_device(): parts = lax.all_to_all(part, 'filt', 0, 0, tiled=True)  3.53 us
  transfers between devices with their start and end apart: 14, of which 7 were waited for; matrix products, arithmetic and copies ran while one was open for 7% of the time, Pallas kernels for 0%

profile of v1, /device:TPU:8, one launch (start us, length us, event | category | flops | bytes accessed | tf_op | source)
XLA Modules:
  0.0 110.1 jit_solution(13791477796358275784)
XLA Ops:
  0.6 0.7 fusion.138
  1.4 1.7 %collective-permute-start = (bf16[8,1,8,128]{3,2,1,0:T(8,128)(2,1)S(1)}, bf16[8,1,8,128]{3,2,1,0:T(8,128)(2,1)S(1)}, u32[]{:S(2)}, u32[]{:S(2)}) collective-permute-start(bf16[8,1,8,128]{3,2,1,0:T(8,128)(2,1)S(1)} %get-tuple-element.121), channel_id=1, source_target_pairs={{0,64},{64,128},{128,192},{192,256},{256,320},{320,384},{384,448},... | collective-permute-start | bytes 49160 | tf_op jit(solution)/shard_map/ppermute | solution.py:18
  3.1 1.3 %collective-permute-start.1 = (bf16[8,1,8,128]{3,2,1,0:T(8,128)(2,1)S(1)}, bf16[8,1,8,128]{3,2,1,0:T(8,128)(2,1)S(1)}, u32[]{:S(2)}, u32[]{:S(2)}) collective-permute-start(bf16[8,1,8,128]{3,2,1,0:T(8,128)(2,1)S(1)} %get-tuple-element.120), channel_id=1, source_target_pairs={{64,0},{128,64},{192,128},{256,192},{320,256},{384,320},{448,384},... | collective-permute-start | bytes 49160 | tf_op jit(solution)/shard_map/ppermute | solution.py:20
  4.4 0.8 constant_dynamic-update-slice_fusion.1
  5.2 3.4 %collective-permute-done.1 = bf16[8,1,8,128]{3,2,1,0:T(8,128)(2,1)S(1)} collective-permute-done((bf16[8,1,8,128]{3,2,1,0:T(8,128)(2,1)S(1)}, bf16[8,1,8,128]{3,2,1,0:T(8,128)(2,1)S(1)}, u32[]{:S(2)}, u32[]{:S(2)}) %collective-permute-start.1) | collective-permute-done | bytes 16416 | tf_op jit(solution)/shard_map/ppermute | solution.py:20
  8.6 4.3 %collective-permute-start.2 = (bf16[8,4,1,128]{3,2,1,0:T(2,128)(2,1)S(1)}, bf16[8,4,1,128]{3,2,1,0:T(2,128)(2,1)S(1)}, u32[]{:S(2)}, u32[]{:S(2)}) collective-permute-start(bf16[8,4,1,128]{3,2,1,0:T(2,128)(2,1)S(1)} %get-tuple-element.118), channel_id=1, source_target_pairs={{0,8},{8,16},{16,24},{24,32},{32,40},{40,48},{48,56},{1,9},{9,17},... | collective-permute-start | bytes 24584 | tf_op jit(solution)/shard_map/ppermute | solution.py:18
  12.9 1.3 %collective-permute-start.3 = (bf16[8,4,1,128]{3,2,1,0:T(2,128)(2,1)S(1)}, bf16[8,4,1,128]{3,2,1,0:T(2,128)(2,1)S(1)}, u32[]{:S(2)}, u32[]{:S(2)}) collective-permute-start(bf16[8,4,1,128]{3,2,1,0:T(2,128)(2,1)S(1)} %get-tuple-element.119), channel_id=1, source_target_pairs={{8,0},{16,8},{24,16},{32,24},{40,32},{48,40},{56,48},{9,1},{17,9},... | collective-permute-start | bytes 24584 | tf_op jit(solution)/shard_map/ppermute | solution.py:20
  14.3 4.6 %collective-permute-done.3 = bf16[8,4,1,128]{3,2,1,0:T(2,128)(2,1)S(1)} collective-permute-done((bf16[8,4,1,128]{3,2,1,0:T(2,128)(2,1)S(1)}, bf16[8,4,1,128]{3,2,1,0:T(2,128)(2,1)S(1)}, u32[]{:S(2)}, u32[]{:S(2)}) %collective-permute-start.3) | collective-permute-done | bytes 8224 | tf_op jit(solution)/shard_map/ppermute | solution.py:20
  19.0 0.9 broadcast_in_dim.8
  20.0 5.9 %all-to-all-start = ((bf16[8,8,4,10,128]{4,1,3,2,0:T(8,128)(2,1)}), bf16[8,8,4,10,128]{4,1,3,2,0:T(8,128)(2,1)S(1)}, u32[]{:S(2)}, u32[]{:S(2)}) async-start(bf16[8,8,4,10,128]{4,1,3,2,0:T(8,128)(2,1)} %broadcast_in_dim.8), calls=%async_computation | async-start | bytes 1310720 | tf_op jit(solution)/shard_map/all_to_all | solution.py:30
  26.8 9.7 %all-to-all-done = bf16[8,8,4,10,128]{4,1,3,2,0:T(8,128)(2,1)S(1)} async-done(((bf16[8,8,4,10,128]{4,1,3,2,0:T(8,128)(2,1)}), bf16[8,8,4,10,128]{4,1,3,2,0:T(8,128)(2,1)S(1)}, u32[]{:S(2)}, u32[]{:S(2)}) %all-to-all-start) | async-done | bytes 655392 | tf_op jit(solution)/shard_map/all_to_all | solution.py:30
  36.6 1.4 %pad_slice_fusion.1 = (bf16[64,2,8,128]{3,0,2,1:T(8,128)(2,1)S(1)}, bf16[64,2,8,128]{3,0,2,1:T(8,128)(2,1)S(1)}, bf16[64,2,8,128]{3,0,2,1:T(8,128)(2,1)S(1)}, bf...) fusion(bf16[64,4,10,128]{3,0,2,1:T(8,128)(2,1)S(1)} %bitcast.199), kind=kLoop, calls=%fused_computation.1 | loop fusion | bytes 6160384 | tf_op jit(solution)/shard_map/slice | solution.py:40
  38.0 0.5 fusion.131
  40.4 0.6 copy-done.1
  41.0 0.4 convert_reduce_fusion.1
  41.4 0.3 convolution_bitcast_fusion.5
  41.7 0.3 convolution_bitcast_fusion.6
  42.0 0.3 convolution_bitcast_fusion.7
  42.4 0.3 convolution_bitcast_fusion.8
  42.7 0.3 convolution_bitcast_fusion.4
  43.0 0.3 convolution_bitcast_fusion
  43.3 0.3 convolution_bitcast_fusion.1
  43.7 0.3 convolution_bitcast_fusion.2
  44.0 0.3 convolution_bitcast_fusion.3
  44.4 2.9 %collective-permute-start.4 = (bf16[16,1,8,128]{3,0,2,1:T(8,128)(2,1)S(1)}, bf16[16,1,8,128]{3,0,2,1:T(8,128)(2,1)S(1)}, u32[]{:S(2)}, u32[]{:S(2)}) collective-permute-start(bf16[16,1,8,128]{3,0,2,1:T(8,128)(2,1)S(1)} %get-tuple-element.116), channel_id=1, source_target_pairs={{0,64},{64,128},{128,192},{192,256},{256,320},{320,384},{384,448},... | collective-permute-start | bytes 98312 | tf_op jit(solution)/shard_map/ppermute | solution.py:18
  47.3 1.3 %collective-permute-start.5 = (bf16[16,1,8,128]{3,0,2,1:T(8,128)(2,1)S(1)}, bf16[16,1,8,128]{3,0,2,1:T(8,128)(2,1)S(1)}, u32[]{:S(2)}, u32[]{:S(2)}) collective-permute-start(bf16[16,1,8,128]{3,0,2,1:T(8,128)(2,1)S(1)} %get-tuple-element.117), channel_id=1, source_target_pairs={{64,0},{128,64},{192,128},{256,192},{320,256},{384,320},{448,384},... | collective-permute-start | bytes 98312 | tf_op jit(solution)/shard_map/ppermute | solution.py:20
  48.8 3.8 %collective-permute-start.8 = (bf16[16,896]{1,0:T(8,128)(2,1)S(1)}, bf16[16,896]{1,0:T(8,128)(2,1)S(1)}, u32[]{:S(2)}, u32[]{:S(2)}) collective-permute-start(bf16[16,896]{1,0:T(8,128)(2,1)S(1)} %select_convert_fusion), channel_id=1, source_target_pairs={{0,64},{64,0},{128,192},{192,128},{256,320},{320,256},{384,448},{4... | collective-permute-start | bytes 86024 | tf_op jit(solution)/shard_map/ppermute | solution.py:74
  52.7 4.3 %collective-permute-start.6 = (bf16[16,4,1,128]{3,0,2,1:T(8,128)(2,1)S(1)}, bf16[16,4,1,128]{3,0,2,1:T(8,128)(2,1)S(1)}, u32[]{:S(2)}, u32[]{:S(2)}) collective-permute-start(bf16[16,4,1,128]{3,0,2,1:T(8,128)(2,1)S(1)} %get-tuple-element.75), channel_id=1, source_target_pairs={{0,8},{8,16},{16,24},{24,32},{32,40},{40,48},{48,56},{1,9},{9,17},... | collective-permute-start | bytes 49160 | tf_op jit(solution)/shard_map/ppermute | solution.py:18
  57.0 1.3 %collective-permute-start.7 = (bf16[16,4,1,128]{3,0,2,1:T(8,128)(2,1)S(1)}, bf16[16,4,1,128]{3,0,2,1:T(8,128)(2,1)S(1)}, u32[]{:S(2)}, u32[]{:S(2)}) collective-permute-start(bf16[16,4,1,128]{3,0,2,1:T(8,128)(2,1)S(1)} %get-tuple-element.76), channel_id=1, source_target_pairs={{8,0},{16,8},{24,16},{32,24},{40,32},{48,40},{56,48},{9,1},{17,9},... | collective-permute-start | bytes 49160 | tf_op jit(solution)/shard_map/ppermute | solution.py:20
  58.3 0.7 broadcast_in_dim.10
  59.0 8.2 %all-to-all-start.2 = ((bf16[4,16,896]{2,1,0:T(8,128)(2,1)}), bf16[4,16,896]{2,1,0:T(8,128)(2,1)S(1)}, u32[]{:S(2)}, u32[]{:S(2)}) async-start(bf16[4,16,896]{2,1,0:T(8,128)(2,1)} %broadcast_in_dim.10), calls=%async_computation.2 | async-start | bytes 229376 | tf_op jit(solution)/shard_map/all_to_all | solution.py:30
  67.3 0.3 fusion.132
  68.0 0.3 convolution_add_fusion.7
  68.5 0.3 convolution_add_fusion.5
  68.8 0.3 convolution_add_fusion.4
  69.5 6.7 %all-to-all-done.2 = bf16[4,16,896]{2,1,0:T(8,128)(2,1)S(1)} async-done(((bf16[4,16,896]{2,1,0:T(8,128)(2,1)}), bf16[4,16,896]{2,1,0:T(8,128)(2,1)S(1)}, u32[]{:S(2)}, u32[]{:S(2)}) %all-to-all-start.2) | async-done | bytes 114720 | tf_op jit(solution)/shard_map/all_to_all | solution.py:30
  76.3 0.7 broadcast_in_dim.11
  77.0 10.2 %all-to-all-start.3 = ((bf16[8,16,896]{2,1,0:T(8,128)(2,1)}), bf16[8,16,896]{2,1,0:T(8,128)(2,1)S(1)}, u32[]{:S(2)}, u32[]{:S(2)}) async-start(bf16[8,16,896]{2,1,0:T(8,128)(2,1)} %broadcast_in_dim.11), calls=%async_computation.3 | async-start | bytes 458752 | tf_op jit(solution)/shard_map/all_to_all | solution.py:30
  87.4 0.3 fusion
  87.7 0.9 copy.66
  88.5 8.7 %all-to-all-done.3 = bf16[8,16,896]{2,1,0:T(8,128)(2,1)S(1)} async-done(((bf16[8,16,896]{2,1,0:T(8,128)(2,1)}), bf16[8,16,896]{2,1,0:T(8,128)(2,1)S(1)}, u32[]{:S(2)}, u32[]{:S(2)}) %all-to-all-start.3) | async-done | bytes 229408 | tf_op jit(solution)/shard_map/all_to_all | solution.py:30
  97.3 4.4 %all-to-all-start.1 = ((bf16[64,2,8,128]{3,2,1,0:T(8,128)(2,1)}), bf16[64,2,8,128]{3,2,1,0:T(8,128)(2,1)S(1)}, u32[]{:S(2)}, u32[]{:S(2)}) async-start(bf16[64,2,8,128]{3,2,1,0:T(8,128)(2,1)} %copy.66), calls=%async_computation.1 | async-start | bytes 524288 | tf_op jit(solution)/shard_map/all_to_all | solution.py:111
  101.7 1.9 %collective-permute-start.9 = (f32[16,896]{1,0:T(8,128)S(1)}, f32[16,896]{1,0:T(8,128)S(1)}, u32[]{:S(2)}, u32[]{:S(2)}) collective-permute-start(f32[16,896]{1,0:T(8,128)S(1)} %convert_reduce_fusion), channel_id=1, source_target_pairs={{0,64},{64,0},{128,192},{192,128},{256,320},{320,256},{384,448},{4... | collective-permute-start | bytes 172040 | tf_op jit(solution)/shard_map/ppermute | solution.py:77
  103.6 0.6 copy.69
  104.2 3.5 %all-to-all-done.1 = bf16[64,2,8,128]{3,2,1,0:T(8,128)(2,1)S(1)} async-done(((bf16[64,2,8,128]{3,2,1,0:T(8,128)(2,1)}), bf16[64,2,8,128]{3,2,1,0:T(8,128)(2,1)S(1)}, u32[]{:S(2)}, u32[]{:S(2)}) %all-to-all-start.1) | async-done | bytes 262176 | tf_op jit(solution)/shard_map/all_to_all | solution.py:111
  107.8 0.7 reduce_sum.42
  108.5 0.7 slice_reduce_fusion
  109.3 0.8 copy.71
  (69 shorter events, 5.3 us)
Async XLA Ops:
  1.4 3.0 %collective-permute-start = (bf16[8,1,8,128]{3,2,1,0:T(8,128)(2,1)S(1)}, bf16[8,1,8,128]{3,2,1,0:T(8,128)(2,1)S(1)}, u32[]{:S(2)}, u32[]{:S(2)}) collective-permute-start(bf16[8,1,8,128]{3,2,1,0:T(8,128)(2,1)S(1)} %get-tuple-element.121), channel_id=1, source_target_pairs={{0,64},{64,128},{128,192},{192,256},{256,320},{320,384},{384,448},... | collective-permute-start | bytes 49160 | tf_op jit(solution)/shard_map/ppermute | solution.py:18
  3.1 5.5 %collective-permute-start.1 = (bf16[8,1,8,128]{3,2,1,0:T(8,128)(2,1)S(1)}, bf16[8,1,8,128]{3,2,1,0:T(8,128)(2,1)S(1)}, u32[]{:S(2)}, u32[]{:S(2)}) collective-permute-start(bf16[8,1,8,128]{3,2,1,0:T(8,128)(2,1)S(1)} %get-tuple-element.120), channel_id=1, source_target_pairs={{64,0},{128,64},{192,128},{256,192},{320,256},{384,320},{448,384},... | collective-permute-start | bytes 49160 | tf_op jit(solution)/shard_map/ppermute | solution.py:20
  8.6 5.7 %collective-permute-start.2 = (bf16[8,4,1,128]{3,2,1,0:T(2,128)(2,1)S(1)}, bf16[8,4,1,128]{3,2,1,0:T(2,128)(2,1)S(1)}, u32[]{:S(2)}, u32[]{:S(2)}) collective-permute-start(bf16[8,4,1,128]{3,2,1,0:T(2,128)(2,1)S(1)} %get-tuple-element.118), channel_id=1, source_target_pairs={{0,8},{8,16},{16,24},{24,32},{32,40},{40,48},{48,56},{1,9},{9,17},... | collective-permute-start | bytes 24584 | tf_op jit(solution)/shard_map/ppermute | solution.py:18
  12.9 6.0 %collective-permute-start.3 = (bf16[8,4,1,128]{3,2,1,0:T(2,128)(2,1)S(1)}, bf16[8,4,1,128]{3,2,1,0:T(2,128)(2,1)S(1)}, u32[]{:S(2)}, u32[]{:S(2)}) collective-permute-start(bf16[8,4,1,128]{3,2,1,0:T(2,128)(2,1)S(1)} %get-tuple-element.119), channel_id=1, source_target_pairs={{8,0},{16,8},{24,16},{32,24},{40,32},{48,40},{56,48},{9,1},{17,9},... | collective-permute-start | bytes 24584 | tf_op jit(solution)/shard_map/ppermute | solution.py:20
  20.0 5.9 %copy-start = (bf16[27,64,16]{1,2,0:T(8,128)(2,1)S(1)}, bf16[27,64,16]{1,2,0:T(8,128)(2,1)}, u32[]{:S(2)}) copy-start(bf16[27,64,16]{1,2,0:T(8,128)(2,1)} %param.5) | copy-start | bytes 165892
  20.0 16.5 %all-to-all-start = ((bf16[8,8,4,10,128]{4,1,3,2,0:T(8,128)(2,1)}), bf16[8,8,4,10,128]{4,1,3,2,0:T(8,128)(2,1)S(1)}, u32[]{:S(2)}, u32[]{:S(2)}) async-start(bf16[8,8,4,10,128]{4,1,3,2,0:T(8,128)(2,1)} %broadcast_in_dim.8), calls=%async_computation | async-start | bytes 1310720 | tf_op jit(solution)/shard_map/all_to_all | solution.py:30
  38.0 0.7 copy-start.2
  40.2 0.8 copy-start.1
  44.4 8.2 %collective-permute-start.4 = (bf16[16,1,8,128]{3,0,2,1:T(8,128)(2,1)S(1)}, bf16[16,1,8,128]{3,0,2,1:T(8,128)(2,1)S(1)}, u32[]{:S(2)}, u32[]{:S(2)}) collective-permute-start(bf16[16,1,8,128]{3,0,2,1:T(8,128)(2,1)S(1)} %get-tuple-element.116), channel_id=1, source_target_pairs={{0,64},{64,128},{128,192},{192,256},{256,320},{320,384},{384,448},... | collective-permute-start | bytes 98312 | tf_op jit(solution)/shard_map/ppermute | solution.py:18
  47.3 5.4 %collective-permute-start.5 = (bf16[16,1,8,128]{3,0,2,1:T(8,128)(2,1)S(1)}, bf16[16,1,8,128]{3,0,2,1:T(8,128)(2,1)S(1)}, u32[]{:S(2)}, u32[]{:S(2)}) collective-permute-start(bf16[16,1,8,128]{3,0,2,1:T(8,128)(2,1)S(1)} %get-tuple-element.117), channel_id=1, source_target_pairs={{64,0},{128,64},{192,128},{256,192},{320,256},{384,320},{448,384},... | collective-permute-start | bytes 98312 | tf_op jit(solution)/shard_map/ppermute | solution.py:20
  48.8 9.5 %collective-permute-start.8 = (bf16[16,896]{1,0:T(8,128)(2,1)S(1)}, bf16[16,896]{1,0:T(8,128)(2,1)S(1)}, u32[]{:S(2)}, u32[]{:S(2)}) collective-permute-start(bf16[16,896]{1,0:T(8,128)(2,1)S(1)} %select_convert_fusion), channel_id=1, source_target_pairs={{0,64},{64,0},{128,192},{192,128},{256,320},{320,256},{384,448},{4... | collective-permute-start | bytes 86024 | tf_op jit(solution)/shard_map/ppermute | solution.py:74
  52.7 14.4 %collective-permute-start.6 = (bf16[16,4,1,128]{3,0,2,1:T(8,128)(2,1)S(1)}, bf16[16,4,1,128]{3,0,2,1:T(8,128)(2,1)S(1)}, u32[]{:S(2)}, u32[]{:S(2)}) collective-permute-start(bf16[16,4,1,128]{3,0,2,1:T(8,128)(2,1)S(1)} %get-tuple-element.75), channel_id=1, source_target_pairs={{0,8},{8,16},{16,24},{24,32},{32,40},{40,48},{48,56},{1,9},{9,17},... | collective-permute-start | bytes 49160 | tf_op jit(solution)/shard_map/ppermute | solution.py:18
  57.0 10.2 %collective-permute-start.7 = (bf16[16,4,1,128]{3,0,2,1:T(8,128)(2,1)S(1)}, bf16[16,4,1,128]{3,0,2,1:T(8,128)(2,1)S(1)}, u32[]{:S(2)}, u32[]{:S(2)}) collective-permute-start(bf16[16,4,1,128]{3,0,2,1:T(8,128)(2,1)S(1)} %get-tuple-element.76), channel_id=1, source_target_pairs={{8,0},{16,8},{24,16},{32,24},{40,32},{48,40},{56,48},{9,1},{17,9},... | collective-permute-start | bytes 49160 | tf_op jit(solution)/shard_map/ppermute | solution.py:20
  59.0 17.3 %all-to-all-start.2 = ((bf16[4,16,896]{2,1,0:T(8,128)(2,1)}), bf16[4,16,896]{2,1,0:T(8,128)(2,1)S(1)}, u32[]{:S(2)}, u32[]{:S(2)}) async-start(bf16[4,16,896]{2,1,0:T(8,128)(2,1)} %broadcast_in_dim.10), calls=%async_computation.2 | async-start | bytes 229376 | tf_op jit(solution)/shard_map/all_to_all | solution.py:30
  77.0 20.3 %all-to-all-start.3 = ((bf16[8,16,896]{2,1,0:T(8,128)(2,1)}), bf16[8,16,896]{2,1,0:T(8,128)(2,1)S(1)}, u32[]{:S(2)}, u32[]{:S(2)}) async-start(bf16[8,16,896]{2,1,0:T(8,128)(2,1)} %broadcast_in_dim.11), calls=%async_computation.3 | async-start | bytes 458752 | tf_op jit(solution)/shard_map/all_to_all | solution.py:30
  97.3 10.5 %all-to-all-start.1 = ((bf16[64,2,8,128]{3,2,1,0:T(8,128)(2,1)}), bf16[64,2,8,128]{3,2,1,0:T(8,128)(2,1)S(1)}, u32[]{:S(2)}, u32[]{:S(2)}) async-start(bf16[64,2,8,128]{3,2,1,0:T(8,128)(2,1)} %copy.66), calls=%async_computation.1 | async-start | bytes 524288 | tf_op jit(solution)/shard_map/all_to_all | solution.py:111
  101.7 6.8 %collective-permute-start.9 = (f32[16,896]{1,0:T(8,128)S(1)}, f32[16,896]{1,0:T(8,128)S(1)}, u32[]{:S(2)}, u32[]{:S(2)}) collective-permute-start(f32[16,896]{1,0:T(8,128)S(1)} %convert_reduce_fusion), channel_id=1, source_target_pairs={{0,64},{64,0},{128,192},{192,128},{256,320},{320,256},{384,448},{4... | collective-permute-start | bytes 172040 | tf_op jit(solution)/shard_map/ppermute | solution.py:77

commit v2 on v0

v2 whole, which is shorter than its diff:
```python
import functools

import jax
import jax.numpy as jnp
from jax import lax
from jax.experimental import pallas as pl
from jax.experimental.pallas import tpu as pltpu
from jax.sharding import PartitionSpec as P

BF16 = jnp.bfloat16
F32 = jnp.float32


def exchange(first, last, axis):
    ends = lax.axis_size(axis) - 1
    before = lax.ppermute(last, axis, [(i, i + 1) for i in range(ends)])
    after = lax.ppermute(first, axis, [(i + 1, i) for i in range(ends)])
    return before, after


def spread(block, axis, groups=None):
    members = lax.axis_size(axis) if groups is None else len(groups[0])
    copies = jnp.broadcast_to(block[None], (members,) + block.shape)
    return lax.all_to_all(copies, axis, 0, 0, tiled=True, axis_index_groups=groups)


def rim_rows(planes, count):
    return (
        jnp.concatenate([p[:count] for p in planes], axis=0),
        jnp.concatenate([p[-count:] for p in planes], axis=0),
    )


def shifted(value, lane):
    width = value.shape[-1]
    ahead = jnp.where(lane == width - 1, 0.0, pltpu.roll(value, width - 1, 1))
    behind = jnp.where(lane == 0, 0.0, pltpu.roll(value, 1, 1))
    return jnp.concatenate([ahead, value, behind], axis=0)


def three_rows(plane, before, after, p, h, rows, count):
    if h == 0:
        return jnp.concatenate([before[p * count : (p + 1) * count, :], plane[: 2 * count, :]], axis=0)
    if h == rows - 1:
        return jnp.concatenate([plane[(h - 1) * count :, :], after[p * count : (p + 1) * count, :]], axis=0)
    return plane[(h - 1) * count : (h + 2) * count, :]


def forward_kernel(
    rows, planes, core, w_ref, bias_ref, cot_ref, *refs
):
    grid = refs[: planes + 2]
    before, after, out_ref, pg_ref, sent_ref, kept_ref, total = refs[planes + 2 :]
    cin = before.shape[0] // (planes + 2)
    cout, width = cot_ref.shape[1:]
    lane = lax.broadcasted_iota(jnp.int32, (cout, width), 1)
    bias = bias_ref[...]
    sums = [None] * 3
    bias_sum = jnp.zeros((cout, width), F32)
    for d in range(planes):
        for h in range(0, rows, 2):
            cells = [
                jnp.concatenate(
                    [three_rows(grid[d + kd], before, after, d + kd, h + e, rows, cin) for e in range(2)],
                    axis=1,
                )
                for kd in range(3)
            ]
            acc = jnp.dot(w_ref[0], cells[0], preferred_element_type=F32)
            for kd in range(1, 3):
                acc = acc + jnp.dot(w_ref[kd], cells[kd], preferred_element_type=F32)
            grads = []
            for e in range(2):
                z = acc[:, e * width : (e + 1) * width]
                pre = (
                    z[cout : 2 * cout]
                    + jnp.where(lane == 0, 0.0, pltpu.roll(z[:cout], 1, 1))
                    + jnp.where(lane == width - 1, 0.0, pltpu.roll(z[2 * cout :], width - 1, 1))
                    + bias
                )
                small = jnp.exp(-jnp.abs(pre))
                softplus = jnp.maximum(pre, 0.0) + jnp.log1p(small)
                sigmoid = jnp.where(pre >= 0, 1.0, small) / (1.0 + small)
                at = d * rows + h + e
                out_ref[at] = (0.2 * pre + 0.8 * softplus).astype(BF16)
                grad = (cot_ref[at].astype(F32) * (0.2 + 0.8 * sigmoid)).astype(BF16)
                pg_ref[at] = grad
                grad = grad.astype(F32)
                bias_sum = bias_sum + grad
                grads.append(shifted(grad, lane).astype(BF16))
            both = jnp.concatenate(grads, axis=1)
            for kd in range(3):
                term = lax.dot_general(
                    both, cells[kd], (((1,), (1,)), ((), ())), preferred_element_type=F32
                )
                sums[kd] = term if sums[kd] is None else sums[kd] + term
    for kw in range(3):
        for kd in range(3):
            for kh in range(3):
                at = (kw * 9 + kd * 3 + kh) * cin
                total[:, at : at + cin] = sums[kd][kw * cout : (kw + 1) * cout, kh * cin : (kh + 1) * cin]
    total[:, 27 * cin :] = jnp.broadcast_to(jnp.sum(bias_sum, axis=1, keepdims=True), (cout, cin))
    half = 14 * cin
    even = core[0] == 0
    low, high = total[:, :half], total[:, half:]
    sent_ref[...] = jnp.where(even, high, low).astype(BF16)
    kept_ref[...] = jnp.where(even, low, high)


def backward_kernel(rows, planes, w_ref, own, low, high, before, after, out_ref, stack):
    cout, width = own.shape[1:]
    cin = w_ref.shape[0]
    groups = out_ref.shape[0]
    part = cin // groups
    lane = lax.broadcasted_iota(jnp.int32, (cout, width), 1)
    step = 3 * cout
    for p in range(planes + 2):
        for r in range(rows + 2):
            if r == 0:
                value = before[p]
            elif r == rows + 1:
                value = after[p]
            elif p == 0:
                value = low[r - 1]
            elif p == planes + 1:
                value = high[r - 1]
            else:
                value = own[(p - 1) * rows + r - 1]
            stack[p, r * step : (r + 1) * step, :] = shifted(value.astype(F32), lane).astype(BF16)
    w = w_ref[...]
    for d in range(planes):
        for h in range(0, rows, 2):
            cells = jnp.concatenate(
                [
                    jnp.concatenate(
                        [stack[d + a, (h + e) * step : (h + e + 3) * step, :] for a in range(3)], axis=0
                    )
                    for e in range(2)
                ],
                axis=1,
            )
            acc = jnp.dot(w, cells, preferred_element_type=F32)
            at = (d * rows + h) // 2
            for f in range(groups):
                piece = acc[f * part : (f + 1) * part]
                out_ref[f, at] = jnp.concatenate([piece[:, :width], piece[:, width:]], axis=0).astype(BF16)


def per_device(activations, weights, bias, cotangent):
    cin_dev, planes, rows, width = activations.shape
    taps, cin, cout = weights.shape
    cells = planes * rows
    depth = lax.axis_size("depth")
    core = lax.axis_index("depth") % 2
    pairs = [(i, i ^ 1) for i in range(depth)]
    groups = [[i for i in range(depth) if i % 2 == c] for c in range(2)]
    struct = jax.ShapeDtypeStruct

    mine = activations.transpose(1, 2, 0, 3)
    full = spread(mine, "filt").transpose(1, 2, 0, 3, 4).reshape(planes, rows * cin, width)
    low, high = exchange(full[0], full[planes - 1], "depth")
    grid = [low] + [full[d] for d in range(planes)] + [high]
    before, after = exchange(*rim_rows(grid, cin), "height")

    split = weights.reshape(3, 3, 3, cin, cout)
    w_forward = split.transpose(0, 2, 4, 1, 3).reshape(3, 3 * cout, 3 * cin)
    w_back = split[::-1, ::-1].transpose(3, 0, 1, 2, 4).reshape(cin, taps * cout)
    cot = cotangent.transpose(1, 2, 0, 3).reshape(cells, cout, width)
    work = 2 * cells * width * taps * cin * cout
    half = 14 * cin
    vmem = pl.BlockSpec(memory_space=pltpu.VMEM)
    out, grad, sent, kept = pl.pallas_call(
        functools.partial(forward_kernel, rows, planes),
        out_shape=(
            struct((cells, cout, width), BF16),
            struct((cells, cout, width), BF16),
            struct((cout, half), BF16),
            struct((cout, half), F32),
        ),
        in_specs=[pl.BlockSpec(memory_space=pltpu.SMEM)] + [vmem] * (planes + 7),
        out_specs=(vmem,) * 4,
        scratch_shapes=[pltpu.VMEM((cout, 2 * half), F32)],
        cost_estimate=pl.CostEstimate(flops=2 * work, bytes_accessed=1 << 20, transcendentals=1 << 17),
        name="forward",
    )(
        core.reshape(1).astype(jnp.int32),
        w_forward,
        jnp.broadcast_to(bias[:, None], (cout, width)),
        cot,
        *grid,
        before,
        after,
    )
    output = out.reshape(planes, rows, cout, width).transpose(2, 0, 1, 3)

    mine = (kept + lax.ppermute(sent, "depth", pairs).astype(F32)).astype(BF16)
    mine, grad = lax.optimization_barrier((mine, grad))
    mine = jnp.sum(spread(mine, "depth", groups).astype(F32), axis=0).astype(BF16)
    mine = jnp.sum(spread(mine, "height").astype(F32), axis=0)
    other = lax.ppermute(mine, "depth", pairs)
    total = jnp.concatenate(
        [jnp.where(core == 0, mine, other), jnp.where(core == 0, other, mine)], axis=1
    )
    weight_grad = total[:, : taps * cin].reshape(cout, 3, 3, 3, cin)
    weight_grad = weight_grad.transpose(2, 3, 1, 4, 0).reshape(taps, cin, cout)
    bias_grad = total[:, taps * cin]

    by_plane = grad.reshape(planes, rows, cout, width)
    low, high = exchange(by_plane[0], by_plane[planes - 1], "depth")
    edge = [low] + [by_plane[d] for d in range(planes)] + [high]
    before, after = exchange(
        jnp.stack([p[0] for p in edge]), jnp.stack([p[rows - 1] for p in edge]), "height"
    )
    filt = lax.axis_size("filt")
    parts = pl.pallas_call(
        functools.partial(backward_kernel, rows, planes),
        out_shape=struct((filt, cells // 2, 2 * cin_dev, width), BF16),
        in_specs=[vmem] * 6,
        out_specs=vmem,
        scratch_shapes=[pltpu.VMEM((planes + 2, (rows + 2) * 3 * cout, width), BF16)],
        cost_estimate=pl.CostEstimate(flops=work, bytes_accessed=1 << 19, transcendentals=0),
        name="backward",
    )(w_back, grad, low, high, before, after)
    parts = lax.all_to_all(parts, "filt", 0, 0, tiled=True)
    summed = jnp.sum(parts.astype(F32), axis=0).astype(BF16)
    summed = summed.reshape(planes, rows, cin_dev, width).transpose(2, 0, 1, 3)
    return (output, summed, weight_grad, bias_grad)


def solution(mesh):
    placed = (
        P("filt", "depth", "height", None),
        P(None, None, "filt"),
        P("filt"),
        P("filt", "depth", "height", None),
    )
    return jax.shard_map(
        per_device,
        mesh=mesh,
        in_specs=placed,
        out_specs=(
            P("filt", "depth", "height", None),
            P("filt", "depth", "height", None),
            P(None, None, "filt"),
            P("filt"),
        ),
        check_vma=False,
    )
```

time: 607 us -> 100 us (0.16)
  the two profiles are of different devices: /device:TPU:8 before, /device:TPU:1 now
where the time goes in v2:
time: 100 us; the launch traced here: 99.2 us
  starting transfers between devices  48.8 us (49%)
  waiting for transfers between devices  19.5 us (20%)
  blocking collectives  11.8 us (12%)
  local copies, waits for them, and re-layouts  9.98 us (10%)
  Pallas kernels  7.04 us (7%)
  between operations  1.07 us (1%)
    ppermute x4, starting transfers between devices, exchange(): before = lax.ppermute(last, axis, [(i, i + 1) for i in range(ends)])  20.6 us
    all_to_all x2, starting transfers between devices, spread(): lax.all_to_all(copies, axis, 0, 0, tiled=True, axis_index_groups=groups)  13.8 us
    all_to_all x1, blocking collectives, spread(): lax.all_to_all(copies, axis, 0, 0, tiled=True, axis_index_groups=groups)  11.8 us
    ppermute x4, waiting for transfers between devices, exchange(): after = lax.ppermute(first, axis, [(i + 1, i) for i in range(ends)])  8.37 us
    ppermute x4, starting transfers between devices, exchange(): after = lax.ppermute(first, axis, [(i + 1, i) for i in range(ends)])  6.56 us
    all_to_all x2, waiting for transfers between devices, spread(): lax.all_to_all(copies, axis, 0, 0, tiled=True, axis_index_groups=groups)  6.37 us
    pallas_call x1, Pallas kernels, per_device(): pl.pallas_call(functools.partial(forward_kernel, rows, planes), out_shape...  4.93 us
    all_to_all x1, waiting for transfers between devices, per_device(): parts = lax.all_to_all(parts, 'filt', 0, 0, tiled=True)  3.43 us
  transfers between devices with their start and end apart: 13, of which 6 were waited for; matrix products, arithmetic and copies ran while one was open for 5% of the time, Pallas kernels for 2%

profile of v2, /device:TPU:1, one launch (start us, length us, event | category | flops | bytes accessed | tf_op | source)
XLA Modules:
  0.0 99.2 jit_solution(15100314815400254329)
XLA Ops:
  0.6 0.8 copy.49
  1.5 11.8 %all_to_all.20 = bf16[8,2,8,8,128]{4,3,2,1,0:T(8,128)(2,1)S(1)} all-to-all(bf16[8,2,8,8,128]{4,3,2,1,0:T(8,128)(2,1)S(1)} %broadcast_in_dim.9), channel_id=1, replica_groups=mesh['depth'=8,'height'=8,'filt'=8] {'filt'}, dimensions={0} | all-to-all | bytes 524288 | tf_op jit(solution)/shard_map/all_to_all | solution.py:24
  13.3 6.2 %collective-permute-start = (bf16[512,128]{1,0:T(8,128)(2,1)S(1)}, bf16[512,128]{1,0:T(8,128)(2,1)S(1)}, u32[]{:S(2)}, u32[]{:S(2)}) collective-permute-start(bf16[512,128]{1,0:T(8,128)(2,1)S(1)} %bitcast.38), channel_id=1, source_target_pairs={{0,64},{64,128},{128,192},{192,256},{256,320},{320,384},{384,448},... | collective-permute-start | bytes 393224 | tf_op jit(solution)/shard_map/ppermute | solution.py:16
  19.6 1.9 %collective-permute-start.1 = (bf16[512,128]{1,0:T(8,128)(2,1)S(1)}, bf16[512,128]{1,0:T(8,128)(2,1)S(1)}, u32[]{:S(2)}, u32[]{:S(2)}) collective-permute-start(bf16[512,128]{1,0:T(8,128)(2,1)S(1)} %bitcast.40), channel_id=1, source_target_pairs={{64,0},{128,64},{192,128},{256,192},{320,256},{384,320},{448,384},... | collective-permute-start | bytes 393224 | tf_op jit(solution)/shard_map/ppermute | solution.py:17
  21.5 0.0 collective-permute-done.refs_0_
  21.5 0.0 copy-start.10
  21.6 6.6 %collective-permute-done.1.refs_3_ = bf16[512,128]{1,0:T(8,128)(2,1)S(1)} collective-permute-done((bf16[512,128]{1,0:T(8,128)(2,1)S(1)}, bf16[512,128]{1,0:T(8,128)(2,1)S(1)}, u32[]{:S(2)}, u32[]{:S(2)}) %collective-permute-start.1) | collective-permute-done | bytes 131104 | tf_op jit(solution)/shard_map/ppermute | solution.py:17
  28.2 0.0 copy-start
  28.2 1.4 %collective-permute-start.3 = (bf16[256,128]{1,0:T(8,128)(2,1)S(1)}, bf16[256,128]{1,0:T(8,128)(2,1)S(1)}, u32[]{:S(2)}, u32[]{:S(2)}) collective-permute-start(bf16[256,128]{1,0:T(8,128)(2,1)S(1)} %pad_maximum_fusion.2), channel_id=1, source_target_pairs={{8,0},{16,8},{24,16},{32,24},{40,32},{48,40},{56,48},{9,1},{17,9},... | collective-permute-start | bytes 196616 | tf_op jit(solution)/shard_map/ppermute | solution.py:17
  29.7 4.6 %collective-permute-start.2 = (bf16[256,128]{1,0:T(8,128)(2,1)S(1)}, bf16[256,128]{1,0:T(8,128)(2,1)S(1)}, u32[]{:S(2)}, u32[]{:S(2)}) collective-permute-start(bf16[256,128]{1,0:T(8,128)(2,1)S(1)} %pad_maximum_fusion.1), channel_id=1, source_target_pairs={{0,8},{8,16},{16,24},{24,32},{32,40},{40,48},{48,56},{1,9},{9,17},... | collective-permute-start | bytes 196616 | tf_op jit(solution)/shard_map/ppermute | solution.py:16
  34.3 0.1 copy.47
  34.4 0.0 copy-start.4
  34.4 0.8 reshape.55.w_ref
  35.2 0.1 copy-done.4
  35.2 0.6 copy.48
  35.9 0.0 collective-permute-done.3.refs_5_
  35.9 0.0 copy-start.12
  35.9 0.7 copy-done.12
  36.6 0.7 broadcast_in_dim.8.bias_ref
  37.3 4.9 %forward.1 = (bf16[16,16,128]{2,1,0:T(8,128)(2,1)}, bf16[16,16,128]{2,1,0:T(8,128)(2,1)}, bf16[16,896]{1,0:T(8,128)(2,1)}, f32[16,896]{1,0:T(8,128)}) custom-call(s32[1]{0:T(128)} %bitcast.core, bf16[3,48,192]{2,1,0:T(8,128)(2,1)} %reshape.55.w_ref, f32[16,128]{1,0:T(8,128)} %broadcast_in_dim.8.bias_ref, bf16[16,16,128]{2,1,0:T(8,128)(2,1)} %bitcast.45, ...), custom_call_target="tpu_custom_call" | custom-call | flops 226492416 | bytes 1048576 | tf_op jit(solution)/shard_map/forward/pallas_call | solution.py:172
  42.2 2.0 %collective-permute-start.4 = (bf16[16,896]{1,0:T(8,128)(2,1)}, bf16[16,896]{1,0:T(8,128)(2,1)S(1)}, u32[]{:S(2)}, u32[]{:S(2)}) collective-permute-start(bf16[16,896]{1,0:T(8,128)(2,1)} %get-tuple-element.12), channel_id=1, source_target_pairs={{0,64},{64,0},{128,192},{192,128},{256,320},{320,256},{384,448},{4... | collective-permute-start | bytes 86024 | tf_op jit(solution)/shard_map/ppermute | solution.py:196
  44.3 1.4 %collective-permute-done.4 = bf16[16,896]{1,0:T(8,128)(2,1)S(1)} collective-permute-done((bf16[16,896]{1,0:T(8,128)(2,1)}, bf16[16,896]{1,0:T(8,128)(2,1)S(1)}, u32[]{:S(2)}, u32[]{:S(2)}) %collective-permute-start.4) | collective-permute-done | bytes 28704 | tf_op jit(solution)/shard_map/ppermute | solution.py:196
  45.6 0.8 add_convert_fusion
  46.5 5.8 %collective-permute-start.5 = (bf16[8,16,128]{2,1,0:T(8,128)(2,1)S(1)}, bf16[8,16,128]{2,1,0:T(8,128)(2,1)S(1)}, u32[]{:S(2)}, u32[]{:S(2)}) collective-permute-start(bf16[8,16,128]{2,1,0:T(8,128)(2,1)S(1)} %get-tuple-element.53), channel_id=1, source_target_pairs={{0,64},{64,128},{128,192},{192,256},{256,320},{320,384},{384,448},... | collective-permute-start | bytes 98312 | tf_op jit(solution)/shard_map/ppermute | solution.py:16
  52.3 0.7 broadcast_in_dim.10
  52.9 3.3 %all-to-all-start.2 = ((bf16[4,16,896]{2,1,0:T(8,128)(2,1)}), bf16[4,16,896]{2,1,0:T(8,128)(2,1)S(1)}, u32[]{:S(2)}, u32[]{:S(2)}) async-start(bf16[4,16,896]{2,1,0:T(8,128)(2,1)} %broadcast_in_dim.10), calls=%async_computation.2 | async-start | bytes 229376 | tf_op jit(solution)/shard_map/all_to_all | solution.py:24
  56.3 1.9 %collective-permute-start.6 = (bf16[8,16,128]{2,1,0:T(8,128)(2,1)S(1)}, bf16[8,16,128]{2,1,0:T(8,128)(2,1)S(1)}, u32[]{:S(2)}, u32[]{:S(2)}) collective-permute-start(bf16[8,16,128]{2,1,0:T(8,128)(2,1)S(1)} %get-tuple-element.52), channel_id=1, source_target_pairs={{64,0},{128,64},{192,128},{256,192},{320,256},{384,320},{448,384},... | collective-permute-start | bytes 98312 | tf_op jit(solution)/shard_map/ppermute | solution.py:17
  58.2 0.0 copy-start.6
  58.2 5.8 %all-to-all-done.2 = bf16[4,16,896]{2,1,0:T(8,128)(2,1)S(1)} async-done(((bf16[4,16,896]{2,1,0:T(8,128)(2,1)}), bf16[4,16,896]{2,1,0:T(8,128)(2,1)S(1)}, u32[]{:S(2)}, u32[]{:S(2)}) %all-to-all-start.2) | async-done | bytes 114720 | tf_op jit(solution)/shard_map/all_to_all | solution.py:24
  64.1 0.7 broadcast_in_dim.11
  64.8 10.5 %all-to-all-start.3 = ((bf16[8,16,896]{2,1,0:T(8,128)(2,1)}), bf16[8,16,896]{2,1,0:T(8,128)(2,1)S(1)}, u32[]{:S(2)}, u32[]{:S(2)}) async-start(bf16[8,16,896]{2,1,0:T(8,128)(2,1)} %broadcast_in_dim.11), calls=%async_computation.3 | async-start | bytes 458752 | tf_op jit(solution)/shard_map/all_to_all | solution.py:24
  75.3 0.0 copy-start.7
  75.3 1.3 %collective-permute-start.8 = (bf16[4,16,128]{2,1,0:T(8,128)(2,1)S(1)}, bf16[4,16,128]{2,1,0:T(8,128)(2,1)S(1)}, u32[]{:S(2)}, u32[]{:S(2)}) collective-permute-start(bf16[4,16,128]{2,1,0:T(8,128)(2,1)S(1)} %pad_maximum_fusion.4), channel_id=1, source_target_pairs={{8,0},{16,8},{24,16},{32,24},{40,32},{48,40},{56,48},{9,1},{17,9},... | collective-permute-start | bytes 49160 | tf_op jit(solution)/shard_map/ppermute | solution.py:17
  76.7 4.0 %collective-permute-start.7 = (bf16[4,16,128]{2,1,0:T(8,128)(2,1)S(1)}, bf16[4,16,128]{2,1,0:T(8,128)(2,1)S(1)}, u32[]{:S(2)}, u32[]{:S(2)}) collective-permute-start(bf16[4,16,128]{2,1,0:T(8,128)(2,1)S(1)} %pad_maximum_fusion.3), channel_id=1, source_target_pairs={{0,8},{8,16},{16,24},{24,32},{32,40},{40,48},{48,56},{1,9},{9,17},... | collective-permute-start | bytes 49160 | tf_op jit(solution)/shard_map/ppermute | solution.py:16
  80.7 0.7 copy.53.w_ref
  81.4 1.8 %collective-permute-done.8.after = bf16[4,16,128]{2,1,0:T(8,128)(2,1)S(1)} collective-permute-done((bf16[4,16,128]{2,1,0:T(8,128)(2,1)S(1)}, bf16[4,16,128]{2,1,0:T(8,128)(2,1)S(1)}, u32[]{:S(2)}, u32[]{:S(2)}) %collective-permute-start.8) | collective-permute-done | bytes 16416 | tf_op jit(solution)/shard_map/ppermute | solution.py:17
  83.2 0.6 copy-done.8
  83.7 0.6 copy-done.9
  84.3 2.1 %backward.1 = bf16[8,8,16,128]{3,2,1,0:T(8,128)(2,1)} custom-call(bf16[64,432]{1,0:T(8,128)(2,1)} %copy.53.w_ref, bf16[16,16,128]{2,1,0:T(8,128)(2,1)} %get-tuple-element.14.own, bf16[8,16,128]{2,1,0:T(8,128)(2,1)} %copy-done.6, bf16[8,16,128]{2,1,0:T(8,128)(2,1)} %copy-done.7, bf16[4,16,128]{2,1,0:T(8,128)(2,1)} %copy-done.9, bf16[4,16,128]{2,1,0:T(8,128)(2,1)} %copy-done.8), custom_call_target="tpu_custom_call" | custom-call | flops 113246208 | bytes 524288 | tf_op jit(solution)/shard_map/backward/pallas_call | solution.py:215
  86.5 0.5 all-to-all-done.3
  87.0 3.4 %all-to-all-start.1 = ((bf16[8,8,16,128]{3,2,1,0:T(8,128)(2,1)}), bf16[8,8,16,128]{3,2,1,0:T(8,128)(2,1)S(1)}, u32[]{:S(2)}, u32[]{:S(2)}) async-start(bf16[8,8,16,128]{3,2,1,0:T(8,128)(2,1)} %backward.1), calls=%async_computation.1 | async-start | bytes 524288 | tf_op jit(solution)/shard_map/all_to_all | solution.py:224
  90.5 2.4 %collective-permute-start.9 = (f32[16,896]{1,0:T(8,128)S(1)}, f32[16,896]{1,0:T(8,128)S(1)}, u32[]{:S(2)}, u32[]{:S(2)}) collective-permute-start(f32[16,896]{1,0:T(8,128)S(1)} %convert_reduce_fusion), channel_id=1, source_target_pairs={{0,64},{64,0},{128,192},{192,128},{256,320},{320,256},{384,448},{4... | collective-permute-start | bytes 172040 | tf_op jit(solution)/shard_map/ppermute | solution.py:200
  92.9 0.6 copy.57
  93.5 3.4 %all-to-all-done.1 = bf16[8,8,16,128]{3,2,1,0:T(8,128)(2,1)S(1)} async-done(((bf16[8,8,16,128]{3,2,1,0:T(8,128)(2,1)}), bf16[8,8,16,128]{3,2,1,0:T(8,128)(2,1)S(1)}, u32[]{:S(2)}, u32[]{:S(2)}) %all-to-all-start.1) | async-done | bytes 262176 | tf_op jit(solution)/shard_map/all_to_all | solution.py:224
  97.0 0.6 copy.55
  97.6 0.7 slice_reduce_fusion
  98.3 0.2 reshape.60
  98.5 0.7 copy.54
  (46 shorter events, 0.4 us)
Async XLA Ops:
  13.3 6.3 %copy-start.2 = (bf16[1,8,8,8,128]{4,3,2,1,0:T(8,128)(2,1)}, bf16[1,8,8,8,128]{4,3,2,1,0:T(8,128)(2,1)S(1)}, u32[]{:S(2)}) copy-start(bf16[1,8,8,8,128]{4,3,2,1,0:T(8,128)(2,1)S(1)} %copy.50) | copy-start | bytes 393220
  13.3 8.2 %collective-permute-start = (bf16[512,128]{1,0:T(8,128)(2,1)S(1)}, bf16[512,128]{1,0:T(8,128)(2,1)S(1)}, u32[]{:S(2)}, u32[]{:S(2)}) collective-permute-start(bf16[512,128]{1,0:T(8,128)(2,1)S(1)} %bitcast.38), channel_id=1, source_target_pairs={{0,64},{64,128},{128,192},{192,256},{256,320},{320,384},{384,448},... | collective-permute-start | bytes 393224 | tf_op jit(solution)/shard_map/ppermute | solution.py:16
  19.6 8.6 %copy-start.3 = (bf16[1,8,8,8,128]{4,3,2,1,0:T(8,128)(2,1)}, bf16[1,8,8,8,128]{4,3,2,1,0:T(8,128)(2,1)S(1)}, u32[]{:S(2)}) copy-start(bf16[1,8,8,8,128]{4,3,2,1,0:T(8,128)(2,1)S(1)} %copy.51) | copy-start | bytes 393220
  19.6 8.6 %collective-permute-start.1 = (bf16[512,128]{1,0:T(8,128)(2,1)S(1)}, bf16[512,128]{1,0:T(8,128)(2,1)S(1)}, u32[]{:S(2)}, u32[]{:S(2)}) collective-permute-start(bf16[512,128]{1,0:T(8,128)(2,1)S(1)} %bitcast.40), channel_id=1, source_target_pairs={{64,0},{128,64},{192,128},{256,192},{320,256},{384,320},{448,384},... | collective-permute-start | bytes 393224 | tf_op jit(solution)/shard_map/ppermute | solution.py:17
  21.5 6.7 %copy-start.10 = (bf16[512,128]{1,0:T(8,128)(2,1)}, bf16[512,128]{1,0:T(8,128)(2,1)S(1)}, u32[]{:S(2)}) copy-start(bf16[512,128]{1,0:T(8,128)(2,1)S(1)} %collective-permute-done.refs_0_) | copy-start | bytes 393220
  28.2 1.5 %copy-start.11 = (bf16[512,128]{1,0:T(8,128)(2,1)}, bf16[512,128]{1,0:T(8,128)(2,1)S(1)}, u32[]{:S(2)}) copy-start(bf16[512,128]{1,0:T(8,128)(2,1)S(1)} %collective-permute-done.1.refs_3_) | copy-start | bytes 393220
  28.2 6.1 %copy-start = (bf16[27,64,16]{1,2,0:T(8,128)(2,1)S(1)}, bf16[27,64,16]{1,2,0:T(8,128)(2,1)}, u32[]{:S(2)}) copy-start(bf16[27,64,16]{1,2,0:T(8,128)(2,1)} %param.5) | copy-start | bytes 165892
  28.2 7.7 %collective-permute-start.3 = (bf16[256,128]{1,0:T(8,128)(2,1)S(1)}, bf16[256,128]{1,0:T(8,128)(2,1)S(1)}, u32[]{:S(2)}, u32[]{:S(2)}) collective-permute-start(bf16[256,128]{1,0:T(8,128)(2,1)S(1)} %pad_maximum_fusion.2), channel_id=1, source_target_pairs={{8,0},{16,8},{24,16},{32,24},{40,32},{48,40},{56,48},{9,1},{17,9},... | collective-permute-start | bytes 196616 | tf_op jit(solution)/shard_map/ppermute | solution.py:17
  29.7 6.2 %collective-permute-start.2 = (bf16[256,128]{1,0:T(8,128)(2,1)S(1)}, bf16[256,128]{1,0:T(8,128)(2,1)S(1)}, u32[]{:S(2)}, u32[]{:S(2)}) collective-permute-start(bf16[256,128]{1,0:T(8,128)(2,1)S(1)} %pad_maximum_fusion.1), channel_id=1, source_target_pairs={{0,8},{8,16},{16,24},{24,32},{32,40},{40,48},{48,56},{1,9},{9,17},... | collective-permute-start | bytes 196616 | tf_op jit(solution)/shard_map/ppermute | solution.py:16
  34.4 0.8 copy-start.4
  35.9 1.4 %copy-start.13 = (bf16[256,128]{1,0:T(8,128)(2,1)}, bf16[256,128]{1,0:T(8,128)(2,1)S(1)}, u32[]{:S(2)}) copy-start(bf16[256,128]{1,0:T(8,128)(2,1)S(1)} %collective-permute-done.3.refs_5_) | copy-start | bytes 196612
  35.9 1.4 %copy-start.14 = (bf16[256,128]{1,0:T(8,128)(2,1)}, bf16[256,128]{1,0:T(8,128)(2,1)S(1)}, u32[]{:S(2)}) copy-start(bf16[256,128]{1,0:T(8,128)(2,1)S(1)} %collective-permute-done.2.refs_4_) | copy-start | bytes 196612
  35.9 0.7 copy-start.12
  42.2 4.3 %copy-start.1 = (bf16[16,16,128]{2,1,0:T(8,128)(2,1)S(1)}, bf16[16,16,128]{2,1,0:T(8,128)(2,1)}, u32[]{:S(2)}) copy-start(bf16[16,16,128]{2,1,0:T(8,128)(2,1)} %get-tuple-element.14.own) | copy-start | bytes 196612
  42.2 3.4 %collective-permute-start.4 = (bf16[16,896]{1,0:T(8,128)(2,1)}, bf16[16,896]{1,0:T(8,128)(2,1)S(1)}, u32[]{:S(2)}, u32[]{:S(2)}) collective-permute-start(bf16[16,896]{1,0:T(8,128)(2,1)} %get-tuple-element.12), channel_id=1, source_target_pairs={{0,64},{64,0},{128,192},{192,128},{256,320},{320,256},{384,448},{4... | collective-permute-start | bytes 86024 | tf_op jit(solution)/shard_map/ppermute | solution.py:196
  46.5 11.7 %collective-permute-start.5 = (bf16[8,16,128]{2,1,0:T(8,128)(2,1)S(1)}, bf16[8,16,128]{2,1,0:T(8,128)(2,1)S(1)}, u32[]{:S(2)}, u32[]{:S(2)}) collective-permute-start(bf16[8,16,128]{2,1,0:T(8,128)(2,1)S(1)} %get-tuple-element.53), channel_id=1, source_target_pairs={{0,64},{64,128},{128,192},{192,256},{256,320},{320,384},{384,448},... | collective-permute-start | bytes 98312 | tf_op jit(solution)/shard_map/ppermute | solution.py:16
  52.9 11.1 %all-to-all-start.2 = ((bf16[4,16,896]{2,1,0:T(8,128)(2,1)}), bf16[4,16,896]{2,1,0:T(8,128)(2,1)S(1)}, u32[]{:S(2)}, u32[]{:S(2)}) async-start(bf16[4,16,896]{2,1,0:T(8,128)(2,1)} %broadcast_in_dim.10), calls=%async_computation.2 | async-start | bytes 229376 | tf_op jit(solution)/shard_map/all_to_all | solution.py:24
  56.3 19.0 %collective-permute-start.6 = (bf16[8,16,128]{2,1,0:T(8,128)(2,1)S(1)}, bf16[8,16,128]{2,1,0:T(8,128)(2,1)S(1)}, u32[]{:S(2)}, u32[]{:S(2)}) collective-permute-start(bf16[8,16,128]{2,1,0:T(8,128)(2,1)S(1)} %get-tuple-element.52), channel_id=1, source_target_pairs={{64,0},{128,64},{192,128},{256,192},{320,256},{384,320},{448,384},... | collective-permute-start | bytes 98312 | tf_op jit(solution)/shard_map/ppermute | solution.py:17
  58.2 5.9 %copy-start.6 = (bf16[8,16,128]{2,1,0:T(8,128)(2,1)}, bf16[8,16,128]{2,1,0:T(8,128)(2,1)S(1)}, u32[]{:S(2)}) copy-start(bf16[8,16,128]{2,1,0:T(8,128)(2,1)S(1)} %collective-permute-done.5.low) | copy-start | bytes 98308
  64.8 22.2 %all-to-all-start.3 = ((bf16[8,16,896]{2,1,0:T(8,128)(2,1)}), bf16[8,16,896]{2,1,0:T(8,128)(2,1)S(1)}, u32[]{:S(2)}, u32[]{:S(2)}) async-start(bf16[8,16,896]{2,1,0:T(8,128)(2,1)} %broadcast_in_dim.11), calls=%async_computation.3 | async-start | bytes 458752 | tf_op jit(solution)/shard_map/all_to_all | solution.py:24
  75.3 1.4 %copy-start.7 = (bf16[8,16,128]{2,1,0:T(8,128)(2,1)}, bf16[8,16,128]{2,1,0:T(8,128)(2,1)S(1)}, u32[]{:S(2)}) copy-start(bf16[8,16,128]{2,1,0:T(8,128)(2,1)S(1)} %collective-permute-done.6.high) | copy-start | bytes 98308
  75.3 7.8 %collective-permute-start.8 = (bf16[4,16,128]{2,1,0:T(8,128)(2,1)S(1)}, bf16[4,16,128]{2,1,0:T(8,128)(2,1)S(1)}, u32[]{:S(2)}, u32[]{:S(2)}) collective-permute-start(bf16[4,16,128]{2,1,0:T(8,128)(2,1)S(1)} %pad_maximum_fusion.4), channel_id=1, source_target_pairs={{8,0},{16,8},{24,16},{32,24},{40,32},{48,40},{56,48},{9,1},{17,9},... | collective-permute-start | bytes 49160 | tf_op jit(solution)/shard_map/ppermute | solution.py:17
  76.7 6.5 %collective-permute-start.7 = (bf16[4,16,128]{2,1,0:T(8,128)(2,1)S(1)}, bf16[4,16,128]{2,1,0:T(8,128)(2,1)S(1)}, u32[]{:S(2)}, u32[]{:S(2)}) collective-permute-start(bf16[4,16,128]{2,1,0:T(8,128)(2,1)S(1)} %pad_maximum_fusion.3), channel_id=1, source_target_pairs={{0,8},{8,16},{16,24},{24,32},{32,40},{40,48},{48,56},{1,9},{9,17},... | collective-permute-start | bytes 49160 | tf_op jit(solution)/shard_map/ppermute | solution.py:16
  83.1 0.6 copy-start.8
  83.7 0.6 copy-start.9
  87.0 10.0 %all-to-all-start.1 = ((bf16[8,8,16,128]{3,2,1,0:T(8,128)(2,1)}), bf16[8,8,16,128]{3,2,1,0:T(8,128)(2,1)S(1)}, u32[]{:S(2)}, u32[]{:S(2)}) async-start(bf16[8,8,16,128]{3,2,1,0:T(8,128)(2,1)} %backward.1), calls=%async_computation.1 | async-start | bytes 524288 | tf_op jit(solution)/shard_map/all_to_all | solution.py:224
  90.4 2.5 %copy-start.5 = (bf16[16,16,128]{2,1,0:T(8,128)(2,1)S(1)}, bf16[16,16,128]{2,1,0:T(8,128)(2,1)}, u32[]{:S(2)}) copy-start(bf16[16,16,128]{2,1,0:T(8,128)(2,1)} %get-tuple-element.10) | copy-start | bytes 196612
  90.5 7.2 %collective-permute-start.9 = (f32[16,896]{1,0:T(8,128)S(1)}, f32[16,896]{1,0:T(8,128)S(1)}, u32[]{:S(2)}, u32[]{:S(2)}) collective-permute-start(f32[16,896]{1,0:T(8,128)S(1)} %convert_reduce_fusion), channel_id=1, source_target_pairs={{0,64},{64,0},{128,192},{192,128},{256,320},{320,256},{384,448},{4... | collective-permute-start | bytes 172040 | tf_op jit(solution)/shard_map/ppermute | solution.py:200

commit v3 on v2

v3 whole, which is shorter than its diff:
```python
import functools

import jax
import jax.numpy as jnp
import numpy as np
from jax import lax
from jax.experimental import pallas as pl
from jax.experimental.pallas import tpu as pltpu
from jax.sharding import PartitionSpec as P

BF16 = jnp.bfloat16
F32 = jnp.float32
PART = 8


def spread(block, axis, groups=None):
    members = lax.axis_size(axis) if groups is None else len(groups[0])
    copies = jnp.broadcast_to(block[None], (members,) + block.shape)
    return lax.all_to_all(copies, axis, 0, 0, tiled=True, axis_index_groups=groups)


def neighbours(first, last, axis):
    ends = lax.axis_size(axis) - 1
    before = lax.ppermute(last, axis, [(i, i + 1) for i in range(ends)])
    after = lax.ppermute(first, axis, [(i + 1, i) for i in range(ends)])
    return before, after


def shifted(value, lane):
    width = value.shape[-1]
    ahead = jnp.where(lane == width - 1, 0.0, pltpu.roll(value, width - 1, 1))
    behind = jnp.where(lane == 0, 0.0, pltpu.roll(value, 1, 1))
    return jnp.concatenate([ahead, value, behind], axis=0)


def forward_kernel(planes, rows, at_ref, w_ref, bias_ref, cot, cot_before, cot_after, tiles, *refs):
    out_ref, face_ref, far_ref, kept_ref, grads, halves = refs
    cout, width = cot.shape[1:]
    sources = tiles.shape[0]
    lane = lax.broadcasted_iota(jnp.int32, (cout, width), 1)
    bias = bias_ref[...]
    sums = [None] * 3
    bias_sum = jnp.zeros((cout, width), F32)
    for d in range(planes):
        for pair in range(rows // 2 + 1):
            cells = [
                jnp.concatenate(
                    [tiles[s, d + kd, pair + t] for t in range(2) for s in range(sources)], axis=0
                )
                for kd in range(3)
            ]
            acc = jnp.dot(w_ref[0], cells[0], preferred_element_type=F32)
            for kd in range(1, 3):
                acc = acc + jnp.dot(w_ref[kd], cells[kd], preferred_element_type=F32)
            stacks = []
            for e in range(2):
                z = acc[3 * e * cout : 3 * (e + 1) * cout]
                pre = (
                    z[cout : 2 * cout]
                    + jnp.where(lane == 0, 0.0, pltpu.roll(z[:cout], 1, 1))
                    + jnp.where(lane == width - 1, 0.0, pltpu.roll(z[2 * cout :], width - 1, 1))
                    + bias
                )
                small = jnp.exp(-jnp.abs(pre))
                sigmoid = jnp.where(pre >= 0, 1.0, small) / (1.0 + small)
                row = 2 * pair + e
                if row == 0:
                    cotangent = cot_before[d]
                elif row == rows + 1:
                    cotangent = cot_after[d]
                else:
                    cotangent = cot[d * rows + row - 1]
                grad = (cotangent.astype(F32) * (0.2 + 0.8 * sigmoid)).astype(BF16)
                grads[d, row] = grad
                if row == 0 or row == rows + 1:
                    stacks.append(jnp.zeros((3 * cout, width), BF16))
                    continue
                softplus = jnp.maximum(pre, 0.0) + jnp.log1p(small)
                out_ref[d * rows + row - 1] = (0.2 * pre + 0.8 * softplus).astype(BF16)
                grad = grad.astype(F32)
                bias_sum = bias_sum + grad
                stacks.append(shifted(grad, lane).astype(BF16))
            both = jnp.concatenate(stacks, axis=0)
            for kd in range(3):
                term = lax.dot_general(
                    both, cells[kd], (((1,), (1,)), ((), ())), preferred_element_type=F32
                )
                sums[kd] = term if sums[kd] is None else sums[kd] + term

    even = (lane // PART) % 2 == 0
    blocks, last = [], []
    for kd in range(3):
        for kw in range(3):
            one = sums[kd][kw * cout : (kw + 1) * cout]
            two = sums[kd][(3 + kw) * cout : (4 + kw) * cout]
            back = pltpu.roll(two[:, width:], width - PART, 1)
            blocks.append(
                one[:, :width]
                + jnp.where(
                    even,
                    pltpu.roll(two[:, :width], width - PART, 1),
                    pltpu.roll(two[:, width:], PART, 1),
                )
            )
            last.append(one[:, width:] + back)
    last.append(jnp.broadcast_to(jnp.sum(bias_sum, axis=1, keepdims=True), (cout, width)))
    for k in range(0, len(last), 2):
        blocks.append(jnp.where(even, last[k], pltpu.roll(last[k + 1], PART, 1)))
    source = lax.broadcasted_iota(jnp.int32, (width, width), 0)
    target = (source // PART) % 2 * (width // 2) + source // (2 * PART) * PART + source % PART
    order = jnp.where(lax.broadcasted_iota(jnp.int32, (width, width), 1) == target, 1.0, 0.0).astype(BF16)
    placed = jnp.dot(jnp.concatenate(blocks, axis=0).astype(BF16), order, preferred_element_type=F32)
    count = len(blocks) // 2
    for k in range(2 * count):
        halves[k // count, k % count] = placed[k * cout : (k + 1) * cout].astype(BF16)
    core = at_ref[0]
    face_ref[: rows + 2] = grads[1 - core]
    face_ref[rows + 2 :] = halves[1 - core]
    far_ref[...] = grads[core]
    kept_ref[...] = halves[core]


def backward_kernel(planes, rows, at_ref, w_ref, face, far, face_in, far_in, kept_ref, sent_ref, stack, parts):
    cout, width = far.shape[1:]
    cin = w_ref.shape[0]
    count = 2 * parts.shape[1]
    part = cin // count
    lane = lax.broadcasted_iota(jnp.int32, (cout, width), 1)
    step = 3 * cout
    core = at_ref[0]
    for q, source in enumerate((face_in, face, far, far_in)):
        p = jnp.where(core == 1, q, planes + 1 - q)
        for r in range(rows + 2):
            stack[p, r * step : (r + 1) * step, :] = shifted(source[r].astype(F32), lane).astype(BF16)
    w = w_ref[...]
    for d in range(planes):
        for h in range(0, rows, 2):
            cells = jnp.concatenate(
                [
                    jnp.concatenate(
                        [stack[d + a, (h + e) * step : (h + e + 3) * step, :] for a in range(3)], axis=0
                    )
                    for e in range(2)
                ],
                axis=1,
            )
            acc = jnp.dot(w, cells, preferred_element_type=F32)
            pair = (d * rows + h) // 2
            for f in range(count):
                piece = acc[f * part : (f + 1) * part]
                piece = jnp.concatenate([piece[:, :width], piece[:, width:]], axis=0).astype(BF16)
                parts[(f % 2) ^ at_ref[1], (f // 2) ^ at_ref[2], pair] = piece
    kept_ref[...] = parts[0]
    sent_ref[...] = parts[1]


def placing(cin):
    ones = np.zeros((2, 3, cin, 2, cin // PART, 2, PART), np.float32)
    for e in range(2):
        for kh in range(3):
            for i in range(cin):
                ones[e, kh, i, (kh + e) // 2, i // PART, (kh + e) % 2, i % PART] = 1
    return ones.reshape(2, 3 * cin, 4 * cin)


def per_device(activations, weights, bias, cotangent):
    cin_dev, planes, rows, width = activations.shape
    taps, cin, cout = weights.shape
    cells = planes * rows
    depth, filt = lax.axis_size("depth"), lax.axis_size("filt")
    core = lax.axis_index("depth") % 2
    even = core == 0
    swap = [(i, i ^ 1) for i in range(depth)]
    cross = [(i, i - 1 if i % 2 == 0 else i + 1) for i in range(1, depth - 1)]
    groups = [[i for i in range(depth) if i % 2 == c] for c in range(2)]
    mine = lax.axis_index("filt")
    at = jnp.stack([core, mine % 2, mine // 2]).astype(jnp.int32)
    struct = jax.ShapeDtypeStruct

    grid = activations.transpose(1, 2, 0, 3)
    face_in = lax.ppermute(jnp.where(even, grid[planes - 1], grid[0]), "depth", swap)
    far_in = lax.ppermute(jnp.where(even, grid[0], grid[planes - 1]), "depth", cross)
    low, high = jnp.where(even, far_in, face_in), jnp.where(even, face_in, far_in)
    grid = jnp.concatenate([low[None], grid, high[None]], axis=0)
    before, after = neighbours(grid[:, :2], grid[:, rows - 2 :], "height")
    grid = jnp.concatenate([before, grid, after], axis=1)
    grid = grid.reshape(planes + 2, rows // 2 + 2, 2 * cin_dev, width)
    grid, late = lax.optimization_barrier((grid, cotangent))
    tiles = spread(grid, "filt")

    cot = late.transpose(1, 2, 0, 3)
    cot_before, cot_after = neighbours(cot[:, 0], cot[:, rows - 1], "height")
    cot = cot.reshape(cells, cout, width)
    split = weights.reshape(3, 3, 3, cin, cout)
    w_forward = jnp.einsum(
        "akj,ejn->aekn",
        split.transpose(0, 2, 4, 1, 3).reshape(3, 3 * cout, 3 * cin),
        jnp.asarray(placing(cin), BF16),
        preferred_element_type=F32,
    )
    w_forward = w_forward.astype(BF16).reshape(3, 6 * cout, 4 * cin)
    w_back = split[::-1, ::-1].transpose(3, 0, 1, 2, 4).reshape(cin, taps * cout)
    work = 2 * cells * width * taps * cin * cout
    count = (taps + 1) // 4
    smem, vmem = pl.BlockSpec(memory_space=pltpu.SMEM), pl.BlockSpec(memory_space=pltpu.VMEM)
    out, face, far, kept = pl.pallas_call(
        functools.partial(forward_kernel, planes, rows),
        out_shape=(
            struct((cells, cout, width), BF16),
            struct((rows + 2 + count, cout, width), BF16),
            struct((rows + 2, cout, width), BF16),
            struct((count, cout, width), BF16),
        ),
        in_specs=[smem] + [vmem] * 6,
        out_specs=(vmem,) * 4,
        scratch_shapes=[
            pltpu.VMEM((planes, rows + 2, cout, width), BF16),
            pltpu.VMEM((2, count, cout, width), BF16),
        ],
        cost_estimate=pl.CostEstimate(flops=3 * work, bytes_accessed=1 << 20, transcendentals=1 << 17),
        name="forward",
    )(at, w_forward, jnp.broadcast_to(bias[:, None], (cout, width)), cot, cot_before, cot_after, tiles)
    output = out.reshape(planes, rows, cout, width).transpose(2, 0, 1, 3)

    face_in = lax.ppermute(face, "depth", swap)
    far_in = lax.ppermute(far, "depth", cross)
    total = (kept.astype(F32) + face_in[rows + 2 :].astype(F32)).astype(BF16)
    total = jnp.sum(spread(total, "depth", groups).astype(F32), axis=0).astype(BF16)
    total = jnp.sum(spread(total, "height").astype(F32), axis=0)
    other = lax.ppermute(total, "depth", swap)
    total = jnp.concatenate([jnp.where(even, total, other), jnp.where(even, other, total)], axis=0)
    first = total[:9].reshape(3, 3, cout, 2, cin).transpose(0, 3, 1, 2, 4)
    rest = total[9:].reshape(5, cout, 2, cin).transpose(0, 2, 1, 3).reshape(10, cout, cin)
    third = rest[:9].reshape(3, 1, 3, cout, cin)
    weight_grad = jnp.concatenate([first, third], axis=1).reshape(taps, cout, cin).transpose(0, 2, 1)
    bias_grad = rest[9, :, 0]

    kept, sent = pl.pallas_call(
        functools.partial(backward_kernel, planes, rows),
        out_shape=(struct((filt // 2, cells // 2, 2 * cin_dev, width), BF16),) * 2,
        in_specs=[smem] + [vmem] * 5,
        out_specs=(vmem,) * 2,
        scratch_shapes=[
            pltpu.VMEM((planes + 2, (rows + 2) * 3 * cout, width), BF16),
            pltpu.VMEM((2, filt // 2, cells // 2, 2 * cin_dev, width), BF16),
        ],
        cost_estimate=pl.CostEstimate(flops=work, bytes_accessed=1 << 19, transcendentals=0),
        name="backward",
    )(at, w_back, face, far, face_in, far_in)
    pair = kept.astype(F32) + lax.ppermute(sent, "filt", [(i, i ^ 1) for i in range(filt)]).astype(F32)
    summed = pair[0]
    for k in range(1, filt // 2):
        moved = lax.ppermute(pair[k].astype(BF16), "filt", [(i, i ^ (2 * k)) for i in range(filt)])
        summed = summed + moved.astype(F32)
    summed = summed.astype(BF16).reshape(planes, rows, cin_dev, width).transpose(2, 0, 1, 3)
    return (output, summed, weight_grad, bias_grad)


def solution(mesh):
    placed = (
        P("filt", "depth", "height", None),
        P(None, None, "filt"),
        P("filt"),
        P("filt", "depth", "height", None),
    )
    return jax.shard_map(
        per_device,
        mesh=mesh,
        in_specs=placed,
        out_specs=(
            P("filt", "depth", "height", None),
            P("filt", "depth", "height", None),
            P(None, None, "filt"),
            P("filt"),
        ),
        check_vma=False,
    )
```

time: 100 us -> 94 us (0.940)
  starting transfers between devices: 48.8 us -> 62.5 us
  blocking collectives: 11.8 us -> 0 us
  waiting for transfers between devices: 19.5 us -> 7.88 us
  local copies, waits for them, and re-layouts: 9.98 us -> 11.6 us
    ppermute x10 -> x13, starting transfers between devices: 31.6 us -> 46.8 us  [the longest x3 8.98 us: per_device(): lax.ppermute(pair[k].astype(BF16), 'filt', [(i, i ^ 2 * k) for i in range...]
    all_to_all x1 -> x0, blocking collectives: 11.8 us -> none  [spread(): lax.all_to_all(copies, axis, 0, 0, tiled=True, axis_index_groups=groups)]
    all_to_all x2 -> x3, waiting for transfers between devices: 6.37 us -> 0.01 us  [spread(): lax.all_to_all(copies, axis, 0, 0, tiled=True, axis_index_groups=groups)]
    all_to_all x1 -> x0, waiting for transfers between devices: 3.43 us -> none  [per_device(): parts = lax.all_to_all(parts, 'filt', 0, 0, tiled=True)]
    all_to_all x1 -> x0, starting transfers between devices: 3.41 us -> none  [per_device(): parts = lax.all_to_all(parts, 'filt', 0, 0, tiled=True)]
    all_to_all x2 -> x3, starting transfers between devices: 13.8 us -> 15.7 us  [spread(): lax.all_to_all(copies, axis, 0, 0, tiled=True, axis_index_groups=groups)]
    ppermute x10 -> x13, waiting for transfers between devices: 9.76 us -> 7.88 us  [the longest x2 6.86 us: neighbours(): after = lax.ppermute(first, axis, [(i + 1, i) for i in range(ends)])]
    transpose x4 -> x2, local copies, waits for them, and re-layouts: 2.17 us -> 0.7 us  [the longest x1 0.65 us: per_device(): cot = late.transpose(1, 2, 0, 3)]
  transfers between devices with their start and end apart: 13 -> 16, of which waited for: 6 -> 4; matrix products, arithmetic and copies ran while one was open for 5% -> 7% of each run, Pallas kernels for 2% -> 2%
where the time goes in v3:
time: 94 us; the launch traced here: 92.9 us
  starting transfers between devices  62.5 us (66%)
  local copies, waits for them, and re-layouts  11.6 us (12%)
  Pallas kernels  8.01 us (9%)
  waiting for transfers between devices  7.88 us (8%)
  other arithmetic  1.73 us (2%)
  between operations  0.99 us (1%)
    all_to_all x3, starting transfers between devices, spread(): lax.all_to_all(copies, axis, 0, 0, tiled=True, axis_index_groups=groups)  15.7 us
    ppermute x3, starting transfers between devices, per_device(): lax.ppermute(pair[k].astype(BF16), 'filt', [(i, i ^ 2 * k) for i in range...  8.98 us
    ppermute x2, waiting for transfers between devices, neighbours(): after = lax.ppermute(first, axis, [(i + 1, i) for i in range(ends)])  6.86 us
    ppermute x1, starting transfers between devices, per_device(): other = lax.ppermute(total, 'depth', swap)  6.7 us
    ppermute x2, starting transfers between devices, neighbours(): before = lax.ppermute(last, axis, [(i, i + 1) for i in range(ends)])  6.4 us
    pallas_call x1, Pallas kernels, per_device(): pl.pallas_call(functools.partial(forward_kernel, planes, rows), out_shape...  5.78 us
    ppermute x1, starting transfers between devices, per_device(): lax.ppermute(jnp.where(even, grid[0], grid[planes - 1]), 'depth', cross)  5.61 us
    ppermute x1, starting transfers between devices, per_device(): face_in = lax.ppermute(face, 'depth', swap)  4.64 us
  transfers between devices with their start and end apart: 16, of which 4 were waited for; matrix products, arithmetic and copies ran while one was open for 7% of the time, Pallas kernels for 2%

profile of v3, /device:TPU:1, one launch (start us, length us, event | category | flops | bytes accessed | tf_op | source)
XLA Modules:
  0.0 92.9 jit_solution(6362947006111158446)
XLA Ops:
  0.6 0.8 copy.54
  1.4 5.6 %collective-permute-start = (bf16[8,8,128]{2,1,0:T(8,128)(2,1)S(1)}, bf16[8,8,128]{2,1,0:T(8,128)(2,1)S(1)}, u32[]{:S(2)}, u32[]{:S(2)}) collective-permute-start(bf16[8,8,128]{2,1,0:T(8,128)(2,1)S(1)} %get-tuple-element.35), channel_id=1, source_target_pairs={{64,128},{128,64},{192,256},{256,192},{320,384},{384,320},{65,129}... | collective-permute-start | bytes 49160 | tf_op jit(solution)/shard_map/ppermute | solution.py:182
  7.0 3.8 %collective-permute-start.1 = (bf16[8,8,128]{2,1,0:T(8,128)(2,1)S(1)}, bf16[8,8,128]{2,1,0:T(8,128)(2,1)S(1)}, u32[]{:S(2)}, u32[]{:S(2)}) collective-permute-start(bf16[8,8,128]{2,1,0:T(8,128)(2,1)S(1)} %get-tuple-element.36), channel_id=1, source_target_pairs={{0,64},{64,0},{128,192},{192,128},{256,320},{320,256},{384,448},{4... | collective-permute-start | bytes 49160 | tf_op jit(solution)/shard_map/ppermute | solution.py:181
  10.9 0.8 collective-permute-done.1
  11.7 2.4 %collective-permute-start.2 = (bf16[4,2,8,128]{3,2,1,0:T(8,128)(2,1)S(1)}, bf16[4,2,8,128]{3,2,1,0:T(8,128)(2,1)S(1)}, u32[]{:S(2)}, u32[]{:S(2)}) collective-permute-start(bf16[4,2,8,128]{3,2,1,0:T(8,128)(2,1)S(1)} %get-tuple-element.29), channel_id=1, source_target_pairs={{0,8},{8,16},{16,24},{24,32},{32,40},{40,48},{48,56},{1,9},{9,17},... | collective-permute-start | bytes 49160 | tf_op jit(solution)/shard_map/ppermute | solution.py:24
  14.1 1.3 %collective-permute-start.3 = (bf16[4,2,8,128]{3,2,1,0:T(8,128)(2,1)S(1)}, bf16[4,2,8,128]{3,2,1,0:T(8,128)(2,1)S(1)}, u32[]{:S(2)}, u32[]{:S(2)}) collective-permute-start(bf16[4,2,8,128]{3,2,1,0:T(8,128)(2,1)S(1)} %get-tuple-element.30), channel_id=1, source_target_pairs={{8,0},{16,8},{24,16},{32,24},{40,32},{48,40},{56,48},{9,1},{17,9},... | collective-permute-start | bytes 49160 | tf_op jit(solution)/shard_map/ppermute | solution.py:25
  15.5 3.8 %collective-permute-done.3 = bf16[4,2,8,128]{3,2,1,0:T(8,128)(2,1)S(1)} collective-permute-done((bf16[4,2,8,128]{3,2,1,0:T(8,128)(2,1)S(1)}, bf16[4,2,8,128]{3,2,1,0:T(8,128)(2,1)S(1)}, u32[]{:S(2)}, u32[]{:S(2)}) %collective-permute-start.3) | collective-permute-done | bytes 16416 | tf_op jit(solution)/shard_map/ppermute | solution.py:25
  19.3 1.0 %broadcast_in_dim.15 = bf16[8,4,6,16,128]{4,3,2,1,0:T(8,128)(2,1)} broadcast(bf16[4,6,16,128]{3,2,1,0:T(8,128)(2,1)S(1)} %bitcast.75), dimensions={1,2,3,4} | broadcast | bytes 884736 | tf_op jit(solution)/shard_map/broadcast_in_dim | solution.py:18
  20.3 5.2 %all-to-all-start = ((bf16[8,4,6,16,128]{4,3,2,1,0:T(8,128)(2,1)}), bf16[8,4,6,16,128]{4,3,2,1,0:T(8,128)(2,1)S(1)}, u32[]{:S(2)}, u32[]{:S(2)}) async-start(bf16[8,4,6,16,128]{4,3,2,1,0:T(8,128)(2,1)} %broadcast_in_dim.15), calls=%async_computation | async-start | bytes 1572864 | tf_op jit(solution)/shard_map/all_to_all | solution.py:19
  25.5 0.0 copy-start.3
  25.5 0.1 copy.36
  25.6 0.1 reshape.69
  25.7 0.7 copy-done.3
  26.4 0.2 fusion
  26.6 0.6 copy-done.2
  27.3 4.0 %collective-permute-start.4 = (bf16[2,16,128]{2,1,0:T(8,128)(2,1)S(1)}, bf16[2,16,128]{2,1,0:T(8,128)(2,1)S(1)}, u32[]{:S(2)}, u32[]{:S(2)}) collective-permute-start(bf16[2,16,128]{2,1,0:T(8,128)(2,1)S(1)} %get-tuple-element.28), channel_id=1, source_target_pairs={{0,8},{8,16},{16,24},{24,32},{32,40},{40,48},{48,56},{1,9},{9,17},... | collective-permute-start | bytes 24584 | tf_op jit(solution)/shard_map/ppermute | solution.py:24
  31.3 1.3 %collective-permute-start.5 = (bf16[2,16,128]{2,1,0:T(8,128)(2,1)S(1)}, bf16[2,16,128]{2,1,0:T(8,128)(2,1)S(1)}, u32[]{:S(2)}, u32[]{:S(2)}) collective-permute-start(bf16[2,16,128]{2,1,0:T(8,128)(2,1)S(1)} %get-tuple-element.27), channel_id=1, source_target_pairs={{8,0},{16,8},{24,16},{32,24},{40,32},{48,40},{56,48},{9,1},{17,9},... | collective-permute-start | bytes 24584 | tf_op jit(solution)/shard_map/ppermute | solution.py:25
  32.6 0.6 pad_add_fusion.at_ref
  33.2 0.7 copy.37
  33.9 0.6 copy.40
  34.5 3.0 %collective-permute-done.5.cot_after = bf16[2,16,128]{2,1,0:T(8,128)(2,1)S(1)} collective-permute-done((bf16[2,16,128]{2,1,0:T(8,128)(2,1)S(1)}, bf16[2,16,128]{2,1,0:T(8,128)(2,1)S(1)}, u32[]{:S(2)}, u32[]{:S(2)}) %collective-permute-start.5) | collective-permute-done | bytes 8224 | tf_op jit(solution)/shard_map/ppermute | solution.py:25
  37.6 0.7 copy-done.7
  38.2 0.7 broadcast_in_dim.12.bias_ref
  38.9 5.8 %forward.1 = (bf16[16,16,128]{2,1,0:T(8,128)(2,1)}, bf16[17,16,128]{2,1,0:T(8,128)(2,1)}, bf16[10,16,128]{2,1,0:T(8,128)(2,1)}, bf16[7,16,128]{2,1,0:T(8,128)(2,1)}) custom-call(s32[3]{0:T(128)} %pad_add_fusion.at_ref, bf16[3,96,256]{2,1,0:T(8,128)(2,1)} %bitcast.81, f32[16,128]{1,0:T(8,128)} %broadcast_in_dim.12.bias_ref, bf16[16,16,128]{2,1,0:T(8,128)(2,1)} %bitcast.86, ...), custom_call_target="tpu_custom_call" | custom-call | flops 339738624 | bytes 1048576 | tf_op jit(solution)/shard_map/forward/pallas_call | solution.py:206
  44.7 4.6 %collective-permute-start.6 = (bf16[17,16,128]{2,1,0:T(8,128)(2,1)}, bf16[17,16,128]{2,1,0:T(8,128)(2,1)S(1)}, u32[]{:S(2)}, u32[]{:S(2)}) collective-permute-start(bf16[17,16,128]{2,1,0:T(8,128)(2,1)} %get-tuple-element.15.face), channel_id=1, source_target_pairs={{0,64},{64,0},{128,192},{192,128},{256,320},{320,256},{384,448},{4... | collective-permute-start | bytes 208904 | tf_op jit(solution)/shard_map/ppermute | solution.py:225
  49.3 4.4 %collective-permute-start.7 = (bf16[10,16,128]{2,1,0:T(8,128)(2,1)}, bf16[10,16,128]{2,1,0:T(8,128)(2,1)S(1)}, u32[]{:S(2)}, u32[]{:S(2)}) collective-permute-start(bf16[10,16,128]{2,1,0:T(8,128)(2,1)} %get-tuple-element.16.far), channel_id=1, source_target_pairs={{64,128},{128,64},{192,256},{256,192},{320,384},{384,320},{65,129}... | collective-permute-start | bytes 122888 | tf_op jit(solution)/shard_map/ppermute | solution.py:226
  53.8 0.0 collective-permute-done.6.face_in
  53.8 0.8 add_convert_fusion
  54.6 0.7 broadcast_in_dim.16
  55.2 3.4 %all-to-all-start.1 = ((bf16[4,7,16,128]{3,2,1,0:T(8,128)(2,1)}), bf16[4,7,16,128]{3,2,1,0:T(8,128)(2,1)S(1)}, u32[]{:S(2)}, u32[]{:S(2)}) async-start(bf16[4,7,16,128]{3,2,1,0:T(8,128)(2,1)} %broadcast_in_dim.16), calls=%async_computation.1 | async-start | bytes 229376 | tf_op jit(solution)/shard_map/all_to_all | solution.py:19
  58.7 0.7 copy.42.w_ref
  59.4 0.6 copy-done.8
  60.0 2.2 %backward.1 = (bf16[4,8,16,128]{3,2,1,0:T(8,128)(2,1)}, bf16[4,8,16,128]{3,2,1,0:T(8,128)(2,1)}) custom-call(s32[3]{0:T(128)} %pad_add_fusion.at_ref, bf16[64,432]{1,0:T(8,128)(2,1)} %copy.42.w_ref, bf16[17,16,128]{2,1,0:T(8,128)(2,1)} %get-tuple-element.15.face, bf16[10,16,128]{2,1,0:T(8,128)(2,1)} %get-tuple-element.16.far, ...), custom_call_target="tpu_custom_call" | custom-call | flops 113246208 | bytes 524288 | tf_op jit(solution)/shard_map/backward/pallas_call | solution.py:238
  62.3 3.6 %collective-permute-start.8 = (bf16[4,8,16,128]{3,2,1,0:T(8,128)(2,1)}, bf16[4,8,16,128]{3,2,1,0:T(8,128)(2,1)S(1)}, u32[]{:S(2)}, u32[]{:S(2)}) collective-permute-start(bf16[4,8,16,128]{3,2,1,0:T(8,128)(2,1)} %get-tuple-element.18), channel_id=1, source_target_pairs={{0,1},{1,0},{2,3},{3,2},{4,5},{5,4},{6,7},{7,6},{8,9},{9,8},{10,11... | collective-permute-start | bytes 393224 | tf_op jit(solution)/shard_map/ppermute | solution.py:250
  65.9 0.6 copy.51
  66.6 0.7 broadcast_in_dim.17
  67.3 7.1 %all-to-all-start.2 = ((bf16[8,7,16,128]{3,2,1,0:T(8,128)(2,1)}), bf16[8,7,16,128]{3,2,1,0:T(8,128)(2,1)S(1)}, u32[]{:S(2)}, u32[]{:S(2)}) async-start(bf16[8,7,16,128]{3,2,1,0:T(8,128)(2,1)} %broadcast_in_dim.17), calls=%async_computation.2 | async-start | bytes 458752 | tf_op jit(solution)/shard_map/all_to_all | solution.py:19
  74.5 4.3 %collective-permute-start.10 = (bf16[8,16,128]{2,1,0:T(8,128)(2,1)S(1)}, bf16[8,16,128]{2,1,0:T(8,128)(2,1)S(1)}, u32[]{:S(2)}, u32[]{:S(2)}) collective-permute-start(bf16[8,16,128]{2,1,0:T(8,128)(2,1)S(1)} %get-tuple-element.24), channel_id=1, source_target_pairs={{0,4},{1,5},{2,6},{3,7},{4,0},{5,1},{6,2},{7,3},{8,12},{9,13},{10,... | collective-permute-start | bytes 98312 | tf_op jit(solution)/shard_map/ppermute | solution.py:253
  78.8 2.8 %collective-permute-start.11 = (bf16[8,16,128]{2,1,0:T(8,128)(2,1)S(1)}, bf16[8,16,128]{2,1,0:T(8,128)(2,1)S(1)}, u32[]{:S(2)}, u32[]{:S(2)}) collective-permute-start(bf16[8,16,128]{2,1,0:T(8,128)(2,1)S(1)} %get-tuple-element.23), channel_id=1, source_target_pairs={{0,6},{1,7},{2,4},{3,5},{4,2},{5,3},{6,0},{7,1},{8,14},{9,15},{10,... | collective-permute-start | bytes 98312 | tf_op jit(solution)/shard_map/ppermute | solution.py:253
  81.6 1.9 %collective-permute-start.9 = (bf16[8,16,128]{2,1,0:T(8,128)(2,1)S(1)}, bf16[8,16,128]{2,1,0:T(8,128)(2,1)S(1)}, u32[]{:S(2)}, u32[]{:S(2)}) collective-permute-start(bf16[8,16,128]{2,1,0:T(8,128)(2,1)S(1)} %get-tuple-element.22), channel_id=1, source_target_pairs={{0,2},{1,3},{2,0},{3,1},{4,6},{5,7},{6,4},{7,5},{8,10},{9,11},{10,... | collective-permute-start | bytes 98312 | tf_op jit(solution)/shard_map/ppermute | solution.py:253
  83.6 6.7 %collective-permute-start.12 = (f32[7,16,128]{2,1,0:T(8,128)S(1)}, f32[7,16,128]{2,1,0:T(8,128)S(1)}, u32[]{:S(2)}, u32[]{:S(2)}) collective-permute-start(f32[7,16,128]{2,1,0:T(8,128)S(1)} %convert_reduce_fusion), channel_id=1, source_target_pairs={{0,64},{64,0},{128,192},{192,128},{256,320},{320,256},{384,448},{4... | collective-permute-start | bytes 172040 | tf_op jit(solution)/shard_map/ppermute | solution.py:230
  90.4 0.6 copy.53
  91.0 0.2 collective-permute-done.12
  91.2 0.1 fusion.6
  91.3 0.6 slice_reduce_fusion
  91.9 0.1 reshape.64
  92.1 0.2 pad_maximum_fusion
  92.2 0.7 copy.44
  (44 shorter events, 0.3 us)
Async XLA Ops:
  1.4 9.5 %collective-permute-start = (bf16[8,8,128]{2,1,0:T(8,128)(2,1)S(1)}, bf16[8,8,128]{2,1,0:T(8,128)(2,1)S(1)}, u32[]{:S(2)}, u32[]{:S(2)}) collective-permute-start(bf16[8,8,128]{2,1,0:T(8,128)(2,1)S(1)} %get-tuple-element.35), channel_id=1, source_target_pairs={{64,128},{128,64},{192,256},{256,192},{320,384},{384,320},{65,129}... | collective-permute-start | bytes 49160 | tf_op jit(solution)/shard_map/ppermute | solution.py:182
  7.0 4.7 %collective-permute-start.1 = (bf16[8,8,128]{2,1,0:T(8,128)(2,1)S(1)}, bf16[8,8,128]{2,1,0:T(8,128)(2,1)S(1)}, u32[]{:S(2)}, u32[]{:S(2)}) collective-permute-start(bf16[8,8,128]{2,1,0:T(8,128)(2,1)S(1)} %get-tuple-element.36), channel_id=1, source_target_pairs={{0,64},{64,0},{128,192},{192,128},{256,320},{320,256},{384,448},{4... | collective-permute-start | bytes 49160 | tf_op jit(solution)/shard_map/ppermute | solution.py:181
  11.7 3.7 %collective-permute-start.2 = (bf16[4,2,8,128]{3,2,1,0:T(8,128)(2,1)S(1)}, bf16[4,2,8,128]{3,2,1,0:T(8,128)(2,1)S(1)}, u32[]{:S(2)}, u32[]{:S(2)}) collective-permute-start(bf16[4,2,8,128]{3,2,1,0:T(8,128)(2,1)S(1)} %get-tuple-element.29), channel_id=1, source_target_pairs={{0,8},{8,16},{16,24},{24,32},{32,40},{40,48},{48,56},{1,9},{9,17},... | collective-permute-start | bytes 49160 | tf_op jit(solution)/shard_map/ppermute | solution.py:24
  14.1 5.1 %collective-permute-start.3 = (bf16[4,2,8,128]{3,2,1,0:T(8,128)(2,1)S(1)}, bf16[4,2,8,128]{3,2,1,0:T(8,128)(2,1)S(1)}, u32[]{:S(2)}, u32[]{:S(2)}) collective-permute-start(bf16[4,2,8,128]{3,2,1,0:T(8,128)(2,1)S(1)} %get-tuple-element.30), channel_id=1, source_target_pairs={{8,0},{16,8},{24,16},{32,24},{40,32},{48,40},{56,48},{9,1},{17,9},... | collective-permute-start | bytes 49160 | tf_op jit(solution)/shard_map/ppermute | solution.py:25
  20.3 5.2 %copy-start.1 = (bf16[27,64,16]{1,2,0:T(8,128)(2,1)S(1)}, bf16[27,64,16]{1,2,0:T(8,128)(2,1)}, u32[]{:S(2)}) copy-start(bf16[27,64,16]{1,2,0:T(8,128)(2,1)} %param.6) | copy-start | bytes 165892
  20.3 17.2 %all-to-all-start = ((bf16[8,4,6,16,128]{4,3,2,1,0:T(8,128)(2,1)}), bf16[8,4,6,16,128]{4,3,2,1,0:T(8,128)(2,1)S(1)}, u32[]{:S(2)}, u32[]{:S(2)}) async-start(bf16[8,4,6,16,128]{4,3,2,1,0:T(8,128)(2,1)} %broadcast_in_dim.15), calls=%async_computation | async-start | bytes 1572864 | tf_op jit(solution)/shard_map/all_to_all | solution.py:19
  25.5 0.9 %copy-start.3 = (bf16[2,192,256,1]{2,1,3,0:T(8,128)(2,1)S(1)}, bf16[2,192,256,1]{2,1,3,0:T(8,128)(2,1)}, u32[]{:S(2)}) copy-start(bf16[2,192,256,1]{2,1,3,0:T(8,128)(2,1)} %constant.46) | copy-start | bytes 589828
  26.4 0.8 copy-start.2
  27.3 7.2 %collective-permute-start.4 = (bf16[2,16,128]{2,1,0:T(8,128)(2,1)S(1)}, bf16[2,16,128]{2,1,0:T(8,128)(2,1)S(1)}, u32[]{:S(2)}, u32[]{:S(2)}) collective-permute-start(bf16[2,16,128]{2,1,0:T(8,128)(2,1)S(1)} %get-tuple-element.28), channel_id=1, source_target_pairs={{0,8},{8,16},{16,24},{24,32},{32,40},{40,48},{48,56},{1,9},{9,17},... | collective-permute-start | bytes 24584 | tf_op jit(solution)/shard_map/ppermute | solution.py:24
  31.3 6.2 %collective-permute-start.5 = (bf16[2,16,128]{2,1,0:T(8,128)(2,1)S(1)}, bf16[2,16,128]{2,1,0:T(8,128)(2,1)S(1)}, u32[]{:S(2)}, u32[]{:S(2)}) collective-permute-start(bf16[2,16,128]{2,1,0:T(8,128)(2,1)S(1)} %get-tuple-element.27), channel_id=1, source_target_pairs={{8,0},{16,8},{24,16},{32,24},{40,32},{48,40},{56,48},{9,1},{17,9},... | collective-permute-start | bytes 24584 | tf_op jit(solution)/shard_map/ppermute | solution.py:25
  34.5 4.4 %copy-start.9 = (bf16[2,16,128]{2,1,0:T(8,128)(2,1)}, bf16[2,16,128]{2,1,0:T(8,128)(2,1)S(1)}, u32[]{:S(2)}) copy-start(bf16[2,16,128]{2,1,0:T(8,128)(2,1)S(1)} %collective-permute-done.4.cot_before) | copy-start | bytes 24580
  37.6 1.4 %copy-start.10 = (bf16[2,16,128]{2,1,0:T(8,128)(2,1)}, bf16[2,16,128]{2,1,0:T(8,128)(2,1)S(1)}, u32[]{:S(2)}) copy-start(bf16[2,16,128]{2,1,0:T(8,128)(2,1)S(1)} %collective-permute-done.5.cot_after) | copy-start | bytes 24580
  37.6 1.3 %copy-start = (bf16[8,4,6,16,128]{4,3,2,1,0:T(8,128)(2,1)}, bf16[8,4,6,16,128]{4,3,2,1,0:T(8,128)(2,1)S(1)}, u32[]{:S(2)}) copy-start(bf16[8,4,6,16,128]{4,3,2,1,0:T(8,128)(2,1)S(1)} %all-to-all-done.tiles) | copy-start | bytes 2359300
  37.6 0.7 copy-start.7
  44.7 9.1 %collective-permute-start.6 = (bf16[17,16,128]{2,1,0:T(8,128)(2,1)}, bf16[17,16,128]{2,1,0:T(8,128)(2,1)S(1)}, u32[]{:S(2)}, u32[]{:S(2)}) collective-permute-start(bf16[17,16,128]{2,1,0:T(8,128)(2,1)} %get-tuple-element.15.face), channel_id=1, source_target_pairs={{0,64},{64,0},{128,192},{192,128},{256,320},{320,256},{384,448},{4... | collective-permute-start | bytes 208904 | tf_op jit(solution)/shard_map/ppermute | solution.py:225
  49.3 10.1 %collective-permute-start.7 = (bf16[10,16,128]{2,1,0:T(8,128)(2,1)}, bf16[10,16,128]{2,1,0:T(8,128)(2,1)S(1)}, u32[]{:S(2)}, u32[]{:S(2)}) collective-permute-start(bf16[10,16,128]{2,1,0:T(8,128)(2,1)} %get-tuple-element.16.far), channel_id=1, source_target_pairs={{64,128},{128,64},{192,256},{256,192},{320,384},{384,320},{65,129}... | collective-permute-start | bytes 122888 | tf_op jit(solution)/shard_map/ppermute | solution.py:226
  53.8 1.5 %copy-start.6 = (bf16[17,16,128]{2,1,0:T(8,128)(2,1)}, bf16[17,16,128]{2,1,0:T(8,128)(2,1)S(1)}, u32[]{:S(2)}) copy-start(bf16[17,16,128]{2,1,0:T(8,128)(2,1)S(1)} %collective-permute-done.6.face_in) | copy-start | bytes 208900
  55.2 11.3 %all-to-all-start.1 = ((bf16[4,7,16,128]{3,2,1,0:T(8,128)(2,1)}), bf16[4,7,16,128]{3,2,1,0:T(8,128)(2,1)S(1)}, u32[]{:S(2)}, u32[]{:S(2)}) async-start(bf16[4,7,16,128]{3,2,1,0:T(8,128)(2,1)} %broadcast_in_dim.16), calls=%async_computation.1 | async-start | bytes 229376 | tf_op jit(solution)/shard_map/all_to_all | solution.py:19
  59.4 6.5 %copy-start.5 = (bf16[16,16,128]{2,1,0:T(8,128)(2,1)S(1)}, bf16[16,16,128]{2,1,0:T(8,128)(2,1)}, u32[]{:S(2)}) copy-start(bf16[16,16,128]{2,1,0:T(8,128)(2,1)} %get-tuple-element.14) | copy-start | bytes 196612
  59.4 0.6 copy-start.8
  62.3 12.2 %collective-permute-start.8 = (bf16[4,8,16,128]{3,2,1,0:T(8,128)(2,1)}, bf16[4,8,16,128]{3,2,1,0:T(8,128)(2,1)S(1)}, u32[]{:S(2)}, u32[]{:S(2)}) collective-permute-start(bf16[4,8,16,128]{3,2,1,0:T(8,128)(2,1)} %get-tuple-element.18), channel_id=1, source_target_pairs={{0,1},{1,0},{2,3},{3,2},{4,5},{5,4},{6,7},{7,6},{8,9},{9,8},{10,11... | collective-permute-start | bytes 393224 | tf_op jit(solution)/shard_map/ppermute | solution.py:250
  67.3 7.2 %copy-start.4 = (bf16[4,8,16,128]{3,2,1,0:T(8,128)(2,1)S(1)}, bf16[4,8,16,128]{3,2,1,0:T(8,128)(2,1)}, u32[]{:S(2)}) copy-start(bf16[4,8,16,128]{3,2,1,0:T(8,128)(2,1)} %get-tuple-element.17) | copy-start | bytes 393220
  67.3 16.2 %all-to-all-start.2 = ((bf16[8,7,16,128]{3,2,1,0:T(8,128)(2,1)}), bf16[8,7,16,128]{3,2,1,0:T(8,128)(2,1)S(1)}, u32[]{:S(2)}, u32[]{:S(2)}) async-start(bf16[8,7,16,128]{3,2,1,0:T(8,128)(2,1)} %broadcast_in_dim.17), calls=%async_computation.2 | async-start | bytes 458752 | tf_op jit(solution)/shard_map/all_to_all | solution.py:19
  74.5 15.8 %collective-permute-start.10 = (bf16[8,16,128]{2,1,0:T(8,128)(2,1)S(1)}, bf16[8,16,128]{2,1,0:T(8,128)(2,1)S(1)}, u32[]{:S(2)}, u32[]{:S(2)}) collective-permute-start(bf16[8,16,128]{2,1,0:T(8,128)(2,1)S(1)} %get-tuple-element.24), channel_id=1, source_target_pairs={{0,4},{1,5},{2,6},{3,7},{4,0},{5,1},{6,2},{7,3},{8,12},{9,13},{10,... | collective-permute-start | bytes 98312 | tf_op jit(solution)/shard_map/ppermute | solution.py:253
  78.8 11.5 %collective-permute-start.11 = (bf16[8,16,128]{2,1,0:T(8,128)(2,1)S(1)}, bf16[8,16,128]{2,1,0:T(8,128)(2,1)S(1)}, u32[]{:S(2)}, u32[]{:S(2)}) collective-permute-start(bf16[8,16,128]{2,1,0:T(8,128)(2,1)S(1)} %get-tuple-element.23), channel_id=1, source_target_pairs={{0,6},{1,7},{2,4},{3,5},{4,2},{5,3},{6,0},{7,1},{8,14},{9,15},{10,... | collective-permute-start | bytes 98312 | tf_op jit(solution)/shard_map/ppermute | solution.py:253
  81.6 8.7 %collective-permute-start.9 = (bf16[8,16,128]{2,1,0:T(8,128)(2,1)S(1)}, bf16[8,16,128]{2,1,0:T(8,128)(2,1)S(1)}, u32[]{:S(2)}, u32[]{:S(2)}) collective-permute-start(bf16[8,16,128]{2,1,0:T(8,128)(2,1)S(1)} %get-tuple-element.22), channel_id=1, source_target_pairs={{0,2},{1,3},{2,0},{3,1},{4,6},{5,7},{6,4},{7,5},{8,10},{9,11},{10,... | collective-permute-start | bytes 98312 | tf_op jit(solution)/shard_map/ppermute | solution.py:253
  83.6 7.6 %collective-permute-start.12 = (f32[7,16,128]{2,1,0:T(8,128)S(1)}, f32[7,16,128]{2,1,0:T(8,128)S(1)}, u32[]{:S(2)}, u32[]{:S(2)}) collective-permute-start(f32[7,16,128]{2,1,0:T(8,128)S(1)} %convert_reduce_fusion), channel_id=1, source_target_pairs={{0,64},{64,0},{128,192},{192,128},{256,320},{320,256},{384,448},{4... | collective-permute-start | bytes 172040 | tf_op jit(solution)/shard_map/ppermute | solution.py:230

commit v4 on v3

--- a/solution.py
+++ b/solution.py
@@ -13,10 +13,12 @@
 PART = 8
 
 
-def spread(block, axis, groups=None):
-    members = lax.axis_size(axis) if groups is None else len(groups[0])
-    copies = jnp.broadcast_to(block[None], (members,) + block.shape)
-    return lax.all_to_all(copies, axis, 0, 0, tiled=True, axis_index_groups=groups)
+def copies(block, count):
+    return jnp.broadcast_to(block[None], (count,) + block.shape)
+
+
+def swapped(blocks, axis):
+    return lax.all_to_all(blocks, axis, 0, 0, tiled=True)
 
 
 def neighbours(first, last, axis):
@@ -33,10 +35,19 @@
     return jnp.concatenate([ahead, value, behind], axis=0)
 
 
-def forward_kernel(planes, rows, at_ref, w_ref, bias_ref, cot, cot_before, cot_after, tiles, *refs):
+def forward_kernel(planes, rows, at_ref, w_ref, bias_ref, cot, tiles, before, after, *refs):
     out_ref, face_ref, far_ref, kept_ref, grads, halves = refs
     cout, width = cot.shape[1:]
     sources = tiles.shape[0]
+    edge = sources * (planes + 2)
+
+    def tile(s, p, t):
+        if t == 0:
+            return before[s * (planes + 2) + p]
+        if t == rows // 2 + 1:
+            return after[s * (planes + 2) + p]
+        return tiles[s, p, t - 1]
+
     lane = lax.broadcasted_iota(jnp.int32, (cout, width), 1)
     bias = bias_ref[...]
     sums = [None] * 3
@@ -45,7 +56,7 @@
         for pair in range(rows // 2 + 1):
             cells = [
                 jnp.concatenate(
-                    [tiles[s, d + kd, pair + t] for t in range(2) for s in range(sources)], axis=0
+                    [tile(s, d + kd, pair + t) for t in range(2) for s in range(sources)], axis=0
                 )
                 for kd in range(3)
             ]
@@ -65,9 +76,9 @@
                 sigmoid = jnp.where(pre >= 0, 1.0, small) / (1.0 + small)
                 row = 2 * pair + e
                 if row == 0:
-                    cotangent = cot_before[d]
+                    cotangent = before[edge + d]
                 elif row == rows + 1:
-                    cotangent = cot_after[d]
+                    cotangent = after[edge + d]
                 else:
                     cotangent = cot[d * rows + row - 1]
                 grad = (cotangent.astype(F32) * (0.2 + 0.8 * sigmoid)).astype(BF16)
@@ -172,7 +183,6 @@
     even = core == 0
     swap = [(i, i ^ 1) for i in range(depth)]
     cross = [(i, i - 1 if i % 2 == 0 else i + 1) for i in range(1, depth - 1)]
-    groups = [[i for i in range(depth) if i % 2 == c] for c in range(2)]
     mine = lax.axis_index("filt")
     at = jnp.stack([core, mine % 2, mine // 2]).astype(jnp.int32)
     struct = jax.ShapeDtypeStruct
@@ -182,15 +192,10 @@
     far_in = lax.ppermute(jnp.where(even, grid[0], grid[planes - 1]), "depth", cross)
     low, high = jnp.where(even, far_in, face_in), jnp.where(even, face_in, far_in)
     grid = jnp.concatenate([low[None], grid, high[None]], axis=0)
-    before, after = neighbours(grid[:, :2], grid[:, rows - 2 :], "height")
-    grid = jnp.concatenate([before, grid, after], axis=1)
-    grid = grid.reshape(planes + 2, rows // 2 + 2, 2 * cin_dev, width)
-    grid, late = lax.optimization_barrier((grid, cotangent))
-    tiles = spread(grid, "filt")
-
-    cot = late.transpose(1, 2, 0, 3)
-    cot_before, cot_after = neighbours(cot[:, 0], cot[:, rows - 1], "height")
-    cot = cot.reshape(cells, cout, width)
+    grid = grid.reshape(planes + 2, rows // 2, 2 * cin_dev, width)
+    tiles = swapped(copies(grid, filt), "filt")
+
+    cot = cotangent.transpose(1, 2, 0, 3)
     split = weights.reshape(3, 3, 3, cin, cout)
     w_forward = jnp.einsum(
         "akj,ejn->aekn",
@@ -199,7 +204,13 @@
         preferred_element_type=F32,
     )
     w_forward = w_forward.astype(BF16).reshape(3, 6 * cout, 4 * cin)
+    wide = jnp.broadcast_to(bias[:, None], (cout, width))
     w_back = split[::-1, ::-1].transpose(3, 0, 1, 2, 4).reshape(cin, taps * cout)
+    first = jnp.concatenate([tiles[:, :, 0].reshape(-1, 2 * cin_dev, width), cot[:, 0]], axis=0)
+    last = jnp.concatenate([tiles[:, :, -1].reshape(-1, 2 * cin_dev, width), cot[:, rows - 1]], axis=0)
+    cot = cot.reshape(cells, cout, width)
+    first, last, cot, w_forward, wide = lax.optimization_barrier((first, last, cot, w_forward, wide))
+    before, after = neighbours(first, last, "height")
     work = 2 * cells * width * taps * cin * cout
     count = (taps + 1) // 4
     smem, vmem = pl.BlockSpec(memory_space=pltpu.SMEM), pl.BlockSpec(memory_space=pltpu.VMEM)
@@ -213,22 +224,23 @@
         ),
         in_specs=[smem] + [vmem] * 6,
         out_specs=(vmem,) * 4,
+        compiler_params=pltpu.CompilerParams(vmem_limit_bytes=12 << 20),
         scratch_shapes=[
             pltpu.VMEM((planes, rows + 2, cout, width), BF16),
             pltpu.VMEM((2, count, cout, width), BF16),
         ],
         cost_estimate=pl.CostEstimate(flops=3 * work, bytes_accessed=1 << 20, transcendentals=1 << 17),
         name="forward",
-    )(at, w_forward, jnp.broadcast_to(bias[:, None], (cout, width)), cot, cot_before, cot_after, tiles)
+    )(at, w_forward, wide, cot, tiles, before, after)
     output = out.reshape(planes, rows, cout, width).transpose(2, 0, 1, 3)
 
     face_in = lax.ppermute(face, "depth", swap)
     far_in = lax.ppermute(far, "depth", cross)
     total = (kept.astype(F32) + face_in[rows + 2 :].astype(F32)).astype(BF16)
-    total = jnp.sum(spread(total, "depth", groups).astype(F32), axis=0).astype(BF16)
-    total = jnp.sum(spread(total, "height").astype(F32), axis=0)
-    other = lax.ppermute(total, "depth", swap)
-    total = jnp.concatenate([jnp.where(even, total, other), jnp.where(even, other, total)], axis=0)
+    total = copies(total, lax.axis_size("height"))
+    total = jnp.sum(swapped(total, "height").astype(F32), axis=0).astype(BF16)
+    total = swapped(copies(total, depth), "depth").reshape((depth // 2, 2 * count) + total.shape[1:])
+    total = jnp.sum(total.astype(F32), axis=0)
     first = total[:9].reshape(3, 3, cout, 2, cin).transpose(0, 3, 1, 2, 4)
     rest = total[9:].reshape(5, cout, 2, cin).transpose(0, 2, 1, 3).reshape(10, cout, cin)
     third = rest[:9].reshape(3, 1, 3, cout, cin)
@@ -240,6 +252,7 @@
         out_shape=(struct((filt // 2, cells // 2, 2 * cin_dev, width), BF16),) * 2,
         in_specs=[smem] + [vmem] * 5,
         out_specs=(vmem,) * 2,
+        compiler_params=pltpu.CompilerParams(vmem_limit_bytes=12 << 20),
         scratch_shapes=[
             pltpu.VMEM((planes + 2, (rows + 2) * 3 * cout, width), BF16),
             pltpu.VMEM((2, filt // 2, cells // 2, 2 * cin_dev, width), BF16),

time: 94 us -> 93.2 us (level)
  the two profiles are of different devices: /device:TPU:1 before, /device:TPU:40 now
where the time goes in v4:
time: 93.2 us; the launch traced here: 92.4 us
  starting transfers between devices  53.5 us (57%)
  waiting for transfers between devices  22.3 us (24%)
  local copies, waits for them, and re-layouts  9.45 us (10%)
  Pallas kernels  5.56 us (6%)
  between operations  0.94 us (1%)
    all_to_all x3, starting transfers between devices, swapped(): return lax.all_to_all(blocks, axis, 0, 0, tiled=True)  22.4 us
    ppermute x3, starting transfers between devices, per_device(): lax.ppermute(pair[k].astype(BF16), 'filt', [(i, i ^ 2 * k) for i in range...  10.4 us
    all_to_all x3, waiting for transfers between devices, swapped(): return lax.all_to_all(blocks, axis, 0, 0, tiled=True)  7.64 us
    ppermute x1, starting transfers between devices, per_device(): far_in = lax.ppermute(far, 'depth', cross)  5.35 us
    ppermute x1, waiting for transfers between devices, neighbours(): after = lax.ppermute(first, axis, [(i + 1, i) for i in range(ends)])  4.73 us
    pallas_call x1, Pallas kernels, per_device(): pl.pallas_call(functools.partial(forward_kernel, planes, rows), out_shape...  4.38 us
    ppermute x1, starting transfers between devices, neighbours(): before = lax.ppermute(last, axis, [(i, i + 1) for i in range(ends)])  4.27 us
    ppermute x1, waiting for transfers between devices, per_device(): lax.ppermute(sent, 'filt', [(i, i ^ 1) for i in range(filt)]).astype(F32)  3.77 us
  transfers between devices with their start and end apart: 13, of which 7 were waited for; matrix products, arithmetic and copies ran while one was open for 3% of the time, Pallas kernels for 1%

profile of v4, /device:TPU:40, one launch (start us, length us, event | category | flops | bytes accessed | tf_op | source)
XLA Modules:
  0.0 92.4 jit_solution(10733455426349817972)
XLA Ops:
  0.6 0.8 copy.56
  1.4 2.6 %collective-permute-start = (bf16[8,8,128]{2,1,0:T(8,128)(2,1)S(1)}, bf16[8,8,128]{2,1,0:T(8,128)(2,1)S(1)}, u32[]{:S(2)}, u32[]{:S(2)}) collective-permute-start(bf16[8,8,128]{2,1,0:T(8,128)(2,1)S(1)} %get-tuple-element.41), channel_id=1, source_target_pairs={{64,128},{128,64},{192,256},{256,192},{320,384},{384,320},{65,129}... | collective-permute-start | bytes 49160 | tf_op jit(solution)/shard_map/ppermute | solution.py:192
  4.0 2.1 %collective-permute-start.1 = (bf16[8,8,128]{2,1,0:T(8,128)(2,1)S(1)}, bf16[8,8,128]{2,1,0:T(8,128)(2,1)S(1)}, u32[]{:S(2)}, u32[]{:S(2)}) collective-permute-start(bf16[8,8,128]{2,1,0:T(8,128)(2,1)S(1)} %get-tuple-element.42), channel_id=1, source_target_pairs={{0,64},{64,0},{128,192},{192,128},{256,320},{320,256},{384,448},{4... | collective-permute-start | bytes 49160 | tf_op jit(solution)/shard_map/ppermute | solution.py:191
  6.2 2.4 %collective-permute-done = bf16[8,8,128]{2,1,0:T(8,128)(2,1)S(1)} collective-permute-done((bf16[8,8,128]{2,1,0:T(8,128)(2,1)S(1)}, bf16[8,8,128]{2,1,0:T(8,128)(2,1)S(1)}, u32[]{:S(2)}, u32[]{:S(2)}) %collective-permute-start) | collective-permute-done | bytes 16416 | tf_op jit(solution)/shard_map/ppermute | solution.py:192
  8.6 0.9 %broadcast_in_dim.11 = bf16[8,4,4,16,128]{4,3,2,1,0:T(8,128)(2,1)} broadcast(bf16[4,4,16,128]{3,2,1,0:T(8,128)(2,1)S(1)} %maximum_bitcast_fusion), dimensions={1,2,3,4} | broadcast | bytes 589824 | tf_op jit(solution)/shard_map/broadcast_in_dim | solution.py:17
  9.6 5.9 %all-to-all-start = ((bf16[8,4,4,16,128]{4,3,2,1,0:T(8,128)(2,1)}), bf16[8,4,4,16,128]{4,3,2,1,0:T(8,128)(2,1)S(1)}, u32[]{:S(2)}, u32[]{:S(2)}) async-start(bf16[8,4,4,16,128]{4,3,2,1,0:T(8,128)(2,1)} %broadcast_in_dim.11), calls=%async_computation | async-start | bytes 1048576 | tf_op jit(solution)/shard_map/all_to_all | solution.py:21
  15.5 0.9 copy-done.1
  16.4 0.1 copy.40
  16.4 0.1 reshape.73
  16.6 0.7 copy-done.3
  17.3 0.2 fusion
  17.5 5.7 %all-to-all-done.tiles = bf16[8,4,4,16,128]{4,3,2,1,0:T(8,128)(2,1)S(1)} async-done(((bf16[8,4,4,16,128]{4,3,2,1,0:T(8,128)(2,1)}), bf16[8,4,4,16,128]{4,3,2,1,0:T(8,128)(2,1)S(1)}, u32[]{:S(2)}, u32[]{:S(2)}) %all-to-all-start) | async-done | bytes 524320 | tf_op jit(solution)/shard_map/all_to_all | solution.py:21
  23.3 0.0 copy-start.4
  23.3 0.6 copy-done.4
  24.0 0.1 broadcast_in_dim.12.bias_ref
  24.0 4.3 %collective-permute-start.2 = (bf16[34,16,128]{2,1,0:T(8,128)(2,1)S(1)}, bf16[34,16,128]{2,1,0:T(8,128)(2,1)S(1)}, u32[]{:S(2)}, u32[]{:S(2)}) collective-permute-start(bf16[34,16,128]{2,1,0:T(8,128)(2,1)S(1)} %get-tuple-element.18), channel_id=1, source_target_pairs={{0,8},{8,16},{16,24},{24,32},{32,40},{40,48},{48,56},{1,9},{9,17},... | collective-permute-start | bytes 417800 | tf_op jit(solution)/shard_map/ppermute | solution.py:26
  28.3 1.3 %collective-permute-start.3 = (bf16[34,16,128]{2,1,0:T(8,128)(2,1)S(1)}, bf16[34,16,128]{2,1,0:T(8,128)(2,1)S(1)}, u32[]{:S(2)}, u32[]{:S(2)}) collective-permute-start(bf16[34,16,128]{2,1,0:T(8,128)(2,1)S(1)} %get-tuple-element.19), channel_id=1, source_target_pairs={{8,0},{16,8},{24,16},{32,24},{40,32},{48,40},{56,48},{9,1},{17,9},... | collective-permute-start | bytes 417800 | tf_op jit(solution)/shard_map/ppermute | solution.py:27
  29.6 0.1 pad_add_fusion.at_ref
  29.7 1.2 %collective-permute-done.2.before = bf16[34,16,128]{2,1,0:T(8,128)(2,1)S(1)} collective-permute-done((bf16[34,16,128]{2,1,0:T(8,128)(2,1)S(1)}, bf16[34,16,128]{2,1,0:T(8,128)(2,1)S(1)}, u32[]{:S(2)}, u32[]{:S(2)}) %collective-permute-start.2) | collective-permute-done | bytes 139296 | tf_op jit(solution)/shard_map/ppermute | solution.py:26
  30.9 4.7 %collective-permute-done.3.after = bf16[34,16,128]{2,1,0:T(8,128)(2,1)S(1)} collective-permute-done((bf16[34,16,128]{2,1,0:T(8,128)(2,1)S(1)}, bf16[34,16,128]{2,1,0:T(8,128)(2,1)S(1)}, u32[]{:S(2)}, u32[]{:S(2)}) %collective-permute-start.3) | collective-permute-done | bytes 139296 | tf_op jit(solution)/shard_map/ppermute | solution.py:27
  35.6 4.4 %forward.1 = (bf16[16,16,128]{2,1,0:T(8,128)(2,1)S(1)}, bf16[17,16,128]{2,1,0:T(8,128)(2,1)S(1)}, bf16[10,16,128]{2,1,0:T(8,128)(2,1)S(1)}, bf16[7,16,128]{2,1,0:T(8,128)(2,1)S(1)}) custom-call(s32[3]{0:T(128)S(1)} %pad_add_fusion.at_ref, bf16[3,96,256]{2,1,0:T(8,128)(2,1)S(1)} %bitcast.74, f32[16,128]{1,0:T(8,128)S(1)} %broadcast_in_dim.12.bias_ref, ...), custom_call_target="tpu_custom_call" | custom-call | flops 339738624 | bytes 1048576 | tf_op jit(solution)/shard_map/forward/pallas_call | solution.py:217
  40.0 1.9 %collective-permute-start.4 = (bf16[17,16,128]{2,1,0:T(8,128)(2,1)S(1)}, bf16[17,16,128]{2,1,0:T(8,128)(2,1)S(1)}, u32[]{:S(2)}, u32[]{:S(2)}) collective-permute-start(bf16[17,16,128]{2,1,0:T(8,128)(2,1)S(1)} %get-tuple-element.21.face), channel_id=1, source_target_pairs={{0,64},{64,0},{128,192},{192,128},{256,320},{320,256},{384,448},{4... | collective-permute-start | bytes 208904 | tf_op jit(solution)/shard_map/ppermute | solution.py:237
  41.9 5.3 %collective-permute-start.5 = (bf16[10,16,128]{2,1,0:T(8,128)(2,1)S(1)}, bf16[10,16,128]{2,1,0:T(8,128)(2,1)S(1)}, u32[]{:S(2)}, u32[]{:S(2)}) collective-permute-start(bf16[10,16,128]{2,1,0:T(8,128)(2,1)S(1)} %get-tuple-element.22.far), channel_id=1, source_target_pairs={{64,128},{128,64},{192,256},{256,192},{320,384},{384,320},{65,129}... | collective-permute-start | bytes 122888 | tf_op jit(solution)/shard_map/ppermute | solution.py:238
  47.3 0.0 collective-permute-done.4.face_in
  47.3 0.7 broadcast_in_dim.13
  48.1 9.3 %all-to-all-start.1 = ((bf16[8,7,16,128]{3,2,1,0:T(8,128)(2,1)}), bf16[8,7,16,128]{3,2,1,0:T(8,128)(2,1)S(1)}, u32[]{:S(2)}, u32[]{:S(2)}) async-start(bf16[8,7,16,128]{3,2,1,0:T(8,128)(2,1)} %broadcast_in_dim.13), calls=%async_computation.1 | async-start | bytes 458752 | tf_op jit(solution)/shard_map/all_to_all | solution.py:21
  57.4 0.1 copy.43.w_ref
  57.5 1.2 %backward.1 = (bf16[4,8,16,128]{3,2,1,0:T(8,128)(2,1)S(1)}, bf16[4,8,16,128]{3,2,1,0:T(8,128)(2,1)S(1)}) custom-call(s32[3]{0:T(128)S(1)} %pad_add_fusion.at_ref, bf16[64,432]{1,0:T(8,128)(2,1)S(1)} %copy.43.w_ref, bf16[17,16,128]{2,1,0:T(8,128)(2,1)S(1)} %get-tuple-element.21.face, bf16[10,16,128]{2,1,0:T(8,128)(2,1)S(1)} %get-tuple-element.22.far, ...), custom_call_target="tpu_custom_call" | custom-call | flops 113246208 | bytes 524288 | tf_op jit(solution)/shard_map/backward/pallas_call | solution.py:250
  58.7 3.1 %collective-permute-start.6 = (bf16[4,8,16,128]{3,2,1,0:T(8,128)(2,1)S(1)}, bf16[4,8,16,128]{3,2,1,0:T(8,128)(2,1)S(1)}, u32[]{:S(2)}, u32[]{:S(2)}) collective-permute-start(bf16[4,8,16,128]{3,2,1,0:T(8,128)(2,1)S(1)} %get-tuple-element.24), channel_id=1, source_target_pairs={{0,1},{1,0},{2,3},{3,2},{4,5},{5,4},{6,7},{7,6},{8,9},{9,8},{10,11... | collective-permute-start | bytes 393224 | tf_op jit(solution)/shard_map/ppermute | solution.py:263
  61.8 3.8 %collective-permute-done.6 = bf16[4,8,16,128]{3,2,1,0:T(8,128)(2,1)S(1)} collective-permute-done((bf16[4,8,16,128]{3,2,1,0:T(8,128)(2,1)S(1)}, bf16[4,8,16,128]{3,2,1,0:T(8,128)(2,1)S(1)}, u32[]{:S(2)}, u32[]{:S(2)}) %collective-permute-start.6) | collective-permute-done | bytes 131104 | tf_op jit(solution)/shard_map/ppermute | solution.py:263
  65.6 1.9 %all-to-all-done.1 = bf16[8,7,16,128]{3,2,1,0:T(8,128)(2,1)S(1)} async-done(((bf16[8,7,16,128]{3,2,1,0:T(8,128)(2,1)}), bf16[8,7,16,128]{3,2,1,0:T(8,128)(2,1)S(1)}, u32[]{:S(2)}, u32[]{:S(2)}) %all-to-all-start.1) | async-done | bytes 229408 | tf_op jit(solution)/shard_map/all_to_all | solution.py:21
  67.6 0.7 broadcast_in_dim.14
  68.3 7.2 %all-to-all-start.2 = ((bf16[8,7,16,128]{3,2,1,0:T(8,128)(2,1)}), bf16[8,7,16,128]{3,2,1,0:T(8,128)(2,1)S(1)}, u32[]{:S(2)}, u32[]{:S(2)}) async-start(bf16[8,7,16,128]{3,2,1,0:T(8,128)(2,1)} %broadcast_in_dim.14), calls=%async_computation.2 | async-start | bytes 458752 | tf_op jit(solution)/shard_map/all_to_all | solution.py:21
  75.5 2.6 %collective-permute-start.7 = (bf16[8,16,128]{2,1,0:T(8,128)(2,1)S(1)}, bf16[8,16,128]{2,1,0:T(8,128)(2,1)S(1)}, u32[]{:S(2)}, u32[]{:S(2)}) collective-permute-start(bf16[8,16,128]{2,1,0:T(8,128)(2,1)S(1)} %get-tuple-element.30), channel_id=1, source_target_pairs={{0,2},{1,3},{2,0},{3,1},{4,6},{5,7},{6,4},{7,5},{8,10},{9,11},{10,... | collective-permute-start | bytes 98312 | tf_op jit(solution)/shard_map/ppermute | solution.py:266
  78.1 4.0 %collective-permute-start.8 = (bf16[8,16,128]{2,1,0:T(8,128)(2,1)S(1)}, bf16[8,16,128]{2,1,0:T(8,128)(2,1)S(1)}, u32[]{:S(2)}, u32[]{:S(2)}) collective-permute-start(bf16[8,16,128]{2,1,0:T(8,128)(2,1)S(1)} %get-tuple-element.32), channel_id=1, source_target_pairs={{0,4},{1,5},{2,6},{3,7},{4,0},{5,1},{6,2},{7,3},{8,12},{9,13},{10,... | collective-permute-start | bytes 98312 | tf_op jit(solution)/shard_map/ppermute | solution.py:266
  82.1 3.8 %collective-permute-start.9 = (bf16[8,16,128]{2,1,0:T(8,128)(2,1)S(1)}, bf16[8,16,128]{2,1,0:T(8,128)(2,1)S(1)}, u32[]{:S(2)}, u32[]{:S(2)}) collective-permute-start(bf16[8,16,128]{2,1,0:T(8,128)(2,1)S(1)} %get-tuple-element.31), channel_id=1, source_target_pairs={{0,6},{1,7},{2,4},{3,5},{4,2},{5,3},{6,0},{7,1},{8,14},{9,15},{10,... | collective-permute-start | bytes 98312 | tf_op jit(solution)/shard_map/ppermute | solution.py:266
  85.9 0.6 copy.53
  86.6 2.5 %collective-permute-done.9 = bf16[8,16,128]{2,1,0:T(8,128)(2,1)S(1)} collective-permute-done((bf16[8,16,128]{2,1,0:T(8,128)(2,1)S(1)}, bf16[8,16,128]{2,1,0:T(8,128)(2,1)S(1)}, u32[]{:S(2)}, u32[]{:S(2)}) %collective-permute-start.9) | collective-permute-done | bytes 32800 | tf_op jit(solution)/shard_map/ppermute | solution.py:266
  89.1 0.6 copy.55
  89.8 0.0 copy-start
  89.8 0.1 fusion.7
  89.9 0.6 copy-done
  90.5 0.0 slice-start
  90.5 0.6 slice_reduce_fusion
  91.1 0.2 slice-done
  91.4 0.1 reshape.67
  91.5 0.2 pad_maximum_fusion
  91.7 0.7 copy.45
  (27 shorter events, 0.3 us)
Async XLA Ops:
  1.4 7.2 %collective-permute-start = (bf16[8,8,128]{2,1,0:T(8,128)(2,1)S(1)}, bf16[8,8,128]{2,1,0:T(8,128)(2,1)S(1)}, u32[]{:S(2)}, u32[]{:S(2)}) collective-permute-start(bf16[8,8,128]{2,1,0:T(8,128)(2,1)S(1)} %get-tuple-element.41), channel_id=1, source_target_pairs={{64,128},{128,64},{192,256},{256,192},{320,384},{384,320},{65,129}... | collective-permute-start | bytes 49160 | tf_op jit(solution)/shard_map/ppermute | solution.py:192
  4.0 4.6 %collective-permute-start.1 = (bf16[8,8,128]{2,1,0:T(8,128)(2,1)S(1)}, bf16[8,8,128]{2,1,0:T(8,128)(2,1)S(1)}, u32[]{:S(2)}, u32[]{:S(2)}) collective-permute-start(bf16[8,8,128]{2,1,0:T(8,128)(2,1)S(1)} %get-tuple-element.42), channel_id=1, source_target_pairs={{0,64},{64,0},{128,192},{192,128},{256,320},{320,256},{384,448},{4... | collective-permute-start | bytes 49160 | tf_op jit(solution)/shard_map/ppermute | solution.py:191
  9.6 5.9 %copy-start.2 = (bf16[16,2,8,128]{3,2,1,0:T(8,128)(2,1)S(1)}, bf16[16,2,8,128]{3,2,1,0:T(8,128)(2,1)}, u32[]{:S(2)}) copy-start(bf16[16,2,8,128]{3,2,1,0:T(8,128)(2,1)} %param.8) | copy-start | bytes 196612
  9.6 13.7 %all-to-all-start = ((bf16[8,4,4,16,128]{4,3,2,1,0:T(8,128)(2,1)}), bf16[8,4,4,16,128]{4,3,2,1,0:T(8,128)(2,1)S(1)}, u32[]{:S(2)}, u32[]{:S(2)}) async-start(bf16[8,4,4,16,128]{4,3,2,1,0:T(8,128)(2,1)} %broadcast_in_dim.11), calls=%async_computation | async-start | bytes 1048576 | tf_op jit(solution)/shard_map/all_to_all | solution.py:21
  15.5 0.9 copy-start.1
  16.4 0.9 %copy-start.3 = (bf16[2,192,256,1]{2,1,3,0:T(8,128)(2,1)S(1)}, bf16[2,192,256,1]{2,1,3,0:T(8,128)(2,1)}, u32[]{:S(2)}) copy-start(bf16[2,192,256,1]{2,1,3,0:T(8,128)(2,1)} %constant.46) | copy-start | bytes 589828
  23.3 0.7 copy-start.4
  24.0 6.9 %collective-permute-start.2 = (bf16[34,16,128]{2,1,0:T(8,128)(2,1)S(1)}, bf16[34,16,128]{2,1,0:T(8,128)(2,1)S(1)}, u32[]{:S(2)}, u32[]{:S(2)}) collective-permute-start(bf16[34,16,128]{2,1,0:T(8,128)(2,1)S(1)} %get-tuple-element.18), channel_id=1, source_target_pairs={{0,8},{8,16},{16,24},{24,32},{32,40},{40,48},{48,56},{1,9},{9,17},... | collective-permute-start | bytes 417800 | tf_op jit(solution)/shard_map/ppermute | solution.py:26
  28.3 7.3 %collective-permute-start.3 = (bf16[34,16,128]{2,1,0:T(8,128)(2,1)S(1)}, bf16[34,16,128]{2,1,0:T(8,128)(2,1)S(1)}, u32[]{:S(2)}, u32[]{:S(2)}) collective-permute-start(bf16[34,16,128]{2,1,0:T(8,128)(2,1)S(1)} %get-tuple-element.19), channel_id=1, source_target_pairs={{8,0},{16,8},{24,16},{32,24},{40,32},{48,40},{56,48},{9,1},{17,9},... | collective-permute-start | bytes 417800 | tf_op jit(solution)/shard_map/ppermute | solution.py:27
  40.0 7.3 %collective-permute-start.4 = (bf16[17,16,128]{2,1,0:T(8,128)(2,1)S(1)}, bf16[17,16,128]{2,1,0:T(8,128)(2,1)S(1)}, u32[]{:S(2)}, u32[]{:S(2)}) collective-permute-start(bf16[17,16,128]{2,1,0:T(8,128)(2,1)S(1)} %get-tuple-element.21.face), channel_id=1, source_target_pairs={{0,64},{64,0},{128,192},{192,128},{256,320},{320,256},{384,448},{4... | collective-permute-start | bytes 208904 | tf_op jit(solution)/shard_map/ppermute | solution.py:237
  41.9 15.6 %collective-permute-start.5 = (bf16[10,16,128]{2,1,0:T(8,128)(2,1)S(1)}, bf16[10,16,128]{2,1,0:T(8,128)(2,1)S(1)}, u32[]{:S(2)}, u32[]{:S(2)}) collective-permute-start(bf16[10,16,128]{2,1,0:T(8,128)(2,1)S(1)} %get-tuple-element.22.far), channel_id=1, source_target_pairs={{64,128},{128,64},{192,256},{256,192},{320,384},{384,320},{65,129}... | collective-permute-start | bytes 122888 | tf_op jit(solution)/shard_map/ppermute | solution.py:238
  48.1 19.5 %all-to-all-start.1 = ((bf16[8,7,16,128]{3,2,1,0:T(8,128)(2,1)}), bf16[8,7,16,128]{3,2,1,0:T(8,128)(2,1)S(1)}, u32[]{:S(2)}, u32[]{:S(2)}) async-start(bf16[8,7,16,128]{3,2,1,0:T(8,128)(2,1)} %broadcast_in_dim.13), calls=%async_computation.1 | async-start | bytes 458752 | tf_op jit(solution)/shard_map/all_to_all | solution.py:21
  58.7 6.9 %collective-permute-start.6 = (bf16[4,8,16,128]{3,2,1,0:T(8,128)(2,1)S(1)}, bf16[4,8,16,128]{3,2,1,0:T(8,128)(2,1)S(1)}, u32[]{:S(2)}, u32[]{:S(2)}) collective-permute-start(bf16[4,8,16,128]{3,2,1,0:T(8,128)(2,1)S(1)} %get-tuple-element.24), channel_id=1, source_target_pairs={{0,1},{1,0},{2,3},{3,2},{4,5},{5,4},{6,7},{7,6},{8,9},{9,8},{10,11... | collective-permute-start | bytes 393224 | tf_op jit(solution)/shard_map/ppermute | solution.py:263
  68.3 21.5 %all-to-all-start.2 = ((bf16[8,7,16,128]{3,2,1,0:T(8,128)(2,1)}), bf16[8,7,16,128]{3,2,1,0:T(8,128)(2,1)S(1)}, u32[]{:S(2)}, u32[]{:S(2)}) async-start(bf16[8,7,16,128]{3,2,1,0:T(8,128)(2,1)} %broadcast_in_dim.14), calls=%async_computation.2 | async-start | bytes 458752 | tf_op jit(solution)/shard_map/all_to_all | solution.py:21
  75.5 11.1 %collective-permute-start.7 = (bf16[8,16,128]{2,1,0:T(8,128)(2,1)S(1)}, bf16[8,16,128]{2,1,0:T(8,128)(2,1)S(1)}, u32[]{:S(2)}, u32[]{:S(2)}) collective-permute-start(bf16[8,16,128]{2,1,0:T(8,128)(2,1)S(1)} %get-tuple-element.30), channel_id=1, source_target_pairs={{0,2},{1,3},{2,0},{3,1},{4,6},{5,7},{6,4},{7,5},{8,10},{9,11},{10,... | collective-permute-start | bytes 98312 | tf_op jit(solution)/shard_map/ppermute | solution.py:266
  78.1 8.5 %collective-permute-start.8 = (bf16[8,16,128]{2,1,0:T(8,128)(2,1)S(1)}, bf16[8,16,128]{2,1,0:T(8,128)(2,1)S(1)}, u32[]{:S(2)}, u32[]{:S(2)}) collective-permute-start(bf16[8,16,128]{2,1,0:T(8,128)(2,1)S(1)} %get-tuple-element.32), channel_id=1, source_target_pairs={{0,4},{1,5},{2,6},{3,7},{4,0},{5,1},{6,2},{7,3},{8,12},{9,13},{10,... | collective-permute-start | bytes 98312 | tf_op jit(solution)/shard_map/ppermute | solution.py:266
  82.1 7.0 %collective-permute-start.9 = (bf16[8,16,128]{2,1,0:T(8,128)(2,1)S(1)}, bf16[8,16,128]{2,1,0:T(8,128)(2,1)S(1)}, u32[]{:S(2)}, u32[]{:S(2)}) collective-permute-start(bf16[8,16,128]{2,1,0:T(8,128)(2,1)S(1)} %get-tuple-element.31), channel_id=1, source_target_pairs={{0,6},{1,7},{2,4},{3,5},{4,2},{5,3},{6,0},{7,1},{8,14},{9,15},{10,... | collective-permute-start | bytes 98312 | tf_op jit(solution)/shard_map/ppermute | solution.py:266
  89.8 0.6 copy-start
  90.5 0.9 slice-start

commit v5 on v4

--- a/solution.py
+++ b/solution.py
@@ -131,10 +131,10 @@
     kept_ref[...] = halves[core]
 
 
-def backward_kernel(planes, rows, at_ref, w_ref, face, far, face_in, far_in, kept_ref, sent_ref, stack, parts):
+def backward_kernel(planes, rows, at_ref, w_ref, face, far, face_in, far_in, parts, stack):
     cout, width = far.shape[1:]
     cin = w_ref.shape[0]
-    count = 2 * parts.shape[1]
+    count = parts.shape[0]
     part = cin // count
     lane = lax.broadcasted_iota(jnp.int32, (cout, width), 1)
     step = 3 * cout
@@ -160,9 +160,7 @@
             for f in range(count):
                 piece = acc[f * part : (f + 1) * part]
                 piece = jnp.concatenate([piece[:, :width], piece[:, width:]], axis=0).astype(BF16)
-                parts[(f % 2) ^ at_ref[1], (f // 2) ^ at_ref[2], pair] = piece
-    kept_ref[...] = parts[0]
-    sent_ref[...] = parts[1]
+                parts[f, pair] = piece
 
 
 def placing(cin):
@@ -183,8 +181,7 @@
     even = core == 0
     swap = [(i, i ^ 1) for i in range(depth)]
     cross = [(i, i - 1 if i % 2 == 0 else i + 1) for i in range(1, depth - 1)]
-    mine = lax.axis_index("filt")
-    at = jnp.stack([core, mine % 2, mine // 2]).astype(jnp.int32)
+    at = core.astype(jnp.int32).reshape(1)
     struct = jax.ShapeDtypeStruct
 
     grid = activations.transpose(1, 2, 0, 3)
@@ -239,7 +236,23 @@
     total = (kept.astype(F32) + face_in[rows + 2 :].astype(F32)).astype(BF16)
     total = copies(total, lax.axis_size("height"))
     total = jnp.sum(swapped(total, "height").astype(F32), axis=0).astype(BF16)
-    total = swapped(copies(total, depth), "depth").reshape((depth // 2, 2 * count) + total.shape[1:])
+    total = swapped(copies(total, depth), "depth")
+
+    parts = pl.pallas_call(
+        functools.partial(backward_kernel, planes, rows),
+        out_shape=struct((filt, cells // 2, 2 * cin_dev, width), BF16),
+        in_specs=[smem] + [vmem] * 5,
+        out_specs=vmem,
+        compiler_params=pltpu.CompilerParams(vmem_limit_bytes=12 << 20),
+        scratch_shapes=[pltpu.VMEM((planes + 2, (rows + 2) * 3 * cout, width), BF16)],
+        cost_estimate=pl.CostEstimate(flops=work, bytes_accessed=1 << 19, transcendentals=0),
+        name="backward",
+    )(at, w_back, face, far, face_in, far_in)
+    parts, total = lax.optimization_barrier((parts, total))
+    summed = jnp.sum(swapped(parts, "filt").astype(F32), axis=0).astype(BF16)
+    summed = summed.reshape(planes, rows, cin_dev, width).transpose(2, 0, 1, 3)
+
+    total = total.reshape(depth // 2, 2 * count, cout, width)
     total = jnp.sum(total.astype(F32), axis=0)
     first = total[:9].reshape(3, 3, cout, 2, cin).transpose(0, 3, 1, 2, 4)
     rest = total[9:].reshape(5, cout, 2, cin).transpose(0, 2, 1, 3).reshape(10, cout, cin)
@@ -247,25 +260,6 @@
     weight_grad = jnp.concatenate([first, third], axis=1).reshape(taps, cout, cin).transpose(0, 2, 1)
     bias_grad = rest[9, :, 0]
 
-    kept, sent = pl.pallas_call(
-        functools.partial(backward_kernel, planes, rows),
-        out_shape=(struct((filt // 2, cells // 2, 2 * cin_dev, width), BF16),) * 2,
-        in_specs=[smem] + [vmem] * 5,
-        out_specs=(vmem,) * 2,
-        compiler_params=pltpu.CompilerParams(vmem_limit_bytes=12 << 20),
-        scratch_shapes=[
-            pltpu.VMEM((planes + 2, (rows + 2) * 3 * cout, width), BF16),
-            pltpu.VMEM((2, filt // 2, cells // 2, 2 * cin_dev, width), BF16),
-        ],
-        cost_estimate=pl.CostEstimate(flops=work, bytes_accessed=1 << 19, transcendentals=0),
-        name="backward",
-    )(at, w_back, face, far, face_in, far_in)
-    pair = kept.astype(F32) + lax.ppermute(sent, "filt", [(i, i ^ 1) for i in range(filt)]).astype(F32)
-    summed = pair[0]
-    for k in range(1, filt // 2):
-        moved = lax.ppermute(pair[k].astype(BF16), "filt", [(i, i ^ (2 * k)) for i in range(filt)])
-        summed = summed + moved.astype(F32)
-    summed = summed.astype(BF16).reshape(planes, rows, cin_dev, width).transpose(2, 0, 1, 3)
     return (output, summed, weight_grad, bias_grad)
 
 

time: 93.2 us -> 94.8 us (1.017)
  the two profiles are of different devices: /device:TPU:40 before, /device:TPU:8 now
where the time goes in v5:
time: 94.8 us; the launch traced here: 93.9 us
  starting transfers between devices  30.1 us (32%)
  waiting for transfers between devices  27.8 us (29%)
  blocking collectives  20.6 us (22%)
  local copies, waits for them, and re-layouts  8.81 us (9%)
  Pallas kernels  5.15 us (5%)
    all_to_all x1, blocking collectives, swapped(): return lax.all_to_all(blocks, axis, 0, 0, tiled=True)  20.6 us
    all_to_all x3, waiting for transfers between devices, swapped(): return lax.all_to_all(blocks, axis, 0, 0, tiled=True)  19.8 us
    all_to_all x3, starting transfers between devices, swapped(): return lax.all_to_all(blocks, axis, 0, 0, tiled=True)  15.4 us
    ppermute x1, starting transfers between devices, per_device(): lax.ppermute(jnp.where(even, grid[planes - 1], grid[0]), 'depth', swap)  5.86 us
    ppermute x1, waiting for transfers between devices, neighbours(): after = lax.ppermute(first, axis, [(i + 1, i) for i in range(ends)])  4.73 us
    ppermute x1, starting transfers between devices, neighbours(): before = lax.ppermute(last, axis, [(i, i + 1) for i in range(ends)])  4.27 us
    pallas_call x1, Pallas kernels, per_device(): pl.pallas_call(functools.partial(forward_kernel, planes, rows), out_shape...  3.84 us
    unnamed x13, local copies, waits for them, and re-layouts  3.66 us
  transfers between devices with their start and end apart: 9, of which 7 were waited for; matrix products, arithmetic and copies ran while one was open for 3% of the time, Pallas kernels for 1%

profile of v5, /device:TPU:8, one launch (start us, length us, event | category | flops | bytes accessed | tf_op | source)
XLA Modules:
  0.0 93.9 jit_solution(2527045865233834067)
XLA Ops:
  0.6 0.8 copy.53
  1.4 0.7 collective-permute-start
  2.1 5.9 %collective-permute-start.1 = (bf16[8,8,128]{2,1,0:T(8,128)(2,1)S(1)}, bf16[8,8,128]{2,1,0:T(8,128)(2,1)S(1)}, u32[]{:S(2)}, u32[]{:S(2)}) collective-permute-start(bf16[8,8,128]{2,1,0:T(8,128)(2,1)S(1)} %get-tuple-element.49), channel_id=1, source_target_pairs={{0,64},{64,0},{128,192},{192,128},{256,320},{320,256},{384,448},{4... | collective-permute-start | bytes 49160 | tf_op jit(solution)/shard_map/ppermute | solution.py:188
  8.0 0.0 collective-permute-done
  8.0 0.8 collective-permute-done.1
  8.8 0.9 broadcast_in_dim.11
  9.7 0.0 copy-start.2
  9.7 5.9 %all-to-all-start = ((bf16[8,4,4,16,128]{4,3,2,1,0:T(8,128)(2,1)}), bf16[8,4,4,16,128]{4,3,2,1,0:T(8,128)(2,1)S(1)}, u32[]{:S(2)}, u32[]{:S(2)}) async-start(bf16[8,4,4,16,128]{4,3,2,1,0:T(8,128)(2,1)} %broadcast_in_dim.11), calls=%async_computation | async-start | bytes 1048576 | tf_op jit(solution)/shard_map/all_to_all | solution.py:21
  15.6 0.0 copy-done.2
  15.6 0.0 copy-start.1
  15.6 0.9 copy-done.1
  16.5 0.0 copy-start.3
  16.5 0.1 copy.39
  16.6 0.1 reshape.74
  16.7 0.7 copy-done.3
  17.4 0.2 fusion
  17.7 7.4 %all-to-all-done.tiles = bf16[8,4,4,16,128]{4,3,2,1,0:T(8,128)(2,1)S(1)} async-done(((bf16[8,4,4,16,128]{4,3,2,1,0:T(8,128)(2,1)}), bf16[8,4,4,16,128]{4,3,2,1,0:T(8,128)(2,1)S(1)}, u32[]{:S(2)}, u32[]{:S(2)}) %all-to-all-start) | async-done | bytes 524320 | tf_op jit(solution)/shard_map/all_to_all | solution.py:21
  25.1 0.0 copy-start.4
  25.1 0.6 copy-done.4
  25.8 0.1 broadcast_in_dim.12.bias_ref
  25.8 4.3 %collective-permute-start.2 = (bf16[34,16,128]{2,1,0:T(8,128)(2,1)S(1)}, bf16[34,16,128]{2,1,0:T(8,128)(2,1)S(1)}, u32[]{:S(2)}, u32[]{:S(2)}) collective-permute-start(bf16[34,16,128]{2,1,0:T(8,128)(2,1)S(1)} %get-tuple-element.18), channel_id=1, source_target_pairs={{0,8},{8,16},{16,24},{24,32},{32,40},{40,48},{48,56},{1,9},{9,17},... | collective-permute-start | bytes 417800 | tf_op jit(solution)/shard_map/ppermute | solution.py:26
  30.1 1.3 %collective-permute-start.3 = (bf16[34,16,128]{2,1,0:T(8,128)(2,1)S(1)}, bf16[34,16,128]{2,1,0:T(8,128)(2,1)S(1)}, u32[]{:S(2)}, u32[]{:S(2)}) collective-permute-start(bf16[34,16,128]{2,1,0:T(8,128)(2,1)S(1)} %get-tuple-element.19), channel_id=1, source_target_pairs={{8,0},{16,8},{24,16},{32,24},{40,32},{48,40},{56,48},{9,1},{17,9},... | collective-permute-start | bytes 417800 | tf_op jit(solution)/shard_map/ppermute | solution.py:27
  31.4 1.3 %collective-permute-done.2.before = bf16[34,16,128]{2,1,0:T(8,128)(2,1)S(1)} collective-permute-done((bf16[34,16,128]{2,1,0:T(8,128)(2,1)S(1)}, bf16[34,16,128]{2,1,0:T(8,128)(2,1)S(1)}, u32[]{:S(2)}, u32[]{:S(2)}) %collective-permute-start.2) | collective-permute-done | bytes 139296 | tf_op jit(solution)/shard_map/ppermute | solution.py:26
  32.7 4.7 %collective-permute-done.3.after = bf16[34,16,128]{2,1,0:T(8,128)(2,1)S(1)} collective-permute-done((bf16[34,16,128]{2,1,0:T(8,128)(2,1)S(1)}, bf16[34,16,128]{2,1,0:T(8,128)(2,1)S(1)}, u32[]{:S(2)}, u32[]{:S(2)}) %collective-permute-start.3) | collective-permute-done | bytes 139296 | tf_op jit(solution)/shard_map/ppermute | solution.py:27
  37.4 3.8 %forward.1 = (bf16[16,16,128]{2,1,0:T(8,128)(2,1)S(1)}, bf16[17,16,128]{2,1,0:T(8,128)(2,1)S(1)}, bf16[10,16,128]{2,1,0:T(8,128)(2,1)S(1)}, bf16[7,16,128]{2,1,0:T(8,128)(2,1)S(1)}) custom-call(s32[1]{0:T(128)} %bitcast.at_ref, bf16[3,96,256]{2,1,0:T(8,128)(2,1)S(1)} %bitcast.55, f32[16,128]{1,0:T(8,128)S(1)} %broadcast_in_dim.12.bias_ref, ...), custom_call_target="tpu_custom_call" | custom-call | flops 339738624 | bytes 1048576 | tf_op jit(solution)/shard_map/forward/pallas_call | solution.py:214
  41.3 1.9 %collective-permute-start.4 = (bf16[17,16,128]{2,1,0:T(8,128)(2,1)S(1)}, bf16[17,16,128]{2,1,0:T(8,128)(2,1)S(1)}, u32[]{:S(2)}, u32[]{:S(2)}) collective-permute-start(bf16[17,16,128]{2,1,0:T(8,128)(2,1)S(1)} %get-tuple-element.21.face), channel_id=1, source_target_pairs={{0,64},{64,0},{128,192},{192,128},{256,320},{320,256},{384,448},{4... | collective-permute-start | bytes 208904 | tf_op jit(solution)/shard_map/ppermute | solution.py:234
  43.2 1.2 %collective-permute-done.4.face_in = bf16[17,16,128]{2,1,0:T(8,128)(2,1)S(1)} collective-permute-done((bf16[17,16,128]{2,1,0:T(8,128)(2,1)S(1)}, bf16[17,16,128]{2,1,0:T(8,128)(2,1)S(1)}, u32[]{:S(2)}, u32[]{:S(2)}) %collective-permute-start.4) | collective-permute-done | bytes 69664 | tf_op jit(solution)/shard_map/ppermute | solution.py:234
  44.5 20.6 %all_to_all.20 = bf16[8,7,16,128]{3,2,1,0:T(8,128)(2,1)S(1)} all-to-all(bf16[8,7,16,128]{3,2,1,0:T(8,128)(2,1)S(1)} %broadcast_in_dim.13), channel_id=1, replica_groups=mesh['depth'=8,'height'=8,'filt'=8] {'height'}, dimensions={0} | all-to-all | bytes 458752 | tf_op jit(solution)/shard_map/all_to_all | solution.py:21
  65.1 0.7 broadcast_in_dim.14
  65.8 4.4 %all-to-all-start.2 = ((bf16[8,7,16,128]{3,2,1,0:T(8,128)(2,1)}), bf16[8,7,16,128]{3,2,1,0:T(8,128)(2,1)S(1)}, u32[]{:S(2)}, u32[]{:S(2)}) async-start(bf16[8,7,16,128]{3,2,1,0:T(8,128)(2,1)} %broadcast_in_dim.14), calls=%async_computation.2 | async-start | bytes 458752 | tf_op jit(solution)/shard_map/all_to_all | solution.py:21
  70.2 0.7 collective-permute-start.5
  70.9 0.1 copy.42.w_ref
  71.0 0.6 copy.51
  71.7 0.0 collective-permute-done.5.far_in
  71.7 1.3 %backward.1 = bf16[8,8,16,128]{3,2,1,0:T(8,128)(2,1)} custom-call(s32[1]{0:T(128)} %bitcast.at_ref, bf16[64,432]{1,0:T(8,128)(2,1)S(1)} %copy.42.w_ref, bf16[17,16,128]{2,1,0:T(8,128)(2,1)S(1)} %get-tuple-element.21.face, bf16[10,16,128]{2,1,0:T(8,128)(2,1)S(1)} %get-tuple-element.22.far, bf16[17,16,128]{2,1,0:T(8,128)(2,1)S(1)} %collective-permute-done.4.face_in, ...), custom_call_target="tpu_custom_call" | custom-call | flops 113246208 | bytes 524288 | tf_op jit(solution)/shard_map/backward/pallas_call | solution.py:241
  73.0 8.9 %all-to-all-done.2 = bf16[8,7,16,128]{3,2,1,0:T(8,128)(2,1)S(1)} async-done(((bf16[8,7,16,128]{3,2,1,0:T(8,128)(2,1)}), bf16[8,7,16,128]{3,2,1,0:T(8,128)(2,1)S(1)}, u32[]{:S(2)}, u32[]{:S(2)}) %all-to-all-start.2) | async-done | bytes 229408 | tf_op jit(solution)/shard_map/all_to_all | solution.py:21
  82.0 0.0 copy-start
  82.0 5.2 %all-to-all-start.3 = ((bf16[8,8,16,128]{3,2,1,0:T(8,128)(2,1)}), bf16[8,8,16,128]{3,2,1,0:T(8,128)(2,1)S(1)}, u32[]{:S(2)}, u32[]{:S(2)}) async-start(bf16[8,8,16,128]{3,2,1,0:T(8,128)(2,1)} %backward.1), calls=%async_computation.3 | async-start | bytes 524288 | tf_op jit(solution)/shard_map/all_to_all | solution.py:21
  87.1 0.1 fusion.2
  87.2 0.0 copy-done
  87.2 0.0 slice-start
  87.2 0.9 slice-done
  88.1 0.1 reshape.68
  88.2 0.2 pad_maximum_fusion
  88.4 0.7 copy.43
  89.1 0.6 slice_reduce_fusion
  89.7 3.5 %all-to-all-done.3 = bf16[8,8,16,128]{3,2,1,0:T(8,128)(2,1)S(1)} async-done(((bf16[8,8,16,128]{3,2,1,0:T(8,128)(2,1)}), bf16[8,8,16,128]{3,2,1,0:T(8,128)(2,1)S(1)}, u32[]{:S(2)}, u32[]{:S(2)}) %all-to-all-start.3) | async-done | bytes 262176 | tf_op jit(solution)/shard_map/all_to_all | solution.py:21
  93.3 0.6 copy.44
  (17 shorter events, 0.3 us)
Async XLA Ops:
  1.4 6.5 %collective-permute-start = (bf16[8,8,128]{2,1,0:T(8,128)(2,1)S(1)}, bf16[8,8,128]{2,1,0:T(8,128)(2,1)S(1)}, u32[]{:S(2)}, u32[]{:S(2)}) collective-permute-start(bf16[8,8,128]{2,1,0:T(8,128)(2,1)S(1)} %get-tuple-element.48), channel_id=1, source_target_pairs={{64,128},{128,64},{192,256},{256,192},{320,384},{384,320},{65,129}... | collective-permute-start | bytes 49160 | tf_op jit(solution)/shard_map/ppermute | solution.py:189
  2.1 6.7 %collective-permute-start.1 = (bf16[8,8,128]{2,1,0:T(8,128)(2,1)S(1)}, bf16[8,8,128]{2,1,0:T(8,128)(2,1)S(1)}, u32[]{:S(2)}, u32[]{:S(2)}) collective-permute-start(bf16[8,8,128]{2,1,0:T(8,128)(2,1)S(1)} %get-tuple-element.49), channel_id=1, source_target_pairs={{0,64},{64,0},{128,192},{192,128},{256,320},{320,256},{384,448},{4... | collective-permute-start | bytes 49160 | tf_op jit(solution)/shard_map/ppermute | solution.py:188
  9.7 5.9 %copy-start.2 = (bf16[16,2,8,128]{3,2,1,0:T(8,128)(2,1)S(1)}, bf16[16,2,8,128]{3,2,1,0:T(8,128)(2,1)}, u32[]{:S(2)}) copy-start(bf16[16,2,8,128]{3,2,1,0:T(8,128)(2,1)} %param.8) | copy-start | bytes 196612
  9.7 15.3 %all-to-all-start = ((bf16[8,4,4,16,128]{4,3,2,1,0:T(8,128)(2,1)}), bf16[8,4,4,16,128]{4,3,2,1,0:T(8,128)(2,1)S(1)}, u32[]{:S(2)}, u32[]{:S(2)}) async-start(bf16[8,4,4,16,128]{4,3,2,1,0:T(8,128)(2,1)} %broadcast_in_dim.11), calls=%async_computation | async-start | bytes 1048576 | tf_op jit(solution)/shard_map/all_to_all | solution.py:21
  15.6 0.9 copy-start.1
  16.5 0.9 copy-start.3
  25.1 0.7 copy-start.4
  25.8 6.9 %collective-permute-start.2 = (bf16[34,16,128]{2,1,0:T(8,128)(2,1)S(1)}, bf16[34,16,128]{2,1,0:T(8,128)(2,1)S(1)}, u32[]{:S(2)}, u32[]{:S(2)}) collective-permute-start(bf16[34,16,128]{2,1,0:T(8,128)(2,1)S(1)} %get-tuple-element.18), channel_id=1, source_target_pairs={{0,8},{8,16},{16,24},{24,32},{32,40},{40,48},{48,56},{1,9},{9,17},... | collective-permute-start | bytes 417800 | tf_op jit(solution)/shard_map/ppermute | solution.py:26
  30.1 7.3 %collective-permute-start.3 = (bf16[34,16,128]{2,1,0:T(8,128)(2,1)S(1)}, bf16[34,16,128]{2,1,0:T(8,128)(2,1)S(1)}, u32[]{:S(2)}, u32[]{:S(2)}) collective-permute-start(bf16[34,16,128]{2,1,0:T(8,128)(2,1)S(1)} %get-tuple-element.19), channel_id=1, source_target_pairs={{8,0},{16,8},{24,16},{32,24},{40,32},{48,40},{56,48},{9,1},{17,9},... | collective-permute-start | bytes 417800 | tf_op jit(solution)/shard_map/ppermute | solution.py:27
  41.3 3.2 %collective-permute-start.4 = (bf16[17,16,128]{2,1,0:T(8,128)(2,1)S(1)}, bf16[17,16,128]{2,1,0:T(8,128)(2,1)S(1)}, u32[]{:S(2)}, u32[]{:S(2)}) collective-permute-start(bf16[17,16,128]{2,1,0:T(8,128)(2,1)S(1)} %get-tuple-element.21.face), channel_id=1, source_target_pairs={{0,64},{64,0},{128,192},{192,128},{256,320},{320,256},{384,448},{4... | collective-permute-start | bytes 208904 | tf_op jit(solution)/shard_map/ppermute | solution.py:234
  65.8 16.1 %all-to-all-start.2 = ((bf16[8,7,16,128]{3,2,1,0:T(8,128)(2,1)}), bf16[8,7,16,128]{3,2,1,0:T(8,128)(2,1)S(1)}, u32[]{:S(2)}, u32[]{:S(2)}) async-start(bf16[8,7,16,128]{3,2,1,0:T(8,128)(2,1)} %broadcast_in_dim.14), calls=%async_computation.2 | async-start | bytes 458752 | tf_op jit(solution)/shard_map/all_to_all | solution.py:21
  70.2 1.4 %collective-permute-start.5 = (bf16[10,16,128]{2,1,0:T(8,128)(2,1)S(1)}, bf16[10,16,128]{2,1,0:T(8,128)(2,1)S(1)}, u32[]{:S(2)}, u32[]{:S(2)}) collective-permute-start(bf16[10,16,128]{2,1,0:T(8,128)(2,1)S(1)} %get-tuple-element.22.far), channel_id=1, source_target_pairs={{64,128},{128,64},{192,256},{256,192},{320,384},{384,320},{65,129}... | collective-permute-start | bytes 122888 | tf_op jit(solution)/shard_map/ppermute | solution.py:235
  82.0 5.2 %copy-start = (f32[14,16,128]{2,1,0:T(8,128)}, f32[14,16,128]{2,1,0:T(8,128)S(1)}, u32[]{:S(2)}) copy-start(f32[14,16,128]{2,1,0:T(8,128)S(1)} %convert_reduce_fusion) | copy-start | bytes 344068
  82.0 11.3 %all-to-all-start.3 = ((bf16[8,8,16,128]{3,2,1,0:T(8,128)(2,1)}), bf16[8,8,16,128]{3,2,1,0:T(8,128)(2,1)S(1)}, u32[]{:S(2)}, u32[]{:S(2)}) async-start(bf16[8,8,16,128]{3,2,1,0:T(8,128)(2,1)} %backward.1), calls=%async_computation.3 | async-start | bytes 524288 | tf_op jit(solution)/shard_map/all_to_all | solution.py:21
  87.2 0.9 slice-start

commit v6 on v5

--- a/solution.py
+++ b/solution.py
@@ -35,21 +35,49 @@
     return jnp.concatenate([ahead, value, behind], axis=0)
 
 
-def forward_kernel(planes, rows, at_ref, w_ref, bias_ref, cot, tiles, before, after, *refs):
+def planes_kernel(planes, at_ref, tiles, face_ref, far_ref):
+    core = at_ref[0]
+    face_ref[...] = tiles[:, jnp.where(core == 0, planes - 1, 0)]
+    far_ref[...] = tiles[:, jnp.where(core == 0, 0, planes - 1)]
+
+
+def rows_kernel(planes, rows, at_ref, tiles, facing, beyond, cot, first_ref, last_ref):
+    core = at_ref[0]
+    sources = tiles.shape[0]
+    before = jnp.where(core == 0, 0, (planes + 1) * sources)
+    after = (planes + 1) * sources - before
+    for ref, t, row in ((first_ref, 0, 0), (last_ref, rows // 2 - 1, rows - 1)):
+        ref[pl.ds(before, sources)] = beyond[:, t]
+        ref[pl.ds(after, sources)] = facing[:, t]
+        for d in range(planes):
+            ref[(d + 1) * sources : (d + 2) * sources] = tiles[:, d, t]
+            ref[(planes + 2) * sources + d] = cot[d * rows + row]
+
+
+def forward_kernel(planes, rows, at_ref, bias_ref, w_ref, cot, tiles, facing, beyond, before, after, *refs):
     out_ref, face_ref, far_ref, kept_ref, grads, halves = refs
     cout, width = cot.shape[1:]
     sources = tiles.shape[0]
     edge = sources * (planes + 2)
+    core = at_ref[0]
+    even = core == 0
 
     def tile(s, p, t):
         if t == 0:
-            return before[s * (planes + 2) + p]
+            return before[p * sources + s]
         if t == rows // 2 + 1:
-            return after[s * (planes + 2) + p]
-        return tiles[s, p, t - 1]
+            return after[p * sources + s]
+        if p == 0:
+            return jnp.where(even, beyond[s, t - 1], facing[s, t - 1])
+        if p == planes + 1:
+            return jnp.where(even, facing[s, t - 1], beyond[s, t - 1])
+        return tiles[s, p - 1, t - 1]
 
     lane = lax.broadcasted_iota(jnp.int32, (cout, width), 1)
-    bias = bias_ref[...]
+    channel = lax.broadcasted_iota(jnp.int32, (cout, width), 0)
+    bias = jnp.zeros((cout, width), F32)
+    for o in range(cout):
+        bias = jnp.where(channel == o, bias_ref[o], bias)
     sums = [None] * 3
     bias_sum = jnp.zeros((cout, width), F32)
     for d in range(planes):
@@ -98,7 +126,7 @@
                 )
                 sums[kd] = term if sums[kd] is None else sums[kd] + term
 
-    even = (lane // PART) % 2 == 0
+    first = (lane // PART) % 2 == 0
     blocks, last = [], []
     for kd in range(3):
         for kw in range(3):
@@ -108,7 +136,7 @@
             blocks.append(
                 one[:, :width]
                 + jnp.where(
-                    even,
+                    first,
                     pltpu.roll(two[:, :width], width - PART, 1),
                     pltpu.roll(two[:, width:], PART, 1),
                 )
@@ -116,7 +144,7 @@
             last.append(one[:, width:] + back)
     last.append(jnp.broadcast_to(jnp.sum(bias_sum, axis=1, keepdims=True), (cout, width)))
     for k in range(0, len(last), 2):
-        blocks.append(jnp.where(even, last[k], pltpu.roll(last[k + 1], PART, 1)))
+        blocks.append(jnp.where(first, last[k], pltpu.roll(last[k + 1], PART, 1)))
     source = lax.broadcasted_iota(jnp.int32, (width, width), 0)
     target = (source // PART) % 2 * (width // 2) + source // (2 * PART) * PART + source % PART
     order = jnp.where(lax.broadcasted_iota(jnp.int32, (width, width), 1) == target, 1.0, 0.0).astype(BF16)
@@ -124,7 +152,6 @@
     count = len(blocks) // 2
     for k in range(2 * count):
         halves[k // count, k % count] = placed[k * cout : (k + 1) * cout].astype(BF16)
-    core = at_ref[0]
     face_ref[: rows + 2] = grads[1 - core]
     face_ref[rows + 2 :] = halves[1 - core]
     far_ref[...] = grads[core]
@@ -178,19 +205,26 @@
     cells = planes * rows
     depth, filt = lax.axis_size("depth"), lax.axis_size("filt")
     core = lax.axis_index("depth") % 2
-    even = core == 0
     swap = [(i, i ^ 1) for i in range(depth)]
     cross = [(i, i - 1 if i % 2 == 0 else i + 1) for i in range(1, depth - 1)]
     at = core.astype(jnp.int32).reshape(1)
     struct = jax.ShapeDtypeStruct
 
-    grid = activations.transpose(1, 2, 0, 3)
-    face_in = lax.ppermute(jnp.where(even, grid[planes - 1], grid[0]), "depth", swap)
-    far_in = lax.ppermute(jnp.where(even, grid[0], grid[planes - 1]), "depth", cross)
-    low, high = jnp.where(even, far_in, face_in), jnp.where(even, face_in, far_in)
-    grid = jnp.concatenate([low[None], grid, high[None]], axis=0)
-    grid = grid.reshape(planes + 2, rows // 2, 2 * cin_dev, width)
+    grid = activations.transpose(1, 2, 0, 3).reshape(planes, rows // 2, 2 * cin_dev, width)
     tiles = swapped(copies(grid, filt), "filt")
+    smem, vmem = pl.BlockSpec(memory_space=pltpu.SMEM), pl.BlockSpec(memory_space=pltpu.VMEM)
+    grant = pltpu.CompilerParams(vmem_limit_bytes=12 << 20)
+    face, far = pl.pallas_call(
+        functools.partial(planes_kernel, planes),
+        out_shape=(struct((filt, rows // 2, 2 * cin_dev, width), BF16),) * 2,
+        in_specs=[smem, vmem],
+        out_specs=(vmem,) * 2,
+        compiler_params=grant,
+        cost_estimate=pl.CostEstimate(flops=0, bytes_accessed=1 << 19, transcendentals=0),
+        name="planes",
+    )(at, tiles)
+    facing = lax.ppermute(face, "depth", swap)
+    beyond = lax.ppermute(far, "depth", cross)
 
     cot = cotangent.transpose(1, 2, 0, 3)
     split = weights.reshape(3, 3, 3, cin, cout)
@@ -201,16 +235,21 @@
         preferred_element_type=F32,
     )
     w_forward = w_forward.astype(BF16).reshape(3, 6 * cout, 4 * cin)
-    wide = jnp.broadcast_to(bias[:, None], (cout, width))
     w_back = split[::-1, ::-1].transpose(3, 0, 1, 2, 4).reshape(cin, taps * cout)
-    first = jnp.concatenate([tiles[:, :, 0].reshape(-1, 2 * cin_dev, width), cot[:, 0]], axis=0)
-    last = jnp.concatenate([tiles[:, :, -1].reshape(-1, 2 * cin_dev, width), cot[:, rows - 1]], axis=0)
     cot = cot.reshape(cells, cout, width)
-    first, last, cot, w_forward, wide = lax.optimization_barrier((first, last, cot, w_forward, wide))
+    first, last = pl.pallas_call(
+        functools.partial(rows_kernel, planes, rows),
+        out_shape=(struct(((planes + 2) * filt + planes, cout, width), BF16),) * 2,
+        in_specs=[smem] + [vmem] * 4,
+        out_specs=(vmem,) * 2,
+        compiler_params=grant,
+        cost_estimate=pl.CostEstimate(flops=0, bytes_accessed=1 << 19, transcendentals=0),
+        name="rows",
+    )(at, tiles, facing, beyond, cot)
+    first, last, w_forward = lax.optimization_barrier((first, last, w_forward))
     before, after = neighbours(first, last, "height")
     work = 2 * cells * width * taps * cin * cout
     count = (taps + 1) // 4
-    smem, vmem = pl.BlockSpec(memory_space=pltpu.SMEM), pl.BlockSpec(memory_space=pltpu.VMEM)
     out, face, far, kept = pl.pallas_call(
         functools.partial(forward_kernel, planes, rows),
         out_shape=(
@@ -219,35 +258,36 @@
             struct((rows + 2, cout, width), BF16),
             struct((count, cout, width), BF16),
         ),
-        in_specs=[smem] + [vmem] * 6,
+        in_specs=[smem] * 2 + [vmem] * 7,
         out_specs=(vmem,) * 4,
-        compiler_params=pltpu.CompilerParams(vmem_limit_bytes=12 << 20),
+        compiler_params=grant,
         scratch_shapes=[
             pltpu.VMEM((planes, rows + 2, cout, width), BF16),
             pltpu.VMEM((2, count, cout, width), BF16),
         ],
         cost_estimate=pl.CostEstimate(flops=3 * work, bytes_accessed=1 << 20, transcendentals=1 << 17),
         name="forward",
-    )(at, w_forward, wide, cot, tiles, before, after)
+    )(at, bias, w_forward, cot, tiles, facing, beyond, before, after)
     output = out.reshape(planes, rows, cout, width).transpose(2, 0, 1, 3)
 
     face_in = lax.ppermute(face, "depth", swap)
     far_in = lax.ppermute(far, "depth", cross)
     total = (kept.astype(F32) + face_in[rows + 2 :].astype(F32)).astype(BF16)
-    total = copies(total, lax.axis_size("height"))
-    total = jnp.sum(swapped(total, "height").astype(F32), axis=0).astype(BF16)
-    total = swapped(copies(total, depth), "depth")
+    total = swapped(copies(total, lax.axis_size("height")), "height")
 
     parts = pl.pallas_call(
         functools.partial(backward_kernel, planes, rows),
         out_shape=struct((filt, cells // 2, 2 * cin_dev, width), BF16),
         in_specs=[smem] + [vmem] * 5,
         out_specs=vmem,
-        compiler_params=pltpu.CompilerParams(vmem_limit_bytes=12 << 20),
+        compiler_params=grant,
         scratch_shapes=[pltpu.VMEM((planes + 2, (rows + 2) * 3 * cout, width), BF16)],
         cost_estimate=pl.CostEstimate(flops=work, bytes_accessed=1 << 19, transcendentals=0),
         name="backward",
     )(at, w_back, face, far, face_in, far_in)
+    parts, total = lax.optimization_barrier((parts, total))
+    total = jnp.sum(total.astype(F32), axis=0).astype(BF16)
+    total = swapped(copies(total, depth), "depth")
     parts, total = lax.optimization_barrier((parts, total))
     summed = jnp.sum(swapped(parts, "filt").astype(F32), axis=0).astype(BF16)
     summed = summed.reshape(planes, rows, cin_dev, width).transpose(2, 0, 1, 3)

time: 94.8 us -> 97.4 us (1.027)
  blocking collectives: 20.6 us -> 0 us
  starting transfers between devices: 30.1 us -> 46.5 us
  waiting for transfers between devices: 27.8 us -> 35.1 us
    all_to_all x1 -> x0, blocking collectives: 20.6 us -> none  [swapped(): return lax.all_to_all(blocks, axis, 0, 0, tiled=True)]
    all_to_all x3 -> x4, starting transfers between devices: 15.4 us -> 32.4 us  [swapped(): return lax.all_to_all(blocks, axis, 0, 0, tiled=True)]
    all_to_all x3 -> x4, waiting for transfers between devices: 19.8 us -> 28.2 us  [swapped(): return lax.all_to_all(blocks, axis, 0, 0, tiled=True)]
    ppermute x1, starting transfers between devices: 1.92 us -> 8.24 us  [per_device(): face_in = lax.ppermute(face, 'depth', swap)]
    ppermute x2, starting transfers between devices: 6.52 us -> 2.59 us  [the longest x1 1.92 us: per_device(): facing = lax.ppermute(face, 'depth', swap)]
    ppermute x1, starting transfers between devices: 4.27 us -> 1.3 us  [neighbours(): before = lax.ppermute(last, axis, [(i, i + 1) for i in range(ends)])]
    unnamed x13 -> x12, local copies, waits for them, and re-layouts: 3.66 us -> 2.28 us
  transfers between devices with their start and end apart: 9 -> 10, of which waited for: 7 -> 8; matrix products, arithmetic and copies ran while one was open for 3% -> 3% of each run, Pallas kernels for 1% -> 1%
where the time goes in v6:
time: 97.4 us; the launch traced here: 96.6 us
  starting transfers between devices  46.5 us (48%)
  waiting for transfers between devices  35.1 us (36%)
  local copies, waits for them, and re-layouts  7.85 us (8%)
  Pallas kernels  5.75 us (6%)
    all_to_all x4, starting transfers between devices, swapped(): return lax.all_to_all(blocks, axis, 0, 0, tiled=True)  32.4 us
    all_to_all x4, waiting for transfers between devices, swapped(): return lax.all_to_all(blocks, axis, 0, 0, tiled=True)  28.2 us
    ppermute x1, starting transfers between devices, per_device(): face_in = lax.ppermute(face, 'depth', swap)  8.24 us
    pallas_call x1, Pallas kernels, per_device(): pl.pallas_call(functools.partial(forward_kernel, planes, rows), out_shape...  4.4 us
    ppermute x1, waiting for transfers between devices, neighbours(): after = lax.ppermute(first, axis, [(i + 1, i) for i in range(ends)])  4.38 us
    unnamed x12, local copies, waits for them, and re-layouts  2.28 us
    broadcast_in_dim x3, local copies, waits for them, and re-layouts, copies(): return jnp.broadcast_to(block[None], (count,) + block.shape)  2.18 us
  transfers between devices with their start and end apart: 10, of which 8 were waited for; matrix products, arithmetic and copies ran while one was open for 3% of the time, Pallas kernels for 1%

profile of v6, /device:TPU:8, one launch (start us, length us, event | category | flops | bytes accessed | tf_op | source)
XLA Modules:
  0.0 96.6 jit_solution(9490602047000485891)
XLA Ops:
  0.6 0.8 copy.30
  1.4 0.7 broadcast_in_dim.9
  2.1 0.0 copy-start.4
  2.2 9.3 %all-to-all-start = ((bf16[8,2,4,16,128]{4,3,2,1,0:T(8,128)(2,1)}), bf16[8,2,4,16,128]{4,3,2,1,0:T(8,128)(2,1)S(1)}, u32[]{:S(2)}, u32[]{:S(2)}) async-start(bf16[8,2,4,16,128]{4,3,2,1,0:T(8,128)(2,1)} %broadcast_in_dim.9), calls=%async_computation | async-start | bytes 524288 | tf_op jit(solution)/shard_map/all_to_all | solution.py:21
  11.4 0.0 copy-done.4
  11.4 0.9 copy-done.2
  12.3 0.1 copy.32
  12.4 0.0 copy-start.3
  12.4 0.1 reshape.65
  12.5 5.0 %all-to-all-done.tiles = bf16[8,2,4,16,128]{4,3,2,1,0:T(8,128)(2,1)S(1)} async-done(((bf16[8,2,4,16,128]{4,3,2,1,0:T(8,128)(2,1)}), bf16[8,2,4,16,128]{4,3,2,1,0:T(8,128)(2,1)S(1)}, u32[]{:S(2)}, u32[]{:S(2)}) %all-to-all-start) | async-done | bytes 262176 | tf_op jit(solution)/shard_map/all_to_all | solution.py:21
  17.6 1.9 %collective-permute-start = (bf16[8,4,16,128]{3,2,1,0:T(8,128)(2,1)S(1)}, bf16[8,4,16,128]{3,2,1,0:T(8,128)(2,1)S(1)}, u32[]{:S(2)}, u32[]{:S(2)}) collective-permute-start(bf16[8,4,16,128]{3,2,1,0:T(8,128)(2,1)S(1)} %get-tuple-element.19), channel_id=1, source_target_pairs={{0,64},{64,0},{128,192},{192,128},{256,320},{320,256},{384,448},{4... | collective-permute-start | bytes 393224 | tf_op jit(solution)/shard_map/ppermute | solution.py:226
  19.5 0.7 collective-permute-start.1
  20.2 0.0 copy-done.3
  20.2 0.2 fusion
  20.4 0.4 collective-permute-done.facing
  20.8 0.0 collective-permute-done.1.beyond
  20.9 0.0 copy-start
  20.9 1.3 %collective-permute-start.2 = (bf16[34,16,128]{2,1,0:T(8,128)(2,1)S(1)}, bf16[34,16,128]{2,1,0:T(8,128)(2,1)S(1)}, u32[]{:S(2)}, u32[]{:S(2)}) collective-permute-start(bf16[34,16,128]{2,1,0:T(8,128)(2,1)S(1)} %get-tuple-element.24), channel_id=1, source_target_pairs={{0,8},{8,16},{16,24},{24,32},{32,40},{40,48},{48,56},{1,9},{9,17},... | collective-permute-start | bytes 417800 | tf_op jit(solution)/shard_map/ppermute | solution.py:26
  22.2 1.3 %collective-permute-start.3 = (bf16[34,16,128]{2,1,0:T(8,128)(2,1)S(1)}, bf16[34,16,128]{2,1,0:T(8,128)(2,1)S(1)}, u32[]{:S(2)}, u32[]{:S(2)}) collective-permute-start(bf16[34,16,128]{2,1,0:T(8,128)(2,1)S(1)} %get-tuple-element.25), channel_id=1, source_target_pairs={{8,0},{16,8},{24,16},{32,24},{40,32},{48,40},{56,48},{9,1},{17,9},... | collective-permute-start | bytes 417800 | tf_op jit(solution)/shard_map/ppermute | solution.py:27
  23.5 1.3 %collective-permute-done.2.before = bf16[34,16,128]{2,1,0:T(8,128)(2,1)S(1)} collective-permute-done((bf16[34,16,128]{2,1,0:T(8,128)(2,1)S(1)}, bf16[34,16,128]{2,1,0:T(8,128)(2,1)S(1)}, u32[]{:S(2)}, u32[]{:S(2)}) %collective-permute-start.2) | collective-permute-done | bytes 139296 | tf_op jit(solution)/shard_map/ppermute | solution.py:26
  24.7 4.4 %collective-permute-done.3.after = bf16[34,16,128]{2,1,0:T(8,128)(2,1)S(1)} collective-permute-done((bf16[34,16,128]{2,1,0:T(8,128)(2,1)S(1)}, bf16[34,16,128]{2,1,0:T(8,128)(2,1)S(1)}, u32[]{:S(2)}, u32[]{:S(2)}) %collective-permute-start.3) | collective-permute-done | bytes 139296 | tf_op jit(solution)/shard_map/ppermute | solution.py:27
  29.1 0.0 copy-done
  29.1 4.4 %forward.1 = (bf16[16,16,128]{2,1,0:T(8,128)(2,1)S(1)}, bf16[17,16,128]{2,1,0:T(8,128)(2,1)S(1)}, bf16[10,16,128]{2,1,0:T(8,128)(2,1)S(1)}, bf16[7,16,128]{2,1,0:T(8,128)(2,1)S(1)}) custom-call(s32[1]{0:T(128)} %bitcast.at_ref, f32[16]{0:T(128)S(1)} %copy-done, bf16[3,96,256]{2,1,0:T(8,128)(2,1)S(1)} %bitcast.39, bf16[16,16,128]{2,1,0:T(8,128)(2,1)S(1)} %bitcast.38, ...), custom_call_target="tpu_custom_call" | custom-call | flops 339738624 | bytes 1048576 | tf_op jit(solution)/shard_map/forward/pallas_call | solution.py:253
  33.5 8.2 %collective-permute-start.4 = (bf16[17,16,128]{2,1,0:T(8,128)(2,1)S(1)}, bf16[17,16,128]{2,1,0:T(8,128)(2,1)S(1)}, u32[]{:S(2)}, u32[]{:S(2)}) collective-permute-start(bf16[17,16,128]{2,1,0:T(8,128)(2,1)S(1)} %get-tuple-element.27.face), channel_id=1, source_target_pairs={{0,64},{64,0},{128,192},{192,128},{256,320},{320,256},{384,448},{4... | collective-permute-start | bytes 208904 | tf_op jit(solution)/shard_map/ppermute | solution.py:273
  41.8 0.9 collective-permute-done.4.face_in
  42.7 0.7 broadcast_in_dim.10
  43.4 8.1 %all-to-all-start.1 = ((bf16[8,7,16,128]{3,2,1,0:T(8,128)(2,1)}), bf16[8,7,16,128]{3,2,1,0:T(8,128)(2,1)S(1)}, u32[]{:S(2)}, u32[]{:S(2)}) async-start(bf16[8,7,16,128]{3,2,1,0:T(8,128)(2,1)} %broadcast_in_dim.10), calls=%async_computation.1 | async-start | bytes 458752 | tf_op jit(solution)/shard_map/all_to_all | solution.py:21
  51.5 0.7 collective-permute-start.5
  52.2 0.1 copy.35.w_ref
  52.3 0.0 collective-permute-done.5.far_in
  52.3 1.3 %backward.1 = bf16[8,8,16,128]{3,2,1,0:T(8,128)(2,1)} custom-call(s32[1]{0:T(128)} %bitcast.at_ref, bf16[64,432]{1,0:T(8,128)(2,1)S(1)} %copy.35.w_ref, bf16[17,16,128]{2,1,0:T(8,128)(2,1)S(1)} %get-tuple-element.27.face, bf16[10,16,128]{2,1,0:T(8,128)(2,1)S(1)} %get-tuple-element.28.far, bf16[17,16,128]{2,1,0:T(8,128)(2,1)S(1)} %collective-permute-done.4.face_in, ...), custom_call_target="tpu_custom_call" | custom-call | flops 113246208 | bytes 524288 | tf_op jit(solution)/shard_map/backward/pallas_call | solution.py:278
  53.6 9.6 %all-to-all-done.1 = bf16[8,7,16,128]{3,2,1,0:T(8,128)(2,1)S(1)} async-done(((bf16[8,7,16,128]{3,2,1,0:T(8,128)(2,1)}), bf16[8,7,16,128]{3,2,1,0:T(8,128)(2,1)S(1)}, u32[]{:S(2)}, u32[]{:S(2)}) %all-to-all-start.1) | async-done | bytes 229408 | tf_op jit(solution)/shard_map/all_to_all | solution.py:21
  63.2 0.7 broadcast_in_dim.22
  64.0 9.7 %all-to-all-start.2 = ((bf16[8,7,16,128]{3,2,1,0:T(8,128)(2,1)}), bf16[8,7,16,128]{3,2,1,0:T(8,128)(2,1)S(1)}, u32[]{:S(2)}, u32[]{:S(2)}) async-start(bf16[8,7,16,128]{3,2,1,0:T(8,128)(2,1)} %broadcast_in_dim.22), calls=%async_computation.2 | async-start | bytes 458752 | tf_op jit(solution)/shard_map/all_to_all | solution.py:21
  73.6 0.6 copy.40
  74.3 10.1 %all-to-all-done.2 = bf16[8,7,16,128]{3,2,1,0:T(8,128)(2,1)S(1)} async-done(((bf16[8,7,16,128]{3,2,1,0:T(8,128)(2,1)}), bf16[8,7,16,128]{3,2,1,0:T(8,128)(2,1)S(1)}, u32[]{:S(2)}, u32[]{:S(2)}) %all-to-all-start.2) | async-done | bytes 229408 | tf_op jit(solution)/shard_map/all_to_all | solution.py:21
  84.4 0.0 copy-start.1
  84.4 5.4 %all-to-all-start.3 = ((bf16[8,8,16,128]{3,2,1,0:T(8,128)(2,1)}), bf16[8,8,16,128]{3,2,1,0:T(8,128)(2,1)S(1)}, u32[]{:S(2)}, u32[]{:S(2)}) async-start(bf16[8,8,16,128]{3,2,1,0:T(8,128)(2,1)} %backward.1), calls=%async_computation.3 | async-start | bytes 524288 | tf_op jit(solution)/shard_map/all_to_all | solution.py:21
  89.8 0.1 fusion.1
  89.8 0.0 copy-done.1
  89.8 0.0 slice-start
  89.9 0.9 slice-done
  90.7 0.1 reshape.59
  90.9 0.2 pad_maximum_fusion
  91.1 0.7 copy.36
  91.8 0.6 slice_reduce_fusion
  92.4 3.5 %all-to-all-done.3 = bf16[8,8,16,128]{3,2,1,0:T(8,128)(2,1)S(1)} async-done(((bf16[8,8,16,128]{3,2,1,0:T(8,128)(2,1)}), bf16[8,8,16,128]{3,2,1,0:T(8,128)(2,1)S(1)}, u32[]{:S(2)}, u32[]{:S(2)}) %all-to-all-start.3) | async-done | bytes 262176 | tf_op jit(solution)/shard_map/all_to_all | solution.py:21
  95.9 0.6 copy.37
  (12 shorter events, 0.2 us)
Async XLA Ops:
  2.1 9.3 %copy-start.4 = (bf16[16,2,8,128]{3,2,1,0:T(8,128)(2,1)S(1)}, bf16[16,2,8,128]{3,2,1,0:T(8,128)(2,1)}, u32[]{:S(2)}) copy-start(bf16[16,2,8,128]{3,2,1,0:T(8,128)(2,1)} %param.8) | copy-start | bytes 196612
  2.2 15.4 %all-to-all-start = ((bf16[8,2,4,16,128]{4,3,2,1,0:T(8,128)(2,1)}), bf16[8,2,4,16,128]{4,3,2,1,0:T(8,128)(2,1)S(1)}, u32[]{:S(2)}, u32[]{:S(2)}) async-start(bf16[8,2,4,16,128]{4,3,2,1,0:T(8,128)(2,1)} %broadcast_in_dim.9), calls=%async_computation | async-start | bytes 524288 | tf_op jit(solution)/shard_map/all_to_all | solution.py:21
  11.4 0.9 copy-start.2
  12.4 7.8 %copy-start.3 = (bf16[2,192,256,1]{2,1,3,0:T(8,128)(2,1)S(1)}, bf16[2,192,256,1]{2,1,3,0:T(8,128)(2,1)}, u32[]{:S(2)}) copy-start(bf16[2,192,256,1]{2,1,3,0:T(8,128)(2,1)} %constant.29) | copy-start | bytes 589828
  17.6 3.2 %collective-permute-start = (bf16[8,4,16,128]{3,2,1,0:T(8,128)(2,1)S(1)}, bf16[8,4,16,128]{3,2,1,0:T(8,128)(2,1)S(1)}, u32[]{:S(2)}, u32[]{:S(2)}) collective-permute-start(bf16[8,4,16,128]{3,2,1,0:T(8,128)(2,1)S(1)} %get-tuple-element.19), channel_id=1, source_target_pairs={{0,64},{64,0},{128,192},{192,128},{256,320},{320,256},{384,448},{4... | collective-permute-start | bytes 393224 | tf_op jit(solution)/shard_map/ppermute | solution.py:226
  19.5 1.3 %collective-permute-start.1 = (bf16[8,4,16,128]{3,2,1,0:T(8,128)(2,1)S(1)}, bf16[8,4,16,128]{3,2,1,0:T(8,128)(2,1)S(1)}, u32[]{:S(2)}, u32[]{:S(2)}) collective-permute-start(bf16[8,4,16,128]{3,2,1,0:T(8,128)(2,1)S(1)} %get-tuple-element.20), channel_id=1, source_target_pairs={{64,128},{128,64},{192,256},{256,192},{320,384},{384,320},{65,129}... | collective-permute-start | bytes 393224 | tf_op jit(solution)/shard_map/ppermute | solution.py:227
  20.9 8.3 %copy-start = (f32[16]{0:T(128)S(1)}, f32[16]{0:T(128)}, u32[]{:S(2)}) copy-start(f32[16]{0:T(128)} %bias_ref.1) | copy-start | bytes 196
  20.9 3.9 %collective-permute-start.2 = (bf16[34,16,128]{2,1,0:T(8,128)(2,1)S(1)}, bf16[34,16,128]{2,1,0:T(8,128)(2,1)S(1)}, u32[]{:S(2)}, u32[]{:S(2)}) collective-permute-start(bf16[34,16,128]{2,1,0:T(8,128)(2,1)S(1)} %get-tuple-element.24), channel_id=1, source_target_pairs={{0,8},{8,16},{16,24},{24,32},{32,40},{40,48},{48,56},{1,9},{9,17},... | collective-permute-start | bytes 417800 | tf_op jit(solution)/shard_map/ppermute | solution.py:26
  22.2 6.9 %collective-permute-start.3 = (bf16[34,16,128]{2,1,0:T(8,128)(2,1)S(1)}, bf16[34,16,128]{2,1,0:T(8,128)(2,1)S(1)}, u32[]{:S(2)}, u32[]{:S(2)}) collective-permute-start(bf16[34,16,128]{2,1,0:T(8,128)(2,1)S(1)} %get-tuple-element.25), channel_id=1, source_target_pairs={{8,0},{16,8},{24,16},{32,24},{40,32},{48,40},{56,48},{9,1},{17,9},... | collective-permute-start | bytes 417800 | tf_op jit(solution)/shard_map/ppermute | solution.py:27
  33.5 9.1 %collective-permute-start.4 = (bf16[17,16,128]{2,1,0:T(8,128)(2,1)S(1)}, bf16[17,16,128]{2,1,0:T(8,128)(2,1)S(1)}, u32[]{:S(2)}, u32[]{:S(2)}) collective-permute-start(bf16[17,16,128]{2,1,0:T(8,128)(2,1)S(1)} %get-tuple-element.27.face), channel_id=1, source_target_pairs={{0,64},{64,0},{128,192},{192,128},{256,320},{320,256},{384,448},{4... | collective-permute-start | bytes 208904 | tf_op jit(solution)/shard_map/ppermute | solution.py:273
  43.4 19.8 %all-to-all-start.1 = ((bf16[8,7,16,128]{3,2,1,0:T(8,128)(2,1)}), bf16[8,7,16,128]{3,2,1,0:T(8,128)(2,1)S(1)}, u32[]{:S(2)}, u32[]{:S(2)}) async-start(bf16[8,7,16,128]{3,2,1,0:T(8,128)(2,1)} %broadcast_in_dim.10), calls=%async_computation.1 | async-start | bytes 458752 | tf_op jit(solution)/shard_map/all_to_all | solution.py:21
  51.5 0.8 collective-permute-start.5
  64.0 20.4 %all-to-all-start.2 = ((bf16[8,7,16,128]{3,2,1,0:T(8,128)(2,1)}), bf16[8,7,16,128]{3,2,1,0:T(8,128)(2,1)S(1)}, u32[]{:S(2)}, u32[]{:S(2)}) async-start(bf16[8,7,16,128]{3,2,1,0:T(8,128)(2,1)} %broadcast_in_dim.22), calls=%async_computation.2 | async-start | bytes 458752 | tf_op jit(solution)/shard_map/all_to_all | solution.py:21
  84.4 5.5 %copy-start.1 = (f32[14,16,128]{2,1,0:T(8,128)}, f32[14,16,128]{2,1,0:T(8,128)S(1)}, u32[]{:S(2)}) copy-start(f32[14,16,128]{2,1,0:T(8,128)S(1)} %convert_reduce_fusion) | copy-start | bytes 344068
  84.4 11.5 %all-to-all-start.3 = ((bf16[8,8,16,128]{3,2,1,0:T(8,128)(2,1)}), bf16[8,8,16,128]{3,2,1,0:T(8,128)(2,1)S(1)}, u32[]{:S(2)}, u32[]{:S(2)}) async-start(bf16[8,8,16,128]{3,2,1,0:T(8,128)(2,1)} %backward.1), calls=%async_computation.3 | async-start | bytes 524288 | tf_op jit(solution)/shard_map/all_to_all | solution.py:21
  89.8 0.9 slice-start

commit v7 on v5

v7 whole, which is shorter than its diff:
```python
import functools

import jax
import jax.numpy as jnp
import numpy as np
from jax import lax
from jax.experimental import pallas as pl
from jax.experimental.pallas import tpu as pltpu
from jax.sharding import PartitionSpec as P

BF16 = jnp.bfloat16
F32 = jnp.float32
PART = 8


def swapped(blocks, axis):
    return lax.all_to_all(blocks, axis, 0, 0, tiled=True)


def neighbours(first, last, axis):
    ends = lax.axis_size(axis) - 1
    before = lax.ppermute(last, axis, [(i, i + 1) for i in range(ends)])
    after = lax.ppermute(first, axis, [(i + 1, i) for i in range(ends)])
    return before, after


def shifted(value, lane):
    width = value.shape[-1]
    ahead = jnp.where(lane == width - 1, 0.0, pltpu.roll(value, width - 1, 1))
    behind = jnp.where(lane == 0, 0.0, pltpu.roll(value, 1, 1))
    return jnp.concatenate([ahead, value, behind], axis=0)


def pack_kernel(at_ref, cells, own, face_ref, far_ref, wide):
    planes, pairs = own.shape[:2]
    count, lines = cells.shape[:2]
    for c in range(count):
        wide[c * lines : (c + 1) * lines] = cells[c].astype(F32)
    for d in range(planes):
        for t in range(pairs):
            row = 2 * (d * pairs + t)
            own[d, t] = jnp.concatenate(
                [wide[pl.ds(row + e, count, stride=lines), :] for e in range(2)], axis=0
            ).astype(BF16)
    even = at_ref[0] == 0
    face_ref[...] = own[jnp.where(even, planes - 1, 0)]
    far_ref[...] = own[jnp.where(even, 0, planes - 1)]


def grid_kernel(at_ref, own, facing, beyond, out_ref):
    planes = own.shape[0]
    before = jnp.where(at_ref[0] == 0, 0, planes + 1)
    for k in range(out_ref.shape[0]):
        for d in range(planes):
            out_ref[k, d + 1] = own[d]
        out_ref[k, before] = beyond[...]
        out_ref[k, planes + 1 - before] = facing[...]


def rows_kernel(rows, tiles, cot, first_ref, last_ref):
    sources, count = tiles.shape[:2]
    for ref, t, row in ((first_ref, 0, 0), (last_ref, rows // 2 - 1, rows - 1)):
        for p in range(count):
            ref[p * sources : (p + 1) * sources] = tiles[:, p, t]
        for d in range(count - 2):
            ref[count * sources + d] = cot[d * rows + row]


def sum_kernel(blocks, out_ref):
    for r in range(blocks.shape[1]):
        total = blocks[0, r].astype(F32)
        for k in range(1, blocks.shape[0]):
            total = total + blocks[k, r].astype(F32)
        for k in range(out_ref.shape[0]):
            out_ref[k, r] = total.astype(BF16)


def add_kernel(left, right, out_ref):
    for k in range(left.shape[0]):
        out_ref[k] = (left[k].astype(F32) + right[k].astype(F32)).astype(BF16)


def unpack_kernel(parts, out_ref, wide):
    pairs, size = parts.shape[1:3]
    count, lines = out_ref.shape[:2]
    for t in range(pairs):
        total = parts[0, t].astype(F32)
        for k in range(1, parts.shape[0]):
            total = total + parts[k, t].astype(F32)
        wide[t * size : (t + 1) * size] = total
    for c in range(count):
        out_ref[c] = wide[pl.ds(c, lines, stride=count), :].astype(BF16)


def forward_kernel(planes, rows, at_ref, bias_ref, w_ref, cot, tiles, before, after, *refs):
    out_ref, face_ref, far_ref, sums_ref, grads = refs
    cout, width = cot.shape[1:]
    sources = tiles.shape[0]
    edge = sources * (planes + 2)

    def tile(s, p, t):
        if t == 0:
            return before[p * sources + s]
        if t == rows // 2 + 1:
            return after[p * sources + s]
        return tiles[s, p, t - 1]

    lane = lax.broadcasted_iota(jnp.int32, (cout, width), 1)
    channel = lax.broadcasted_iota(jnp.int32, (cout, width), 0)
    bias = jnp.zeros((cout, width), F32)
    for o in range(cout):
        bias = jnp.where(channel == o, bias_ref[o], bias)
    sums = [None] * 3
    bias_sum = jnp.zeros((cout, width), F32)
    for d in range(planes):
        for pair in range(rows // 2 + 1):
            cells = [
                jnp.concatenate(
                    [tile(s, d + kd, pair + t) for t in range(2) for s in range(sources)], axis=0
                )
                for kd in range(3)
            ]
            acc = jnp.dot(w_ref[0], cells[0], preferred_element_type=F32)
            for kd in range(1, 3):
                acc = acc + jnp.dot(w_ref[kd], cells[kd], preferred_element_type=F32)
            stacks = []
            for e in range(2):
                z = acc[3 * e * cout : 3 * (e + 1) * cout]
                pre = (
                    z[cout : 2 * cout]
                    + jnp.where(lane == 0, 0.0, pltpu.roll(z[:cout], 1, 1))
                    + jnp.where(lane == width - 1, 0.0, pltpu.roll(z[2 * cout :], width - 1, 1))
                    + bias
                )
                small = jnp.exp(-jnp.abs(pre))
                sigmoid = jnp.where(pre >= 0, 1.0, small) / (1.0 + small)
                row = 2 * pair + e
                if row == 0:
                    cotangent = before[edge + d]
                elif row == rows + 1:
                    cotangent = after[edge + d]
                else:
                    cotangent = cot[d * rows + row - 1]
                grad = (cotangent.astype(F32) * (0.2 + 0.8 * sigmoid)).astype(BF16)
                grads[d, row] = grad
                if row == 0 or row == rows + 1:
                    stacks.append(jnp.zeros((3 * cout, width), BF16))
                    continue
                softplus = jnp.maximum(pre, 0.0) + jnp.log1p(small)
                out_ref[d * rows + row - 1] = (0.2 * pre + 0.8 * softplus).astype(BF16)
                grad = grad.astype(F32)
                bias_sum = bias_sum + grad
                stacks.append(shifted(grad, lane).astype(BF16))
            both = jnp.concatenate(stacks, axis=0)
            for kd in range(3):
                term = lax.dot_general(
                    both, cells[kd], (((1,), (1,)), ((), ())), preferred_element_type=F32
                )
                sums[kd] = term if sums[kd] is None else sums[kd] + term

    first = (lane // PART) % 2 == 0
    blocks, last = [], []
    for kd in range(3):
        for kw in range(3):
            one = sums[kd][kw * cout : (kw + 1) * cout]
            two = sums[kd][(3 + kw) * cout : (4 + kw) * cout]
            back = pltpu.roll(two[:, width:], width - PART, 1)
            blocks.append(
                one[:, :width]
                + jnp.where(
                    first,
                    pltpu.roll(two[:, :width], width - PART, 1),
                    pltpu.roll(two[:, width:], PART, 1),
                )
            )
            last.append(one[:, width:] + back)
    last.append(jnp.broadcast_to(jnp.sum(bias_sum, axis=1, keepdims=True), (cout, width)))
    for k in range(0, len(last), 2):
        blocks.append(jnp.where(first, last[k], pltpu.roll(last[k + 1], PART, 1)))
    source = lax.broadcasted_iota(jnp.int32, (width, width), 0)
    target = (source // PART) % 2 * (width // 2) + source // (2 * PART) * PART + source % PART
    order = jnp.where(lax.broadcasted_iota(jnp.int32, (width, width), 1) == target, 1.0, 0.0).astype(BF16)
    placed = jnp.dot(jnp.concatenate(blocks, axis=0).astype(BF16), order, preferred_element_type=F32)
    size = sums_ref.shape[1]
    for k in range(sums_ref.shape[0] * size):
        block = placed[k * cout : (k + 1) * cout] if k < len(blocks) else jnp.zeros((cout, width), F32)
        sums_ref[k // size, k % size] = block.astype(BF16)
    core = at_ref[0]
    face_ref[...] = grads[1 - core]
    far_ref[...] = grads[core]


def backward_kernel(planes, rows, at_ref, w_ref, face, far, face_in, far_in, kept_ref, sent_ref, stack, parts):
    cout, width = far.shape[1:]
    cin = w_ref.shape[0]
    count = 2 * parts.shape[1]
    part = cin // count
    lane = lax.broadcasted_iota(jnp.int32, (cout, width), 1)
    step = 3 * cout
    core = at_ref[0]
    for q, source in enumerate((face_in, face, far, far_in)):
        p = jnp.where(core == 1, q, planes + 1 - q)
        for r in range(rows + 2):
            stack[p, r * step : (r + 1) * step, :] = shifted(source[r].astype(F32), lane).astype(BF16)
    w = w_ref[...]
    for d in range(planes):
        for h in range(0, rows, 2):
            cells = jnp.concatenate(
                [
                    jnp.concatenate(
                        [stack[d + a, (h + e) * step : (h + e + 3) * step, :] for a in range(3)], axis=0
                    )
                    for e in range(2)
                ],
                axis=1,
            )
            acc = jnp.dot(w, cells, preferred_element_type=F32)
            pair = (d * rows + h) // 2
            for f in range(count):
                piece = acc[f * part : (f + 1) * part]
                piece = jnp.concatenate([piece[:, :width], piece[:, width:]], axis=0).astype(BF16)
                parts[(f % 2) ^ at_ref[1], f // 2, pair] = piece
    kept_ref[...] = parts[0]
    sent_ref[...] = parts[1]


def placing(cin):
    ones = np.zeros((2, 3, cin, 2, cin // PART, 2, PART), np.float32)
    for e in range(2):
        for kh in range(3):
            for i in range(cin):
                ones[e, kh, i, (kh + e) // 2, i // PART, (kh + e) % 2, i % PART] = 1
    return ones.reshape(2, 3 * cin, 4 * cin)


def weights_kernel(blocks, w_ref, b_ref):
    cout, width = blocks.shape[2:]
    half = width // 2
    size = blocks.shape[1]
    for k in range(14):
        block = blocks[k // size, k % size].astype(F32)
        for e in range(2):
            piece = block[:, e * half : (e + 1) * half]
            at, kh = (k, e) if k < 9 else (2 * (k - 9) + e, 2)
            if at < 9:
                w_ref[at // 3 * 9 + kh * 3 + at % 3] = piece
    spare = blocks[13 // size, 13 % size].astype(F32)[:, half : half + cout]
    row = lax.broadcasted_iota(jnp.int32, (cout, cout), 0)
    lane = lax.broadcasted_iota(jnp.int32, (cout, cout), 1)
    b_ref[...] = jnp.sum(jnp.where(row == lane, spare, 0.0), axis=0, keepdims=True)


def call(body, name, *args, out, scratch=(), dtype=BF16, flops=0, moved=1 << 18, waves=0, scalars=0):
    smem, vmem = pl.BlockSpec(memory_space=pltpu.SMEM), pl.BlockSpec(memory_space=pltpu.VMEM)
    outs = tuple(jax.ShapeDtypeStruct(shape, dtype) for shape in out)
    results = pl.pallas_call(
        body,
        out_shape=outs,
        in_specs=[smem] * scalars + [vmem] * (len(args) - scalars),
        out_specs=(vmem,) * len(outs),
        scratch_shapes=[pltpu.VMEM(shape, kind) for shape, kind in scratch],
        compiler_params=pltpu.CompilerParams(vmem_limit_bytes=12 << 20),
        cost_estimate=pl.CostEstimate(flops=flops, bytes_accessed=moved, transcendentals=waves),
        name=name,
    )(*args)
    return results[0] if len(outs) == 1 else results


def per_device(activations, weights, bias, cotangent):
    cin_dev, planes, rows, width = activations.shape
    taps, cin, cout = weights.shape
    cells = planes * rows
    depth, height, filt = (lax.axis_size(axis) for axis in ("depth", "height", "filt"))
    swap = [(i, i ^ 1) for i in range(depth)]
    cross = [(i, i - 1 if i % 2 == 0 else i + 1) for i in range(1, depth - 1)]
    at = jnp.stack([lax.axis_index("depth") % 2, lax.axis_index("filt") % 2]).astype(jnp.int32)
    pairs, double = rows // 2, 2 * cin_dev

    own, face, far = call(
        pack_kernel,
        "pack",
        at,
        activations.reshape(cin_dev, cells, width),
        out=[(planes, pairs, double, width)] + [(pairs, double, width)] * 2,
        scratch=[((cin_dev * cells, width), F32)],
        scalars=1,
    )
    facing = lax.ppermute(face, "depth", swap)
    beyond = lax.ppermute(far, "depth", cross)
    grid = call(
        grid_kernel,
        "grid",
        at,
        own,
        facing,
        beyond,
        out=[(filt, planes + 2, pairs, double, width)],
        scalars=1,
    )
    tiles = swapped(grid, "filt")

    cot = cotangent.transpose(1, 2, 0, 3).reshape(cells, cout, width)
    split = weights.reshape(3, 3, 3, cin, cout)
    w_forward = jnp.einsum(
        "akj,ejn->aekn",
        split.transpose(0, 2, 4, 1, 3).reshape(3, 3 * cout, 3 * cin),
        jnp.asarray(placing(cin), BF16),
        preferred_element_type=F32,
    )
    w_forward = w_forward.astype(BF16).reshape(3, 6 * cout, 4 * cin)
    w_back = split[::-1, ::-1].transpose(3, 0, 1, 2, 4).reshape(cin, taps * cout)
    first, last = call(
        functools.partial(rows_kernel, rows),
        "rows",
        tiles,
        cot,
        out=[((planes + 2) * filt + planes, cout, width)] * 2,
    )
    first, last, w_forward = lax.optimization_barrier((first, last, w_forward))
    before, after = neighbours(first, last, "height")

    work = 2 * cells * width * taps * cin * cout
    out, face, far, sums = call(
        functools.partial(forward_kernel, planes, rows),
        "forward",
        at,
        bias,
        w_forward,
        cot,
        tiles,
        before,
        after,
        out=[(cells, cout, width)] + [(rows + 2, cout, width)] * 2 + [(height, 16 // height, cout, width)],
        scratch=[((planes, rows + 2, cout, width), BF16)],
        flops=3 * work,
        waves=1 << 17,
        scalars=2,
    )
    output = out.reshape(planes, rows, cout, width).transpose(2, 0, 1, 3)

    size = sums.shape[1:]
    face_in = lax.ppermute(face, "depth", swap)
    far_in = lax.ppermute(far, "depth", cross)
    sums = swapped(sums, "height")
    sums, face_in, far_in = lax.optimization_barrier((sums, face_in, far_in))
    sums = swapped(call(sum_kernel, "sums", sums, out=[(depth,) + size]), "depth")
    kept, sent = call(
        functools.partial(backward_kernel, planes, rows),
        "backward",
        at,
        w_back,
        face,
        far,
        face_in,
        far_in,
        out=[(filt // 2, cells // 2, double, width)] * 2,
        scratch=[
            ((planes + 2, (rows + 2) * 3 * cout, width), BF16),
            ((2, filt // 2, cells // 2, double, width), BF16),
        ],
        flops=work,
        scalars=1,
    )
    sums, kept, sent = lax.optimization_barrier((sums, kept, sent))
    sums = swapped(call(sum_kernel, "sums", sums, out=[(height,) + size]), "height")
    sent = lax.ppermute(sent, "filt", [(i, i ^ 1) for i in range(filt)])
    parts = call(add_kernel, "add", kept, sent, out=[kept.shape])
    sums, parts = lax.optimization_barrier((sums, parts))
    groups = [[i for i in range(filt) if i % 2 == k] for k in range(2)]
    parts = lax.all_to_all(parts, "filt", 0, 0, tiled=True, axis_index_groups=groups)
    summed = call(
        unpack_kernel,
        "unpack",
        parts,
        out=[(cin_dev, cells, width)],
        scratch=[((cin_dev * cells, width), F32)],
    ).reshape(activations.shape)

    weight_grad, bias_grad = call(
        weights_kernel, "weights", sums, out=[(taps, cout, cin), (1, cout)], dtype=F32
    )
    return (output, summed, weight_grad.transpose(0, 2, 1), bias_grad.reshape(cout))


def solution(mesh):
    placed = (
        P("filt", "depth", "height", None),
        P(None, None, "filt"),
        P("filt"),
        P("filt", "depth", "height", None),
    )
    return jax.shard_map(
        per_device,
        mesh=mesh,
        in_specs=placed,
        out_specs=(
            P("filt", "depth", "height", None),
            P("filt", "depth", "height", None),
            P(None, None, "filt"),
            P("filt"),
        ),
        check_vma=False,
    )
```

time: 94.8 us -> 108 us (1.14)
  starting transfers between devices: 30.1 us -> 56.3 us
  blocking collectives: 20.6 us -> 0 us
  waiting for transfers between devices: 27.8 us -> 34.6 us
  Pallas kernels: 5.15 us -> 11.6 us
  local copies, waits for them, and re-layouts: 8.81 us -> 3.24 us
    all_to_all x3 -> x4, starting transfers between devices: 15.4 us -> 40.1 us  [swapped(): return lax.all_to_all(blocks, axis, 0, 0, tiled=True)]
    all_to_all x1 -> x0, blocking collectives: 20.6 us -> none  [swapped(): return lax.all_to_all(blocks, axis, 0, 0, tiled=True)]
    pallas_call x2 -> x10, Pallas kernels: 5.15 us -> 11.6 us  [call(): pl.pallas_call(body, out_shape=outs, in_specs=[smem] * scalars + [vmem] *...]
    all_to_all x0 -> x1, waiting for transfers between devices: none -> 4.52 us  [per_device(): lax.all_to_all(parts, 'filt', 0, 0, tiled=True, axis_index_groups=groups)]
    all_to_all x3 -> x4, waiting for transfers between devices: 19.8 us -> 23.7 us  [swapped(): return lax.all_to_all(blocks, axis, 0, 0, tiled=True)]
    all_to_all x0 -> x1, starting transfers between devices: none -> 3.32 us  [per_device(): lax.all_to_all(parts, 'filt', 0, 0, tiled=True, axis_index_groups=groups)]
    ppermute x1, starting transfers between devices: 4.27 us -> 1.3 us  [neighbours(): before = lax.ppermute(last, axis, [(i, i + 1) for i in range(ends)])]
    ppermute x1, starting transfers between devices: 1.92 us -> 4.07 us  [per_device(): face_in = lax.ppermute(face, 'depth', swap)]
  transfers between devices with their start and end apart: 9 -> 12, of which waited for: 7 -> 9; matrix products, arithmetic and copies ran while one was open for 3% -> 1% of each run, Pallas kernels for 1% -> 3%
where the time goes in v7:
time: 108 us; the launch traced here: 107 us
  starting transfers between devices  56.3 us (52%)
  waiting for transfers between devices  34.6 us (32%)
  Pallas kernels  11.6 us (11%)
  local copies, waits for them, and re-layouts  3.24 us (3%)
    all_to_all x4, starting transfers between devices, swapped(): return lax.all_to_all(blocks, axis, 0, 0, tiled=True)  40.1 us
    all_to_all x4, waiting for transfers between devices, swapped(): return lax.all_to_all(blocks, axis, 0, 0, tiled=True)  23.7 us
    pallas_call x10, Pallas kernels, call(): pl.pallas_call(body, out_shape=outs, in_specs=[smem] * scalars + [vmem] *...  11.6 us
    all_to_all x1, waiting for transfers between devices, per_device(): lax.all_to_all(parts, 'filt', 0, 0, tiled=True, axis_index_groups=groups)  4.52 us
    ppermute x1, waiting for transfers between devices, neighbours(): after = lax.ppermute(first, axis, [(i + 1, i) for i in range(ends)])  4.38 us
    ppermute x1, starting transfers between devices, per_device(): face_in = lax.ppermute(face, 'depth', swap)  4.07 us
    all_to_all x1, starting transfers between devices, per_device(): lax.all_to_all(parts, 'filt', 0, 0, tiled=True, axis_index_groups=groups)  3.32 us
    ppermute x1, starting transfers between devices, per_device(): sent = lax.ppermute(sent, 'filt', [(i, i ^ 1) for i in range(filt)])  3 us
  transfers between devices with their start and end apart: 12, of which 9 were waited for; matrix products, arithmetic and copies ran while one was open for 1% of the time, Pallas kernels for 3%

profile of v7, /device:TPU:8, one launch (start us, length us, event | category | flops | bytes accessed | tf_op | source)
XLA Modules:
  0.0 106.7 jit_solution(16077651801057173750)
XLA Ops:
  0.6 0.0 copy-start
  0.7 0.1 pad_add_fusion.at_ref
  0.7 0.7 copy-done
  1.4 0.6 pack.1
  2.0 1.9 %collective-permute-start = (bf16[4,16,128]{2,1,0:T(8,128)(2,1)S(1)}, bf16[4,16,128]{2,1,0:T(8,128)(2,1)S(1)}, u32[]{:S(2)}, u32[]{:S(2)}) collective-permute-start(bf16[4,16,128]{2,1,0:T(8,128)(2,1)S(1)} %get-tuple-element.29), channel_id=1, source_target_pairs={{0,64},{64,0},{128,192},{192,128},{256,320},{320,256},{384,448},{4... | collective-permute-start | bytes 49160 | tf_op jit(solution)/shard_map/ppermute | solution.py:288
  3.9 0.7 collective-permute-start.1
  4.6 0.5 collective-permute-done.facing
  5.0 0.0 collective-permute-done.1.beyond
  5.0 1.4 %grid.1 = bf16[8,4,4,16,128]{4,3,2,1,0:T(8,128)(2,1)} custom-call(s32[2]{0:T(128)S(1)} %pad_add_fusion.at_ref, bf16[2,4,16,128]{3,2,1,0:T(8,128)(2,1)S(1)} %get-tuple-element.28.own, bf16[4,16,128]{2,1,0:T(8,128)(2,1)S(1)} %collective-permute-done.facing, bf16[4,16,128]{2,1,0:T(8,128)(2,1)S(1)} %collective-permute-done.1.beyond), custom_call_target="tpu_custom_call" | custom-call | bytes 262144 | tf_op jit(solution)/shard_map/grid/pallas_call | solution.py:256
  6.5 0.0 copy-start.4
  6.5 9.3 %all-to-all-start = ((bf16[8,4,4,16,128]{4,3,2,1,0:T(8,128)(2,1)}), bf16[8,4,4,16,128]{4,3,2,1,0:T(8,128)(2,1)S(1)}, u32[]{:S(2)}, u32[]{:S(2)}) async-start(bf16[8,4,4,16,128]{4,3,2,1,0:T(8,128)(2,1)} %grid.1), calls=%async_computation | async-start | bytes 1048576 | tf_op jit(solution)/shard_map/all_to_all | solution.py:17
  15.8 0.0 copy-start.2
  15.8 0.0 copy-done.4
  15.8 0.9 copy-done.2
  16.7 0.1 copy.15
  16.8 0.1 reshape.45
  16.9 0.7 copy-done.3
  17.6 0.2 fusion
  17.8 5.5 %all-to-all-done.tiles = bf16[8,4,4,16,128]{4,3,2,1,0:T(8,128)(2,1)S(1)} async-done(((bf16[8,4,4,16,128]{4,3,2,1,0:T(8,128)(2,1)}), bf16[8,4,4,16,128]{4,3,2,1,0:T(8,128)(2,1)S(1)}, u32[]{:S(2)}, u32[]{:S(2)}) %all-to-all-start) | async-done | bytes 524320 | tf_op jit(solution)/shard_map/all_to_all | solution.py:17
  23.4 0.0 copy-start.1
  23.4 1.3 %collective-permute-start.2 = (bf16[34,16,128]{2,1,0:T(8,128)(2,1)S(1)}, bf16[34,16,128]{2,1,0:T(8,128)(2,1)S(1)}, u32[]{:S(2)}, u32[]{:S(2)}) collective-permute-start(bf16[34,16,128]{2,1,0:T(8,128)(2,1)S(1)} %get-tuple-element.34), channel_id=1, source_target_pairs={{0,8},{8,16},{16,24},{24,32},{32,40},{40,48},{48,56},{1,9},{9,17},... | collective-permute-start | bytes 417800 | tf_op jit(solution)/shard_map/ppermute | solution.py:22
  24.7 1.3 %collective-permute-start.3 = (bf16[34,16,128]{2,1,0:T(8,128)(2,1)S(1)}, bf16[34,16,128]{2,1,0:T(8,128)(2,1)S(1)}, u32[]{:S(2)}, u32[]{:S(2)}) collective-permute-start(bf16[34,16,128]{2,1,0:T(8,128)(2,1)S(1)} %get-tuple-element.35), channel_id=1, source_target_pairs={{8,0},{16,8},{24,16},{32,24},{40,32},{48,40},{56,48},{9,1},{17,9},... | collective-permute-start | bytes 417800 | tf_op jit(solution)/shard_map/ppermute | solution.py:23
  26.0 1.3 %collective-permute-done.2.before = bf16[34,16,128]{2,1,0:T(8,128)(2,1)S(1)} collective-permute-done((bf16[34,16,128]{2,1,0:T(8,128)(2,1)S(1)}, bf16[34,16,128]{2,1,0:T(8,128)(2,1)S(1)}, u32[]{:S(2)}, u32[]{:S(2)}) %collective-permute-start.2) | collective-permute-done | bytes 139296 | tf_op jit(solution)/shard_map/ppermute | solution.py:22
  27.3 4.4 %collective-permute-done.3.after = bf16[34,16,128]{2,1,0:T(8,128)(2,1)S(1)} collective-permute-done((bf16[34,16,128]{2,1,0:T(8,128)(2,1)S(1)}, bf16[34,16,128]{2,1,0:T(8,128)(2,1)S(1)}, u32[]{:S(2)}, u32[]{:S(2)}) %collective-permute-start.3) | collective-permute-done | bytes 139296 | tf_op jit(solution)/shard_map/ppermute | solution.py:23
  31.6 0.0 copy-done.1
  31.6 5.0 %forward.1 = (bf16[16,16,128]{2,1,0:T(8,128)(2,1)S(1)}, bf16[10,16,128]{2,1,0:T(8,128)(2,1)S(1)}, bf16[10,16,128]{2,1,0:T(8,128)(2,1)S(1)}, bf16[8,2,16,128]{3,2,1,0:T(8,128)(2,1)}) custom-call(s32[2]{0:T(128)S(1)} %pad_add_fusion.at_ref, f32[16]{0:T(128)S(1)} %copy-done.1, bf16[3,96,256]{2,1,0:T(8,128)(2,1)S(1)} %bitcast.28, ...), custom_call_target="tpu_custom_call" | custom-call | flops 339738624 | bytes 262144 | tf_op jit(solution)/shard_map/forward/pallas_call | solution.py:256
  36.7 9.2 %all-to-all-start.1 = ((bf16[8,2,16,128]{3,2,1,0:T(8,128)(2,1)}), bf16[8,2,16,128]{3,2,1,0:T(8,128)(2,1)S(1)}, u32[]{:S(2)}, u32[]{:S(2)}) async-start(bf16[8,2,16,128]{3,2,1,0:T(8,128)(2,1)} %get-tuple-element.37), calls=%async_computation.1 | async-start | bytes 131072 | tf_op jit(solution)/shard_map/all_to_all | solution.py:17
  45.8 4.1 %collective-permute-start.4 = (bf16[10,16,128]{2,1,0:T(8,128)(2,1)S(1)}, bf16[10,16,128]{2,1,0:T(8,128)(2,1)S(1)}, u32[]{:S(2)}, u32[]{:S(2)}) collective-permute-start(bf16[10,16,128]{2,1,0:T(8,128)(2,1)S(1)} %get-tuple-element.38.face), channel_id=1, source_target_pairs={{0,64},{64,0},{128,192},{192,128},{256,320},{320,256},{384,448},{4... | collective-permute-start | bytes 122888 | tf_op jit(solution)/shard_map/ppermute | solution.py:342
  49.9 0.7 collective-permute-start.5
  50.6 0.2 collective-permute-done.4.face_in
  50.8 0.0 collective-permute-done.5.far_in
  50.8 3.5 %all-to-all-done.1.blocks = bf16[8,2,16,128]{3,2,1,0:T(8,128)(2,1)S(1)} async-done(((bf16[8,2,16,128]{3,2,1,0:T(8,128)(2,1)}), bf16[8,2,16,128]{3,2,1,0:T(8,128)(2,1)S(1)}, u32[]{:S(2)}, u32[]{:S(2)}) %all-to-all-start.1) | async-done | bytes 65568 | tf_op jit(solution)/shard_map/all_to_all | solution.py:17
  54.2 0.6 sums.2
  54.9 14.3 %all-to-all-start.2 = ((bf16[8,2,16,128]{3,2,1,0:T(8,128)(2,1)}), bf16[8,2,16,128]{3,2,1,0:T(8,128)(2,1)S(1)}, u32[]{:S(2)}, u32[]{:S(2)}) async-start(bf16[8,2,16,128]{3,2,1,0:T(8,128)(2,1)} %sums.2), calls=%async_computation.2 | async-start | bytes 131072 | tf_op jit(solution)/shard_map/all_to_all | solution.py:17
  69.2 0.1 copy.18.w_ref
  69.3 1.2 %backward.1 = (bf16[4,8,16,128]{3,2,1,0:T(8,128)(2,1)S(1)}, bf16[4,8,16,128]{3,2,1,0:T(8,128)(2,1)S(1)}) custom-call(s32[2]{0:T(128)S(1)} %pad_add_fusion.at_ref, bf16[64,432]{1,0:T(8,128)(2,1)S(1)} %copy.18.w_ref, bf16[10,16,128]{2,1,0:T(8,128)(2,1)S(1)} %get-tuple-element.38.face, bf16[10,16,128]{2,1,0:T(8,128)(2,1)S(1)} %get-tuple-element.39.far, ...), custom_call_target="tpu_custom_call" | custom-call | flops 113246208 | bytes 262144 | tf_op jit(solution)/shard_map/backward/pallas_call | solution.py:256
  70.5 7.1 %all-to-all-done.2.blocks = bf16[8,2,16,128]{3,2,1,0:T(8,128)(2,1)S(1)} async-done(((bf16[8,2,16,128]{3,2,1,0:T(8,128)(2,1)}), bf16[8,2,16,128]{3,2,1,0:T(8,128)(2,1)S(1)}, u32[]{:S(2)}, u32[]{:S(2)}) %all-to-all-start.2) | async-done | bytes 65568 | tf_op jit(solution)/shard_map/all_to_all | solution.py:17
  77.6 3.0 %collective-permute-start.6 = (bf16[4,8,16,128]{3,2,1,0:T(8,128)(2,1)S(1)}, bf16[4,8,16,128]{3,2,1,0:T(8,128)(2,1)S(1)}, u32[]{:S(2)}, u32[]{:S(2)}) collective-permute-start(bf16[4,8,16,128]{3,2,1,0:T(8,128)(2,1)S(1)} %get-tuple-element.47), channel_id=1, source_target_pairs={{0,1},{1,0},{2,3},{3,2},{4,5},{5,4},{6,7},{7,6},{8,9},{9,8},{10,11... | collective-permute-start | bytes 393224 | tf_op jit(solution)/shard_map/ppermute | solution.py:366
  80.6 0.6 sums.3
  81.2 7.2 %all-to-all-start.3 = ((bf16[8,2,16,128]{3,2,1,0:T(8,128)(2,1)}), bf16[8,2,16,128]{3,2,1,0:T(8,128)(2,1)S(1)}, u32[]{:S(2)}, u32[]{:S(2)}) async-start(bf16[8,2,16,128]{3,2,1,0:T(8,128)(2,1)} %sums.3), calls=%async_computation.3 | async-start | bytes 131072 | tf_op jit(solution)/shard_map/all_to_all | solution.py:17
  88.4 0.0 collective-permute-done.6.right
  88.4 0.7 add.12
  89.1 7.7 %all-to-all-done.3.blocks = bf16[8,2,16,128]{3,2,1,0:T(8,128)(2,1)S(1)} async-done(((bf16[8,2,16,128]{3,2,1,0:T(8,128)(2,1)}), bf16[8,2,16,128]{3,2,1,0:T(8,128)(2,1)S(1)}, u32[]{:S(2)}, u32[]{:S(2)}) %all-to-all-start.3) | async-done | bytes 65568 | tf_op jit(solution)/shard_map/all_to_all | solution.py:17
  96.8 3.3 %all-to-all-start.4 = ((bf16[4,8,16,128]{3,2,1,0:T(8,128)(2,1)}), bf16[4,8,16,128]{3,2,1,0:T(8,128)(2,1)S(1)}, u32[]{:S(2)}, u32[]{:S(2)}) async-start(bf16[4,8,16,128]{3,2,1,0:T(8,128)(2,1)} %add.12), calls=%async_computation.4 | async-start | bytes 262144 | tf_op jit(solution)/shard_map/all_to_all | solution.py:370
  100.1 0.6 copy.21
  100.8 0.8 weights.1
  101.5 4.5 %all-to-all-done.4.parts = bf16[4,8,16,128]{3,2,1,0:T(8,128)(2,1)S(1)} async-done(((bf16[4,8,16,128]{3,2,1,0:T(8,128)(2,1)}), bf16[4,8,16,128]{3,2,1,0:T(8,128)(2,1)S(1)}, u32[]{:S(2)}, u32[]{:S(2)}) %all-to-all-start.4) | async-done | bytes 131104 | tf_op jit(solution)/shard_map/all_to_all | solution.py:370
  106.1 0.6 unpack.1
  (5 shorter events, 0.1 us)
Async XLA Ops:
  0.6 0.8 copy-start
  2.0 3.1 %collective-permute-start = (bf16[4,16,128]{2,1,0:T(8,128)(2,1)S(1)}, bf16[4,16,128]{2,1,0:T(8,128)(2,1)S(1)}, u32[]{:S(2)}, u32[]{:S(2)}) collective-permute-start(bf16[4,16,128]{2,1,0:T(8,128)(2,1)S(1)} %get-tuple-element.29), channel_id=1, source_target_pairs={{0,64},{64,0},{128,192},{192,128},{256,320},{320,256},{384,448},{4... | collective-permute-start | bytes 49160 | tf_op jit(solution)/shard_map/ppermute | solution.py:288
  3.9 1.2 %collective-permute-start.1 = (bf16[4,16,128]{2,1,0:T(8,128)(2,1)S(1)}, bf16[4,16,128]{2,1,0:T(8,128)(2,1)S(1)}, u32[]{:S(2)}, u32[]{:S(2)}) collective-permute-start(bf16[4,16,128]{2,1,0:T(8,128)(2,1)S(1)} %get-tuple-element.30), channel_id=1, source_target_pairs={{64,128},{128,64},{192,256},{256,192},{320,384},{384,320},{65,129}... | collective-permute-start | bytes 49160 | tf_op jit(solution)/shard_map/ppermute | solution.py:289
  6.5 9.4 %copy-start.4 = (bf16[16,2,8,128]{3,2,1,0:T(8,128)(2,1)S(1)}, bf16[16,2,8,128]{3,2,1,0:T(8,128)(2,1)}, u32[]{:S(2)}) copy-start(bf16[16,2,8,128]{3,2,1,0:T(8,128)(2,1)} %param.8) | copy-start | bytes 196612
  6.5 16.9 %all-to-all-start = ((bf16[8,4,4,16,128]{4,3,2,1,0:T(8,128)(2,1)}), bf16[8,4,4,16,128]{4,3,2,1,0:T(8,128)(2,1)S(1)}, u32[]{:S(2)}, u32[]{:S(2)}) async-start(bf16[8,4,4,16,128]{4,3,2,1,0:T(8,128)(2,1)} %grid.1), calls=%async_computation | async-start | bytes 1048576 | tf_op jit(solution)/shard_map/all_to_all | solution.py:17
  15.8 0.9 copy-start.2
  16.7 0.9 copy-start.3
  23.4 8.3 %copy-start.1 = (f32[16]{0:T(128)S(1)}, f32[16]{0:T(128)}, u32[]{:S(2)}) copy-start(f32[16]{0:T(128)} %bias_ref.1) | copy-start | bytes 196
  23.4 3.9 %collective-permute-start.2 = (bf16[34,16,128]{2,1,0:T(8,128)(2,1)S(1)}, bf16[34,16,128]{2,1,0:T(8,128)(2,1)S(1)}, u32[]{:S(2)}, u32[]{:S(2)}) collective-permute-start(bf16[34,16,128]{2,1,0:T(8,128)(2,1)S(1)} %get-tuple-element.34), channel_id=1, source_target_pairs={{0,8},{8,16},{16,24},{24,32},{32,40},{40,48},{48,56},{1,9},{9,17},... | collective-permute-start | bytes 417800 | tf_op jit(solution)/shard_map/ppermute | solution.py:22
  24.7 6.9 %collective-permute-start.3 = (bf16[34,16,128]{2,1,0:T(8,128)(2,1)S(1)}, bf16[34,16,128]{2,1,0:T(8,128)(2,1)S(1)}, u32[]{:S(2)}, u32[]{:S(2)}) collective-permute-start(bf16[34,16,128]{2,1,0:T(8,128)(2,1)S(1)} %get-tuple-element.35), channel_id=1, source_target_pairs={{8,0},{16,8},{24,16},{32,24},{40,32},{48,40},{56,48},{9,1},{17,9},... | collective-permute-start | bytes 417800 | tf_op jit(solution)/shard_map/ppermute | solution.py:23
  36.7 17.6 %all-to-all-start.1 = ((bf16[8,2,16,128]{3,2,1,0:T(8,128)(2,1)}), bf16[8,2,16,128]{3,2,1,0:T(8,128)(2,1)S(1)}, u32[]{:S(2)}, u32[]{:S(2)}) async-start(bf16[8,2,16,128]{3,2,1,0:T(8,128)(2,1)} %get-tuple-element.37), calls=%async_computation.1 | async-start | bytes 131072 | tf_op jit(solution)/shard_map/all_to_all | solution.py:17
  45.8 4.9 %collective-permute-start.4 = (bf16[10,16,128]{2,1,0:T(8,128)(2,1)S(1)}, bf16[10,16,128]{2,1,0:T(8,128)(2,1)S(1)}, u32[]{:S(2)}, u32[]{:S(2)}) collective-permute-start(bf16[10,16,128]{2,1,0:T(8,128)(2,1)S(1)} %get-tuple-element.38.face), channel_id=1, source_target_pairs={{0,64},{64,0},{128,192},{192,128},{256,320},{320,256},{384,448},{4... | collective-permute-start | bytes 122888 | tf_op jit(solution)/shard_map/ppermute | solution.py:342
  49.9 0.9 collective-permute-start.5
  54.9 22.7 %all-to-all-start.2 = ((bf16[8,2,16,128]{3,2,1,0:T(8,128)(2,1)}), bf16[8,2,16,128]{3,2,1,0:T(8,128)(2,1)S(1)}, u32[]{:S(2)}, u32[]{:S(2)}) async-start(bf16[8,2,16,128]{3,2,1,0:T(8,128)(2,1)} %sums.2), calls=%async_computation.2 | async-start | bytes 131072 | tf_op jit(solution)/shard_map/all_to_all | solution.py:17
  77.6 10.9 %collective-permute-start.6 = (bf16[4,8,16,128]{3,2,1,0:T(8,128)(2,1)S(1)}, bf16[4,8,16,128]{3,2,1,0:T(8,128)(2,1)S(1)}, u32[]{:S(2)}, u32[]{:S(2)}) collective-permute-start(bf16[4,8,16,128]{3,2,1,0:T(8,128)(2,1)S(1)} %get-tuple-element.47), channel_id=1, source_target_pairs={{0,1},{1,0},{2,3},{3,2},{4,5},{5,4},{6,7},{7,6},{8,9},{9,8},{10,11... | collective-permute-start | bytes 393224 | tf_op jit(solution)/shard_map/ppermute | solution.py:366
  81.2 15.6 %all-to-all-start.3 = ((bf16[8,2,16,128]{3,2,1,0:T(8,128)(2,1)}), bf16[8,2,16,128]{3,2,1,0:T(8,128)(2,1)S(1)}, u32[]{:S(2)}, u32[]{:S(2)}) async-start(bf16[8,2,16,128]{3,2,1,0:T(8,128)(2,1)} %sums.3), calls=%async_computation.3 | async-start | bytes 131072 | tf_op jit(solution)/shard_map/all_to_all | solution.py:17
  96.8 9.3 %all-to-all-start.4 = ((bf16[4,8,16,128]{3,2,1,0:T(8,128)(2,1)}), bf16[4,8,16,128]{3,2,1,0:T(8,128)(2,1)S(1)}, u32[]{:S(2)}, u32[]{:S(2)}) async-start(bf16[4,8,16,128]{3,2,1,0:T(8,128)(2,1)} %add.12), calls=%async_computation.4 | async-start | bytes 262144 | tf_op jit(solution)/shard_map/all_to_all | solution.py:370

commit v8 on v7

--- a/solution.py
+++ b/solution.py
@@ -13,8 +13,8 @@
 PART = 8
 
 
-def swapped(blocks, axis):
-    return lax.all_to_all(blocks, axis, 0, 0, tiled=True)
+def swapped(blocks, axis, groups=None):
+    return lax.all_to_all(blocks, axis, 0, 0, tiled=True, axis_index_groups=groups)
 
 
 def neighbours(first, last, axis):
@@ -75,6 +75,14 @@
             out_ref[k, r] = total.astype(BF16)
 
 
+def pair_kernel(kept, other, out_ref):
+    first = other.shape[0] - kept.shape[0]
+    for r in range(kept.shape[0]):
+        total = (kept[r].astype(F32) + other[first + r].astype(F32)).astype(BF16)
+        for k in range(out_ref.shape[0]):
+            out_ref[k, r] = total
+
+
 def add_kernel(left, right, out_ref):
     for k in range(left.shape[0]):
         out_ref[k] = (left[k].astype(F32) + right[k].astype(F32)).astype(BF16)
@@ -93,7 +101,7 @@
 
 
 def forward_kernel(planes, rows, at_ref, bias_ref, w_ref, cot, tiles, before, after, *refs):
-    out_ref, face_ref, far_ref, sums_ref, grads = refs
+    out_ref, face_ref, far_ref, kept_ref, grads, halves = refs
     cout, width = cot.shape[1:]
     sources = tiles.shape[0]
     edge = sources * (planes + 2)
@@ -181,13 +189,14 @@
     target = (source // PART) % 2 * (width // 2) + source // (2 * PART) * PART + source % PART
     order = jnp.where(lax.broadcasted_iota(jnp.int32, (width, width), 1) == target, 1.0, 0.0).astype(BF16)
     placed = jnp.dot(jnp.concatenate(blocks, axis=0).astype(BF16), order, preferred_element_type=F32)
-    size = sums_ref.shape[1]
-    for k in range(sums_ref.shape[0] * size):
-        block = placed[k * cout : (k + 1) * cout] if k < len(blocks) else jnp.zeros((cout, width), F32)
-        sums_ref[k // size, k % size] = block.astype(BF16)
+    count = len(blocks) // 2
+    for k in range(2 * count):
+        halves[k // count, k % count] = placed[k * cout : (k + 1) * cout].astype(BF16)
     core = at_ref[0]
-    face_ref[...] = grads[1 - core]
+    face_ref[: rows + 2] = grads[1 - core]
+    face_ref[rows + 2 :] = halves[1 - core]
     far_ref[...] = grads[core]
+    kept_ref[...] = halves[core]
 
 
 def backward_kernel(planes, rows, at_ref, w_ref, face, far, face_in, far_in, kept_ref, sent_ref, stack, parts):
@@ -233,18 +242,18 @@
     return ones.reshape(2, 3 * cin, 4 * cin)
 
 
-def weights_kernel(blocks, w_ref, b_ref):
-    cout, width = blocks.shape[2:]
+def weights_kernel(at_ref, mine, other, w_ref, b_ref):
+    count, cout, width = mine.shape
     half = width // 2
-    size = blocks.shape[1]
-    for k in range(14):
-        block = blocks[k // size, k % size].astype(F32)
+    for k in range(2 * count):
+        own = at_ref[0] == k // count
+        block = jnp.where(own, mine[k % count].astype(F32), other[k % count].astype(F32))
         for e in range(2):
             piece = block[:, e * half : (e + 1) * half]
             at, kh = (k, e) if k < 9 else (2 * (k - 9) + e, 2)
             if at < 9:
                 w_ref[at // 3 * 9 + kh * 3 + at % 3] = piece
-    spare = blocks[13 // size, 13 % size].astype(F32)[:, half : half + cout]
+    spare = block[:, half : half + cout]
     row = lax.broadcasted_iota(jnp.int32, (cout, cout), 0)
     lane = lax.broadcasted_iota(jnp.int32, (cout, cout), 1)
     b_ref[...] = jnp.sum(jnp.where(row == lane, spare, 0.0), axis=0, keepdims=True)
@@ -320,7 +329,8 @@
     before, after = neighbours(first, last, "height")
 
     work = 2 * cells * width * taps * cin * cout
-    out, face, far, sums = call(
+    count = (taps + 1) // 4
+    out, face, far, kept_sums = call(
         functools.partial(forward_kernel, planes, rows),
         "forward",
         at,
@@ -330,20 +340,20 @@
         tiles,
         before,
         after,
-        out=[(cells, cout, width)] + [(rows + 2, cout, width)] * 2 + [(height, 16 // height, cout, width)],
-        scratch=[((planes, rows + 2, cout, width), BF16)],
+        out=[(k, cout, width) for k in (cells, rows + 2 + count, rows + 2, count)],
+        scratch=[((planes, rows + 2, cout, width), BF16), ((2, count, cout, width), BF16)],
         flops=3 * work,
         waves=1 << 17,
         scalars=2,
     )
     output = out.reshape(planes, rows, cout, width).transpose(2, 0, 1, 3)
 
-    size = sums.shape[1:]
+    size = kept_sums.shape
     face_in = lax.ppermute(face, "depth", swap)
+    sums = call(pair_kernel, "pair", kept_sums, face_in, out=[(height,) + size])
+    sums, far = lax.optimization_barrier((sums, far))
     far_in = lax.ppermute(far, "depth", cross)
     sums = swapped(sums, "height")
-    sums, face_in, far_in = lax.optimization_barrier((sums, face_in, far_in))
-    sums = swapped(call(sum_kernel, "sums", sums, out=[(depth,) + size]), "depth")
     kept, sent = call(
         functools.partial(backward_kernel, planes, rows),
         "backward",
@@ -362,12 +372,13 @@
         scalars=1,
     )
     sums, kept, sent = lax.optimization_barrier((sums, kept, sent))
-    sums = swapped(call(sum_kernel, "sums", sums, out=[(height,) + size]), "height")
+    groups = [[i for i in range(depth) if i % 2 == k] for k in range(2)]
+    sums = swapped(call(sum_kernel, "sums", sums, out=[(depth // 2,) + size]), "depth", groups)
     sent = lax.ppermute(sent, "filt", [(i, i ^ 1) for i in range(filt)])
     parts = call(add_kernel, "add", kept, sent, out=[kept.shape])
     sums, parts = lax.optimization_barrier((sums, parts))
     groups = [[i for i in range(filt) if i % 2 == k] for k in range(2)]
-    parts = lax.all_to_all(parts, "filt", 0, 0, tiled=True, axis_index_groups=groups)
+    parts = swapped(parts, "filt", groups)
     summed = call(
         unpack_kernel,
         "unpack",
@@ -376,8 +387,17 @@
         scratch=[((cin_dev * cells, width), F32)],
     ).reshape(activations.shape)
 
+    mine = call(sum_kernel, "sums", sums, out=[(1,) + size])[0]
+    other = lax.ppermute(mine, "depth", swap)
     weight_grad, bias_grad = call(
-        weights_kernel, "weights", sums, out=[(taps, cout, cin), (1, cout)], dtype=F32
+        weights_kernel,
+        "weights",
+        at,
+        mine,
+        other,
+        out=[(taps, cout, cin), (1, cout)],
+        dtype=F32,
+        scalars=1,
     )
     return (output, summed, weight_grad.transpose(0, 2, 1), bias_grad.reshape(cout))
 

time: 108 us -> 94.9 us (0.88)
  the two profiles are of different devices: /device:TPU:8 before, /device:TPU:1 now
where the time goes in v8:
time: 94.9 us; the launch traced here: 94.1 us
  starting transfers between devices  56.5 us (60%)
  waiting for transfers between devices  21.7 us (23%)
  Pallas kernels  11.6 us (12%)
  local copies, waits for them, and re-layouts  3.23 us (3%)
    all_to_all x4, starting transfers between devices, swapped(): lax.all_to_all(blocks, axis, 0, 0, tiled=True, axis_index_groups=groups)  22.7 us
    pallas_call x11, Pallas kernels, call(): pl.pallas_call(body, out_shape=outs, in_specs=[smem] * scalars + [vmem] *...  11.6 us
    ppermute x1, starting transfers between devices, per_device(): far_in = lax.ppermute(far, 'depth', cross)  10.2 us
    ppermute x1, starting transfers between devices, per_device(): facing = lax.ppermute(face, 'depth', swap)  8.79 us
    ppermute x1, starting transfers between devices, per_device(): other = lax.ppermute(mine, 'depth', swap)  5.86 us
    all_to_all x4, waiting for transfers between devices, swapped(): lax.all_to_all(blocks, axis, 0, 0, tiled=True, axis_index_groups=groups)  5.44 us
    ppermute x1, waiting for transfers between devices, per_device(): sent = lax.ppermute(sent, 'filt', [(i, i ^ 1) for i in range(filt)])  4.31 us
    ppermute x1, waiting for transfers between devices, per_device(): beyond = lax.ppermute(far, 'depth', cross)  4.02 us
  transfers between devices with their start and end apart: 12, of which 8 were waited for; matrix products, arithmetic and copies ran while one was open for 1% of the time, Pallas kernels for 3%

profile of v8, /device:TPU:1, one launch (start us, length us, event | category | flops | bytes accessed | tf_op | source)
XLA Modules:
  0.0 94.1 jit_solution(750684046422202345)
XLA Ops:
  0.6 0.0 copy-start
  0.7 0.1 pad_add_fusion.at_ref
  0.7 0.7 copy-done
  1.4 0.6 pack.1
  2.0 8.8 %collective-permute-start = (bf16[4,16,128]{2,1,0:T(8,128)(2,1)S(1)}, bf16[4,16,128]{2,1,0:T(8,128)(2,1)S(1)}, u32[]{:S(2)}, u32[]{:S(2)}) collective-permute-start(bf16[4,16,128]{2,1,0:T(8,128)(2,1)S(1)} %get-tuple-element.28), channel_id=1, source_target_pairs={{0,64},{64,0},{128,192},{192,128},{256,320},{320,256},{384,448},{4... | collective-permute-start | bytes 49160 | tf_op jit(solution)/shard_map/ppermute | solution.py:297
  10.8 1.9 %collective-permute-start.1 = (bf16[4,16,128]{2,1,0:T(8,128)(2,1)S(1)}, bf16[4,16,128]{2,1,0:T(8,128)(2,1)S(1)}, u32[]{:S(2)}, u32[]{:S(2)}) collective-permute-start(bf16[4,16,128]{2,1,0:T(8,128)(2,1)S(1)} %get-tuple-element.29), channel_id=1, source_target_pairs={{64,128},{128,64},{192,256},{256,192},{320,384},{384,320},{65,129}... | collective-permute-start | bytes 49160 | tf_op jit(solution)/shard_map/ppermute | solution.py:298
  12.7 0.0 collective-permute-done.facing
  12.7 4.0 %collective-permute-done.1.beyond = bf16[4,16,128]{2,1,0:T(8,128)(2,1)S(1)} collective-permute-done((bf16[4,16,128]{2,1,0:T(8,128)(2,1)S(1)}, bf16[4,16,128]{2,1,0:T(8,128)(2,1)S(1)}, u32[]{:S(2)}, u32[]{:S(2)}) %collective-permute-start.1) | collective-permute-done | bytes 16416 | tf_op jit(solution)/shard_map/ppermute | solution.py:298
  16.7 1.4 %grid.1 = bf16[8,4,4,16,128]{4,3,2,1,0:T(8,128)(2,1)} custom-call(s32[2]{0:T(128)S(1)} %pad_add_fusion.at_ref, bf16[2,4,16,128]{3,2,1,0:T(8,128)(2,1)S(1)} %get-tuple-element.27.own, bf16[4,16,128]{2,1,0:T(8,128)(2,1)S(1)} %collective-permute-done.facing, bf16[4,16,128]{2,1,0:T(8,128)(2,1)S(1)} %collective-permute-done.1.beyond), custom_call_target="tpu_custom_call" | custom-call | bytes 262144 | tf_op jit(solution)/shard_map/grid/pallas_call | solution.py:265
  18.1 0.0 copy-start.4
  18.1 3.6 %all-to-all-start = ((bf16[8,4,4,16,128]{4,3,2,1,0:T(8,128)(2,1)}), bf16[8,4,4,16,128]{4,3,2,1,0:T(8,128)(2,1)S(1)}, u32[]{:S(2)}, u32[]{:S(2)}) async-start(bf16[8,4,4,16,128]{4,3,2,1,0:T(8,128)(2,1)} %grid.1), calls=%async_computation | async-start | bytes 1048576 | tf_op jit(solution)/shard_map/all_to_all | solution.py:17
  21.8 0.0 copy-start.2
  21.8 0.0 copy-done.4
  21.8 0.9 copy-done.2
  22.7 0.1 copy.15
  22.7 0.1 reshape.45
  22.9 0.7 copy-done.3
  23.6 0.2 fusion
  23.8 5.4 %all-to-all-done.tiles = bf16[8,4,4,16,128]{4,3,2,1,0:T(8,128)(2,1)S(1)} async-done(((bf16[8,4,4,16,128]{4,3,2,1,0:T(8,128)(2,1)}), bf16[8,4,4,16,128]{4,3,2,1,0:T(8,128)(2,1)S(1)}, u32[]{:S(2)}, u32[]{:S(2)}) %all-to-all-start) | async-done | bytes 524320 | tf_op jit(solution)/shard_map/all_to_all | solution.py:17
  29.3 0.0 copy-start.1
  29.3 1.3 %collective-permute-start.2 = (bf16[34,16,128]{2,1,0:T(8,128)(2,1)S(1)}, bf16[34,16,128]{2,1,0:T(8,128)(2,1)S(1)}, u32[]{:S(2)}, u32[]{:S(2)}) collective-permute-start(bf16[34,16,128]{2,1,0:T(8,128)(2,1)S(1)} %get-tuple-element.33), channel_id=1, source_target_pairs={{0,8},{8,16},{16,24},{24,32},{32,40},{40,48},{48,56},{1,9},{9,17},... | collective-permute-start | bytes 417800 | tf_op jit(solution)/shard_map/ppermute | solution.py:22
  30.6 1.3 %collective-permute-start.3 = (bf16[34,16,128]{2,1,0:T(8,128)(2,1)S(1)}, bf16[34,16,128]{2,1,0:T(8,128)(2,1)S(1)}, u32[]{:S(2)}, u32[]{:S(2)}) collective-permute-start(bf16[34,16,128]{2,1,0:T(8,128)(2,1)S(1)} %get-tuple-element.34), channel_id=1, source_target_pairs={{8,0},{16,8},{24,16},{32,24},{40,32},{48,40},{56,48},{9,1},{17,9},... | collective-permute-start | bytes 417800 | tf_op jit(solution)/shard_map/ppermute | solution.py:23
  31.9 0.7 collective-permute-done.2.before
  32.6 3.8 %collective-permute-done.3.after = bf16[34,16,128]{2,1,0:T(8,128)(2,1)S(1)} collective-permute-done((bf16[34,16,128]{2,1,0:T(8,128)(2,1)S(1)}, bf16[34,16,128]{2,1,0:T(8,128)(2,1)S(1)}, u32[]{:S(2)}, u32[]{:S(2)}) %collective-permute-start.3) | collective-permute-done | bytes 139296 | tf_op jit(solution)/shard_map/ppermute | solution.py:23
  36.4 0.0 copy-done.1
  36.4 4.4 %forward.1 = (bf16[16,16,128]{2,1,0:T(8,128)(2,1)S(1)}, bf16[17,16,128]{2,1,0:T(8,128)(2,1)S(1)}, bf16[10,16,128]{2,1,0:T(8,128)(2,1)S(1)}, bf16[7,16,128]{2,1,0:T(8,128)(2,1)S(1)}) custom-call(s32[2]{0:T(128)S(1)} %pad_add_fusion.at_ref, f32[16]{0:T(128)S(1)} %copy-done.1, bf16[3,96,256]{2,1,0:T(8,128)(2,1)S(1)} %bitcast.29, ...), custom_call_target="tpu_custom_call" | custom-call | flops 339738624 | bytes 262144 | tf_op jit(solution)/shard_map/forward/pallas_call | solution.py:265
  40.8 1.9 %collective-permute-start.4 = (bf16[17,16,128]{2,1,0:T(8,128)(2,1)S(1)}, bf16[17,16,128]{2,1,0:T(8,128)(2,1)S(1)}, u32[]{:S(2)}, u32[]{:S(2)}) collective-permute-start(bf16[17,16,128]{2,1,0:T(8,128)(2,1)S(1)} %get-tuple-element.37.face), channel_id=1, source_target_pairs={{0,64},{64,0},{128,192},{192,128},{256,320},{320,256},{384,448},{4... | collective-permute-start | bytes 208904 | tf_op jit(solution)/shard_map/ppermute | solution.py:352
  42.7 1.2 %collective-permute-done.4.other.face_in = bf16[17,16,128]{2,1,0:T(8,128)(2,1)S(1)} collective-permute-done((bf16[17,16,128]{2,1,0:T(8,128)(2,1)S(1)}, bf16[17,16,128]{2,1,0:T(8,128)(2,1)S(1)}, u32[]{:S(2)}, u32[]{:S(2)}) %collective-permute-start.4) | collective-permute-done | bytes 69664 | tf_op jit(solution)/shard_map/ppermute | solution.py:352
  43.9 0.7 pair.1
  44.6 8.3 %all-to-all-start.1 = ((bf16[8,7,16,128]{3,2,1,0:T(8,128)(2,1)}), bf16[8,7,16,128]{3,2,1,0:T(8,128)(2,1)S(1)}, u32[]{:S(2)}, u32[]{:S(2)}) async-start(bf16[8,7,16,128]{3,2,1,0:T(8,128)(2,1)} %pair.1), calls=%async_computation.1 | async-start | bytes 458752 | tf_op jit(solution)/shard_map/all_to_all | solution.py:17
  53.0 10.2 %collective-permute-start.5 = (bf16[10,16,128]{2,1,0:T(8,128)(2,1)S(1)}, bf16[10,16,128]{2,1,0:T(8,128)(2,1)S(1)}, u32[]{:S(2)}, u32[]{:S(2)}) collective-permute-start(bf16[10,16,128]{2,1,0:T(8,128)(2,1)S(1)} %get-tuple-element.40.far), channel_id=1, source_target_pairs={{64,128},{128,64},{192,256},{256,192},{320,384},{384,320},{65,129}... | collective-permute-start | bytes 122888 | tf_op jit(solution)/shard_map/ppermute | solution.py:355
  63.2 0.1 copy.18.w_ref
  63.3 2.0 %collective-permute-done.5.far_in = bf16[10,16,128]{2,1,0:T(8,128)(2,1)S(1)} collective-permute-done((bf16[10,16,128]{2,1,0:T(8,128)(2,1)S(1)}, bf16[10,16,128]{2,1,0:T(8,128)(2,1)S(1)}, u32[]{:S(2)}, u32[]{:S(2)}) %collective-permute-start.5) | collective-permute-done | bytes 40992 | tf_op jit(solution)/shard_map/ppermute | solution.py:355
  65.3 1.2 %backward.1 = (bf16[4,8,16,128]{3,2,1,0:T(8,128)(2,1)S(1)}, bf16[4,8,16,128]{3,2,1,0:T(8,128)(2,1)S(1)}) custom-call(s32[2]{0:T(128)S(1)} %pad_add_fusion.at_ref, bf16[64,432]{1,0:T(8,128)(2,1)S(1)} %copy.18.w_ref, bf16[17,16,128]{2,1,0:T(8,128)(2,1)S(1)} %get-tuple-element.37.face, bf16[10,16,128]{2,1,0:T(8,128)(2,1)S(1)} %get-tuple-element.40.far, ...), custom_call_target="tpu_custom_call" | custom-call | flops 113246208 | bytes 262144 | tf_op jit(solution)/shard_map/backward/pallas_call | solution.py:265
  66.5 0.0 all-to-all-done.1.blocks
  66.5 0.7 sums.2
  67.2 7.4 %all-to-all-start.2 = ((bf16[4,7,16,128]{3,2,1,0:T(8,128)(2,1)}), bf16[4,7,16,128]{3,2,1,0:T(8,128)(2,1)S(1)}, u32[]{:S(2)}, u32[]{:S(2)}) async-start(bf16[4,7,16,128]{3,2,1,0:T(8,128)(2,1)} %sums.2), calls=%async_computation.2 | async-start | bytes 229376 | tf_op jit(solution)/shard_map/all_to_all | solution.py:17
  74.6 2.5 %collective-permute-start.6 = (bf16[4,8,16,128]{3,2,1,0:T(8,128)(2,1)S(1)}, bf16[4,8,16,128]{3,2,1,0:T(8,128)(2,1)S(1)}, u32[]{:S(2)}, u32[]{:S(2)}) collective-permute-start(bf16[4,8,16,128]{3,2,1,0:T(8,128)(2,1)S(1)} %get-tuple-element.45), channel_id=1, source_target_pairs={{0,1},{1,0},{2,3},{3,2},{4,5},{5,4},{6,7},{7,6},{8,9},{9,8},{10,11... | collective-permute-start | bytes 393224 | tf_op jit(solution)/shard_map/ppermute | solution.py:377
  77.1 4.3 %collective-permute-done.6.right = bf16[4,8,16,128]{3,2,1,0:T(8,128)(2,1)S(1)} collective-permute-done((bf16[4,8,16,128]{3,2,1,0:T(8,128)(2,1)S(1)}, bf16[4,8,16,128]{3,2,1,0:T(8,128)(2,1)S(1)}, u32[]{:S(2)}, u32[]{:S(2)}) %collective-permute-start.6) | collective-permute-done | bytes 131104 | tf_op jit(solution)/shard_map/ppermute | solution.py:377
  81.4 0.7 add.12
  82.1 0.0 all-to-all-done.2.blocks
  82.1 3.3 %all-to-all-start.3 = ((bf16[4,8,16,128]{3,2,1,0:T(8,128)(2,1)}), bf16[4,8,16,128]{3,2,1,0:T(8,128)(2,1)S(1)}, u32[]{:S(2)}, u32[]{:S(2)}) async-start(bf16[4,8,16,128]{3,2,1,0:T(8,128)(2,1)} %add.12), calls=%async_computation.3 | async-start | bytes 262144 | tf_op jit(solution)/shard_map/all_to_all | solution.py:17
  85.4 5.9 %collective-permute-start.7 = (bf16[7,16,128]{2,1,0:T(8,128)(2,1)S(1)}, bf16[7,16,128]{2,1,0:T(8,128)(2,1)S(1)}, u32[]{:S(2)}, u32[]{:S(2)}) collective-permute-start(bf16[7,16,128]{2,1,0:T(8,128)(2,1)S(1)} %bitcast.30), channel_id=1, source_target_pairs={{0,64},{64,0},{128,192},{192,128},{256,320},{320,256},{384,448},{4... | collective-permute-start | bytes 86024 | tf_op jit(solution)/shard_map/ppermute | solution.py:391
  91.3 0.6 copy.21
  92.0 0.2 collective-permute-done.7.other
  92.1 1.3 %weights.1 = (f32[27,16,64]{2,1,0:T(8,128)}, f32[1,16]{1,0:T(1,128)}) custom-call(s32[2]{0:T(128)S(1)} %pad_add_fusion.at_ref, bf16[7,16,128]{2,1,0:T(8,128)(2,1)S(1)} %bitcast.31, bf16[7,16,128]{2,1,0:T(8,128)(2,1)S(1)} %collective-permute-done.7.other), custom_call_target="tpu_custom_call" | custom-call | bytes 262144 | tf_op jit(solution)/shard_map/weights/pallas_call | solution.py:265
  93.5 0.0 all-to-all-done.3.parts
  93.5 0.6 unpack.1
  (6 shorter events, 0.1 us)
Async XLA Ops:
  0.6 0.8 copy-start
  2.0 10.7 %collective-permute-start = (bf16[4,16,128]{2,1,0:T(8,128)(2,1)S(1)}, bf16[4,16,128]{2,1,0:T(8,128)(2,1)S(1)}, u32[]{:S(2)}, u32[]{:S(2)}) collective-permute-start(bf16[4,16,128]{2,1,0:T(8,128)(2,1)S(1)} %get-tuple-element.28), channel_id=1, source_target_pairs={{0,64},{64,0},{128,192},{192,128},{256,320},{320,256},{384,448},{4... | collective-permute-start | bytes 49160 | tf_op jit(solution)/shard_map/ppermute | solution.py:297
  10.8 6.0 %collective-permute-start.1 = (bf16[4,16,128]{2,1,0:T(8,128)(2,1)S(1)}, bf16[4,16,128]{2,1,0:T(8,128)(2,1)S(1)}, u32[]{:S(2)}, u32[]{:S(2)}) collective-permute-start(bf16[4,16,128]{2,1,0:T(8,128)(2,1)S(1)} %get-tuple-element.29), channel_id=1, source_target_pairs={{64,128},{128,64},{192,256},{256,192},{320,384},{384,320},{65,129}... | collective-permute-start | bytes 49160 | tf_op jit(solution)/shard_map/ppermute | solution.py:298
  18.1 3.6 %copy-start.4 = (bf16[16,2,8,128]{3,2,1,0:T(8,128)(2,1)S(1)}, bf16[16,2,8,128]{3,2,1,0:T(8,128)(2,1)}, u32[]{:S(2)}) copy-start(bf16[16,2,8,128]{3,2,1,0:T(8,128)(2,1)} %param.8) | copy-start | bytes 196612
  18.1 11.1 %all-to-all-start = ((bf16[8,4,4,16,128]{4,3,2,1,0:T(8,128)(2,1)}), bf16[8,4,4,16,128]{4,3,2,1,0:T(8,128)(2,1)S(1)}, u32[]{:S(2)}, u32[]{:S(2)}) async-start(bf16[8,4,4,16,128]{4,3,2,1,0:T(8,128)(2,1)} %grid.1), calls=%async_computation | async-start | bytes 1048576 | tf_op jit(solution)/shard_map/all_to_all | solution.py:17
  21.8 0.9 copy-start.2
  22.7 0.9 copy-start.3
  29.3 7.1 %copy-start.1 = (f32[16]{0:T(128)S(1)}, f32[16]{0:T(128)}, u32[]{:S(2)}) copy-start(f32[16]{0:T(128)} %bias_ref.1) | copy-start | bytes 196
  29.3 3.3 %collective-permute-start.2 = (bf16[34,16,128]{2,1,0:T(8,128)(2,1)S(1)}, bf16[34,16,128]{2,1,0:T(8,128)(2,1)S(1)}, u32[]{:S(2)}, u32[]{:S(2)}) collective-permute-start(bf16[34,16,128]{2,1,0:T(8,128)(2,1)S(1)} %get-tuple-element.33), channel_id=1, source_target_pairs={{0,8},{8,16},{16,24},{24,32},{32,40},{40,48},{48,56},{1,9},{9,17},... | collective-permute-start | bytes 417800 | tf_op jit(solution)/shard_map/ppermute | solution.py:22
  30.6 5.8 %collective-permute-start.3 = (bf16[34,16,128]{2,1,0:T(8,128)(2,1)S(1)}, bf16[34,16,128]{2,1,0:T(8,128)(2,1)S(1)}, u32[]{:S(2)}, u32[]{:S(2)}) collective-permute-start(bf16[34,16,128]{2,1,0:T(8,128)(2,1)S(1)} %get-tuple-element.34), channel_id=1, source_target_pairs={{8,0},{16,8},{24,16},{32,24},{40,32},{48,40},{56,48},{9,1},{17,9},... | collective-permute-start | bytes 417800 | tf_op jit(solution)/shard_map/ppermute | solution.py:23
  40.8 3.2 %collective-permute-start.4 = (bf16[17,16,128]{2,1,0:T(8,128)(2,1)S(1)}, bf16[17,16,128]{2,1,0:T(8,128)(2,1)S(1)}, u32[]{:S(2)}, u32[]{:S(2)}) collective-permute-start(bf16[17,16,128]{2,1,0:T(8,128)(2,1)S(1)} %get-tuple-element.37.face), channel_id=1, source_target_pairs={{0,64},{64,0},{128,192},{192,128},{256,320},{320,256},{384,448},{4... | collective-permute-start | bytes 208904 | tf_op jit(solution)/shard_map/ppermute | solution.py:352
  44.6 21.8 %all-to-all-start.1 = ((bf16[8,7,16,128]{3,2,1,0:T(8,128)(2,1)}), bf16[8,7,16,128]{3,2,1,0:T(8,128)(2,1)S(1)}, u32[]{:S(2)}, u32[]{:S(2)}) async-start(bf16[8,7,16,128]{3,2,1,0:T(8,128)(2,1)} %pair.1), calls=%async_computation.1 | async-start | bytes 458752 | tf_op jit(solution)/shard_map/all_to_all | solution.py:17
  53.0 12.3 %collective-permute-start.5 = (bf16[10,16,128]{2,1,0:T(8,128)(2,1)S(1)}, bf16[10,16,128]{2,1,0:T(8,128)(2,1)S(1)}, u32[]{:S(2)}, u32[]{:S(2)}) collective-permute-start(bf16[10,16,128]{2,1,0:T(8,128)(2,1)S(1)} %get-tuple-element.40.far), channel_id=1, source_target_pairs={{64,128},{128,64},{192,256},{256,192},{320,384},{384,320},{65,129}... | collective-permute-start | bytes 122888 | tf_op jit(solution)/shard_map/ppermute | solution.py:355
  67.2 14.9 %all-to-all-start.2 = ((bf16[4,7,16,128]{3,2,1,0:T(8,128)(2,1)}), bf16[4,7,16,128]{3,2,1,0:T(8,128)(2,1)S(1)}, u32[]{:S(2)}, u32[]{:S(2)}) async-start(bf16[4,7,16,128]{3,2,1,0:T(8,128)(2,1)} %sums.2), calls=%async_computation.2 | async-start | bytes 229376 | tf_op jit(solution)/shard_map/all_to_all | solution.py:17
  74.6 6.8 %collective-permute-start.6 = (bf16[4,8,16,128]{3,2,1,0:T(8,128)(2,1)S(1)}, bf16[4,8,16,128]{3,2,1,0:T(8,128)(2,1)S(1)}, u32[]{:S(2)}, u32[]{:S(2)}) collective-permute-start(bf16[4,8,16,128]{3,2,1,0:T(8,128)(2,1)S(1)} %get-tuple-element.45), channel_id=1, source_target_pairs={{0,1},{1,0},{2,3},{3,2},{4,5},{5,4},{6,7},{7,6},{8,9},{9,8},{10,11... | collective-permute-start | bytes 393224 | tf_op jit(solution)/shard_map/ppermute | solution.py:377
  82.1 11.4 %all-to-all-start.3 = ((bf16[4,8,16,128]{3,2,1,0:T(8,128)(2,1)}), bf16[4,8,16,128]{3,2,1,0:T(8,128)(2,1)S(1)}, u32[]{:S(2)}, u32[]{:S(2)}) async-start(bf16[4,8,16,128]{3,2,1,0:T(8,128)(2,1)} %add.12), calls=%async_computation.3 | async-start | bytes 262144 | tf_op jit(solution)/shard_map/all_to_all | solution.py:17
  85.4 6.7 %collective-permute-start.7 = (bf16[7,16,128]{2,1,0:T(8,128)(2,1)S(1)}, bf16[7,16,128]{2,1,0:T(8,128)(2,1)S(1)}, u32[]{:S(2)}, u32[]{:S(2)}) collective-permute-start(bf16[7,16,128]{2,1,0:T(8,128)(2,1)S(1)} %bitcast.30), channel_id=1, source_target_pairs={{0,64},{64,0},{128,192},{192,128},{256,320},{320,256},{384,448},{4... | collective-permute-start | bytes 86024 | tf_op jit(solution)/shard_map/ppermute | solution.py:391

commit v9 on v8

--- a/solution.py
+++ b/solution.py
@@ -81,11 +81,6 @@
         total = (kept[r].astype(F32) + other[first + r].astype(F32)).astype(BF16)
         for k in range(out_ref.shape[0]):
             out_ref[k, r] = total
-
-
-def add_kernel(left, right, out_ref):
-    for k in range(left.shape[0]):
-        out_ref[k] = (left[k].astype(F32) + right[k].astype(F32)).astype(BF16)
 
 
 def unpack_kernel(parts, out_ref, wide):
@@ -199,10 +194,10 @@
     kept_ref[...] = halves[core]
 
 
-def backward_kernel(planes, rows, at_ref, w_ref, face, far, face_in, far_in, kept_ref, sent_ref, stack, parts):
+def backward_kernel(planes, rows, at_ref, w_ref, face, far, face_in, far_in, parts, stack):
     cout, width = far.shape[1:]
     cin = w_ref.shape[0]
-    count = 2 * parts.shape[1]
+    count = parts.shape[0]
     part = cin // count
     lane = lax.broadcasted_iota(jnp.int32, (cout, width), 1)
     step = 3 * cout
@@ -228,9 +223,7 @@
             for f in range(count):
                 piece = acc[f * part : (f + 1) * part]
                 piece = jnp.concatenate([piece[:, :width], piece[:, width:]], axis=0).astype(BF16)
-                parts[(f % 2) ^ at_ref[1], f // 2, pair] = piece
-    kept_ref[...] = parts[0]
-    sent_ref[...] = parts[1]
+                parts[f, pair] = piece
 
 
 def placing(cin):
@@ -282,7 +275,7 @@
     depth, height, filt = (lax.axis_size(axis) for axis in ("depth", "height", "filt"))
     swap = [(i, i ^ 1) for i in range(depth)]
     cross = [(i, i - 1 if i % 2 == 0 else i + 1) for i in range(1, depth - 1)]
-    at = jnp.stack([lax.axis_index("depth") % 2, lax.axis_index("filt") % 2]).astype(jnp.int32)
+    at = (lax.axis_index("depth") % 2).astype(jnp.int32).reshape(1)
     pairs, double = rows // 2, 2 * cin_dev
 
     own, face, far = call(
@@ -325,7 +318,7 @@
         cot,
         out=[((planes + 2) * filt + planes, cout, width)] * 2,
     )
-    first, last, w_forward = lax.optimization_barrier((first, last, w_forward))
+    first, last, w_forward, w_back = lax.optimization_barrier((first, last, w_forward, w_back))
     before, after = neighbours(first, last, "height")
 
     work = 2 * cells * width * taps * cin * cout
@@ -350,11 +343,9 @@
 
     size = kept_sums.shape
     face_in = lax.ppermute(face, "depth", swap)
-    sums = call(pair_kernel, "pair", kept_sums, face_in, out=[(height,) + size])
-    sums, far = lax.optimization_barrier((sums, far))
     far_in = lax.ppermute(far, "depth", cross)
-    sums = swapped(sums, "height")
-    kept, sent = call(
+    sums = swapped(call(pair_kernel, "pair", kept_sums, face_in, out=[(height,) + size]), "height")
+    parts = call(
         functools.partial(backward_kernel, planes, rows),
         "backward",
         at,
@@ -363,22 +354,16 @@
         far,
         face_in,
         far_in,
-        out=[(filt // 2, cells // 2, double, width)] * 2,
-        scratch=[
-            ((planes + 2, (rows + 2) * 3 * cout, width), BF16),
-            ((2, filt // 2, cells // 2, double, width), BF16),
-        ],
-        flops=work,
+        out=[(filt, cells // 2, double, width)],
+        scratch=[((planes + 2, (rows + 2) * 3 * cout, width), BF16)],
+        flops=64 * work,
         scalars=1,
     )
-    sums, kept, sent = lax.optimization_barrier((sums, kept, sent))
+    sums, parts = lax.optimization_barrier((sums, parts))
     groups = [[i for i in range(depth) if i % 2 == k] for k in range(2)]
     sums = swapped(call(sum_kernel, "sums", sums, out=[(depth // 2,) + size]), "depth", groups)
-    sent = lax.ppermute(sent, "filt", [(i, i ^ 1) for i in range(filt)])
-    parts = call(add_kernel, "add", kept, sent, out=[kept.shape])
     sums, parts = lax.optimization_barrier((sums, parts))
-    groups = [[i for i in range(filt) if i % 2 == k] for k in range(2)]
-    parts = swapped(parts, "filt", groups)
+    parts = swapped(parts, "filt")
     summed = call(
         unpack_kernel,
         "unpack",

time: 94.9 us -> 94.4 us (level)
  the two profiles are of different devices: /device:TPU:1 before, /device:TPU:8 now
where the time goes in v9:
time: 94.4 us; the launch traced here: 93.7 us
  starting transfers between devices  35.1 us (37%)
  waiting for transfers between devices  23.3 us (25%)
  blocking collectives  22.1 us (23%)
  Pallas kernels  8.81 us (9%)
  local copies, waits for them, and re-layouts  3.33 us (4%)
    all_to_all x3, starting transfers between devices, swapped(): lax.all_to_all(blocks, axis, 0, 0, tiled=True, axis_index_groups=groups)  22.4 us
    all_to_all x1, blocking collectives, swapped(): lax.all_to_all(blocks, axis, 0, 0, tiled=True, axis_index_groups=groups)  22.1 us
    all_to_all x3, waiting for transfers between devices, swapped(): lax.all_to_all(blocks, axis, 0, 0, tiled=True, axis_index_groups=groups)  16.6 us
    pallas_call x10, Pallas kernels, call(): pl.pallas_call(body, out_shape=outs, in_specs=[smem] * scalars + [vmem] *...  8.81 us
    ppermute x1, starting transfers between devices, per_device(): face_in = lax.ppermute(face, 'depth', swap)  4.91 us
    ppermute x1, waiting for transfers between devices, neighbours(): after = lax.ppermute(first, axis, [(i + 1, i) for i in range(ends)])  4.38 us
    unnamed x10, local copies, waits for them, and re-layouts  2.34 us
    ppermute x1, starting transfers between devices, per_device(): other = lax.ppermute(mine, 'depth', swap)  1.92 us
  transfers between devices with their start and end apart: 10, of which 8 were waited for; matrix products, arithmetic and copies ran while one was open for 1% of the time, Pallas kernels for 3%

profile of v9, /device:TPU:8, one launch (start us, length us, event | category | flops | bytes accessed | tf_op | source)
XLA Modules:
  0.0 93.7 jit_solution(3067340844409904132)
XLA Ops:
  0.6 0.0 copy-start
  0.7 0.7 copy-done
  1.4 1.9 %collective-permute-start = (bf16[4,16,128]{2,1,0:T(8,128)(2,1)S(1)}, bf16[4,16,128]{2,1,0:T(8,128)(2,1)S(1)}, u32[]{:S(2)}, u32[]{:S(2)}) collective-permute-start(bf16[4,16,128]{2,1,0:T(8,128)(2,1)S(1)} %get-tuple-element.24), channel_id=1, source_target_pairs={{0,64},{64,0},{128,192},{192,128},{256,320},{320,256},{384,448},{4... | collective-permute-start | bytes 49160 | tf_op jit(solution)/shard_map/ppermute | solution.py:290
  3.4 0.7 collective-permute-start.1
  4.0 0.5 collective-permute-done.facing
  4.5 0.0 collective-permute-done.1.beyond
  4.5 0.9 grid.1
  5.4 0.0 copy-start.4
  5.4 9.3 %all-to-all-start = ((bf16[8,4,4,16,128]{4,3,2,1,0:T(8,128)(2,1)}), bf16[8,4,4,16,128]{4,3,2,1,0:T(8,128)(2,1)S(1)}, u32[]{:S(2)}, u32[]{:S(2)}) async-start(bf16[8,4,4,16,128]{4,3,2,1,0:T(8,128)(2,1)} %grid.1), calls=%async_computation | async-start | bytes 1048576 | tf_op jit(solution)/shard_map/all_to_all | solution.py:17
  14.7 0.0 copy-start.2
  14.7 0.0 copy-done.4
  14.8 0.9 copy-done.2
  15.6 0.0 copy-start.3
  15.6 0.1 copy.15
  15.7 0.1 reshape.49
  15.8 0.7 copy-done.3
  16.6 0.2 fusion
  16.8 5.5 %all-to-all-done.tiles = bf16[8,4,4,16,128]{4,3,2,1,0:T(8,128)(2,1)S(1)} async-done(((bf16[8,4,4,16,128]{4,3,2,1,0:T(8,128)(2,1)}), bf16[8,4,4,16,128]{4,3,2,1,0:T(8,128)(2,1)S(1)}, u32[]{:S(2)}, u32[]{:S(2)}) %all-to-all-start) | async-done | bytes 524320 | tf_op jit(solution)/shard_map/all_to_all | solution.py:17
  22.3 0.0 copy-start.1
  22.3 1.3 %collective-permute-start.2 = (bf16[34,16,128]{2,1,0:T(8,128)(2,1)S(1)}, bf16[34,16,128]{2,1,0:T(8,128)(2,1)S(1)}, u32[]{:S(2)}, u32[]{:S(2)}) collective-permute-start(bf16[34,16,128]{2,1,0:T(8,128)(2,1)S(1)} %get-tuple-element.29), channel_id=1, source_target_pairs={{0,8},{8,16},{16,24},{24,32},{32,40},{40,48},{48,56},{1,9},{9,17},... | collective-permute-start | bytes 417800 | tf_op jit(solution)/shard_map/ppermute | solution.py:22
  23.6 1.3 %collective-permute-start.3 = (bf16[34,16,128]{2,1,0:T(8,128)(2,1)S(1)}, bf16[34,16,128]{2,1,0:T(8,128)(2,1)S(1)}, u32[]{:S(2)}, u32[]{:S(2)}) collective-permute-start(bf16[34,16,128]{2,1,0:T(8,128)(2,1)S(1)} %get-tuple-element.30), channel_id=1, source_target_pairs={{8,0},{16,8},{24,16},{32,24},{40,32},{48,40},{56,48},{9,1},{17,9},... | collective-permute-start | bytes 417800 | tf_op jit(solution)/shard_map/ppermute | solution.py:23
  24.9 1.3 %collective-permute-done.2.before = bf16[34,16,128]{2,1,0:T(8,128)(2,1)S(1)} collective-permute-done((bf16[34,16,128]{2,1,0:T(8,128)(2,1)S(1)}, bf16[34,16,128]{2,1,0:T(8,128)(2,1)S(1)}, u32[]{:S(2)}, u32[]{:S(2)}) %collective-permute-start.2) | collective-permute-done | bytes 139296 | tf_op jit(solution)/shard_map/ppermute | solution.py:22
  26.2 4.4 %collective-permute-done.3.after = bf16[34,16,128]{2,1,0:T(8,128)(2,1)S(1)} collective-permute-done((bf16[34,16,128]{2,1,0:T(8,128)(2,1)S(1)}, bf16[34,16,128]{2,1,0:T(8,128)(2,1)S(1)}, u32[]{:S(2)}, u32[]{:S(2)}) %collective-permute-start.3) | collective-permute-done | bytes 139296 | tf_op jit(solution)/shard_map/ppermute | solution.py:23
  30.6 0.0 copy-done.1
  30.6 4.4 %forward.1 = (bf16[16,16,128]{2,1,0:T(8,128)(2,1)S(1)}, bf16[17,16,128]{2,1,0:T(8,128)(2,1)S(1)}, bf16[10,16,128]{2,1,0:T(8,128)(2,1)S(1)}, bf16[7,16,128]{2,1,0:T(8,128)(2,1)S(1)}) custom-call(s32[1]{0:T(128)} %bitcast.at_ref, f32[16]{0:T(128)S(1)} %copy-done.1, bf16[3,96,256]{2,1,0:T(8,128)(2,1)S(1)} %bitcast.28, bf16[16,16,128]{2,1,0:T(8,128)(2,1)S(1)} %bitcast.27, ...), custom_call_target="tpu_custom_call" | custom-call | flops 339738624 | bytes 262144 | tf_op jit(solution)/shard_map/forward/pallas_call | solution.py:258
  35.0 4.9 %collective-permute-start.4 = (bf16[17,16,128]{2,1,0:T(8,128)(2,1)S(1)}, bf16[17,16,128]{2,1,0:T(8,128)(2,1)S(1)}, u32[]{:S(2)}, u32[]{:S(2)}) collective-permute-start(bf16[17,16,128]{2,1,0:T(8,128)(2,1)S(1)} %get-tuple-element.33.face), channel_id=1, source_target_pairs={{0,64},{64,0},{128,192},{192,128},{256,320},{320,256},{384,448},{4... | collective-permute-start | bytes 208904 | tf_op jit(solution)/shard_map/ppermute | solution.py:345
  39.9 0.7 collective-permute-start.5
  40.5 0.1 copy.18.w_ref
  40.7 0.1 collective-permute-done.4.other.face_in
  40.8 0.7 pair.1
  41.5 8.6 %all-to-all-start.1 = ((bf16[8,7,16,128]{3,2,1,0:T(8,128)(2,1)}), bf16[8,7,16,128]{3,2,1,0:T(8,128)(2,1)S(1)}, u32[]{:S(2)}, u32[]{:S(2)}) async-start(bf16[8,7,16,128]{3,2,1,0:T(8,128)(2,1)} %pair.1), calls=%async_computation.1 | async-start | bytes 458752 | tf_op jit(solution)/shard_map/all_to_all | solution.py:17
  50.1 0.0 collective-permute-done.5.far_in
  50.1 1.3 %backward.1 = bf16[8,8,16,128]{3,2,1,0:T(8,128)(2,1)} custom-call(s32[1]{0:T(128)} %bitcast.at_ref, bf16[64,432]{1,0:T(8,128)(2,1)S(1)} %copy.18.w_ref, bf16[17,16,128]{2,1,0:T(8,128)(2,1)S(1)} %get-tuple-element.33.face, bf16[10,16,128]{2,1,0:T(8,128)(2,1)S(1)} %get-tuple-element.35.far, bf16[17,16,128]{2,1,0:T(8,128)(2,1)S(1)} %collective-permute-done.4.other.face_in, ...), custom_call_target="tpu_custom_call" | custom-call | flops 7247757312 | bytes 262144 | tf_op jit(solution)/shard_map/backward/pallas_call | solution.py:258
  51.4 8.8 %all-to-all-done.1.blocks = bf16[8,7,16,128]{3,2,1,0:T(8,128)(2,1)S(1)} async-done(((bf16[8,7,16,128]{3,2,1,0:T(8,128)(2,1)}), bf16[8,7,16,128]{3,2,1,0:T(8,128)(2,1)S(1)}, u32[]{:S(2)}, u32[]{:S(2)}) %all-to-all-start.1) | async-done | bytes 229408 | tf_op jit(solution)/shard_map/all_to_all | solution.py:17
  60.2 22.1 %all_to_all.20.blocks = bf16[4,7,16,128]{3,2,1,0:T(8,128)(2,1)S(1)} all-to-all(bf16[4,7,16,128]{3,2,1,0:T(8,128)(2,1)S(1)} %sums.2), channel_id=1, replica_groups={{0,128,256,384},{64,192,320,448},{1,129,257,385},{65,193,321,449},{2,13..., dimensions={0} | all-to-all | bytes 229376 | tf_op jit(solution)/shard_map/all_to_all | solution.py:17
  82.4 4.5 %all-to-all-start.3 = ((bf16[8,8,16,128]{3,2,1,0:T(8,128)(2,1)}), bf16[8,8,16,128]{3,2,1,0:T(8,128)(2,1)S(1)}, u32[]{:S(2)}, u32[]{:S(2)}) async-start(bf16[8,8,16,128]{3,2,1,0:T(8,128)(2,1)} %backward.1), calls=%async_computation.3 | async-start | bytes 524288 | tf_op jit(solution)/shard_map/all_to_all | solution.py:17
  86.9 1.9 %collective-permute-start.6 = (bf16[7,16,128]{2,1,0:T(8,128)(2,1)S(1)}, bf16[7,16,128]{2,1,0:T(8,128)(2,1)S(1)}, u32[]{:S(2)}, u32[]{:S(2)}) collective-permute-start(bf16[7,16,128]{2,1,0:T(8,128)(2,1)S(1)} %bitcast.29), channel_id=1, source_target_pairs={{0,64},{64,0},{128,192},{192,128},{256,320},{320,256},{384,448},{4... | collective-permute-start | bytes 86024 | tf_op jit(solution)/shard_map/ppermute | solution.py:376
  88.8 0.6 copy.21
  89.5 0.5 collective-permute-done.6.other
  90.0 0.8 weights.1
  90.8 2.3 %all-to-all-done.3.parts = bf16[8,8,16,128]{3,2,1,0:T(8,128)(2,1)S(1)} async-done(((bf16[8,8,16,128]{3,2,1,0:T(8,128)(2,1)}), bf16[8,8,16,128]{3,2,1,0:T(8,128)(2,1)S(1)}, u32[]{:S(2)}, u32[]{:S(2)}) %all-to-all-start.3) | async-done | bytes 262176 | tf_op jit(solution)/shard_map/all_to_all | solution.py:17
  93.0 0.7 unpack.1
  (7 shorter events, 0.2 us)
Async XLA Ops:
  0.6 0.8 copy-start
  1.4 3.1 %collective-permute-start = (bf16[4,16,128]{2,1,0:T(8,128)(2,1)S(1)}, bf16[4,16,128]{2,1,0:T(8,128)(2,1)S(1)}, u32[]{:S(2)}, u32[]{:S(2)}) collective-permute-start(bf16[4,16,128]{2,1,0:T(8,128)(2,1)S(1)} %get-tuple-element.24), channel_id=1, source_target_pairs={{0,64},{64,0},{128,192},{192,128},{256,320},{320,256},{384,448},{4... | collective-permute-start | bytes 49160 | tf_op jit(solution)/shard_map/ppermute | solution.py:290
  3.4 1.2 %collective-permute-start.1 = (bf16[4,16,128]{2,1,0:T(8,128)(2,1)S(1)}, bf16[4,16,128]{2,1,0:T(8,128)(2,1)S(1)}, u32[]{:S(2)}, u32[]{:S(2)}) collective-permute-start(bf16[4,16,128]{2,1,0:T(8,128)(2,1)S(1)} %get-tuple-element.25), channel_id=1, source_target_pairs={{64,128},{128,64},{192,256},{256,192},{320,384},{384,320},{65,129}... | collective-permute-start | bytes 49160 | tf_op jit(solution)/shard_map/ppermute | solution.py:291
  5.4 9.4 %copy-start.4 = (bf16[16,2,8,128]{3,2,1,0:T(8,128)(2,1)S(1)}, bf16[16,2,8,128]{3,2,1,0:T(8,128)(2,1)}, u32[]{:S(2)}) copy-start(bf16[16,2,8,128]{3,2,1,0:T(8,128)(2,1)} %param.8) | copy-start | bytes 196612
  5.4 16.9 %all-to-all-start = ((bf16[8,4,4,16,128]{4,3,2,1,0:T(8,128)(2,1)}), bf16[8,4,4,16,128]{4,3,2,1,0:T(8,128)(2,1)S(1)}, u32[]{:S(2)}, u32[]{:S(2)}) async-start(bf16[8,4,4,16,128]{4,3,2,1,0:T(8,128)(2,1)} %grid.1), calls=%async_computation | async-start | bytes 1048576 | tf_op jit(solution)/shard_map/all_to_all | solution.py:17
  14.7 0.9 copy-start.2
  15.6 0.9 copy-start.3
  22.3 8.3 %copy-start.1 = (f32[16]{0:T(128)S(1)}, f32[16]{0:T(128)}, u32[]{:S(2)}) copy-start(f32[16]{0:T(128)} %bias_ref.1) | copy-start | bytes 196
  22.3 3.9 %collective-permute-start.2 = (bf16[34,16,128]{2,1,0:T(8,128)(2,1)S(1)}, bf16[34,16,128]{2,1,0:T(8,128)(2,1)S(1)}, u32[]{:S(2)}, u32[]{:S(2)}) collective-permute-start(bf16[34,16,128]{2,1,0:T(8,128)(2,1)S(1)} %get-tuple-element.29), channel_id=1, source_target_pairs={{0,8},{8,16},{16,24},{24,32},{32,40},{40,48},{48,56},{1,9},{9,17},... | collective-permute-start | bytes 417800 | tf_op jit(solution)/shard_map/ppermute | solution.py:22
  23.6 6.9 %collective-permute-start.3 = (bf16[34,16,128]{2,1,0:T(8,128)(2,1)S(1)}, bf16[34,16,128]{2,1,0:T(8,128)(2,1)S(1)}, u32[]{:S(2)}, u32[]{:S(2)}) collective-permute-start(bf16[34,16,128]{2,1,0:T(8,128)(2,1)S(1)} %get-tuple-element.30), channel_id=1, source_target_pairs={{8,0},{16,8},{24,16},{32,24},{40,32},{48,40},{56,48},{9,1},{17,9},... | collective-permute-start | bytes 417800 | tf_op jit(solution)/shard_map/ppermute | solution.py:23
  35.0 5.8 %collective-permute-start.4 = (bf16[17,16,128]{2,1,0:T(8,128)(2,1)S(1)}, bf16[17,16,128]{2,1,0:T(8,128)(2,1)S(1)}, u32[]{:S(2)}, u32[]{:S(2)}) collective-permute-start(bf16[17,16,128]{2,1,0:T(8,128)(2,1)S(1)} %get-tuple-element.33.face), channel_id=1, source_target_pairs={{0,64},{64,0},{128,192},{192,128},{256,320},{320,256},{384,448},{4... | collective-permute-start | bytes 208904 | tf_op jit(solution)/shard_map/ppermute | solution.py:345
  39.9 10.2 %collective-permute-start.5 = (bf16[10,16,128]{2,1,0:T(8,128)(2,1)S(1)}, bf16[10,16,128]{2,1,0:T(8,128)(2,1)S(1)}, u32[]{:S(2)}, u32[]{:S(2)}) collective-permute-start(bf16[10,16,128]{2,1,0:T(8,128)(2,1)S(1)} %get-tuple-element.35.far), channel_id=1, source_target_pairs={{64,128},{128,64},{192,256},{256,192},{320,384},{384,320},{65,129}... | collective-permute-start | bytes 122888 | tf_op jit(solution)/shard_map/ppermute | solution.py:346
  41.5 18.7 %all-to-all-start.1 = ((bf16[8,7,16,128]{3,2,1,0:T(8,128)(2,1)}), bf16[8,7,16,128]{3,2,1,0:T(8,128)(2,1)S(1)}, u32[]{:S(2)}, u32[]{:S(2)}) async-start(bf16[8,7,16,128]{3,2,1,0:T(8,128)(2,1)} %pair.1), calls=%async_computation.1 | async-start | bytes 458752 | tf_op jit(solution)/shard_map/all_to_all | solution.py:17
  82.4 10.6 %all-to-all-start.3 = ((bf16[8,8,16,128]{3,2,1,0:T(8,128)(2,1)}), bf16[8,8,16,128]{3,2,1,0:T(8,128)(2,1)S(1)}, u32[]{:S(2)}, u32[]{:S(2)}) async-start(bf16[8,8,16,128]{3,2,1,0:T(8,128)(2,1)} %backward.1), calls=%async_computation.3 | async-start | bytes 524288 | tf_op jit(solution)/shard_map/all_to_all | solution.py:17
  86.9 3.1 %collective-permute-start.6 = (bf16[7,16,128]{2,1,0:T(8,128)(2,1)S(1)}, bf16[7,16,128]{2,1,0:T(8,128)(2,1)S(1)}, u32[]{:S(2)}, u32[]{:S(2)}) collective-permute-start(bf16[7,16,128]{2,1,0:T(8,128)(2,1)S(1)} %bitcast.29), channel_id=1, source_target_pairs={{0,64},{64,0},{128,192},{192,128},{256,320},{320,256},{384,448},{4... | collective-permute-start | bytes 86024 | tf_op jit(solution)/shard_map/ppermute | solution.py:376

commit v10 on v9

--- a/solution.py
+++ b/solution.py
@@ -31,7 +31,7 @@
     return jnp.concatenate([ahead, value, behind], axis=0)
 
 
-def pack_kernel(at_ref, cells, own, face_ref, far_ref, wide):
+def pack_kernel(at_ref, cells, own, face_ref, wide):
     planes, pairs = own.shape[:2]
     count, lines = cells.shape[:2]
     for c in range(count):
@@ -42,27 +42,28 @@
             own[d, t] = jnp.concatenate(
                 [wide[pl.ds(row + e, count, stride=lines), :] for e in range(2)], axis=0
             ).astype(BF16)
-    even = at_ref[0] == 0
-    face_ref[...] = own[jnp.where(even, planes - 1, 0)]
-    far_ref[...] = own[jnp.where(even, 0, planes - 1)]
-
-
-def grid_kernel(at_ref, own, facing, beyond, out_ref):
+    face_ref[...] = own[jnp.where(at_ref[0] == 0, planes - 1, 0)]
+
+
+def grid_kernel(at_ref, own, facing, out_ref):
     planes = own.shape[0]
-    before = jnp.where(at_ref[0] == 0, 0, planes + 1)
+    core = at_ref[0]
     for k in range(out_ref.shape[0]):
         for d in range(planes):
-            out_ref[k, d + 1] = own[d]
-        out_ref[k, before] = beyond[...]
-        out_ref[k, planes + 1 - before] = facing[...]
-
-
-def rows_kernel(rows, tiles, cot, first_ref, last_ref):
-    sources, count = tiles.shape[:2]
-    for ref, t, row in ((first_ref, 0, 0), (last_ref, rows // 2 - 1, rows - 1)):
+            out_ref[k, d + core] = own[d]
+        out_ref[k, (1 - core) * planes] = facing[...]
+
+
+def rows_kernel(rows, at_ref, tiles, cot, far_ref, far_first, far_last, first_ref, last_ref):
+    sources, count, pairs = tiles.shape[:3]
+    plane = at_ref[0] * (count - 1)
+    far_ref[...] = tiles[:, plane]
+    far_first[...] = tiles[:, plane, 0]
+    far_last[...] = tiles[:, plane, pairs - 1]
+    for ref, t, row in ((first_ref, 0, 0), (last_ref, pairs - 1, rows - 1)):
         for p in range(count):
             ref[p * sources : (p + 1) * sources] = tiles[:, p, t]
-        for d in range(count - 2):
+        for d in range(count - 1):
             ref[count * sources + d] = cot[d * rows + row]
 
 
@@ -95,18 +96,32 @@
         out_ref[c] = wide[pl.ds(c, lines, stride=count), :].astype(BF16)
 
 
-def forward_kernel(planes, rows, at_ref, bias_ref, w_ref, cot, tiles, before, after, *refs):
+def forward_kernel(planes, rows, at_ref, bias_ref, w_ref, cot, tiles, before, after, far, far_before, far_after, *refs):
     out_ref, face_ref, far_ref, kept_ref, grads, halves = refs
     cout, width = cot.shape[1:]
     sources = tiles.shape[0]
-    edge = sources * (planes + 2)
+    edge = sources * (planes + 1)
+    core = at_ref[0]
 
     def tile(s, p, t):
+        def near(q):
+            if t == 0:
+                return before[q * sources + s]
+            if t == rows // 2 + 1:
+                return after[q * sources + s]
+            return tiles[s, q, t - 1]
+
+        if 0 < p < planes + 1:
+            return near(p - 1 + core)
         if t == 0:
-            return before[p * sources + s]
-        if t == rows // 2 + 1:
-            return after[p * sources + s]
-        return tiles[s, p, t - 1]
+            beyond = far_before[s]
+        elif t == rows // 2 + 1:
+            beyond = far_after[s]
+        else:
+            beyond = far[s, t - 1]
+        if p == 0:
+            return jnp.where(core == 0, beyond, near(0))
+        return jnp.where(core == 1, beyond, near(planes))
 
     lane = lax.broadcasted_iota(jnp.int32, (cout, width), 1)
     channel = lax.broadcasted_iota(jnp.int32, (cout, width), 0)
@@ -187,7 +202,6 @@
     count = len(blocks) // 2
     for k in range(2 * count):
         halves[k // count, k % count] = placed[k * cout : (k + 1) * cout].astype(BF16)
-    core = at_ref[0]
     face_ref[: rows + 2] = grads[1 - core]
     face_ref[rows + 2 :] = halves[1 - core]
     far_ref[...] = grads[core]
@@ -278,25 +292,23 @@
     at = (lax.axis_index("depth") % 2).astype(jnp.int32).reshape(1)
     pairs, double = rows // 2, 2 * cin_dev
 
-    own, face, far = call(
+    own, face = call(
         pack_kernel,
         "pack",
         at,
         activations.reshape(cin_dev, cells, width),
-        out=[(planes, pairs, double, width)] + [(pairs, double, width)] * 2,
+        out=[(planes, pairs, double, width), (pairs, double, width)],
         scratch=[((cin_dev * cells, width), F32)],
         scalars=1,
     )
     facing = lax.ppermute(face, "depth", swap)
-    beyond = lax.ppermute(far, "depth", cross)
     grid = call(
         grid_kernel,
         "grid",
         at,
         own,
         facing,
-        beyond,
-        out=[(filt, planes + 2, pairs, double, width)],
+        out=[(filt, planes + 1, pairs, double, width)],
         scalars=1,
     )
     tiles = swapped(grid, "filt")
@@ -311,14 +323,25 @@
     )
     w_forward = w_forward.astype(BF16).reshape(3, 6 * cout, 4 * cin)
     w_back = split[::-1, ::-1].transpose(3, 0, 1, 2, 4).reshape(cin, taps * cout)
-    first, last = call(
+    sends = call(
         functools.partial(rows_kernel, rows),
         "rows",
+        at,
         tiles,
         cot,
-        out=[((planes + 2) * filt + planes, cout, width)] * 2,
-    )
-    first, last, w_forward, w_back = lax.optimization_barrier((first, last, w_forward, w_back))
+        out=[(filt, pairs, double, width)]
+        + [(filt, double, width)] * 2
+        + [((planes + 1) * filt + planes, cout, width)] * 2,
+        scalars=1,
+    )
+    sends, w_forward, w_back = lax.optimization_barrier((sends, w_forward, w_back))
+    far, far_first, far_last, first, last = sends
+    corner = ("depth", "height")
+    up = [(i * height + k, j * height + k + 1) for i, j in cross for k in range(height - 1)]
+    down = [(i * height + k + 1, j * height + k) for i, j in cross for k in range(height - 1)]
+    far_plane = lax.ppermute(far, "depth", cross)
+    far_before = lax.ppermute(far_last, corner, up)
+    far_after = lax.ppermute(far_first, corner, down)
     before, after = neighbours(first, last, "height")
 
     work = 2 * cells * width * taps * cin * cout
@@ -333,6 +356,9 @@
         tiles,
         before,
         after,
+        far_plane,
+        far_before,
+        far_after,
         out=[(k, cout, width) for k in (cells, rows + 2 + count, rows + 2, count)],
         scratch=[((planes, rows + 2, cout, width), BF16), ((2, count, cout, width), BF16)],
         flops=3 * work,

time: 94.4 us -> 101 us (1.070)
  starting transfers between devices: 35.1 us -> 44.6 us
  blocking collectives: 22.1 us -> 19.2 us
    ppermute x1, starting transfers between devices: 4.91 us -> 11.9 us  [per_device(): face_in = lax.ppermute(face, 'depth', swap)]
    all_to_all x1, blocking collectives: 22.1 us -> 19.2 us  [swapped(): lax.all_to_all(blocks, axis, 0, 0, tiled=True, axis_index_groups=groups)]
    ppermute x1 -> x3, starting transfers between devices: 0.66 us -> 2 us  [the longest x1 0.67 us: per_device(): far_plane = lax.ppermute(far, 'depth', cross)]
    ppermute x1, waiting for transfers between devices: 1.27 us -> 0.01 us  [neighbours(): before = lax.ppermute(last, axis, [(i, i + 1) for i in range(ends)])]
    all_to_all x3, starting transfers between devices: 22.4 us -> 23.6 us  [swapped(): lax.all_to_all(blocks, axis, 0, 0, tiled=True, axis_index_groups=groups)]
  transfers between devices with their start and end apart: 10 -> 12, of which waited for: 8 -> 7; matrix products, arithmetic and copies ran while one was open for 1% -> 1% of each run, Pallas kernels for 3% -> 3%
where the time goes in v10:
time: 101 us; the launch traced here: 99.9 us
  starting transfers between devices  44.6 us (44%)
  waiting for transfers between devices  23 us (23%)
  blocking collectives  19.2 us (19%)
  Pallas kernels  8.76 us (9%)
  local copies, waits for them, and re-layouts  3.32 us (3%)
    all_to_all x3, starting transfers between devices, swapped(): lax.all_to_all(blocks, axis, 0, 0, tiled=True, axis_index_groups=groups)  23.6 us
    all_to_all x1, blocking collectives, swapped(): lax.all_to_all(blocks, axis, 0, 0, tiled=True, axis_index_groups=groups)  19.2 us
    all_to_all x3, waiting for transfers between devices, swapped(): lax.all_to_all(blocks, axis, 0, 0, tiled=True, axis_index_groups=groups)  17.3 us
    ppermute x1, starting transfers between devices, per_device(): face_in = lax.ppermute(face, 'depth', swap)  11.9 us
    pallas_call x10, Pallas kernels, call(): pl.pallas_call(body, out_shape=outs, in_specs=[smem] * scalars + [vmem] *...  8.76 us
    ppermute x1, waiting for transfers between devices, neighbours(): after = lax.ppermute(first, axis, [(i + 1, i) for i in range(ends)])  3.92 us
    unnamed x10, local copies, waits for them, and re-layouts  2.34 us
  transfers between devices with their start and end apart: 12, of which 7 were waited for; matrix products, arithmetic and copies ran while one was open for 1% of the time, Pallas kernels for 3%

profile of v10, /device:TPU:8, one launch (start us, length us, event | category | flops | bytes accessed | tf_op | source)
XLA Modules:
  0.0 99.9 jit_solution(16770056138187680768)
XLA Ops:
  0.6 0.0 copy-start
  0.7 0.7 copy-done
  1.4 1.9 %collective-permute-start = (bf16[4,16,128]{2,1,0:T(8,128)(2,1)S(1)}, bf16[4,16,128]{2,1,0:T(8,128)(2,1)S(1)}, u32[]{:S(2)}, u32[]{:S(2)}) collective-permute-start(bf16[4,16,128]{2,1,0:T(8,128)(2,1)S(1)} %get-tuple-element.29), channel_id=1, source_target_pairs={{0,64},{64,0},{128,192},{192,128},{256,320},{320,256},{384,448},{4... | collective-permute-start | bytes 49160 | tf_op jit(solution)/shard_map/ppermute | solution.py:304
  3.4 1.1 %collective-permute-done.facing = bf16[4,16,128]{2,1,0:T(8,128)(2,1)S(1)} collective-permute-done((bf16[4,16,128]{2,1,0:T(8,128)(2,1)S(1)}, bf16[4,16,128]{2,1,0:T(8,128)(2,1)S(1)}, u32[]{:S(2)}, u32[]{:S(2)}) %collective-permute-start) | collective-permute-done | bytes 16416 | tf_op jit(solution)/shard_map/ppermute | solution.py:304
  4.5 0.8 grid.1
  5.3 0.0 copy-start.4
  5.3 9.3 %all-to-all-start = ((bf16[8,3,4,16,128]{4,3,2,1,0:T(8,128)(2,1)}), bf16[8,3,4,16,128]{4,3,2,1,0:T(8,128)(2,1)S(1)}, u32[]{:S(2)}, u32[]{:S(2)}) async-start(bf16[8,3,4,16,128]{4,3,2,1,0:T(8,128)(2,1)} %grid.1), calls=%async_computation | async-start | bytes 786432 | tf_op jit(solution)/shard_map/all_to_all | solution.py:17
  14.6 0.0 copy-start.2
  14.6 0.0 copy-done.4
  14.6 0.9 copy-done.2
  15.5 0.0 copy-start.3
  15.5 0.1 copy.15
  15.6 0.1 reshape.49
  15.7 0.7 copy-done.3
  16.5 0.2 fusion
  16.7 6.1 %all-to-all-done.tiles = bf16[8,3,4,16,128]{4,3,2,1,0:T(8,128)(2,1)S(1)} async-done(((bf16[8,3,4,16,128]{4,3,2,1,0:T(8,128)(2,1)}), bf16[8,3,4,16,128]{4,3,2,1,0:T(8,128)(2,1)S(1)}, u32[]{:S(2)}, u32[]{:S(2)}) %all-to-all-start) | async-done | bytes 393248 | tf_op jit(solution)/shard_map/all_to_all | solution.py:17
  22.8 0.0 copy-start.1
  22.8 0.7 collective-permute-start.3
  23.5 1.3 %collective-permute-start.1 = (bf16[26,16,128]{2,1,0:T(8,128)(2,1)S(1)}, bf16[26,16,128]{2,1,0:T(8,128)(2,1)S(1)}, u32[]{:S(2)}, u32[]{:S(2)}) collective-permute-start(bf16[26,16,128]{2,1,0:T(8,128)(2,1)S(1)} %get-tuple-element.36), channel_id=1, source_target_pairs={{0,8},{8,16},{16,24},{24,32},{32,40},{40,48},{48,56},{1,9},{9,17},... | collective-permute-start | bytes 319496 | tf_op jit(solution)/shard_map/ppermute | solution.py:22
  24.8 1.3 %collective-permute-start.2 = (bf16[26,16,128]{2,1,0:T(8,128)(2,1)S(1)}, bf16[26,16,128]{2,1,0:T(8,128)(2,1)S(1)}, u32[]{:S(2)}, u32[]{:S(2)}) collective-permute-start(bf16[26,16,128]{2,1,0:T(8,128)(2,1)S(1)} %get-tuple-element.37), channel_id=1, source_target_pairs={{8,0},{16,8},{24,16},{32,24},{40,32},{48,40},{56,48},{9,1},{17,9},... | collective-permute-start | bytes 319496 | tf_op jit(solution)/shard_map/ppermute | solution.py:23
  26.1 0.7 collective-permute-start.4
  26.8 0.7 collective-permute-start.5
  27.4 0.0 collective-permute-done.4.far_before
  27.4 0.0 collective-permute-done.5.far_after
  27.5 0.0 collective-permute-done.1.before
  27.5 3.9 %collective-permute-done.2.after = bf16[26,16,128]{2,1,0:T(8,128)(2,1)S(1)} collective-permute-done((bf16[26,16,128]{2,1,0:T(8,128)(2,1)S(1)}, bf16[26,16,128]{2,1,0:T(8,128)(2,1)S(1)}, u32[]{:S(2)}, u32[]{:S(2)}) %collective-permute-start.2) | collective-permute-done | bytes 106528 | tf_op jit(solution)/shard_map/ppermute | solution.py:23
  31.4 0.0 collective-permute-done.3.far
  31.4 0.0 copy-done.1
  31.4 4.4 %forward.1 = (bf16[16,16,128]{2,1,0:T(8,128)(2,1)S(1)}, bf16[17,16,128]{2,1,0:T(8,128)(2,1)S(1)}, bf16[10,16,128]{2,1,0:T(8,128)(2,1)S(1)}, bf16[7,16,128]{2,1,0:T(8,128)(2,1)S(1)}) custom-call(s32[1]{0:T(128)} %bitcast.at_ref, f32[16]{0:T(128)S(1)} %copy-done.1, bf16[3,96,256]{2,1,0:T(8,128)(2,1)S(1)} %bitcast.28, bf16[16,16,128]{2,1,0:T(8,128)(2,1)S(1)} %bitcast.27, ...), custom_call_target="tpu_custom_call" | custom-call | flops 339738624 | bytes 262144 | tf_op jit(solution)/shard_map/forward/pallas_call | solution.py:272
  35.8 11.9 %collective-permute-start.6 = (bf16[17,16,128]{2,1,0:T(8,128)(2,1)S(1)}, bf16[17,16,128]{2,1,0:T(8,128)(2,1)S(1)}, u32[]{:S(2)}, u32[]{:S(2)}) collective-permute-start(bf16[17,16,128]{2,1,0:T(8,128)(2,1)S(1)} %get-tuple-element.43.face), channel_id=1, source_target_pairs={{0,64},{64,0},{128,192},{192,128},{256,320},{320,256},{384,448},{4... | collective-permute-start | bytes 208904 | tf_op jit(solution)/shard_map/ppermute | solution.py:371
  47.7 0.7 collective-permute-start.7
  48.4 0.1 copy.18.w_ref
  48.5 0.1 collective-permute-done.6.other.face_in
  48.6 0.7 pair.1
  49.3 9.9 %all-to-all-start.1 = ((bf16[8,7,16,128]{3,2,1,0:T(8,128)(2,1)}), bf16[8,7,16,128]{3,2,1,0:T(8,128)(2,1)S(1)}, u32[]{:S(2)}, u32[]{:S(2)}) async-start(bf16[8,7,16,128]{3,2,1,0:T(8,128)(2,1)} %pair.1), calls=%async_computation.1 | async-start | bytes 458752 | tf_op jit(solution)/shard_map/all_to_all | solution.py:17
  59.2 0.0 collective-permute-done.7.far_in
  59.2 1.3 %backward.1 = bf16[8,8,16,128]{3,2,1,0:T(8,128)(2,1)} custom-call(s32[1]{0:T(128)} %bitcast.at_ref, bf16[64,432]{1,0:T(8,128)(2,1)S(1)} %copy.18.w_ref, bf16[17,16,128]{2,1,0:T(8,128)(2,1)S(1)} %get-tuple-element.43.face, bf16[10,16,128]{2,1,0:T(8,128)(2,1)S(1)} %get-tuple-element.45.far, bf16[17,16,128]{2,1,0:T(8,128)(2,1)S(1)} %collective-permute-done.6.other.face_in, ...), custom_call_target="tpu_custom_call" | custom-call | flops 7247757312 | bytes 262144 | tf_op jit(solution)/shard_map/backward/pallas_call | solution.py:272
  60.5 8.9 %all-to-all-done.1.blocks = bf16[8,7,16,128]{3,2,1,0:T(8,128)(2,1)S(1)} async-done(((bf16[8,7,16,128]{3,2,1,0:T(8,128)(2,1)}), bf16[8,7,16,128]{3,2,1,0:T(8,128)(2,1)S(1)}, u32[]{:S(2)}, u32[]{:S(2)}) %all-to-all-start.1) | async-done | bytes 229408 | tf_op jit(solution)/shard_map/all_to_all | solution.py:17
  69.5 19.2 %all_to_all.20.blocks = bf16[4,7,16,128]{3,2,1,0:T(8,128)(2,1)S(1)} all-to-all(bf16[4,7,16,128]{3,2,1,0:T(8,128)(2,1)S(1)} %sums.2), channel_id=1, replica_groups={{0,128,256,384},{64,192,320,448},{1,129,257,385},{65,193,321,449},{2,13..., dimensions={0} | all-to-all | bytes 229376 | tf_op jit(solution)/shard_map/all_to_all | solution.py:17
  88.7 4.3 %all-to-all-start.3 = ((bf16[8,8,16,128]{3,2,1,0:T(8,128)(2,1)}), bf16[8,8,16,128]{3,2,1,0:T(8,128)(2,1)S(1)}, u32[]{:S(2)}, u32[]{:S(2)}) async-start(bf16[8,8,16,128]{3,2,1,0:T(8,128)(2,1)} %backward.1), calls=%async_computation.3 | async-start | bytes 524288 | tf_op jit(solution)/shard_map/all_to_all | solution.py:17
  93.1 1.9 %collective-permute-start.8 = (bf16[7,16,128]{2,1,0:T(8,128)(2,1)S(1)}, bf16[7,16,128]{2,1,0:T(8,128)(2,1)S(1)}, u32[]{:S(2)}, u32[]{:S(2)}) collective-permute-start(bf16[7,16,128]{2,1,0:T(8,128)(2,1)S(1)} %bitcast.29), channel_id=1, source_target_pairs={{0,64},{64,0},{128,192},{192,128},{256,320},{320,256},{384,448},{4... | collective-permute-start | bytes 86024 | tf_op jit(solution)/shard_map/ppermute | solution.py:402
  95.0 0.6 copy.21
  95.7 0.5 collective-permute-done.8.other
  96.2 0.8 weights.1
  97.0 2.3 %all-to-all-done.3.parts = bf16[8,8,16,128]{3,2,1,0:T(8,128)(2,1)S(1)} async-done(((bf16[8,8,16,128]{3,2,1,0:T(8,128)(2,1)}), bf16[8,8,16,128]{3,2,1,0:T(8,128)(2,1)S(1)}, u32[]{:S(2)}, u32[]{:S(2)}) %all-to-all-start.3) | async-done | bytes 262176 | tf_op jit(solution)/shard_map/all_to_all | solution.py:17
  99.2 0.7 unpack.1
  (7 shorter events, 0.2 us)
Async XLA Ops:
  0.6 0.8 copy-start
  1.4 3.1 %collective-permute-start = (bf16[4,16,128]{2,1,0:T(8,128)(2,1)S(1)}, bf16[4,16,128]{2,1,0:T(8,128)(2,1)S(1)}, u32[]{:S(2)}, u32[]{:S(2)}) collective-permute-start(bf16[4,16,128]{2,1,0:T(8,128)(2,1)S(1)} %get-tuple-element.29), channel_id=1, source_target_pairs={{0,64},{64,0},{128,192},{192,128},{256,320},{320,256},{384,448},{4... | collective-permute-start | bytes 49160 | tf_op jit(solution)/shard_map/ppermute | solution.py:304
  5.3 9.3 %copy-start.4 = (bf16[16,2,8,128]{3,2,1,0:T(8,128)(2,1)S(1)}, bf16[16,2,8,128]{3,2,1,0:T(8,128)(2,1)}, u32[]{:S(2)}) copy-start(bf16[16,2,8,128]{3,2,1,0:T(8,128)(2,1)} %param.8) | copy-start | bytes 196612
  5.3 17.5 %all-to-all-start = ((bf16[8,3,4,16,128]{4,3,2,1,0:T(8,128)(2,1)}), bf16[8,3,4,16,128]{4,3,2,1,0:T(8,128)(2,1)S(1)}, u32[]{:S(2)}, u32[]{:S(2)}) async-start(bf16[8,3,4,16,128]{4,3,2,1,0:T(8,128)(2,1)} %grid.1), calls=%async_computation | async-start | bytes 786432 | tf_op jit(solution)/shard_map/all_to_all | solution.py:17
  14.6 0.9 copy-start.2
  15.5 0.9 copy-start.3
  22.8 8.6 %copy-start.1 = (f32[16]{0:T(128)S(1)}, f32[16]{0:T(128)}, u32[]{:S(2)}) copy-start(f32[16]{0:T(128)} %bias_ref.1) | copy-start | bytes 196
  22.8 8.6 %collective-permute-start.3 = (bf16[8,4,16,128]{3,2,1,0:T(8,128)(2,1)S(1)}, bf16[8,4,16,128]{3,2,1,0:T(8,128)(2,1)S(1)}, u32[]{:S(2)}, u32[]{:S(2)}) collective-permute-start(bf16[8,4,16,128]{3,2,1,0:T(8,128)(2,1)S(1)} %get-tuple-element.38), channel_id=1, source_target_pairs={{64,128},{128,64},{192,256},{256,192},{320,384},{384,320},{65,129}... | collective-permute-start | bytes 393224 | tf_op jit(solution)/shard_map/ppermute | solution.py:342
  23.5 4.0 %collective-permute-start.1 = (bf16[26,16,128]{2,1,0:T(8,128)(2,1)S(1)}, bf16[26,16,128]{2,1,0:T(8,128)(2,1)S(1)}, u32[]{:S(2)}, u32[]{:S(2)}) collective-permute-start(bf16[26,16,128]{2,1,0:T(8,128)(2,1)S(1)} %get-tuple-element.36), channel_id=1, source_target_pairs={{0,8},{8,16},{16,24},{24,32},{32,40},{40,48},{48,56},{1,9},{9,17},... | collective-permute-start | bytes 319496 | tf_op jit(solution)/shard_map/ppermute | solution.py:22
  24.8 6.6 %collective-permute-start.2 = (bf16[26,16,128]{2,1,0:T(8,128)(2,1)S(1)}, bf16[26,16,128]{2,1,0:T(8,128)(2,1)S(1)}, u32[]{:S(2)}, u32[]{:S(2)}) collective-permute-start(bf16[26,16,128]{2,1,0:T(8,128)(2,1)S(1)} %get-tuple-element.37), channel_id=1, source_target_pairs={{8,0},{16,8},{24,16},{32,24},{40,32},{48,40},{56,48},{9,1},{17,9},... | collective-permute-start | bytes 319496 | tf_op jit(solution)/shard_map/ppermute | solution.py:23
  26.1 1.3 %collective-permute-start.4 = (bf16[8,16,128]{2,1,0:T(8,128)(2,1)S(1)}, bf16[8,16,128]{2,1,0:T(8,128)(2,1)S(1)}, u32[]{:S(2)}, u32[]{:S(2)}) collective-permute-start(bf16[8,16,128]{2,1,0:T(8,128)(2,1)S(1)} %get-tuple-element.39), channel_id=1, source_target_pairs={{64,136},{72,144},{80,152},{88,160},{96,168},{104,176},{112,184},{... | collective-permute-start | bytes 98312 | tf_op jit(solution)/shard_map/ppermute | solution.py:343
  26.8 0.7 collective-permute-start.5
  35.8 12.8 %collective-permute-start.6 = (bf16[17,16,128]{2,1,0:T(8,128)(2,1)S(1)}, bf16[17,16,128]{2,1,0:T(8,128)(2,1)S(1)}, u32[]{:S(2)}, u32[]{:S(2)}) collective-permute-start(bf16[17,16,128]{2,1,0:T(8,128)(2,1)S(1)} %get-tuple-element.43.face), channel_id=1, source_target_pairs={{0,64},{64,0},{128,192},{192,128},{256,320},{320,256},{384,448},{4... | collective-permute-start | bytes 208904 | tf_op jit(solution)/shard_map/ppermute | solution.py:371
  47.7 11.5 %collective-permute-start.7 = (bf16[10,16,128]{2,1,0:T(8,128)(2,1)S(1)}, bf16[10,16,128]{2,1,0:T(8,128)(2,1)S(1)}, u32[]{:S(2)}, u32[]{:S(2)}) collective-permute-start(bf16[10,16,128]{2,1,0:T(8,128)(2,1)S(1)} %get-tuple-element.45.far), channel_id=1, source_target_pairs={{64,128},{128,64},{192,256},{256,192},{320,384},{384,320},{65,129}... | collective-permute-start | bytes 122888 | tf_op jit(solution)/shard_map/ppermute | solution.py:372
  49.3 20.1 %all-to-all-start.1 = ((bf16[8,7,16,128]{3,2,1,0:T(8,128)(2,1)}), bf16[8,7,16,128]{3,2,1,0:T(8,128)(2,1)S(1)}, u32[]{:S(2)}, u32[]{:S(2)}) async-start(bf16[8,7,16,128]{3,2,1,0:T(8,128)(2,1)} %pair.1), calls=%async_computation.1 | async-start | bytes 458752 | tf_op jit(solution)/shard_map/all_to_all | solution.py:17
  88.7 10.5 %all-to-all-start.3 = ((bf16[8,8,16,128]{3,2,1,0:T(8,128)(2,1)}), bf16[8,8,16,128]{3,2,1,0:T(8,128)(2,1)S(1)}, u32[]{:S(2)}, u32[]{:S(2)}) async-start(bf16[8,8,16,128]{3,2,1,0:T(8,128)(2,1)} %backward.1), calls=%async_computation.3 | async-start | bytes 524288 | tf_op jit(solution)/shard_map/all_to_all | solution.py:17
  93.1 3.1 %collective-permute-start.8 = (bf16[7,16,128]{2,1,0:T(8,128)(2,1)S(1)}, bf16[7,16,128]{2,1,0:T(8,128)(2,1)S(1)}, u32[]{:S(2)}, u32[]{:S(2)}) collective-permute-start(bf16[7,16,128]{2,1,0:T(8,128)(2,1)S(1)} %bitcast.29), channel_id=1, source_target_pairs={{0,64},{64,0},{128,192},{192,128},{256,320},{320,256},{384,448},{4... | collective-permute-start | bytes 86024 | tf_op jit(solution)/shard_map/ppermute | solution.py:402

commit v11 on v9

--- a/solution.py
+++ b/solution.py
@@ -31,39 +31,36 @@
     return jnp.concatenate([ahead, value, behind], axis=0)
 
 
-def pack_kernel(at_ref, cells, own, face_ref, far_ref, wide):
-    planes, pairs = own.shape[:2]
+def pack_kernel(cells, out_ref, wide):
+    planes, pairs = out_ref.shape[1:3]
     count, lines = cells.shape[:2]
     for c in range(count):
         wide[c * lines : (c + 1) * lines] = cells[c].astype(F32)
     for d in range(planes):
         for t in range(pairs):
             row = 2 * (d * pairs + t)
-            own[d, t] = jnp.concatenate(
+            tile = jnp.concatenate(
                 [wide[pl.ds(row + e, count, stride=lines), :] for e in range(2)], axis=0
             ).astype(BF16)
-    even = at_ref[0] == 0
-    face_ref[...] = own[jnp.where(even, planes - 1, 0)]
-    far_ref[...] = own[jnp.where(even, 0, planes - 1)]
-
-
-def grid_kernel(at_ref, own, facing, beyond, out_ref):
-    planes = own.shape[0]
-    before = jnp.where(at_ref[0] == 0, 0, planes + 1)
-    for k in range(out_ref.shape[0]):
+            for k in range(out_ref.shape[0]):
+                out_ref[k, d, t] = tile
+
+
+def plane_kernel(even, odd, at_ref, tiles, out_ref):
+    out_ref[...] = tiles[:, jnp.where(at_ref[0] == 0, even, odd)]
+
+
+def rows_kernel(planes, rows, at_ref, tiles, facing, beyond, cot, first_ref, last_ref):
+    core = at_ref[0]
+    sources = tiles.shape[0]
+    before = jnp.where(core == 0, 0, (planes + 1) * sources)
+    after = (planes + 1) * sources - before
+    for ref, t, row in ((first_ref, 0, 0), (last_ref, rows // 2 - 1, rows - 1)):
+        ref[pl.ds(before, sources)] = beyond[:, t]
+        ref[pl.ds(after, sources)] = facing[:, t]
         for d in range(planes):
-            out_ref[k, d + 1] = own[d]
-        out_ref[k, before] = beyond[...]
-        out_ref[k, planes + 1 - before] = facing[...]
-
-
-def rows_kernel(rows, tiles, cot, first_ref, last_ref):
-    sources, count = tiles.shape[:2]
-    for ref, t, row in ((first_ref, 0, 0), (last_ref, rows // 2 - 1, rows - 1)):
-        for p in range(count):
-            ref[p * sources : (p + 1) * sources] = tiles[:, p, t]
-        for d in range(count - 2):
-            ref[count * sources + d] = cot[d * rows + row]
+            ref[(d + 1) * sources : (d + 2) * sources] = tiles[:, d, t]
+            ref[(planes + 2) * sources + d] = cot[d * rows + row]
 
 
 def sum_kernel(blocks, out_ref):
@@ -95,18 +92,24 @@
         out_ref[c] = wide[pl.ds(c, lines, stride=count), :].astype(BF16)
 
 
-def forward_kernel(planes, rows, at_ref, bias_ref, w_ref, cot, tiles, before, after, *refs):
+def forward_kernel(planes, rows, at_ref, bias_ref, w_ref, cot, tiles, facing, beyond, before, after, *refs):
     out_ref, face_ref, far_ref, kept_ref, grads, halves = refs
     cout, width = cot.shape[1:]
     sources = tiles.shape[0]
     edge = sources * (planes + 2)
+    core = at_ref[0]
+    even = core == 0
 
     def tile(s, p, t):
         if t == 0:
             return before[p * sources + s]
         if t == rows // 2 + 1:
             return after[p * sources + s]
-        return tiles[s, p, t - 1]
+        if p == 0:
+            return jnp.where(even, beyond[s, t - 1], facing[s, t - 1])
+        if p == planes + 1:
+            return jnp.where(even, facing[s, t - 1], beyond[s, t - 1])
+        return tiles[s, p - 1, t - 1]
 
     lane = lax.broadcasted_iota(jnp.int32, (cout, width), 1)
     channel = lax.broadcasted_iota(jnp.int32, (cout, width), 0)
@@ -187,7 +190,6 @@
     count = len(blocks) // 2
     for k in range(2 * count):
         halves[k // count, k % count] = placed[k * cout : (k + 1) * cout].astype(BF16)
-    core = at_ref[0]
     face_ref[: rows + 2] = grads[1 - core]
     face_ref[rows + 2 :] = halves[1 - core]
     far_ref[...] = grads[core]
@@ -196,7 +198,7 @@
 
 def backward_kernel(planes, rows, at_ref, w_ref, face, far, face_in, far_in, parts, stack):
     cout, width = far.shape[1:]
-    cin = w_ref.shape[0]
+    cin = w_ref.shape[1]
     count = parts.shape[0]
     part = cin // count
     lane = lax.broadcasted_iota(jnp.int32, (cout, width), 1)
@@ -206,13 +208,18 @@
         p = jnp.where(core == 1, q, planes + 1 - q)
         for r in range(rows + 2):
             stack[p, r * step : (r + 1) * step, :] = shifted(source[r].astype(F32), lane).astype(BF16)
-    w = w_ref[...]
+    w = jnp.transpose(w_ref[...].astype(F32)).astype(BF16)
     for d in range(planes):
         for h in range(0, rows, 2):
             cells = jnp.concatenate(
                 [
                     jnp.concatenate(
-                        [stack[d + a, (h + e) * step : (h + e + 3) * step, :] for a in range(3)], axis=0
+                        [
+                            stack[d + 2 - kd, (h + e + 2 - kh) * step : (h + e + 3 - kh) * step, :]
+                            for kd in range(3)
+                            for kh in range(3)
+                        ],
+                        axis=0,
                     )
                     for e in range(2)
                 ],
@@ -278,28 +285,29 @@
     at = (lax.axis_index("depth") % 2).astype(jnp.int32).reshape(1)
     pairs, double = rows // 2, 2 * cin_dev
 
-    own, face, far = call(
+    grid = call(
         pack_kernel,
         "pack",
-        at,
         activations.reshape(cin_dev, cells, width),
-        out=[(planes, pairs, double, width)] + [(pairs, double, width)] * 2,
+        out=[(filt, planes, pairs, double, width)],
         scratch=[((cin_dev * cells, width), F32)],
-        scalars=1,
-    )
+    )
+    tiles = swapped(grid, "filt")
+    work = 2 * cells * width * taps * cin * cout
+    far, face = (
+        call(
+            functools.partial(plane_kernel, *order),
+            "plane",
+            at,
+            tiles,
+            out=[(filt, pairs, double, width)],
+            flops=cost,
+            scalars=1,
+        )
+        for order, cost in (((0, planes - 1), 0), ((planes - 1, 0), 64 * work))
+    )
+    beyond = lax.ppermute(far, "depth", cross)
     facing = lax.ppermute(face, "depth", swap)
-    beyond = lax.ppermute(far, "depth", cross)
-    grid = call(
-        grid_kernel,
-        "grid",
-        at,
-        own,
-        facing,
-        beyond,
-        out=[(filt, planes + 2, pairs, double, width)],
-        scalars=1,
-    )
-    tiles = swapped(grid, "filt")
 
     cot = cotangent.transpose(1, 2, 0, 3).reshape(cells, cout, width)
     split = weights.reshape(3, 3, 3, cin, cout)
@@ -310,18 +318,21 @@
         preferred_element_type=F32,
     )
     w_forward = w_forward.astype(BF16).reshape(3, 6 * cout, 4 * cin)
-    w_back = split[::-1, ::-1].transpose(3, 0, 1, 2, 4).reshape(cin, taps * cout)
+    w_back = weights.transpose(0, 2, 1).reshape(taps * cout, cin)
     first, last = call(
-        functools.partial(rows_kernel, rows),
+        functools.partial(rows_kernel, planes, rows),
         "rows",
+        at,
         tiles,
+        facing,
+        beyond,
         cot,
         out=[((planes + 2) * filt + planes, cout, width)] * 2,
-    )
-    first, last, w_forward, w_back = lax.optimization_barrier((first, last, w_forward, w_back))
+        scalars=1,
+    )
+    first, last, w_forward = lax.optimization_barrier((first, last, w_forward))
     before, after = neighbours(first, last, "height")
 
-    work = 2 * cells * width * taps * cin * cout
     count = (taps + 1) // 4
     out, face, far, kept_sums = call(
         functools.partial(forward_kernel, planes, rows),
@@ -331,6 +342,8 @@
         w_forward,
         cot,
         tiles,
+        facing,
+        beyond,
         before,
         after,
         out=[(k, cout, width) for k in (cells, rows + 2 + count, rows + 2, count)],

time: 94.4 us -> 93.9 us (level)
  starting transfers between devices: 35.1 us -> 37.4 us
  blocking collectives: 22.1 us -> 20.7 us
    ppermute x1, starting transfers between devices: 4.91 us -> 8.26 us  [per_device(): face_in = lax.ppermute(face, 'depth', swap)]
    all_to_all x1, blocking collectives: 22.1 us -> 20.7 us  [swapped(): lax.all_to_all(blocks, axis, 0, 0, tiled=True, axis_index_groups=groups)]
    all_to_all x3, starting transfers between devices: 22.4 us -> 21.3 us  [swapped(): lax.all_to_all(blocks, axis, 0, 0, tiled=True, axis_index_groups=groups)]
    pallas_call x10 -> x11, Pallas kernels: 8.81 us -> 8.7 us  [call(): pl.pallas_call(body, out_shape=outs, in_specs=[smem] * scalars + [vmem] *...]
where the time goes in v11:
time: 93.9 us; the launch traced here: 93.1 us
  starting transfers between devices  37.4 us (40%)
  waiting for transfers between devices  22.8 us (24%)
  blocking collectives  20.7 us (22%)
  Pallas kernels  8.7 us (9%)
  local copies, waits for them, and re-layouts  2.52 us (3%)
    all_to_all x3, starting transfers between devices, swapped(): lax.all_to_all(blocks, axis, 0, 0, tiled=True, axis_index_groups=groups)  21.3 us
    all_to_all x1, blocking collectives, swapped(): lax.all_to_all(blocks, axis, 0, 0, tiled=True, axis_index_groups=groups)  20.7 us
    all_to_all x3, waiting for transfers between devices, swapped(): lax.all_to_all(blocks, axis, 0, 0, tiled=True, axis_index_groups=groups)  16.1 us
    pallas_call x11, Pallas kernels, call(): pl.pallas_call(body, out_shape=outs, in_specs=[smem] * scalars + [vmem] *...  8.7 us
    ppermute x1, starting transfers between devices, per_device(): face_in = lax.ppermute(face, 'depth', swap)  8.26 us
    ppermute x1, waiting for transfers between devices, neighbours(): after = lax.ppermute(first, axis, [(i + 1, i) for i in range(ends)])  4.38 us
    ppermute x1, starting transfers between devices, per_device(): facing = lax.ppermute(face, 'depth', swap)  2.05 us
    ppermute x1, starting transfers between devices, per_device(): other = lax.ppermute(mine, 'depth', swap)  1.92 us
  transfers between devices with their start and end apart: 10, of which 8 were waited for; matrix products, arithmetic and copies ran while one was open for 1% of the time, Pallas kernels for 3%

profile of v11, /device:TPU:8, one launch (start us, length us, event | category | flops | bytes accessed | tf_op | source)
XLA Modules:
  0.0 93.1 jit_solution(4334392468709071536)
XLA Ops:
  0.6 0.0 copy-start.1
  0.6 0.7 copy-done.1
  1.4 0.7 pack.1
  2.1 0.0 copy-start.4
  2.1 9.3 %all-to-all-start = ((bf16[8,2,4,16,128]{4,3,2,1,0:T(8,128)(2,1)}), bf16[8,2,4,16,128]{4,3,2,1,0:T(8,128)(2,1)S(1)}, u32[]{:S(2)}, u32[]{:S(2)}) async-start(bf16[8,2,4,16,128]{4,3,2,1,0:T(8,128)(2,1)} %pack.1), calls=%async_computation | async-start | bytes 524288 | tf_op jit(solution)/shard_map/all_to_all | solution.py:17
  11.4 0.0 copy-start
  11.4 0.0 copy-done.4
  11.4 0.9 copy-done
  12.3 0.1 copy.20
  12.4 0.1 reshape.49
  12.5 5.0 %all-to-all-done.tiles = bf16[8,2,4,16,128]{4,3,2,1,0:T(8,128)(2,1)S(1)} async-done(((bf16[8,2,4,16,128]{4,3,2,1,0:T(8,128)(2,1)}), bf16[8,2,4,16,128]{4,3,2,1,0:T(8,128)(2,1)S(1)}, u32[]{:S(2)}, u32[]{:S(2)}) %all-to-all-start) | async-done | bytes 262176 | tf_op jit(solution)/shard_map/all_to_all | solution.py:17
  17.6 0.0 copy-start.3
  17.6 2.1 %collective-permute-start = (bf16[8,4,16,128]{3,2,1,0:T(8,128)(2,1)S(1)}, bf16[8,4,16,128]{3,2,1,0:T(8,128)(2,1)S(1)}, u32[]{:S(2)}, u32[]{:S(2)}) collective-permute-start(bf16[8,4,16,128]{3,2,1,0:T(8,128)(2,1)S(1)} %plane.2), channel_id=1, source_target_pairs={{0,64},{64,0},{128,192},{192,128},{256,320},{320,256},{384,448},{4... | collective-permute-start | bytes 393224 | tf_op jit(solution)/shard_map/ppermute | solution.py:310
  19.6 0.7 collective-permute-start.1
  20.3 0.0 copy-done.3
  20.3 0.2 fusion
  20.5 0.4 collective-permute-done.facing
  20.9 0.0 collective-permute-done.1.beyond
  21.0 0.0 copy-start.2
  21.0 1.3 %collective-permute-start.2 = (bf16[34,16,128]{2,1,0:T(8,128)(2,1)S(1)}, bf16[34,16,128]{2,1,0:T(8,128)(2,1)S(1)}, u32[]{:S(2)}, u32[]{:S(2)}) collective-permute-start(bf16[34,16,128]{2,1,0:T(8,128)(2,1)S(1)} %get-tuple-element.22), channel_id=1, source_target_pairs={{0,8},{8,16},{16,24},{24,32},{32,40},{40,48},{48,56},{1,9},{9,17},... | collective-permute-start | bytes 417800 | tf_op jit(solution)/shard_map/ppermute | solution.py:22
  22.3 1.3 %collective-permute-start.3 = (bf16[34,16,128]{2,1,0:T(8,128)(2,1)S(1)}, bf16[34,16,128]{2,1,0:T(8,128)(2,1)S(1)}, u32[]{:S(2)}, u32[]{:S(2)}) collective-permute-start(bf16[34,16,128]{2,1,0:T(8,128)(2,1)S(1)} %get-tuple-element.23), channel_id=1, source_target_pairs={{8,0},{16,8},{24,16},{32,24},{40,32},{48,40},{56,48},{9,1},{17,9},... | collective-permute-start | bytes 417800 | tf_op jit(solution)/shard_map/ppermute | solution.py:23
  23.6 1.3 %collective-permute-done.2.before = bf16[34,16,128]{2,1,0:T(8,128)(2,1)S(1)} collective-permute-done((bf16[34,16,128]{2,1,0:T(8,128)(2,1)S(1)}, bf16[34,16,128]{2,1,0:T(8,128)(2,1)S(1)}, u32[]{:S(2)}, u32[]{:S(2)}) %collective-permute-start.2) | collective-permute-done | bytes 139296 | tf_op jit(solution)/shard_map/ppermute | solution.py:22
  24.9 4.4 %collective-permute-done.3.after = bf16[34,16,128]{2,1,0:T(8,128)(2,1)S(1)} collective-permute-done((bf16[34,16,128]{2,1,0:T(8,128)(2,1)S(1)}, bf16[34,16,128]{2,1,0:T(8,128)(2,1)S(1)}, u32[]{:S(2)}, u32[]{:S(2)}) %collective-permute-start.3) | collective-permute-done | bytes 139296 | tf_op jit(solution)/shard_map/ppermute | solution.py:23
  29.2 0.0 copy-done.2
  29.2 4.4 %forward.1 = (bf16[16,16,128]{2,1,0:T(8,128)(2,1)S(1)}, bf16[17,16,128]{2,1,0:T(8,128)(2,1)S(1)}, bf16[10,16,128]{2,1,0:T(8,128)(2,1)S(1)}, bf16[7,16,128]{2,1,0:T(8,128)(2,1)S(1)}) custom-call(s32[1]{0:T(128)} %bitcast.at_ref, f32[16]{0:T(128)S(1)} %copy-done.2, bf16[3,96,256]{2,1,0:T(8,128)(2,1)S(1)} %bitcast.29, bf16[16,16,128]{2,1,0:T(8,128)(2,1)S(1)} %bitcast.28, ...), custom_call_target="tpu_custom_call" | custom-call | flops 339738624 | bytes 262144 | tf_op jit(solution)/shard_map/forward/pallas_call | solution.py:265
  33.6 8.3 %collective-permute-start.4 = (bf16[17,16,128]{2,1,0:T(8,128)(2,1)S(1)}, bf16[17,16,128]{2,1,0:T(8,128)(2,1)S(1)}, u32[]{:S(2)}, u32[]{:S(2)}) collective-permute-start(bf16[17,16,128]{2,1,0:T(8,128)(2,1)S(1)} %get-tuple-element.26.face), channel_id=1, source_target_pairs={{0,64},{64,0},{128,192},{192,128},{256,320},{320,256},{384,448},{4... | collective-permute-start | bytes 208904 | tf_op jit(solution)/shard_map/ppermute | solution.py:358
  41.9 0.7 collective-permute-start.5
  42.6 0.2 collective-permute-done.4.other.face_in
  42.8 0.7 pair.1
  43.5 8.1 %all-to-all-start.1 = ((bf16[8,7,16,128]{3,2,1,0:T(8,128)(2,1)}), bf16[8,7,16,128]{3,2,1,0:T(8,128)(2,1)S(1)}, u32[]{:S(2)}, u32[]{:S(2)}) async-start(bf16[8,7,16,128]{3,2,1,0:T(8,128)(2,1)} %pair.1), calls=%async_computation.1 | async-start | bytes 458752 | tf_op jit(solution)/shard_map/all_to_all | solution.py:17
  51.6 0.0 collective-permute-done.5.far_in
  51.6 1.3 %backward.1 = bf16[8,8,16,128]{3,2,1,0:T(8,128)(2,1)} custom-call(s32[1]{0:T(128)} %bitcast.at_ref, bf16[432,64]{1,0:T(8,128)(2,1)S(1)} %bitcast.33, bf16[17,16,128]{2,1,0:T(8,128)(2,1)S(1)} %get-tuple-element.26.face, bf16[10,16,128]{2,1,0:T(8,128)(2,1)S(1)} %get-tuple-element.27.far, bf16[17,16,128]{2,1,0:T(8,128)(2,1)S(1)} %collective-permute-done.4.other.face_in, ...), custom_call_target="tpu_custom_call" | custom-call | flops 7247757312 | bytes 262144 | tf_op jit(solution)/shard_map/backward/pallas_call | solution.py:265
  52.9 8.8 %all-to-all-done.1.blocks = bf16[8,7,16,128]{3,2,1,0:T(8,128)(2,1)S(1)} async-done(((bf16[8,7,16,128]{3,2,1,0:T(8,128)(2,1)}), bf16[8,7,16,128]{3,2,1,0:T(8,128)(2,1)S(1)}, u32[]{:S(2)}, u32[]{:S(2)}) %all-to-all-start.1) | async-done | bytes 229408 | tf_op jit(solution)/shard_map/all_to_all | solution.py:17
  61.8 20.7 %all_to_all.20.blocks = bf16[4,7,16,128]{3,2,1,0:T(8,128)(2,1)S(1)} all-to-all(bf16[4,7,16,128]{3,2,1,0:T(8,128)(2,1)S(1)} %sums.2), channel_id=1, replica_groups={{0,128,256,384},{64,192,320,448},{1,129,257,385},{65,193,321,449},{2,13..., dimensions={0} | all-to-all | bytes 229376 | tf_op jit(solution)/shard_map/all_to_all | solution.py:17
  82.5 3.9 %all-to-all-start.3 = ((bf16[8,8,16,128]{3,2,1,0:T(8,128)(2,1)}), bf16[8,8,16,128]{3,2,1,0:T(8,128)(2,1)S(1)}, u32[]{:S(2)}, u32[]{:S(2)}) async-start(bf16[8,8,16,128]{3,2,1,0:T(8,128)(2,1)} %backward.1), calls=%async_computation.3 | async-start | bytes 524288 | tf_op jit(solution)/shard_map/all_to_all | solution.py:17
  86.4 1.9 %collective-permute-start.6 = (bf16[7,16,128]{2,1,0:T(8,128)(2,1)S(1)}, bf16[7,16,128]{2,1,0:T(8,128)(2,1)S(1)}, u32[]{:S(2)}, u32[]{:S(2)}) collective-permute-start(bf16[7,16,128]{2,1,0:T(8,128)(2,1)S(1)} %bitcast.30), channel_id=1, source_target_pairs={{0,64},{64,0},{128,192},{192,128},{256,320},{320,256},{384,448},{4... | collective-permute-start | bytes 86024 | tf_op jit(solution)/shard_map/ppermute | solution.py:389
  88.3 0.6 copy.21
  88.9 0.5 collective-permute-done.6.other
  89.5 0.8 weights.1
  90.2 2.2 %all-to-all-done.3.parts = bf16[8,8,16,128]{3,2,1,0:T(8,128)(2,1)S(1)} async-done(((bf16[8,8,16,128]{3,2,1,0:T(8,128)(2,1)}), bf16[8,8,16,128]{3,2,1,0:T(8,128)(2,1)S(1)}, u32[]{:S(2)}, u32[]{:S(2)}) %all-to-all-start.3) | async-done | bytes 262176 | tf_op jit(solution)/shard_map/all_to_all | solution.py:17
  92.5 0.7 unpack.1
  (7 shorter events, 0.1 us)
Async XLA Ops:
  0.6 0.8 copy-start.1
  2.1 9.3 %copy-start.4 = (bf16[16,2,8,128]{3,2,1,0:T(8,128)(2,1)S(1)}, bf16[16,2,8,128]{3,2,1,0:T(8,128)(2,1)}, u32[]{:S(2)}) copy-start(bf16[16,2,8,128]{3,2,1,0:T(8,128)(2,1)} %param.8) | copy-start | bytes 196612
  2.1 15.4 %all-to-all-start = ((bf16[8,2,4,16,128]{4,3,2,1,0:T(8,128)(2,1)}), bf16[8,2,4,16,128]{4,3,2,1,0:T(8,128)(2,1)S(1)}, u32[]{:S(2)}, u32[]{:S(2)}) async-start(bf16[8,2,4,16,128]{4,3,2,1,0:T(8,128)(2,1)} %pack.1), calls=%async_computation | async-start | bytes 524288 | tf_op jit(solution)/shard_map/all_to_all | solution.py:17
  11.4 0.9 copy-start
  17.6 2.8 %copy-start.3 = (bf16[2,192,256,1]{2,1,3,0:T(8,128)(2,1)S(1)}, bf16[2,192,256,1]{2,1,3,0:T(8,128)(2,1)}, u32[]{:S(2)}) copy-start(bf16[2,192,256,1]{2,1,3,0:T(8,128)(2,1)} %constant.24) | copy-start | bytes 589828
  17.6 3.4 %collective-permute-start = (bf16[8,4,16,128]{3,2,1,0:T(8,128)(2,1)S(1)}, bf16[8,4,16,128]{3,2,1,0:T(8,128)(2,1)S(1)}, u32[]{:S(2)}, u32[]{:S(2)}) collective-permute-start(bf16[8,4,16,128]{3,2,1,0:T(8,128)(2,1)S(1)} %plane.2), channel_id=1, source_target_pairs={{0,64},{64,0},{128,192},{192,128},{256,320},{320,256},{384,448},{4... | collective-permute-start | bytes 393224 | tf_op jit(solution)/shard_map/ppermute | solution.py:310
  19.6 1.3 %collective-permute-start.1 = (bf16[8,4,16,128]{3,2,1,0:T(8,128)(2,1)S(1)}, bf16[8,4,16,128]{3,2,1,0:T(8,128)(2,1)S(1)}, u32[]{:S(2)}, u32[]{:S(2)}) collective-permute-start(bf16[8,4,16,128]{3,2,1,0:T(8,128)(2,1)S(1)} %plane.3), channel_id=1, source_target_pairs={{64,128},{128,64},{192,256},{256,192},{320,384},{384,320},{65,129}... | collective-permute-start | bytes 393224 | tf_op jit(solution)/shard_map/ppermute | solution.py:309
  21.0 8.3 %copy-start.2 = (f32[16]{0:T(128)S(1)}, f32[16]{0:T(128)}, u32[]{:S(2)}) copy-start(f32[16]{0:T(128)} %bias_ref.1) | copy-start | bytes 196
  21.0 3.9 %collective-permute-start.2 = (bf16[34,16,128]{2,1,0:T(8,128)(2,1)S(1)}, bf16[34,16,128]{2,1,0:T(8,128)(2,1)S(1)}, u32[]{:S(2)}, u32[]{:S(2)}) collective-permute-start(bf16[34,16,128]{2,1,0:T(8,128)(2,1)S(1)} %get-tuple-element.22), channel_id=1, source_target_pairs={{0,8},{8,16},{16,24},{24,32},{32,40},{40,48},{48,56},{1,9},{9,17},... | collective-permute-start | bytes 417800 | tf_op jit(solution)/shard_map/ppermute | solution.py:22
  22.3 6.9 %collective-permute-start.3 = (bf16[34,16,128]{2,1,0:T(8,128)(2,1)S(1)}, bf16[34,16,128]{2,1,0:T(8,128)(2,1)S(1)}, u32[]{:S(2)}, u32[]{:S(2)}) collective-permute-start(bf16[34,16,128]{2,1,0:T(8,128)(2,1)S(1)} %get-tuple-element.23), channel_id=1, source_target_pairs={{8,0},{16,8},{24,16},{32,24},{40,32},{48,40},{56,48},{9,1},{17,9},... | collective-permute-start | bytes 417800 | tf_op jit(solution)/shard_map/ppermute | solution.py:23
  33.6 9.2 %collective-permute-start.4 = (bf16[17,16,128]{2,1,0:T(8,128)(2,1)S(1)}, bf16[17,16,128]{2,1,0:T(8,128)(2,1)S(1)}, u32[]{:S(2)}, u32[]{:S(2)}) collective-permute-start(bf16[17,16,128]{2,1,0:T(8,128)(2,1)S(1)} %get-tuple-element.26.face), channel_id=1, source_target_pairs={{0,64},{64,0},{128,192},{192,128},{256,320},{320,256},{384,448},{4... | collective-permute-start | bytes 208904 | tf_op jit(solution)/shard_map/ppermute | solution.py:358
  41.9 9.7 %collective-permute-start.5 = (bf16[10,16,128]{2,1,0:T(8,128)(2,1)S(1)}, bf16[10,16,128]{2,1,0:T(8,128)(2,1)S(1)}, u32[]{:S(2)}, u32[]{:S(2)}) collective-permute-start(bf16[10,16,128]{2,1,0:T(8,128)(2,1)S(1)} %get-tuple-element.27.far), channel_id=1, source_target_pairs={{64,128},{128,64},{192,256},{256,192},{320,384},{384,320},{65,129}... | collective-permute-start | bytes 122888 | tf_op jit(solution)/shard_map/ppermute | solution.py:359
  43.5 18.2 %all-to-all-start.1 = ((bf16[8,7,16,128]{3,2,1,0:T(8,128)(2,1)}), bf16[8,7,16,128]{3,2,1,0:T(8,128)(2,1)S(1)}, u32[]{:S(2)}, u32[]{:S(2)}) async-start(bf16[8,7,16,128]{3,2,1,0:T(8,128)(2,1)} %pair.1), calls=%async_computation.1 | async-start | bytes 458752 | tf_op jit(solution)/shard_map/all_to_all | solution.py:17
  82.5 10.0 %all-to-all-start.3 = ((bf16[8,8,16,128]{3,2,1,0:T(8,128)(2,1)}), bf16[8,8,16,128]{3,2,1,0:T(8,128)(2,1)S(1)}, u32[]{:S(2)}, u32[]{:S(2)}) async-start(bf16[8,8,16,128]{3,2,1,0:T(8,128)(2,1)} %backward.1), calls=%async_computation.3 | async-start | bytes 524288 | tf_op jit(solution)/shard_map/all_to_all | solution.py:17
  86.4 3.1 %collective-permute-start.6 = (bf16[7,16,128]{2,1,0:T(8,128)(2,1)S(1)}, bf16[7,16,128]{2,1,0:T(8,128)(2,1)S(1)}, u32[]{:S(2)}, u32[]{:S(2)}) collective-permute-start(bf16[7,16,128]{2,1,0:T(8,128)(2,1)S(1)} %bitcast.30), channel_id=1, source_target_pairs={{0,64},{64,0},{128,192},{192,128},{256,320},{320,256},{384,448},{4... | collective-permute-start | bytes 86024 | tf_op jit(solution)/shard_map/ppermute | solution.py:389

commit v12 on v11

--- a/solution.py
+++ b/solution.py
@@ -116,7 +116,7 @@
     bias = jnp.zeros((cout, width), F32)
     for o in range(cout):
         bias = jnp.where(channel == o, bias_ref[o], bias)
-    sums = [None] * 3
+    lefts, rights = [], []
     bias_sum = jnp.zeros((cout, width), F32)
     for d in range(planes):
         for pair in range(rows // 2 + 1):
@@ -157,12 +157,18 @@
                 grad = grad.astype(F32)
                 bias_sum = bias_sum + grad
                 stacks.append(shifted(grad, lane).astype(BF16))
-            both = jnp.concatenate(stacks, axis=0)
-            for kd in range(3):
-                term = lax.dot_general(
-                    both, cells[kd], (((1,), (1,)), ((), ())), preferred_element_type=F32
-                )
-                sums[kd] = term if sums[kd] is None else sums[kd] + term
+            lefts.append(jnp.concatenate(stacks, axis=0))
+            rights.append(cells)
+    left = jnp.concatenate(lefts, axis=1)
+    sums = [
+        lax.dot_general(
+            left,
+            jnp.concatenate([cells[kd] for cells in rights], axis=1),
+            (((1,), (1,)), ((), ())),
+            preferred_element_type=F32,
+        )
+        for kd in range(3)
+    ]
 
     first = (lane // PART) % 2 == 0
     blocks, last = [], []

time: 93.9 us -> 91.6 us (0.976)
  Pallas kernels: 8.7 us -> 6.42 us
    pallas_call x11, Pallas kernels: 8.7 us -> 6.42 us  [call(): pl.pallas_call(body, out_shape=outs, in_specs=[smem] * scalars + [vmem] *...]
where the time goes in v12:
time: 91.6 us; the launch traced here: 90.9 us
  starting transfers between devices  37.4 us (41%)
  waiting for transfers between devices  22.8 us (25%)
  blocking collectives  20.7 us (23%)
  Pallas kernels  6.42 us (7%)
  local copies, waits for them, and re-layouts  2.52 us (3%)
    all_to_all x3, starting transfers between devices, swapped(): lax.all_to_all(blocks, axis, 0, 0, tiled=True, axis_index_groups=groups)  21.3 us
    all_to_all x1, blocking collectives, swapped(): lax.all_to_all(blocks, axis, 0, 0, tiled=True, axis_index_groups=groups)  20.7 us
    all_to_all x3, waiting for transfers between devices, swapped(): lax.all_to_all(blocks, axis, 0, 0, tiled=True, axis_index_groups=groups)  16.1 us
    ppermute x1, starting transfers between devices, per_device(): face_in = lax.ppermute(face, 'depth', swap)  8.26 us
    pallas_call x11, Pallas kernels, call(): pl.pallas_call(body, out_shape=outs, in_specs=[smem] * scalars + [vmem] *...  6.42 us
    ppermute x1, waiting for transfers between devices, neighbours(): after = lax.ppermute(first, axis, [(i + 1, i) for i in range(ends)])  4.38 us
    ppermute x1, starting transfers between devices, per_device(): facing = lax.ppermute(face, 'depth', swap)  2.05 us
    ppermute x1, starting transfers between devices, per_device(): other = lax.ppermute(mine, 'depth', swap)  1.92 us
  transfers between devices with their start and end apart: 10, of which 8 were waited for; matrix products, arithmetic and copies ran while one was open for 1% of the time, Pallas kernels for 3%

profile of v12, /device:TPU:8, one launch (start us, length us, event | category | flops | bytes accessed | tf_op | source)
XLA Modules:
  0.0 90.9 jit_solution(8229525746943484887)
XLA Ops:
  0.6 0.0 copy-start.1
  0.6 0.7 copy-done.1
  1.4 0.7 pack.1
  2.1 0.0 copy-start.4
  2.1 9.3 %all-to-all-start = ((bf16[8,2,4,16,128]{4,3,2,1,0:T(8,128)(2,1)}), bf16[8,2,4,16,128]{4,3,2,1,0:T(8,128)(2,1)S(1)}, u32[]{:S(2)}, u32[]{:S(2)}) async-start(bf16[8,2,4,16,128]{4,3,2,1,0:T(8,128)(2,1)} %pack.1), calls=%async_computation | async-start | bytes 524288 | tf_op jit(solution)/shard_map/all_to_all | solution.py:17
  11.4 0.0 copy-start
  11.4 0.0 copy-done.4
  11.4 0.9 copy-done
  12.3 0.1 copy.20
  12.4 0.1 reshape.49
  12.5 5.0 %all-to-all-done.tiles = bf16[8,2,4,16,128]{4,3,2,1,0:T(8,128)(2,1)S(1)} async-done(((bf16[8,2,4,16,128]{4,3,2,1,0:T(8,128)(2,1)}), bf16[8,2,4,16,128]{4,3,2,1,0:T(8,128)(2,1)S(1)}, u32[]{:S(2)}, u32[]{:S(2)}) %all-to-all-start) | async-done | bytes 262176 | tf_op jit(solution)/shard_map/all_to_all | solution.py:17
  17.6 0.0 copy-start.3
  17.6 2.1 %collective-permute-start = (bf16[8,4,16,128]{3,2,1,0:T(8,128)(2,1)S(1)}, bf16[8,4,16,128]{3,2,1,0:T(8,128)(2,1)S(1)}, u32[]{:S(2)}, u32[]{:S(2)}) collective-permute-start(bf16[8,4,16,128]{3,2,1,0:T(8,128)(2,1)S(1)} %plane.2), channel_id=1, source_target_pairs={{0,64},{64,0},{128,192},{192,128},{256,320},{320,256},{384,448},{4... | collective-permute-start | bytes 393224 | tf_op jit(solution)/shard_map/ppermute | solution.py:316
  19.6 0.7 collective-permute-start.1
  20.3 0.0 copy-done.3
  20.3 0.2 fusion
  20.5 0.4 collective-permute-done.facing
  20.9 0.0 collective-permute-done.1.beyond
  21.0 0.0 copy-start.2
  21.0 1.3 %collective-permute-start.2 = (bf16[34,16,128]{2,1,0:T(8,128)(2,1)S(1)}, bf16[34,16,128]{2,1,0:T(8,128)(2,1)S(1)}, u32[]{:S(2)}, u32[]{:S(2)}) collective-permute-start(bf16[34,16,128]{2,1,0:T(8,128)(2,1)S(1)} %get-tuple-element.22), channel_id=1, source_target_pairs={{0,8},{8,16},{16,24},{24,32},{32,40},{40,48},{48,56},{1,9},{9,17},... | collective-permute-start | bytes 417800 | tf_op jit(solution)/shard_map/ppermute | solution.py:22
  22.3 1.3 %collective-permute-start.3 = (bf16[34,16,128]{2,1,0:T(8,128)(2,1)S(1)}, bf16[34,16,128]{2,1,0:T(8,128)(2,1)S(1)}, u32[]{:S(2)}, u32[]{:S(2)}) collective-permute-start(bf16[34,16,128]{2,1,0:T(8,128)(2,1)S(1)} %get-tuple-element.23), channel_id=1, source_target_pairs={{8,0},{16,8},{24,16},{32,24},{40,32},{48,40},{56,48},{9,1},{17,9},... | collective-permute-start | bytes 417800 | tf_op jit(solution)/shard_map/ppermute | solution.py:23
  23.6 1.3 %collective-permute-done.2.before = bf16[34,16,128]{2,1,0:T(8,128)(2,1)S(1)} collective-permute-done((bf16[34,16,128]{2,1,0:T(8,128)(2,1)S(1)}, bf16[34,16,128]{2,1,0:T(8,128)(2,1)S(1)}, u32[]{:S(2)}, u32[]{:S(2)}) %collective-permute-start.2) | collective-permute-done | bytes 139296 | tf_op jit(solution)/shard_map/ppermute | solution.py:22
  24.9 4.4 %collective-permute-done.3.after = bf16[34,16,128]{2,1,0:T(8,128)(2,1)S(1)} collective-permute-done((bf16[34,16,128]{2,1,0:T(8,128)(2,1)S(1)}, bf16[34,16,128]{2,1,0:T(8,128)(2,1)S(1)}, u32[]{:S(2)}, u32[]{:S(2)}) %collective-permute-start.3) | collective-permute-done | bytes 139296 | tf_op jit(solution)/shard_map/ppermute | solution.py:23
  29.2 0.0 copy-done.2
  29.2 2.1 %forward.1 = (bf16[16,16,128]{2,1,0:T(8,128)(2,1)S(1)}, bf16[17,16,128]{2,1,0:T(8,128)(2,1)S(1)}, bf16[10,16,128]{2,1,0:T(8,128)(2,1)S(1)}, bf16[7,16,128]{2,1,0:T(8,128)(2,1)S(1)}) custom-call(s32[1]{0:T(128)} %bitcast.at_ref, f32[16]{0:T(128)S(1)} %copy-done.2, bf16[3,96,256]{2,1,0:T(8,128)(2,1)S(1)} %bitcast.29, bf16[16,16,128]{2,1,0:T(8,128)(2,1)S(1)} %bitcast.28, ...), custom_call_target="tpu_custom_call" | custom-call | flops 339738624 | bytes 262144 | tf_op jit(solution)/shard_map/forward/pallas_call | solution.py:271
  31.3 8.3 %collective-permute-start.4 = (bf16[17,16,128]{2,1,0:T(8,128)(2,1)S(1)}, bf16[17,16,128]{2,1,0:T(8,128)(2,1)S(1)}, u32[]{:S(2)}, u32[]{:S(2)}) collective-permute-start(bf16[17,16,128]{2,1,0:T(8,128)(2,1)S(1)} %get-tuple-element.26.face), channel_id=1, source_target_pairs={{0,64},{64,0},{128,192},{192,128},{256,320},{320,256},{384,448},{4... | collective-permute-start | bytes 208904 | tf_op jit(solution)/shard_map/ppermute | solution.py:364
  39.6 0.7 collective-permute-start.5
  40.3 0.2 collective-permute-done.4.other.face_in
  40.5 0.7 pair.1
  41.2 8.1 %all-to-all-start.1 = ((bf16[8,7,16,128]{3,2,1,0:T(8,128)(2,1)}), bf16[8,7,16,128]{3,2,1,0:T(8,128)(2,1)S(1)}, u32[]{:S(2)}, u32[]{:S(2)}) async-start(bf16[8,7,16,128]{3,2,1,0:T(8,128)(2,1)} %pair.1), calls=%async_computation.1 | async-start | bytes 458752 | tf_op jit(solution)/shard_map/all_to_all | solution.py:17
  49.3 0.0 collective-permute-done.5.far_in
  49.3 1.3 %backward.1 = bf16[8,8,16,128]{3,2,1,0:T(8,128)(2,1)} custom-call(s32[1]{0:T(128)} %bitcast.at_ref, bf16[432,64]{1,0:T(8,128)(2,1)S(1)} %bitcast.33, bf16[17,16,128]{2,1,0:T(8,128)(2,1)S(1)} %get-tuple-element.26.face, bf16[10,16,128]{2,1,0:T(8,128)(2,1)S(1)} %get-tuple-element.27.far, bf16[17,16,128]{2,1,0:T(8,128)(2,1)S(1)} %collective-permute-done.4.other.face_in, ...), custom_call_target="tpu_custom_call" | custom-call | flops 7247757312 | bytes 262144 | tf_op jit(solution)/shard_map/backward/pallas_call | solution.py:271
  50.7 8.8 %all-to-all-done.1.blocks = bf16[8,7,16,128]{3,2,1,0:T(8,128)(2,1)S(1)} async-done(((bf16[8,7,16,128]{3,2,1,0:T(8,128)(2,1)}), bf16[8,7,16,128]{3,2,1,0:T(8,128)(2,1)S(1)}, u32[]{:S(2)}, u32[]{:S(2)}) %all-to-all-start.1) | async-done | bytes 229408 | tf_op jit(solution)/shard_map/all_to_all | solution.py:17
  59.5 20.7 %all_to_all.20.blocks = bf16[4,7,16,128]{3,2,1,0:T(8,128)(2,1)S(1)} all-to-all(bf16[4,7,16,128]{3,2,1,0:T(8,128)(2,1)S(1)} %sums.2), channel_id=1, replica_groups={{0,128,256,384},{64,192,320,448},{1,129,257,385},{65,193,321,449},{2,13..., dimensions={0} | all-to-all | bytes 229376 | tf_op jit(solution)/shard_map/all_to_all | solution.py:17
  80.2 3.9 %all-to-all-start.3 = ((bf16[8,8,16,128]{3,2,1,0:T(8,128)(2,1)}), bf16[8,8,16,128]{3,2,1,0:T(8,128)(2,1)S(1)}, u32[]{:S(2)}, u32[]{:S(2)}) async-start(bf16[8,8,16,128]{3,2,1,0:T(8,128)(2,1)} %backward.1), calls=%async_computation.3 | async-start | bytes 524288 | tf_op jit(solution)/shard_map/all_to_all | solution.py:17
  84.1 1.9 %collective-permute-start.6 = (bf16[7,16,128]{2,1,0:T(8,128)(2,1)S(1)}, bf16[7,16,128]{2,1,0:T(8,128)(2,1)S(1)}, u32[]{:S(2)}, u32[]{:S(2)}) collective-permute-start(bf16[7,16,128]{2,1,0:T(8,128)(2,1)S(1)} %bitcast.30), channel_id=1, source_target_pairs={{0,64},{64,0},{128,192},{192,128},{256,320},{320,256},{384,448},{4... | collective-permute-start | bytes 86024 | tf_op jit(solution)/shard_map/ppermute | solution.py:395
  86.0 0.6 copy.21
  86.7 0.5 collective-permute-done.6.other
  87.2 0.8 weights.1
  88.0 2.2 %all-to-all-done.3.parts = bf16[8,8,16,128]{3,2,1,0:T(8,128)(2,1)S(1)} async-done(((bf16[8,8,16,128]{3,2,1,0:T(8,128)(2,1)}), bf16[8,8,16,128]{3,2,1,0:T(8,128)(2,1)S(1)}, u32[]{:S(2)}, u32[]{:S(2)}) %all-to-all-start.3) | async-done | bytes 262176 | tf_op jit(solution)/shard_map/all_to_all | solution.py:17
  90.2 0.7 unpack.1
  (7 shorter events, 0.1 us)
Async XLA Ops:
  0.6 0.8 copy-start.1
  2.1 9.3 %copy-start.4 = (bf16[16,2,8,128]{3,2,1,0:T(8,128)(2,1)S(1)}, bf16[16,2,8,128]{3,2,1,0:T(8,128)(2,1)}, u32[]{:S(2)}) copy-start(bf16[16,2,8,128]{3,2,1,0:T(8,128)(2,1)} %param.8) | copy-start | bytes 196612
  2.1 15.4 %all-to-all-start = ((bf16[8,2,4,16,128]{4,3,2,1,0:T(8,128)(2,1)}), bf16[8,2,4,16,128]{4,3,2,1,0:T(8,128)(2,1)S(1)}, u32[]{:S(2)}, u32[]{:S(2)}) async-start(bf16[8,2,4,16,128]{4,3,2,1,0:T(8,128)(2,1)} %pack.1), calls=%async_computation | async-start | bytes 524288 | tf_op jit(solution)/shard_map/all_to_all | solution.py:17
  11.4 0.9 copy-start
  17.6 2.8 %copy-start.3 = (bf16[2,192,256,1]{2,1,3,0:T(8,128)(2,1)S(1)}, bf16[2,192,256,1]{2,1,3,0:T(8,128)(2,1)}, u32[]{:S(2)}) copy-start(bf16[2,192,256,1]{2,1,3,0:T(8,128)(2,1)} %constant.24) | copy-start | bytes 589828
  17.6 3.4 %collective-permute-start = (bf16[8,4,16,128]{3,2,1,0:T(8,128)(2,1)S(1)}, bf16[8,4,16,128]{3,2,1,0:T(8,128)(2,1)S(1)}, u32[]{:S(2)}, u32[]{:S(2)}) collective-permute-start(bf16[8,4,16,128]{3,2,1,0:T(8,128)(2,1)S(1)} %plane.2), channel_id=1, source_target_pairs={{0,64},{64,0},{128,192},{192,128},{256,320},{320,256},{384,448},{4... | collective-permute-start | bytes 393224 | tf_op jit(solution)/shard_map/ppermute | solution.py:316
  19.6 1.3 %collective-permute-start.1 = (bf16[8,4,16,128]{3,2,1,0:T(8,128)(2,1)S(1)}, bf16[8,4,16,128]{3,2,1,0:T(8,128)(2,1)S(1)}, u32[]{:S(2)}, u32[]{:S(2)}) collective-permute-start(bf16[8,4,16,128]{3,2,1,0:T(8,128)(2,1)S(1)} %plane.3), channel_id=1, source_target_pairs={{64,128},{128,64},{192,256},{256,192},{320,384},{384,320},{65,129}... | collective-permute-start | bytes 393224 | tf_op jit(solution)/shard_map/ppermute | solution.py:315
  21.0 8.3 %copy-start.2 = (f32[16]{0:T(128)S(1)}, f32[16]{0:T(128)}, u32[]{:S(2)}) copy-start(f32[16]{0:T(128)} %bias_ref.1) | copy-start | bytes 196
  21.0 3.9 %collective-permute-start.2 = (bf16[34,16,128]{2,1,0:T(8,128)(2,1)S(1)}, bf16[34,16,128]{2,1,0:T(8,128)(2,1)S(1)}, u32[]{:S(2)}, u32[]{:S(2)}) collective-permute-start(bf16[34,16,128]{2,1,0:T(8,128)(2,1)S(1)} %get-tuple-element.22), channel_id=1, source_target_pairs={{0,8},{8,16},{16,24},{24,32},{32,40},{40,48},{48,56},{1,9},{9,17},... | collective-permute-start | bytes 417800 | tf_op jit(solution)/shard_map/ppermute | solution.py:22
  22.3 6.9 %collective-permute-start.3 = (bf16[34,16,128]{2,1,0:T(8,128)(2,1)S(1)}, bf16[34,16,128]{2,1,0:T(8,128)(2,1)S(1)}, u32[]{:S(2)}, u32[]{:S(2)}) collective-permute-start(bf16[34,16,128]{2,1,0:T(8,128)(2,1)S(1)} %get-tuple-element.23), channel_id=1, source_target_pairs={{8,0},{16,8},{24,16},{32,24},{40,32},{48,40},{56,48},{9,1},{17,9},... | collective-permute-start | bytes 417800 | tf_op jit(solution)/shard_map/ppermute | solution.py:23
  31.3 9.2 %collective-permute-start.4 = (bf16[17,16,128]{2,1,0:T(8,128)(2,1)S(1)}, bf16[17,16,128]{2,1,0:T(8,128)(2,1)S(1)}, u32[]{:S(2)}, u32[]{:S(2)}) collective-permute-start(bf16[17,16,128]{2,1,0:T(8,128)(2,1)S(1)} %get-tuple-element.26.face), channel_id=1, source_target_pairs={{0,64},{64,0},{128,192},{192,128},{256,320},{320,256},{384,448},{4... | collective-permute-start | bytes 208904 | tf_op jit(solution)/shard_map/ppermute | solution.py:364
  39.6 9.7 %collective-permute-start.5 = (bf16[10,16,128]{2,1,0:T(8,128)(2,1)S(1)}, bf16[10,16,128]{2,1,0:T(8,128)(2,1)S(1)}, u32[]{:S(2)}, u32[]{:S(2)}) collective-permute-start(bf16[10,16,128]{2,1,0:T(8,128)(2,1)S(1)} %get-tuple-element.27.far), channel_id=1, source_target_pairs={{64,128},{128,64},{192,256},{256,192},{320,384},{384,320},{65,129}... | collective-permute-start | bytes 122888 | tf_op jit(solution)/shard_map/ppermute | solution.py:365
  41.2 18.2 %all-to-all-start.1 = ((bf16[8,7,16,128]{3,2,1,0:T(8,128)(2,1)}), bf16[8,7,16,128]{3,2,1,0:T(8,128)(2,1)S(1)}, u32[]{:S(2)}, u32[]{:S(2)}) async-start(bf16[8,7,16,128]{3,2,1,0:T(8,128)(2,1)} %pair.1), calls=%async_computation.1 | async-start | bytes 458752 | tf_op jit(solution)/shard_map/all_to_all | solution.py:17
  80.2 10.0 %all-to-all-start.3 = ((bf16[8,8,16,128]{3,2,1,0:T(8,128)(2,1)}), bf16[8,8,16,128]{3,2,1,0:T(8,128)(2,1)S(1)}, u32[]{:S(2)}, u32[]{:S(2)}) async-start(bf16[8,8,16,128]{3,2,1,0:T(8,128)(2,1)} %backward.1), calls=%async_computation.3 | async-start | bytes 524288 | tf_op jit(solution)/shard_map/all_to_all | solution.py:17
  84.1 3.1 %collective-permute-start.6 = (bf16[7,16,128]{2,1,0:T(8,128)(2,1)S(1)}, bf16[7,16,128]{2,1,0:T(8,128)(2,1)S(1)}, u32[]{:S(2)}, u32[]{:S(2)}) collective-permute-start(bf16[7,16,128]{2,1,0:T(8,128)(2,1)S(1)} %bitcast.30), channel_id=1, source_target_pairs={{0,64},{64,0},{128,192},{192,128},{256,320},{320,256},{384,448},{4... | collective-permute-start | bytes 86024 | tf_op jit(solution)/shard_map/ppermute | solution.py:395

commit v13 on v9

--- a/solution.py
+++ b/solution.py
@@ -31,7 +31,7 @@
     return jnp.concatenate([ahead, value, behind], axis=0)
 
 
-def pack_kernel(at_ref, cells, own, face_ref, far_ref, wide):
+def pack_kernel(at_ref, cells, own, far_ref, wide):
     planes, pairs = own.shape[:2]
     count, lines = cells.shape[:2]
     for c in range(count):
@@ -42,9 +42,11 @@
             own[d, t] = jnp.concatenate(
                 [wide[pl.ds(row + e, count, stride=lines), :] for e in range(2)], axis=0
             ).astype(BF16)
-    even = at_ref[0] == 0
-    face_ref[...] = own[jnp.where(even, planes - 1, 0)]
-    far_ref[...] = own[jnp.where(even, 0, planes - 1)]
+    far_ref[...] = own[jnp.where(at_ref[0] == 0, 0, planes - 1)]
+
+
+def face_kernel(at_ref, own, face_ref):
+    face_ref[...] = own[jnp.where(at_ref[0] == 0, own.shape[0] - 1, 0)]
 
 
 def grid_kernel(at_ref, own, facing, beyond, out_ref):
@@ -100,6 +102,7 @@
     cout, width = cot.shape[1:]
     sources = tiles.shape[0]
     edge = sources * (planes + 2)
+    core = at_ref[0]
 
     def tile(s, p, t):
         if t == 0:
@@ -113,7 +116,7 @@
     bias = jnp.zeros((cout, width), F32)
     for o in range(cout):
         bias = jnp.where(channel == o, bias_ref[o], bias)
-    sums = [None] * 3
+    lefts, rights = [], []
     bias_sum = jnp.zeros((cout, width), F32)
     for d in range(planes):
         for pair in range(rows // 2 + 1):
@@ -154,12 +157,18 @@
                 grad = grad.astype(F32)
                 bias_sum = bias_sum + grad
                 stacks.append(shifted(grad, lane).astype(BF16))
-            both = jnp.concatenate(stacks, axis=0)
-            for kd in range(3):
-                term = lax.dot_general(
-                    both, cells[kd], (((1,), (1,)), ((), ())), preferred_element_type=F32
-                )
-                sums[kd] = term if sums[kd] is None else sums[kd] + term
+            lefts.append(jnp.concatenate(stacks, axis=0))
+            rights.append(cells)
+    left = jnp.concatenate(lefts, axis=1)
+    sums = [
+        lax.dot_general(
+            left,
+            jnp.concatenate([cells[kd] for cells in rights], axis=1),
+            (((1,), (1,)), ((), ())),
+            preferred_element_type=F32,
+        )
+        for kd in range(3)
+    ]
 
     first = (lane // PART) % 2 == 0
     blocks, last = [], []
@@ -187,7 +196,6 @@
     count = len(blocks) // 2
     for k in range(2 * count):
         halves[k // count, k % count] = placed[k * cout : (k + 1) * cout].astype(BF16)
-    core = at_ref[0]
     face_ref[: rows + 2] = grads[1 - core]
     face_ref[rows + 2 :] = halves[1 - core]
     far_ref[...] = grads[core]
@@ -196,7 +204,7 @@
 
 def backward_kernel(planes, rows, at_ref, w_ref, face, far, face_in, far_in, parts, stack):
     cout, width = far.shape[1:]
-    cin = w_ref.shape[0]
+    cin = w_ref.shape[1]
     count = parts.shape[0]
     part = cin // count
     lane = lax.broadcasted_iota(jnp.int32, (cout, width), 1)
@@ -206,13 +214,18 @@
         p = jnp.where(core == 1, q, planes + 1 - q)
         for r in range(rows + 2):
             stack[p, r * step : (r + 1) * step, :] = shifted(source[r].astype(F32), lane).astype(BF16)
-    w = w_ref[...]
+    w = jnp.transpose(w_ref[...].astype(F32)).astype(BF16)
     for d in range(planes):
         for h in range(0, rows, 2):
             cells = jnp.concatenate(
                 [
                     jnp.concatenate(
-                        [stack[d + a, (h + e) * step : (h + e + 3) * step, :] for a in range(3)], axis=0
+                        [
+                            stack[d + 2 - kd, (h + e + 2 - kh) * step : (h + e + 3 - kh) * step, :]
+                            for kd in range(3)
+                            for kh in range(3)
+                        ],
+                        axis=0,
                     )
                     for e in range(2)
                 ],
@@ -278,17 +291,19 @@
     at = (lax.axis_index("depth") % 2).astype(jnp.int32).reshape(1)
     pairs, double = rows // 2, 2 * cin_dev
 
-    own, face, far = call(
+    work = 2 * cells * width * taps * cin * cout
+    own, far = call(
         pack_kernel,
         "pack",
         at,
         activations.reshape(cin_dev, cells, width),
-        out=[(planes, pairs, double, width)] + [(pairs, double, width)] * 2,
+        out=[(planes, pairs, double, width), (pairs, double, width)],
         scratch=[((cin_dev * cells, width), F32)],
         scalars=1,
     )
+    beyond = lax.ppermute(far, "depth", cross)
+    face = call(face_kernel, "face", at, own, out=[far.shape], flops=64 * work, scalars=1)
     facing = lax.ppermute(face, "depth", swap)
-    beyond = lax.ppermute(far, "depth", cross)
     grid = call(
         grid_kernel,
         "grid",
@@ -310,7 +325,7 @@
         preferred_element_type=F32,
     )
     w_forward = w_forward.astype(BF16).reshape(3, 6 * cout, 4 * cin)
-    w_back = split[::-1, ::-1].transpose(3, 0, 1, 2, 4).reshape(cin, taps * cout)
+    w_back = weights.transpose(0, 2, 1).reshape(taps * cout, cin)
     first, last = call(
         functools.partial(rows_kernel, rows),
         "rows",
@@ -318,10 +333,9 @@
         cot,
         out=[((planes + 2) * filt + planes, cout, width)] * 2,
     )
-    first, last, w_forward, w_back = lax.optimization_barrier((first, last, w_forward, w_back))
+    first, last, w_forward = lax.optimization_barrier((first, last, w_forward))
     before, after = neighbours(first, last, "height")
 
-    work = 2 * cells * width * taps * cin * cout
     count = (taps + 1) // 4
     out, face, far, kept_sums = call(
         functools.partial(forward_kernel, planes, rows),

time: 94.4 us -> 92.1 us (0.976)
  Pallas kernels: 8.81 us -> 6.56 us
    pallas_call x10 -> x11, Pallas kernels: 8.81 us -> 6.56 us  [call(): pl.pallas_call(body, out_shape=outs, in_specs=[smem] * scalars + [vmem] *...]
where the time goes in v13:
time: 92.1 us; the launch traced here: 91.3 us
  starting transfers between devices  35.1 us (38%)
  waiting for transfers between devices  23.4 us (25%)
  blocking collectives  22 us (24%)
  Pallas kernels  6.56 us (7%)
  local copies, waits for them, and re-layouts  3.22 us (3%)
    all_to_all x3, starting transfers between devices, swapped(): lax.all_to_all(blocks, axis, 0, 0, tiled=True, axis_index_groups=groups)  22.5 us
    all_to_all x1, blocking collectives, swapped(): lax.all_to_all(blocks, axis, 0, 0, tiled=True, axis_index_groups=groups)  22 us
    all_to_all x3, waiting for transfers between devices, swapped(): lax.all_to_all(blocks, axis, 0, 0, tiled=True, axis_index_groups=groups)  16.6 us
    pallas_call x11, Pallas kernels, call(): pl.pallas_call(body, out_shape=outs, in_specs=[smem] * scalars + [vmem] *...  6.56 us
    ppermute x1, starting transfers between devices, per_device(): face_in = lax.ppermute(face, 'depth', swap)  4.91 us
    ppermute x1, waiting for transfers between devices, neighbours(): after = lax.ppermute(first, axis, [(i + 1, i) for i in range(ends)])  4.38 us
    unnamed x10, local copies, waits for them, and re-layouts  2.34 us
    ppermute x1, starting transfers between devices, per_device(): other = lax.ppermute(mine, 'depth', swap)  1.92 us
  transfers between devices with their start and end apart: 10, of which 8 were waited for; matrix products, arithmetic and copies ran while one was open for 1% of the time, Pallas kernels for 3%

profile of v13, /device:TPU:8, one launch (start us, length us, event | category | flops | bytes accessed | tf_op | source)
XLA Modules:
  0.0 91.3 jit_solution(2817995695529608894)
XLA Ops:
  0.6 0.0 copy-start.1
  0.7 0.7 copy-done.1
  1.4 1.9 %collective-permute-start = (bf16[4,16,128]{2,1,0:T(8,128)(2,1)S(1)}, bf16[4,16,128]{2,1,0:T(8,128)(2,1)S(1)}, u32[]{:S(2)}, u32[]{:S(2)}) collective-permute-start(bf16[4,16,128]{2,1,0:T(8,128)(2,1)S(1)} %face.1), channel_id=1, source_target_pairs={{0,64},{64,0},{128,192},{192,128},{256,320},{320,256},{384,448},{4... | collective-permute-start | bytes 49160 | tf_op jit(solution)/shard_map/ppermute | solution.py:306
  3.4 0.7 collective-permute-start.1
  4.0 0.5 collective-permute-done.facing
  4.5 0.0 collective-permute-done.1.beyond
  4.5 0.9 grid.1
  5.4 0.0 copy-start.4
  5.4 9.3 %all-to-all-start = ((bf16[8,4,4,16,128]{4,3,2,1,0:T(8,128)(2,1)}), bf16[8,4,4,16,128]{4,3,2,1,0:T(8,128)(2,1)S(1)}, u32[]{:S(2)}, u32[]{:S(2)}) async-start(bf16[8,4,4,16,128]{4,3,2,1,0:T(8,128)(2,1)} %grid.1), calls=%async_computation | async-start | bytes 1048576 | tf_op jit(solution)/shard_map/all_to_all | solution.py:17
  14.8 0.0 copy-start
  14.8 0.0 copy-done.4
  14.8 0.9 copy-done
  15.7 0.0 copy-start.3
  15.7 0.1 copy.20
  15.7 0.1 reshape.49
  15.9 0.7 copy-done.3
  16.6 0.2 fusion
  16.8 5.5 %all-to-all-done.tiles = bf16[8,4,4,16,128]{4,3,2,1,0:T(8,128)(2,1)S(1)} async-done(((bf16[8,4,4,16,128]{4,3,2,1,0:T(8,128)(2,1)}), bf16[8,4,4,16,128]{4,3,2,1,0:T(8,128)(2,1)S(1)}, u32[]{:S(2)}, u32[]{:S(2)}) %all-to-all-start) | async-done | bytes 524320 | tf_op jit(solution)/shard_map/all_to_all | solution.py:17
  22.3 0.0 copy-start.2
  22.3 1.3 %collective-permute-start.2 = (bf16[34,16,128]{2,1,0:T(8,128)(2,1)S(1)}, bf16[34,16,128]{2,1,0:T(8,128)(2,1)S(1)}, u32[]{:S(2)}, u32[]{:S(2)}) collective-permute-start(bf16[34,16,128]{2,1,0:T(8,128)(2,1)S(1)} %get-tuple-element.26), channel_id=1, source_target_pairs={{0,8},{8,16},{16,24},{24,32},{32,40},{40,48},{48,56},{1,9},{9,17},... | collective-permute-start | bytes 417800 | tf_op jit(solution)/shard_map/ppermute | solution.py:22
  23.6 1.3 %collective-permute-start.3 = (bf16[34,16,128]{2,1,0:T(8,128)(2,1)S(1)}, bf16[34,16,128]{2,1,0:T(8,128)(2,1)S(1)}, u32[]{:S(2)}, u32[]{:S(2)}) collective-permute-start(bf16[34,16,128]{2,1,0:T(8,128)(2,1)S(1)} %get-tuple-element.27), channel_id=1, source_target_pairs={{8,0},{16,8},{24,16},{32,24},{40,32},{48,40},{56,48},{9,1},{17,9},... | collective-permute-start | bytes 417800 | tf_op jit(solution)/shard_map/ppermute | solution.py:23
  24.9 1.3 %collective-permute-done.2.before = bf16[34,16,128]{2,1,0:T(8,128)(2,1)S(1)} collective-permute-done((bf16[34,16,128]{2,1,0:T(8,128)(2,1)S(1)}, bf16[34,16,128]{2,1,0:T(8,128)(2,1)S(1)}, u32[]{:S(2)}, u32[]{:S(2)}) %collective-permute-start.2) | collective-permute-done | bytes 139296 | tf_op jit(solution)/shard_map/ppermute | solution.py:22
  26.2 4.4 %collective-permute-done.3.after = bf16[34,16,128]{2,1,0:T(8,128)(2,1)S(1)} collective-permute-done((bf16[34,16,128]{2,1,0:T(8,128)(2,1)S(1)}, bf16[34,16,128]{2,1,0:T(8,128)(2,1)S(1)}, u32[]{:S(2)}, u32[]{:S(2)}) %collective-permute-start.3) | collective-permute-done | bytes 139296 | tf_op jit(solution)/shard_map/ppermute | solution.py:23
  30.6 0.0 copy-done.2
  30.6 2.1 %forward.1 = (bf16[16,16,128]{2,1,0:T(8,128)(2,1)S(1)}, bf16[17,16,128]{2,1,0:T(8,128)(2,1)S(1)}, bf16[10,16,128]{2,1,0:T(8,128)(2,1)S(1)}, bf16[7,16,128]{2,1,0:T(8,128)(2,1)S(1)}) custom-call(s32[1]{0:T(128)} %bitcast.at_ref, f32[16]{0:T(128)S(1)} %copy-done.2, bf16[3,96,256]{2,1,0:T(8,128)(2,1)S(1)} %bitcast.29, bf16[16,16,128]{2,1,0:T(8,128)(2,1)S(1)} %bitcast.28, ...), custom_call_target="tpu_custom_call" | custom-call | flops 339738624 | bytes 262144 | tf_op jit(solution)/shard_map/forward/pallas_call | solution.py:271
  32.7 4.9 %collective-permute-start.4 = (bf16[17,16,128]{2,1,0:T(8,128)(2,1)S(1)}, bf16[17,16,128]{2,1,0:T(8,128)(2,1)S(1)}, u32[]{:S(2)}, u32[]{:S(2)}) collective-permute-start(bf16[17,16,128]{2,1,0:T(8,128)(2,1)S(1)} %get-tuple-element.30.face), channel_id=1, source_target_pairs={{0,64},{64,0},{128,192},{192,128},{256,320},{320,256},{384,448},{4... | collective-permute-start | bytes 208904 | tf_op jit(solution)/shard_map/ppermute | solution.py:359
  37.6 0.7 collective-permute-start.5
  38.3 0.2 collective-permute-done.4.other.face_in
  38.5 0.7 pair.1
  39.2 8.6 %all-to-all-start.1 = ((bf16[8,7,16,128]{3,2,1,0:T(8,128)(2,1)}), bf16[8,7,16,128]{3,2,1,0:T(8,128)(2,1)S(1)}, u32[]{:S(2)}, u32[]{:S(2)}) async-start(bf16[8,7,16,128]{3,2,1,0:T(8,128)(2,1)} %pair.1), calls=%async_computation.1 | async-start | bytes 458752 | tf_op jit(solution)/shard_map/all_to_all | solution.py:17
  47.8 0.0 collective-permute-done.5.far_in
  47.8 1.3 %backward.1 = bf16[8,8,16,128]{3,2,1,0:T(8,128)(2,1)} custom-call(s32[1]{0:T(128)} %bitcast.at_ref, bf16[432,64]{1,0:T(8,128)(2,1)S(1)} %bitcast.33, bf16[17,16,128]{2,1,0:T(8,128)(2,1)S(1)} %get-tuple-element.30.face, bf16[10,16,128]{2,1,0:T(8,128)(2,1)S(1)} %get-tuple-element.31.far, bf16[17,16,128]{2,1,0:T(8,128)(2,1)S(1)} %collective-permute-done.4.other.face_in, ...), custom_call_target="tpu_custom_call" | custom-call | flops 7247757312 | bytes 262144 | tf_op jit(solution)/shard_map/backward/pallas_call | solution.py:271
  49.2 8.8 %all-to-all-done.1.blocks = bf16[8,7,16,128]{3,2,1,0:T(8,128)(2,1)S(1)} async-done(((bf16[8,7,16,128]{3,2,1,0:T(8,128)(2,1)}), bf16[8,7,16,128]{3,2,1,0:T(8,128)(2,1)S(1)}, u32[]{:S(2)}, u32[]{:S(2)}) %all-to-all-start.1) | async-done | bytes 229408 | tf_op jit(solution)/shard_map/all_to_all | solution.py:17
  58.0 22.0 %all_to_all.20.blocks = bf16[4,7,16,128]{3,2,1,0:T(8,128)(2,1)S(1)} all-to-all(bf16[4,7,16,128]{3,2,1,0:T(8,128)(2,1)S(1)} %sums.2), channel_id=1, replica_groups={{0,128,256,384},{64,192,320,448},{1,129,257,385},{65,193,321,449},{2,13..., dimensions={0} | all-to-all | bytes 229376 | tf_op jit(solution)/shard_map/all_to_all | solution.py:17
  80.0 4.5 %all-to-all-start.3 = ((bf16[8,8,16,128]{3,2,1,0:T(8,128)(2,1)}), bf16[8,8,16,128]{3,2,1,0:T(8,128)(2,1)S(1)}, u32[]{:S(2)}, u32[]{:S(2)}) async-start(bf16[8,8,16,128]{3,2,1,0:T(8,128)(2,1)} %backward.1), calls=%async_computation.3 | async-start | bytes 524288 | tf_op jit(solution)/shard_map/all_to_all | solution.py:17
  84.5 1.9 %collective-permute-start.6 = (bf16[7,16,128]{2,1,0:T(8,128)(2,1)S(1)}, bf16[7,16,128]{2,1,0:T(8,128)(2,1)S(1)}, u32[]{:S(2)}, u32[]{:S(2)}) collective-permute-start(bf16[7,16,128]{2,1,0:T(8,128)(2,1)S(1)} %bitcast.30), channel_id=1, source_target_pairs={{0,64},{64,0},{128,192},{192,128},{256,320},{320,256},{384,448},{4... | collective-permute-start | bytes 86024 | tf_op jit(solution)/shard_map/ppermute | solution.py:390
  86.5 0.6 copy.21
  87.1 0.5 collective-permute-done.6.other
  87.6 0.8 weights.1
  88.4 2.3 %all-to-all-done.3.parts = bf16[8,8,16,128]{3,2,1,0:T(8,128)(2,1)S(1)} async-done(((bf16[8,8,16,128]{3,2,1,0:T(8,128)(2,1)}), bf16[8,8,16,128]{3,2,1,0:T(8,128)(2,1)S(1)}, u32[]{:S(2)}, u32[]{:S(2)}) %all-to-all-start.3) | async-done | bytes 262176 | tf_op jit(solution)/shard_map/all_to_all | solution.py:17
  90.7 0.7 unpack.1
  (7 shorter events, 0.1 us)
Async XLA Ops:
  0.6 0.8 copy-start.1
  1.4 3.1 %collective-permute-start = (bf16[4,16,128]{2,1,0:T(8,128)(2,1)S(1)}, bf16[4,16,128]{2,1,0:T(8,128)(2,1)S(1)}, u32[]{:S(2)}, u32[]{:S(2)}) collective-permute-start(bf16[4,16,128]{2,1,0:T(8,128)(2,1)S(1)} %face.1), channel_id=1, source_target_pairs={{0,64},{64,0},{128,192},{192,128},{256,320},{320,256},{384,448},{4... | collective-permute-start | bytes 49160 | tf_op jit(solution)/shard_map/ppermute | solution.py:306
  3.4 1.2 %collective-permute-start.1 = (bf16[4,16,128]{2,1,0:T(8,128)(2,1)S(1)}, bf16[4,16,128]{2,1,0:T(8,128)(2,1)S(1)}, u32[]{:S(2)}, u32[]{:S(2)}) collective-permute-start(bf16[4,16,128]{2,1,0:T(8,128)(2,1)S(1)} %get-tuple-element.22), channel_id=1, source_target_pairs={{64,128},{128,64},{192,256},{256,192},{320,384},{384,320},{65,129}... | collective-permute-start | bytes 49160 | tf_op jit(solution)/shard_map/ppermute | solution.py:304
  5.4 9.4 %copy-start.4 = (bf16[16,2,8,128]{3,2,1,0:T(8,128)(2,1)S(1)}, bf16[16,2,8,128]{3,2,1,0:T(8,128)(2,1)}, u32[]{:S(2)}) copy-start(bf16[16,2,8,128]{3,2,1,0:T(8,128)(2,1)} %param.8) | copy-start | bytes 196612
  5.4 16.9 %all-to-all-start = ((bf16[8,4,4,16,128]{4,3,2,1,0:T(8,128)(2,1)}), bf16[8,4,4,16,128]{4,3,2,1,0:T(8,128)(2,1)S(1)}, u32[]{:S(2)}, u32[]{:S(2)}) async-start(bf16[8,4,4,16,128]{4,3,2,1,0:T(8,128)(2,1)} %grid.1), calls=%async_computation | async-start | bytes 1048576 | tf_op jit(solution)/shard_map/all_to_all | solution.py:17
  14.8 0.9 copy-start
  15.7 0.9 %copy-start.3 = (bf16[2,192,256,1]{2,1,3,0:T(8,128)(2,1)S(1)}, bf16[2,192,256,1]{2,1,3,0:T(8,128)(2,1)}, u32[]{:S(2)}) copy-start(bf16[2,192,256,1]{2,1,3,0:T(8,128)(2,1)} %constant.24) | copy-start | bytes 589828
  22.3 8.3 %copy-start.2 = (f32[16]{0:T(128)S(1)}, f32[16]{0:T(128)}, u32[]{:S(2)}) copy-start(f32[16]{0:T(128)} %bias_ref.1) | copy-start | bytes 196
  22.3 3.9 %collective-permute-start.2 = (bf16[34,16,128]{2,1,0:T(8,128)(2,1)S(1)}, bf16[34,16,128]{2,1,0:T(8,128)(2,1)S(1)}, u32[]{:S(2)}, u32[]{:S(2)}) collective-permute-start(bf16[34,16,128]{2,1,0:T(8,128)(2,1)S(1)} %get-tuple-element.26), channel_id=1, source_target_pairs={{0,8},{8,16},{16,24},{24,32},{32,40},{40,48},{48,56},{1,9},{9,17},... | collective-permute-start | bytes 417800 | tf_op jit(solution)/shard_map/ppermute | solution.py:22
  23.6 6.9 %collective-permute-start.3 = (bf16[34,16,128]{2,1,0:T(8,128)(2,1)S(1)}, bf16[34,16,128]{2,1,0:T(8,128)(2,1)S(1)}, u32[]{:S(2)}, u32[]{:S(2)}) collective-permute-start(bf16[34,16,128]{2,1,0:T(8,128)(2,1)S(1)} %get-tuple-element.27), channel_id=1, source_target_pairs={{8,0},{16,8},{24,16},{32,24},{40,32},{48,40},{56,48},{9,1},{17,9},... | collective-permute-start | bytes 417800 | tf_op jit(solution)/shard_map/ppermute | solution.py:23
  32.7 5.8 %collective-permute-start.4 = (bf16[17,16,128]{2,1,0:T(8,128)(2,1)S(1)}, bf16[17,16,128]{2,1,0:T(8,128)(2,1)S(1)}, u32[]{:S(2)}, u32[]{:S(2)}) collective-permute-start(bf16[17,16,128]{2,1,0:T(8,128)(2,1)S(1)} %get-tuple-element.30.face), channel_id=1, source_target_pairs={{0,64},{64,0},{128,192},{192,128},{256,320},{320,256},{384,448},{4... | collective-permute-start | bytes 208904 | tf_op jit(solution)/shard_map/ppermute | solution.py:359
  37.6 10.2 %collective-permute-start.5 = (bf16[10,16,128]{2,1,0:T(8,128)(2,1)S(1)}, bf16[10,16,128]{2,1,0:T(8,128)(2,1)S(1)}, u32[]{:S(2)}, u32[]{:S(2)}) collective-permute-start(bf16[10,16,128]{2,1,0:T(8,128)(2,1)S(1)} %get-tuple-element.31.far), channel_id=1, source_target_pairs={{64,128},{128,64},{192,256},{256,192},{320,384},{384,320},{65,129}... | collective-permute-start | bytes 122888 | tf_op jit(solution)/shard_map/ppermute | solution.py:360
  39.2 18.8 %all-to-all-start.1 = ((bf16[8,7,16,128]{3,2,1,0:T(8,128)(2,1)}), bf16[8,7,16,128]{3,2,1,0:T(8,128)(2,1)S(1)}, u32[]{:S(2)}, u32[]{:S(2)}) async-start(bf16[8,7,16,128]{3,2,1,0:T(8,128)(2,1)} %pair.1), calls=%async_computation.1 | async-start | bytes 458752 | tf_op jit(solution)/shard_map/all_to_all | solution.py:17
  80.0 10.6 %all-to-all-start.3 = ((bf16[8,8,16,128]{3,2,1,0:T(8,128)(2,1)}), bf16[8,8,16,128]{3,2,1,0:T(8,128)(2,1)S(1)}, u32[]{:S(2)}, u32[]{:S(2)}) async-start(bf16[8,8,16,128]{3,2,1,0:T(8,128)(2,1)} %backward.1), calls=%async_computation.3 | async-start | bytes 524288 | tf_op jit(solution)/shard_map/all_to_all | solution.py:17
  84.5 3.1 %collective-permute-start.6 = (bf16[7,16,128]{2,1,0:T(8,128)(2,1)S(1)}, bf16[7,16,128]{2,1,0:T(8,128)(2,1)S(1)}, u32[]{:S(2)}, u32[]{:S(2)}) collective-permute-start(bf16[7,16,128]{2,1,0:T(8,128)(2,1)S(1)} %bitcast.30), channel_id=1, source_target_pairs={{0,64},{64,0},{128,192},{192,128},{256,320},{320,256},{384,448},{4... | collective-permute-start | bytes 86024 | tf_op jit(solution)/shard_map/ppermute | solution.py:390

commit v14 on v13

--- a/solution.py
+++ b/solution.py
@@ -31,7 +31,7 @@
     return jnp.concatenate([ahead, value, behind], axis=0)
 
 
-def pack_kernel(at_ref, cells, own, far_ref, wide):
+def pack_kernel(at_ref, cells, own, face_ref, wide):
     planes, pairs = own.shape[:2]
     count, lines = cells.shape[:2]
     for c in range(count):
@@ -42,11 +42,11 @@
             own[d, t] = jnp.concatenate(
                 [wide[pl.ds(row + e, count, stride=lines), :] for e in range(2)], axis=0
             ).astype(BF16)
-    far_ref[...] = own[jnp.where(at_ref[0] == 0, 0, planes - 1)]
-
-
-def face_kernel(at_ref, own, face_ref):
-    face_ref[...] = own[jnp.where(at_ref[0] == 0, own.shape[0] - 1, 0)]
+    face_ref[...] = own[jnp.where(at_ref[0] == 0, planes - 1, 0)]
+
+
+def far_kernel(at_ref, own, far_ref):
+    far_ref[...] = own[jnp.where(at_ref[0] == 0, 0, own.shape[0] - 1)]
 
 
 def grid_kernel(at_ref, own, facing, beyond, out_ref):
@@ -292,7 +292,7 @@
     pairs, double = rows // 2, 2 * cin_dev
 
     work = 2 * cells * width * taps * cin * cout
-    own, far = call(
+    own, face = call(
         pack_kernel,
         "pack",
         at,
@@ -301,9 +301,9 @@
         scratch=[((cin_dev * cells, width), F32)],
         scalars=1,
     )
+    facing = lax.ppermute(face, "depth", swap)
+    far = call(far_kernel, "far", at, own, out=[face.shape], flops=64 * work, scalars=1)
     beyond = lax.ppermute(far, "depth", cross)
-    face = call(face_kernel, "face", at, own, out=[far.shape], flops=64 * work, scalars=1)
-    facing = lax.ppermute(face, "depth", swap)
     grid = call(
         grid_kernel,
         "grid",

time: 92.1 us -> 90.8 us (0.986)
  blocking collectives: 22 us -> 16.5 us
  waiting for transfers between devices: 23.4 us -> 26.4 us
  starting transfers between devices: 35.1 us -> 36.3 us
    all_to_all x1, blocking collectives: 22 us -> 16.5 us  [swapped(): lax.all_to_all(blocks, axis, 0, 0, tiled=True, axis_index_groups=groups)]
    ppermute x1, starting transfers between devices: 1.92 us -> 5.86 us  [per_device(): facing = lax.ppermute(face, 'depth', swap)]
    ppermute x1, starting transfers between devices: 4.91 us -> 1.92 us  [per_device(): face_in = lax.ppermute(face, 'depth', swap)]
    ppermute x1, starting transfers between devices: 1.3 us -> 4.28 us  [neighbours(): before = lax.ppermute(last, axis, [(i, i + 1) for i in range(ends)])]
    all_to_all x3, starting transfers between devices: 22.5 us -> 19.7 us  [swapped(): lax.all_to_all(blocks, axis, 0, 0, tiled=True, axis_index_groups=groups)]
    all_to_all x3, waiting for transfers between devices: 16.6 us -> 18.5 us  [swapped(): lax.all_to_all(blocks, axis, 0, 0, tiled=True, axis_index_groups=groups)]
where the time goes in v14:
time: 90.8 us; the launch traced here: 90 us
  starting transfers between devices  36.3 us (40%)
  waiting for transfers between devices  26.4 us (29%)
  blocking collectives  16.5 us (18%)
  Pallas kernels  6.56 us (7%)
  local copies, waits for them, and re-layouts  3.22 us (4%)
    all_to_all x3, starting transfers between devices, swapped(): lax.all_to_all(blocks, axis, 0, 0, tiled=True, axis_index_groups=groups)  19.7 us
    all_to_all x3, waiting for transfers between devices, swapped(): lax.all_to_all(blocks, axis, 0, 0, tiled=True, axis_index_groups=groups)  18.5 us
    all_to_all x1, blocking collectives, swapped(): lax.all_to_all(blocks, axis, 0, 0, tiled=True, axis_index_groups=groups)  16.5 us
    pallas_call x11, Pallas kernels, call(): pl.pallas_call(body, out_shape=outs, in_specs=[smem] * scalars + [vmem] *...  6.56 us
    ppermute x1, starting transfers between devices, per_device(): facing = lax.ppermute(face, 'depth', swap)  5.86 us
    ppermute x1, waiting for transfers between devices, neighbours(): after = lax.ppermute(first, axis, [(i + 1, i) for i in range(ends)])  4.73 us
    ppermute x1, starting transfers between devices, neighbours(): before = lax.ppermute(last, axis, [(i, i + 1) for i in range(ends)])  4.28 us
    unnamed x10, local copies, waits for them, and re-layouts  2.34 us
  transfers between devices with their start and end apart: 10, of which 8 were waited for; matrix products, arithmetic and copies ran while one was open for 1% of the time, Pallas kernels for 3%

profile of v14, /device:TPU:8, one launch (start us, length us, event | category | flops | bytes accessed | tf_op | source)
XLA Modules:
  0.0 90.0 jit_solution(13435885168694562076)
XLA Ops:
  0.6 0.0 copy-start.1
  0.7 0.7 copy-done.1
  1.4 0.7 collective-permute-start.1
  2.1 5.9 %collective-permute-start = (bf16[4,16,128]{2,1,0:T(8,128)(2,1)S(1)}, bf16[4,16,128]{2,1,0:T(8,128)(2,1)S(1)}, u32[]{:S(2)}, u32[]{:S(2)}) collective-permute-start(bf16[4,16,128]{2,1,0:T(8,128)(2,1)S(1)} %get-tuple-element.22), channel_id=1, source_target_pairs={{0,64},{64,0},{128,192},{192,128},{256,320},{320,256},{384,448},{4... | collective-permute-start | bytes 49160 | tf_op jit(solution)/shard_map/ppermute | solution.py:304
  8.0 0.0 collective-permute-done.1.beyond
  8.0 0.8 collective-permute-done.facing
  8.8 0.9 grid.1
  9.7 0.0 copy-start.4
  9.7 5.9 %all-to-all-start = ((bf16[8,4,4,16,128]{4,3,2,1,0:T(8,128)(2,1)}), bf16[8,4,4,16,128]{4,3,2,1,0:T(8,128)(2,1)S(1)}, u32[]{:S(2)}, u32[]{:S(2)}) async-start(bf16[8,4,4,16,128]{4,3,2,1,0:T(8,128)(2,1)} %grid.1), calls=%async_computation | async-start | bytes 1048576 | tf_op jit(solution)/shard_map/all_to_all | solution.py:17
  15.6 0.0 copy-start
  15.6 0.0 copy-done.4
  15.6 0.9 copy-done
  16.5 0.0 copy-start.3
  16.5 0.1 copy.20
  16.5 0.1 reshape.49
  16.7 0.7 copy-done.3
  17.4 0.2 fusion
  17.6 7.4 %all-to-all-done.tiles = bf16[8,4,4,16,128]{4,3,2,1,0:T(8,128)(2,1)S(1)} async-done(((bf16[8,4,4,16,128]{4,3,2,1,0:T(8,128)(2,1)}), bf16[8,4,4,16,128]{4,3,2,1,0:T(8,128)(2,1)S(1)}, u32[]{:S(2)}, u32[]{:S(2)}) %all-to-all-start) | async-done | bytes 524320 | tf_op jit(solution)/shard_map/all_to_all | solution.py:17
  25.0 0.0 copy-start.2
  25.0 4.3 %collective-permute-start.2 = (bf16[34,16,128]{2,1,0:T(8,128)(2,1)S(1)}, bf16[34,16,128]{2,1,0:T(8,128)(2,1)S(1)}, u32[]{:S(2)}, u32[]{:S(2)}) collective-permute-start(bf16[34,16,128]{2,1,0:T(8,128)(2,1)S(1)} %get-tuple-element.26), channel_id=1, source_target_pairs={{0,8},{8,16},{16,24},{24,32},{32,40},{40,48},{48,56},{1,9},{9,17},... | collective-permute-start | bytes 417800 | tf_op jit(solution)/shard_map/ppermute | solution.py:22
  29.3 1.3 %collective-permute-start.3 = (bf16[34,16,128]{2,1,0:T(8,128)(2,1)S(1)}, bf16[34,16,128]{2,1,0:T(8,128)(2,1)S(1)}, u32[]{:S(2)}, u32[]{:S(2)}) collective-permute-start(bf16[34,16,128]{2,1,0:T(8,128)(2,1)S(1)} %get-tuple-element.27), channel_id=1, source_target_pairs={{8,0},{16,8},{24,16},{32,24},{40,32},{48,40},{56,48},{9,1},{17,9},... | collective-permute-start | bytes 417800 | tf_op jit(solution)/shard_map/ppermute | solution.py:23
  30.6 1.3 %collective-permute-done.2.before = bf16[34,16,128]{2,1,0:T(8,128)(2,1)S(1)} collective-permute-done((bf16[34,16,128]{2,1,0:T(8,128)(2,1)S(1)}, bf16[34,16,128]{2,1,0:T(8,128)(2,1)S(1)}, u32[]{:S(2)}, u32[]{:S(2)}) %collective-permute-start.2) | collective-permute-done | bytes 139296 | tf_op jit(solution)/shard_map/ppermute | solution.py:22
  31.9 4.7 %collective-permute-done.3.after = bf16[34,16,128]{2,1,0:T(8,128)(2,1)S(1)} collective-permute-done((bf16[34,16,128]{2,1,0:T(8,128)(2,1)S(1)}, bf16[34,16,128]{2,1,0:T(8,128)(2,1)S(1)}, u32[]{:S(2)}, u32[]{:S(2)}) %collective-permute-start.3) | collective-permute-done | bytes 139296 | tf_op jit(solution)/shard_map/ppermute | solution.py:23
  36.6 0.0 copy-done.2
  36.6 2.1 %forward.1 = (bf16[16,16,128]{2,1,0:T(8,128)(2,1)S(1)}, bf16[17,16,128]{2,1,0:T(8,128)(2,1)S(1)}, bf16[10,16,128]{2,1,0:T(8,128)(2,1)S(1)}, bf16[7,16,128]{2,1,0:T(8,128)(2,1)S(1)}) custom-call(s32[1]{0:T(128)} %bitcast.at_ref, f32[16]{0:T(128)S(1)} %copy-done.2, bf16[3,96,256]{2,1,0:T(8,128)(2,1)S(1)} %bitcast.29, bf16[16,16,128]{2,1,0:T(8,128)(2,1)S(1)} %bitcast.28, ...), custom_call_target="tpu_custom_call" | custom-call | flops 339738624 | bytes 262144 | tf_op jit(solution)/shard_map/forward/pallas_call | solution.py:271
  38.7 1.9 %collective-permute-start.4 = (bf16[17,16,128]{2,1,0:T(8,128)(2,1)S(1)}, bf16[17,16,128]{2,1,0:T(8,128)(2,1)S(1)}, u32[]{:S(2)}, u32[]{:S(2)}) collective-permute-start(bf16[17,16,128]{2,1,0:T(8,128)(2,1)S(1)} %get-tuple-element.30.face), channel_id=1, source_target_pairs={{0,64},{64,0},{128,192},{192,128},{256,320},{320,256},{384,448},{4... | collective-permute-start | bytes 208904 | tf_op jit(solution)/shard_map/ppermute | solution.py:359
  40.7 0.7 collective-permute-start.5
  41.3 0.6 collective-permute-done.4.other.face_in
  41.9 0.7 pair.1
  42.6 9.3 %all-to-all-start.1 = ((bf16[8,7,16,128]{3,2,1,0:T(8,128)(2,1)}), bf16[8,7,16,128]{3,2,1,0:T(8,128)(2,1)S(1)}, u32[]{:S(2)}, u32[]{:S(2)}) async-start(bf16[8,7,16,128]{3,2,1,0:T(8,128)(2,1)} %pair.1), calls=%async_computation.1 | async-start | bytes 458752 | tf_op jit(solution)/shard_map/all_to_all | solution.py:17
  51.9 0.0 collective-permute-done.5.far_in
  51.9 1.3 %backward.1 = bf16[8,8,16,128]{3,2,1,0:T(8,128)(2,1)} custom-call(s32[1]{0:T(128)} %bitcast.at_ref, bf16[432,64]{1,0:T(8,128)(2,1)S(1)} %bitcast.33, bf16[17,16,128]{2,1,0:T(8,128)(2,1)S(1)} %get-tuple-element.30.face, bf16[10,16,128]{2,1,0:T(8,128)(2,1)S(1)} %get-tuple-element.31.far, bf16[17,16,128]{2,1,0:T(8,128)(2,1)S(1)} %collective-permute-done.4.other.face_in, ...), custom_call_target="tpu_custom_call" | custom-call | flops 7247757312 | bytes 262144 | tf_op jit(solution)/shard_map/backward/pallas_call | solution.py:271
  53.3 8.9 %all-to-all-done.1.blocks = bf16[8,7,16,128]{3,2,1,0:T(8,128)(2,1)S(1)} async-done(((bf16[8,7,16,128]{3,2,1,0:T(8,128)(2,1)}), bf16[8,7,16,128]{3,2,1,0:T(8,128)(2,1)S(1)}, u32[]{:S(2)}, u32[]{:S(2)}) %all-to-all-start.1) | async-done | bytes 229408 | tf_op jit(solution)/shard_map/all_to_all | solution.py:17
  62.2 16.5 %all_to_all.20.blocks = bf16[4,7,16,128]{3,2,1,0:T(8,128)(2,1)S(1)} all-to-all(bf16[4,7,16,128]{3,2,1,0:T(8,128)(2,1)S(1)} %sums.2), channel_id=1, replica_groups={{0,128,256,384},{64,192,320,448},{1,129,257,385},{65,193,321,449},{2,13..., dimensions={0} | all-to-all | bytes 229376 | tf_op jit(solution)/shard_map/all_to_all | solution.py:17
  78.7 4.5 %all-to-all-start.3 = ((bf16[8,8,16,128]{3,2,1,0:T(8,128)(2,1)}), bf16[8,8,16,128]{3,2,1,0:T(8,128)(2,1)S(1)}, u32[]{:S(2)}, u32[]{:S(2)}) async-start(bf16[8,8,16,128]{3,2,1,0:T(8,128)(2,1)} %backward.1), calls=%async_computation.3 | async-start | bytes 524288 | tf_op jit(solution)/shard_map/all_to_all | solution.py:17
  83.2 1.9 %collective-permute-start.6 = (bf16[7,16,128]{2,1,0:T(8,128)(2,1)S(1)}, bf16[7,16,128]{2,1,0:T(8,128)(2,1)S(1)}, u32[]{:S(2)}, u32[]{:S(2)}) collective-permute-start(bf16[7,16,128]{2,1,0:T(8,128)(2,1)S(1)} %bitcast.30), channel_id=1, source_target_pairs={{0,64},{64,0},{128,192},{192,128},{256,320},{320,256},{384,448},{4... | collective-permute-start | bytes 86024 | tf_op jit(solution)/shard_map/ppermute | solution.py:390
  85.2 0.6 copy.21
  85.8 0.5 collective-permute-done.6.other
  86.3 0.8 weights.1
  87.1 2.3 %all-to-all-done.3.parts = bf16[8,8,16,128]{3,2,1,0:T(8,128)(2,1)S(1)} async-done(((bf16[8,8,16,128]{3,2,1,0:T(8,128)(2,1)}), bf16[8,8,16,128]{3,2,1,0:T(8,128)(2,1)S(1)}, u32[]{:S(2)}, u32[]{:S(2)}) %all-to-all-start.3) | async-done | bytes 262176 | tf_op jit(solution)/shard_map/all_to_all | solution.py:17
  89.4 0.7 unpack.1
  (7 shorter events, 0.1 us)
Async XLA Ops:
  0.6 0.8 copy-start.1
  1.4 6.5 %collective-permute-start.1 = (bf16[4,16,128]{2,1,0:T(8,128)(2,1)S(1)}, bf16[4,16,128]{2,1,0:T(8,128)(2,1)S(1)}, u32[]{:S(2)}, u32[]{:S(2)}) collective-permute-start(bf16[4,16,128]{2,1,0:T(8,128)(2,1)S(1)} %far.1), channel_id=1, source_target_pairs={{64,128},{128,64},{192,256},{256,192},{320,384},{384,320},{65,129}... | collective-permute-start | bytes 49160 | tf_op jit(solution)/shard_map/ppermute | solution.py:306
  2.1 6.7 %collective-permute-start = (bf16[4,16,128]{2,1,0:T(8,128)(2,1)S(1)}, bf16[4,16,128]{2,1,0:T(8,128)(2,1)S(1)}, u32[]{:S(2)}, u32[]{:S(2)}) collective-permute-start(bf16[4,16,128]{2,1,0:T(8,128)(2,1)S(1)} %get-tuple-element.22), channel_id=1, source_target_pairs={{0,64},{64,0},{128,192},{192,128},{256,320},{320,256},{384,448},{4... | collective-permute-start | bytes 49160 | tf_op jit(solution)/shard_map/ppermute | solution.py:304
  9.7 5.9 %copy-start.4 = (bf16[16,2,8,128]{3,2,1,0:T(8,128)(2,1)S(1)}, bf16[16,2,8,128]{3,2,1,0:T(8,128)(2,1)}, u32[]{:S(2)}) copy-start(bf16[16,2,8,128]{3,2,1,0:T(8,128)(2,1)} %param.8) | copy-start | bytes 196612
  9.7 15.3 %all-to-all-start = ((bf16[8,4,4,16,128]{4,3,2,1,0:T(8,128)(2,1)}), bf16[8,4,4,16,128]{4,3,2,1,0:T(8,128)(2,1)S(1)}, u32[]{:S(2)}, u32[]{:S(2)}) async-start(bf16[8,4,4,16,128]{4,3,2,1,0:T(8,128)(2,1)} %grid.1), calls=%async_computation | async-start | bytes 1048576 | tf_op jit(solution)/shard_map/all_to_all | solution.py:17
  15.6 0.9 copy-start
  16.5 0.9 %copy-start.3 = (bf16[2,192,256,1]{2,1,3,0:T(8,128)(2,1)S(1)}, bf16[2,192,256,1]{2,1,3,0:T(8,128)(2,1)}, u32[]{:S(2)}) copy-start(bf16[2,192,256,1]{2,1,3,0:T(8,128)(2,1)} %constant.24) | copy-start | bytes 589828
  25.0 11.6 %copy-start.2 = (f32[16]{0:T(128)S(1)}, f32[16]{0:T(128)}, u32[]{:S(2)}) copy-start(f32[16]{0:T(128)} %bias_ref.1) | copy-start | bytes 196
  25.0 6.9 %collective-permute-start.2 = (bf16[34,16,128]{2,1,0:T(8,128)(2,1)S(1)}, bf16[34,16,128]{2,1,0:T(8,128)(2,1)S(1)}, u32[]{:S(2)}, u32[]{:S(2)}) collective-permute-start(bf16[34,16,128]{2,1,0:T(8,128)(2,1)S(1)} %get-tuple-element.26), channel_id=1, source_target_pairs={{0,8},{8,16},{16,24},{24,32},{32,40},{40,48},{48,56},{1,9},{9,17},... | collective-permute-start | bytes 417800 | tf_op jit(solution)/shard_map/ppermute | solution.py:22
  29.3 7.3 %collective-permute-start.3 = (bf16[34,16,128]{2,1,0:T(8,128)(2,1)S(1)}, bf16[34,16,128]{2,1,0:T(8,128)(2,1)S(1)}, u32[]{:S(2)}, u32[]{:S(2)}) collective-permute-start(bf16[34,16,128]{2,1,0:T(8,128)(2,1)S(1)} %get-tuple-element.27), channel_id=1, source_target_pairs={{8,0},{16,8},{24,16},{32,24},{40,32},{48,40},{56,48},{9,1},{17,9},... | collective-permute-start | bytes 417800 | tf_op jit(solution)/shard_map/ppermute | solution.py:23
  38.7 3.2 %collective-permute-start.4 = (bf16[17,16,128]{2,1,0:T(8,128)(2,1)S(1)}, bf16[17,16,128]{2,1,0:T(8,128)(2,1)S(1)}, u32[]{:S(2)}, u32[]{:S(2)}) collective-permute-start(bf16[17,16,128]{2,1,0:T(8,128)(2,1)S(1)} %get-tuple-element.30.face), channel_id=1, source_target_pairs={{0,64},{64,0},{128,192},{192,128},{256,320},{320,256},{384,448},{4... | collective-permute-start | bytes 208904 | tf_op jit(solution)/shard_map/ppermute | solution.py:359
  40.7 11.3 %collective-permute-start.5 = (bf16[10,16,128]{2,1,0:T(8,128)(2,1)S(1)}, bf16[10,16,128]{2,1,0:T(8,128)(2,1)S(1)}, u32[]{:S(2)}, u32[]{:S(2)}) collective-permute-start(bf16[10,16,128]{2,1,0:T(8,128)(2,1)S(1)} %get-tuple-element.31.far), channel_id=1, source_target_pairs={{64,128},{128,64},{192,256},{256,192},{320,384},{384,320},{65,129}... | collective-permute-start | bytes 122888 | tf_op jit(solution)/shard_map/ppermute | solution.py:360
  42.6 19.6 %all-to-all-start.1 = ((bf16[8,7,16,128]{3,2,1,0:T(8,128)(2,1)}), bf16[8,7,16,128]{3,2,1,0:T(8,128)(2,1)S(1)}, u32[]{:S(2)}, u32[]{:S(2)}) async-start(bf16[8,7,16,128]{3,2,1,0:T(8,128)(2,1)} %pair.1), calls=%async_computation.1 | async-start | bytes 458752 | tf_op jit(solution)/shard_map/all_to_all | solution.py:17
  78.7 10.6 %all-to-all-start.3 = ((bf16[8,8,16,128]{3,2,1,0:T(8,128)(2,1)}), bf16[8,8,16,128]{3,2,1,0:T(8,128)(2,1)S(1)}, u32[]{:S(2)}, u32[]{:S(2)}) async-start(bf16[8,8,16,128]{3,2,1,0:T(8,128)(2,1)} %backward.1), calls=%async_computation.3 | async-start | bytes 524288 | tf_op jit(solution)/shard_map/all_to_all | solution.py:17
  83.2 3.1 %collective-permute-start.6 = (bf16[7,16,128]{2,1,0:T(8,128)(2,1)S(1)}, bf16[7,16,128]{2,1,0:T(8,128)(2,1)S(1)}, u32[]{:S(2)}, u32[]{:S(2)}) collective-permute-start(bf16[7,16,128]{2,1,0:T(8,128)(2,1)S(1)} %bitcast.30), channel_id=1, source_target_pairs={{0,64},{64,0},{128,192},{192,128},{256,320},{320,256},{384,448},{4... | collective-permute-start | bytes 86024 | tf_op jit(solution)/shard_map/ppermute | solution.py:390

commit v15 on v14

--- a/solution.py
+++ b/solution.py
@@ -370,7 +370,7 @@
         far_in,
         out=[(filt, cells // 2, double, width)],
         scratch=[((planes + 2, (rows + 2) * 3 * cout, width), BF16)],
-        flops=64 * work,
+        flops=work,
         scalars=1,
     )
     sums, parts = lax.optimization_barrier((sums, parts))

time: 90.8 us -> 88 us (0.969)
  blocking collectives: 16.5 us -> 12.5 us
  waiting for transfers between devices: 26.4 us -> 27.7 us
    all_to_all x1, blocking collectives: 16.5 us -> 12.5 us  [swapped(): lax.all_to_all(blocks, axis, 0, 0, tiled=True, axis_index_groups=groups)]
  transfers between devices with their start and end apart: 10 -> 10, of which waited for: 8 -> 8; matrix products, arithmetic and copies ran while one was open for 1% -> 1% of each run, Pallas kernels for 3% -> 2%
where the time goes in v15:
time: 88 us; the launch traced here: 87.2 us
  starting transfers between devices  36.3 us (41%)
  waiting for transfers between devices  27.7 us (31%)
  blocking collectives  12.5 us (14%)
  Pallas kernels  6.57 us (7%)
  local copies, waits for them, and re-layouts  3.22 us (4%)
    all_to_all x3, starting transfers between devices, swapped(): lax.all_to_all(blocks, axis, 0, 0, tiled=True, axis_index_groups=groups)  19.7 us
    all_to_all x3, waiting for transfers between devices, swapped(): lax.all_to_all(blocks, axis, 0, 0, tiled=True, axis_index_groups=groups)  19.1 us
    all_to_all x1, blocking collectives, swapped(): lax.all_to_all(blocks, axis, 0, 0, tiled=True, axis_index_groups=groups)  12.5 us
    pallas_call x11, Pallas kernels, call(): pl.pallas_call(body, out_shape=outs, in_specs=[smem] * scalars + [vmem] *...  6.57 us
    ppermute x1, starting transfers between devices, per_device(): facing = lax.ppermute(face, 'depth', swap)  5.86 us
    ppermute x1, waiting for transfers between devices, neighbours(): after = lax.ppermute(first, axis, [(i + 1, i) for i in range(ends)])  4.73 us
    ppermute x1, starting transfers between devices, neighbours(): before = lax.ppermute(last, axis, [(i, i + 1) for i in range(ends)])  4.28 us
    unnamed x10, local copies, waits for them, and re-layouts  2.34 us
  transfers between devices with their start and end apart: 10, of which 8 were waited for; matrix products, arithmetic and copies ran while one was open for 1% of the time, Pallas kernels for 2%

profile of v15, /device:TPU:8, one launch (start us, length us, event | category | flops | bytes accessed | tf_op | source)
XLA Modules:
  0.0 87.2 jit_solution(3521984514130970401)
XLA Ops:
  0.6 0.0 copy-start.1
  0.7 0.7 copy-done.1
  1.4 0.7 collective-permute-start.1
  2.1 5.9 %collective-permute-start = (bf16[4,16,128]{2,1,0:T(8,128)(2,1)S(1)}, bf16[4,16,128]{2,1,0:T(8,128)(2,1)S(1)}, u32[]{:S(2)}, u32[]{:S(2)}) collective-permute-start(bf16[4,16,128]{2,1,0:T(8,128)(2,1)S(1)} %get-tuple-element.22), channel_id=1, source_target_pairs={{0,64},{64,0},{128,192},{192,128},{256,320},{320,256},{384,448},{4... | collective-permute-start | bytes 49160 | tf_op jit(solution)/shard_map/ppermute | solution.py:304
  8.0 0.0 collective-permute-done.1.beyond
  8.0 0.8 collective-permute-done.facing
  8.8 0.9 %grid.1 = bf16[8,4,4,16,128]{4,3,2,1,0:T(8,128)(2,1)} custom-call(s32[1]{0:T(128)} %bitcast.at_ref, bf16[2,4,16,128]{3,2,1,0:T(8,128)(2,1)S(1)} %get-tuple-element.21.own, bf16[4,16,128]{2,1,0:T(8,128)(2,1)S(1)} %collective-permute-done.facing, bf16[4,16,128]{2,1,0:T(8,128)(2,1)S(1)} %collective-permute-done.1.beyond), custom_call_target="tpu_custom_call" | custom-call | bytes 262144 | tf_op jit(solution)/shard_map/grid/pallas_call | solution.py:271
  9.7 0.0 copy-start.4
  9.7 5.9 %all-to-all-start = ((bf16[8,4,4,16,128]{4,3,2,1,0:T(8,128)(2,1)}), bf16[8,4,4,16,128]{4,3,2,1,0:T(8,128)(2,1)S(1)}, u32[]{:S(2)}, u32[]{:S(2)}) async-start(bf16[8,4,4,16,128]{4,3,2,1,0:T(8,128)(2,1)} %grid.1), calls=%async_computation | async-start | bytes 1048576 | tf_op jit(solution)/shard_map/all_to_all | solution.py:17
  15.6 0.0 copy-start
  15.6 0.0 copy-done.4
  15.6 0.9 copy-done
  16.5 0.0 copy-start.3
  16.5 0.1 copy.20
  16.5 0.1 reshape.49
  16.7 0.7 copy-done.3
  17.4 0.2 fusion
  17.6 7.4 %all-to-all-done.tiles = bf16[8,4,4,16,128]{4,3,2,1,0:T(8,128)(2,1)S(1)} async-done(((bf16[8,4,4,16,128]{4,3,2,1,0:T(8,128)(2,1)}), bf16[8,4,4,16,128]{4,3,2,1,0:T(8,128)(2,1)S(1)}, u32[]{:S(2)}, u32[]{:S(2)}) %all-to-all-start) | async-done | bytes 524320 | tf_op jit(solution)/shard_map/all_to_all | solution.py:17
  25.0 0.0 copy-start.2
  25.0 4.3 %collective-permute-start.2 = (bf16[34,16,128]{2,1,0:T(8,128)(2,1)S(1)}, bf16[34,16,128]{2,1,0:T(8,128)(2,1)S(1)}, u32[]{:S(2)}, u32[]{:S(2)}) collective-permute-start(bf16[34,16,128]{2,1,0:T(8,128)(2,1)S(1)} %get-tuple-element.26), channel_id=1, source_target_pairs={{0,8},{8,16},{16,24},{24,32},{32,40},{40,48},{48,56},{1,9},{9,17},... | collective-permute-start | bytes 417800 | tf_op jit(solution)/shard_map/ppermute | solution.py:22
  29.3 1.3 %collective-permute-start.3 = (bf16[34,16,128]{2,1,0:T(8,128)(2,1)S(1)}, bf16[34,16,128]{2,1,0:T(8,128)(2,1)S(1)}, u32[]{:S(2)}, u32[]{:S(2)}) collective-permute-start(bf16[34,16,128]{2,1,0:T(8,128)(2,1)S(1)} %get-tuple-element.27), channel_id=1, source_target_pairs={{8,0},{16,8},{24,16},{32,24},{40,32},{48,40},{56,48},{9,1},{17,9},... | collective-permute-start | bytes 417800 | tf_op jit(solution)/shard_map/ppermute | solution.py:23
  30.6 1.3 %collective-permute-done.2.before = bf16[34,16,128]{2,1,0:T(8,128)(2,1)S(1)} collective-permute-done((bf16[34,16,128]{2,1,0:T(8,128)(2,1)S(1)}, bf16[34,16,128]{2,1,0:T(8,128)(2,1)S(1)}, u32[]{:S(2)}, u32[]{:S(2)}) %collective-permute-start.2) | collective-permute-done | bytes 139296 | tf_op jit(solution)/shard_map/ppermute | solution.py:22
  31.9 4.7 %collective-permute-done.3.after = bf16[34,16,128]{2,1,0:T(8,128)(2,1)S(1)} collective-permute-done((bf16[34,16,128]{2,1,0:T(8,128)(2,1)S(1)}, bf16[34,16,128]{2,1,0:T(8,128)(2,1)S(1)}, u32[]{:S(2)}, u32[]{:S(2)}) %collective-permute-start.3) | collective-permute-done | bytes 139296 | tf_op jit(solution)/shard_map/ppermute | solution.py:23
  36.6 0.0 copy-done.2
  36.6 2.1 %forward.1 = (bf16[16,16,128]{2,1,0:T(8,128)(2,1)S(1)}, bf16[17,16,128]{2,1,0:T(8,128)(2,1)S(1)}, bf16[10,16,128]{2,1,0:T(8,128)(2,1)S(1)}, bf16[7,16,128]{2,1,0:T(8,128)(2,1)S(1)}) custom-call(s32[1]{0:T(128)} %bitcast.at_ref, f32[16]{0:T(128)S(1)} %copy-done.2, bf16[3,96,256]{2,1,0:T(8,128)(2,1)S(1)} %bitcast.31, bf16[16,16,128]{2,1,0:T(8,128)(2,1)S(1)} %bitcast.30, ...), custom_call_target="tpu_custom_call" | custom-call | flops 339738624 | bytes 262144 | tf_op jit(solution)/shard_map/forward/pallas_call | solution.py:271
  38.7 1.9 %collective-permute-start.4 = (bf16[17,16,128]{2,1,0:T(8,128)(2,1)S(1)}, bf16[17,16,128]{2,1,0:T(8,128)(2,1)S(1)}, u32[]{:S(2)}, u32[]{:S(2)}) collective-permute-start(bf16[17,16,128]{2,1,0:T(8,128)(2,1)S(1)} %get-tuple-element.30.face), channel_id=1, source_target_pairs={{0,64},{64,0},{128,192},{192,128},{256,320},{320,256},{384,448},{4... | collective-permute-start | bytes 208904 | tf_op jit(solution)/shard_map/ppermute | solution.py:359
  40.7 1.2 %collective-permute-done.4.other.face_in = bf16[17,16,128]{2,1,0:T(8,128)(2,1)S(1)} collective-permute-done((bf16[17,16,128]{2,1,0:T(8,128)(2,1)S(1)}, bf16[17,16,128]{2,1,0:T(8,128)(2,1)S(1)}, u32[]{:S(2)}, u32[]{:S(2)}) %collective-permute-start.4) | collective-permute-done | bytes 69664 | tf_op jit(solution)/shard_map/ppermute | solution.py:359
  41.9 0.7 pair.1
  42.6 9.3 %all-to-all-start.1 = ((bf16[8,7,16,128]{3,2,1,0:T(8,128)(2,1)}), bf16[8,7,16,128]{3,2,1,0:T(8,128)(2,1)S(1)}, u32[]{:S(2)}, u32[]{:S(2)}) async-start(bf16[8,7,16,128]{3,2,1,0:T(8,128)(2,1)} %pair.1), calls=%async_computation.1 | async-start | bytes 458752 | tf_op jit(solution)/shard_map/all_to_all | solution.py:17
  51.9 0.7 collective-permute-start.5
  52.6 0.0 collective-permute-done.5.far_in
  52.6 1.3 %backward.1 = bf16[8,8,16,128]{3,2,1,0:T(8,128)(2,1)} custom-call(s32[1]{0:T(128)} %bitcast.at_ref, bf16[432,64]{1,0:T(8,128)(2,1)S(1)} %bitcast.28, bf16[17,16,128]{2,1,0:T(8,128)(2,1)S(1)} %get-tuple-element.30.face, bf16[10,16,128]{2,1,0:T(8,128)(2,1)S(1)} %get-tuple-element.31.far, bf16[17,16,128]{2,1,0:T(8,128)(2,1)S(1)} %collective-permute-done.4.other.face_in, ...), custom_call_target="tpu_custom_call" | custom-call | flops 113246208 | bytes 262144 | tf_op jit(solution)/shard_map/backward/pallas_call | solution.py:271
  53.9 9.5 %all-to-all-done.1.blocks = bf16[8,7,16,128]{3,2,1,0:T(8,128)(2,1)S(1)} async-done(((bf16[8,7,16,128]{3,2,1,0:T(8,128)(2,1)}), bf16[8,7,16,128]{3,2,1,0:T(8,128)(2,1)S(1)}, u32[]{:S(2)}, u32[]{:S(2)}) %all-to-all-start.1) | async-done | bytes 229408 | tf_op jit(solution)/shard_map/all_to_all | solution.py:17
  63.5 12.5 %all_to_all.20.blocks = bf16[4,7,16,128]{3,2,1,0:T(8,128)(2,1)S(1)} all-to-all(bf16[4,7,16,128]{3,2,1,0:T(8,128)(2,1)S(1)} %sums.2), channel_id=1, replica_groups={{0,128,256,384},{64,192,320,448},{1,129,257,385},{65,193,321,449},{2,13..., dimensions={0} | all-to-all | bytes 229376 | tf_op jit(solution)/shard_map/all_to_all | solution.py:17
  76.0 4.5 %all-to-all-start.3 = ((bf16[8,8,16,128]{3,2,1,0:T(8,128)(2,1)}), bf16[8,8,16,128]{3,2,1,0:T(8,128)(2,1)S(1)}, u32[]{:S(2)}, u32[]{:S(2)}) async-start(bf16[8,8,16,128]{3,2,1,0:T(8,128)(2,1)} %backward.1), calls=%async_computation.3 | async-start | bytes 524288 | tf_op jit(solution)/shard_map/all_to_all | solution.py:17
  80.5 1.9 %collective-permute-start.6 = (bf16[7,16,128]{2,1,0:T(8,128)(2,1)S(1)}, bf16[7,16,128]{2,1,0:T(8,128)(2,1)S(1)}, u32[]{:S(2)}, u32[]{:S(2)}) collective-permute-start(bf16[7,16,128]{2,1,0:T(8,128)(2,1)S(1)} %bitcast.32), channel_id=1, source_target_pairs={{0,64},{64,0},{128,192},{192,128},{256,320},{320,256},{384,448},{4... | collective-permute-start | bytes 86024 | tf_op jit(solution)/shard_map/ppermute | solution.py:390
  82.4 0.6 copy.21
  83.0 0.5 collective-permute-done.6.other
  83.6 0.8 weights.1
  84.3 2.3 %all-to-all-done.3.parts = bf16[8,8,16,128]{3,2,1,0:T(8,128)(2,1)S(1)} async-done(((bf16[8,8,16,128]{3,2,1,0:T(8,128)(2,1)}), bf16[8,8,16,128]{3,2,1,0:T(8,128)(2,1)S(1)}, u32[]{:S(2)}, u32[]{:S(2)}) %all-to-all-start.3) | async-done | bytes 262176 | tf_op jit(solution)/shard_map/all_to_all | solution.py:17
  86.6 0.7 unpack.1
  (7 shorter events, 0.1 us)
Async XLA Ops:
  0.6 0.8 copy-start.1
  1.4 6.5 %collective-permute-start.1 = (bf16[4,16,128]{2,1,0:T(8,128)(2,1)S(1)}, bf16[4,16,128]{2,1,0:T(8,128)(2,1)S(1)}, u32[]{:S(2)}, u32[]{:S(2)}) collective-permute-start(bf16[4,16,128]{2,1,0:T(8,128)(2,1)S(1)} %far.1), channel_id=1, source_target_pairs={{64,128},{128,64},{192,256},{256,192},{320,384},{384,320},{65,129}... | collective-permute-start | bytes 49160 | tf_op jit(solution)/shard_map/ppermute | solution.py:306
  2.1 6.7 %collective-permute-start = (bf16[4,16,128]{2,1,0:T(8,128)(2,1)S(1)}, bf16[4,16,128]{2,1,0:T(8,128)(2,1)S(1)}, u32[]{:S(2)}, u32[]{:S(2)}) collective-permute-start(bf16[4,16,128]{2,1,0:T(8,128)(2,1)S(1)} %get-tuple-element.22), channel_id=1, source_target_pairs={{0,64},{64,0},{128,192},{192,128},{256,320},{320,256},{384,448},{4... | collective-permute-start | bytes 49160 | tf_op jit(solution)/shard_map/ppermute | solution.py:304
  9.7 5.9 %copy-start.4 = (bf16[16,2,8,128]{3,2,1,0:T(8,128)(2,1)S(1)}, bf16[16,2,8,128]{3,2,1,0:T(8,128)(2,1)}, u32[]{:S(2)}) copy-start(bf16[16,2,8,128]{3,2,1,0:T(8,128)(2,1)} %param.8) | copy-start | bytes 196612
  9.7 15.3 %all-to-all-start = ((bf16[8,4,4,16,128]{4,3,2,1,0:T(8,128)(2,1)}), bf16[8,4,4,16,128]{4,3,2,1,0:T(8,128)(2,1)S(1)}, u32[]{:S(2)}, u32[]{:S(2)}) async-start(bf16[8,4,4,16,128]{4,3,2,1,0:T(8,128)(2,1)} %grid.1), calls=%async_computation | async-start | bytes 1048576 | tf_op jit(solution)/shard_map/all_to_all | solution.py:17
  15.6 0.9 %copy-start = (bf16[27,64,16]{1,2,0:T(8,128)(2,1)S(1)}, bf16[27,64,16]{1,2,0:T(8,128)(2,1)}, u32[]{:S(2)}) copy-start(bf16[27,64,16]{1,2,0:T(8,128)(2,1)} %param.6) | copy-start | bytes 165892
  16.5 0.9 %copy-start.3 = (bf16[2,192,256,1]{2,1,3,0:T(8,128)(2,1)S(1)}, bf16[2,192,256,1]{2,1,3,0:T(8,128)(2,1)}, u32[]{:S(2)}) copy-start(bf16[2,192,256,1]{2,1,3,0:T(8,128)(2,1)} %constant.24) | copy-start | bytes 589828
  25.0 11.6 %copy-start.2 = (f32[16]{0:T(128)S(1)}, f32[16]{0:T(128)}, u32[]{:S(2)}) copy-start(f32[16]{0:T(128)} %bias_ref.1) | copy-start | bytes 196
  25.0 6.9 %collective-permute-start.2 = (bf16[34,16,128]{2,1,0:T(8,128)(2,1)S(1)}, bf16[34,16,128]{2,1,0:T(8,128)(2,1)S(1)}, u32[]{:S(2)}, u32[]{:S(2)}) collective-permute-start(bf16[34,16,128]{2,1,0:T(8,128)(2,1)S(1)} %get-tuple-element.26), channel_id=1, source_target_pairs={{0,8},{8,16},{16,24},{24,32},{32,40},{40,48},{48,56},{1,9},{9,17},... | collective-permute-start | bytes 417800 | tf_op jit(solution)/shard_map/ppermute | solution.py:22
  29.3 7.3 %collective-permute-start.3 = (bf16[34,16,128]{2,1,0:T(8,128)(2,1)S(1)}, bf16[34,16,128]{2,1,0:T(8,128)(2,1)S(1)}, u32[]{:S(2)}, u32[]{:S(2)}) collective-permute-start(bf16[34,16,128]{2,1,0:T(8,128)(2,1)S(1)} %get-tuple-element.27), channel_id=1, source_target_pairs={{8,0},{16,8},{24,16},{32,24},{40,32},{48,40},{56,48},{9,1},{17,9},... | collective-permute-start | bytes 417800 | tf_op jit(solution)/shard_map/ppermute | solution.py:23
  38.7 3.2 %collective-permute-start.4 = (bf16[17,16,128]{2,1,0:T(8,128)(2,1)S(1)}, bf16[17,16,128]{2,1,0:T(8,128)(2,1)S(1)}, u32[]{:S(2)}, u32[]{:S(2)}) collective-permute-start(bf16[17,16,128]{2,1,0:T(8,128)(2,1)S(1)} %get-tuple-element.30.face), channel_id=1, source_target_pairs={{0,64},{64,0},{128,192},{192,128},{256,320},{320,256},{384,448},{4... | collective-permute-start | bytes 208904 | tf_op jit(solution)/shard_map/ppermute | solution.py:359
  42.6 20.8 %all-to-all-start.1 = ((bf16[8,7,16,128]{3,2,1,0:T(8,128)(2,1)}), bf16[8,7,16,128]{3,2,1,0:T(8,128)(2,1)S(1)}, u32[]{:S(2)}, u32[]{:S(2)}) async-start(bf16[8,7,16,128]{3,2,1,0:T(8,128)(2,1)} %pair.1), calls=%async_computation.1 | async-start | bytes 458752 | tf_op jit(solution)/shard_map/all_to_all | solution.py:17
  51.9 0.7 collective-permute-start.5
  76.0 10.6 %all-to-all-start.3 = ((bf16[8,8,16,128]{3,2,1,0:T(8,128)(2,1)}), bf16[8,8,16,128]{3,2,1,0:T(8,128)(2,1)S(1)}, u32[]{:S(2)}, u32[]{:S(2)}) async-start(bf16[8,8,16,128]{3,2,1,0:T(8,128)(2,1)} %backward.1), calls=%async_computation.3 | async-start | bytes 524288 | tf_op jit(solution)/shard_map/all_to_all | solution.py:17
  80.5 3.1 %collective-permute-start.6 = (bf16[7,16,128]{2,1,0:T(8,128)(2,1)S(1)}, bf16[7,16,128]{2,1,0:T(8,128)(2,1)S(1)}, u32[]{:S(2)}, u32[]{:S(2)}) collective-permute-start(bf16[7,16,128]{2,1,0:T(8,128)(2,1)S(1)} %bitcast.32), channel_id=1, source_target_pairs={{0,64},{64,0},{128,192},{192,128},{256,320},{320,256},{384,448},{4... | collective-permute-start | bytes 86024 | tf_op jit(solution)/shard_map/ppermute | solution.py:390

commit v16 on v14

--- a/solution.py
+++ b/solution.py
@@ -373,7 +373,6 @@
         flops=64 * work,
         scalars=1,
     )
-    sums, parts = lax.optimization_barrier((sums, parts))
     groups = [[i for i in range(depth) if i % 2 == k] for k in range(2)]
     sums = swapped(call(sum_kernel, "sums", sums, out=[(depth // 2,) + size]), "depth", groups)
     sums, parts = lax.optimization_barrier((sums, parts))

time: 90.8 us -> 88.9 us (0.979)
  blocking collectives: 16.5 us -> 0 us
  waiting for transfers between devices: 26.4 us -> 36 us
  starting transfers between devices: 36.3 us -> 40.7 us
    all_to_all x1 -> x0, blocking collectives: 16.5 us -> none  [swapped(): lax.all_to_all(blocks, axis, 0, 0, tiled=True, axis_index_groups=groups)]
    all_to_all x3 -> x4, waiting for transfers between devices: 18.5 us -> 27.5 us  [swapped(): lax.all_to_all(blocks, axis, 0, 0, tiled=True, axis_index_groups=groups)]
    all_to_all x3 -> x4, starting transfers between devices: 19.7 us -> 24.1 us  [swapped(): lax.all_to_all(blocks, axis, 0, 0, tiled=True, axis_index_groups=groups)]
  transfers between devices with their start and end apart: 10 -> 11, of which waited for: 8 -> 9; matrix products, arithmetic and copies ran while one was open for 1% -> 1% of each run, Pallas kernels for 3% -> 3%
where the time goes in v16:
time: 88.9 us; the launch traced here: 88.1 us
  starting transfers between devices  40.7 us (46%)
  waiting for transfers between devices  36 us (40%)
  Pallas kernels  7.2 us (8%)
  local copies, waits for them, and re-layouts  3.22 us (4%)
    all_to_all x4, waiting for transfers between devices, swapped(): lax.all_to_all(blocks, axis, 0, 0, tiled=True, axis_index_groups=groups)  27.5 us
    all_to_all x4, starting transfers between devices, swapped(): lax.all_to_all(blocks, axis, 0, 0, tiled=True, axis_index_groups=groups)  24.1 us
    pallas_call x11, Pallas kernels, call(): pl.pallas_call(body, out_shape=outs, in_specs=[smem] * scalars + [vmem] *...  7.2 us
    ppermute x1, starting transfers between devices, per_device(): facing = lax.ppermute(face, 'depth', swap)  5.86 us
    ppermute x1, waiting for transfers between devices, neighbours(): after = lax.ppermute(first, axis, [(i + 1, i) for i in range(ends)])  4.73 us
    ppermute x1, starting transfers between devices, neighbours(): before = lax.ppermute(last, axis, [(i, i + 1) for i in range(ends)])  4.28 us
    unnamed x10, local copies, waits for them, and re-layouts  2.34 us
    ppermute x1, starting transfers between devices, per_device(): other = lax.ppermute(mine, 'depth', swap)  1.92 us
  transfers between devices with their start and end apart: 11, of which 9 were waited for; matrix products, arithmetic and copies ran while one was open for 1% of the time, Pallas kernels for 3%

profile of v16, /device:TPU:8, one launch (start us, length us, event | category | flops | bytes accessed | tf_op | source)
XLA Modules:
  0.0 88.1 jit_solution(3557050944340085746)
XLA Ops:
  0.6 0.0 copy-start.1
  0.7 0.7 copy-done.1
  1.4 0.7 collective-permute-start.1
  2.1 5.9 %collective-permute-start = (bf16[4,16,128]{2,1,0:T(8,128)(2,1)S(1)}, bf16[4,16,128]{2,1,0:T(8,128)(2,1)S(1)}, u32[]{:S(2)}, u32[]{:S(2)}) collective-permute-start(bf16[4,16,128]{2,1,0:T(8,128)(2,1)S(1)} %get-tuple-element.20), channel_id=1, source_target_pairs={{0,64},{64,0},{128,192},{192,128},{256,320},{320,256},{384,448},{4... | collective-permute-start | bytes 49160 | tf_op jit(solution)/shard_map/ppermute | solution.py:304
  8.0 0.0 collective-permute-done.1.beyond
  8.0 0.8 collective-permute-done.facing
  8.8 0.9 grid.1
  9.7 0.0 copy-start.4
  9.7 5.9 %all-to-all-start = ((bf16[8,4,4,16,128]{4,3,2,1,0:T(8,128)(2,1)}), bf16[8,4,4,16,128]{4,3,2,1,0:T(8,128)(2,1)S(1)}, u32[]{:S(2)}, u32[]{:S(2)}) async-start(bf16[8,4,4,16,128]{4,3,2,1,0:T(8,128)(2,1)} %grid.1), calls=%async_computation | async-start | bytes 1048576 | tf_op jit(solution)/shard_map/all_to_all | solution.py:17
  15.6 0.0 copy-start
  15.6 0.0 copy-done.4
  15.6 0.9 copy-done
  16.5 0.0 copy-start.3
  16.5 0.1 copy.20
  16.5 0.1 reshape.49
  16.7 0.7 copy-done.3
  17.4 0.2 fusion
  17.6 7.4 %all-to-all-done.tiles = bf16[8,4,4,16,128]{4,3,2,1,0:T(8,128)(2,1)S(1)} async-done(((bf16[8,4,4,16,128]{4,3,2,1,0:T(8,128)(2,1)}), bf16[8,4,4,16,128]{4,3,2,1,0:T(8,128)(2,1)S(1)}, u32[]{:S(2)}, u32[]{:S(2)}) %all-to-all-start) | async-done | bytes 524320 | tf_op jit(solution)/shard_map/all_to_all | solution.py:17
  25.0 0.0 copy-start.2
  25.0 4.3 %collective-permute-start.2 = (bf16[34,16,128]{2,1,0:T(8,128)(2,1)S(1)}, bf16[34,16,128]{2,1,0:T(8,128)(2,1)S(1)}, u32[]{:S(2)}, u32[]{:S(2)}) collective-permute-start(bf16[34,16,128]{2,1,0:T(8,128)(2,1)S(1)} %get-tuple-element.24), channel_id=1, source_target_pairs={{0,8},{8,16},{16,24},{24,32},{32,40},{40,48},{48,56},{1,9},{9,17},... | collective-permute-start | bytes 417800 | tf_op jit(solution)/shard_map/ppermute | solution.py:22
  29.3 1.3 %collective-permute-start.3 = (bf16[34,16,128]{2,1,0:T(8,128)(2,1)S(1)}, bf16[34,16,128]{2,1,0:T(8,128)(2,1)S(1)}, u32[]{:S(2)}, u32[]{:S(2)}) collective-permute-start(bf16[34,16,128]{2,1,0:T(8,128)(2,1)S(1)} %get-tuple-element.25), channel_id=1, source_target_pairs={{8,0},{16,8},{24,16},{32,24},{40,32},{48,40},{56,48},{9,1},{17,9},... | collective-permute-start | bytes 417800 | tf_op jit(solution)/shard_map/ppermute | solution.py:23
  30.6 1.3 %collective-permute-done.2.before = bf16[34,16,128]{2,1,0:T(8,128)(2,1)S(1)} collective-permute-done((bf16[34,16,128]{2,1,0:T(8,128)(2,1)S(1)}, bf16[34,16,128]{2,1,0:T(8,128)(2,1)S(1)}, u32[]{:S(2)}, u32[]{:S(2)}) %collective-permute-start.2) | collective-permute-done | bytes 139296 | tf_op jit(solution)/shard_map/ppermute | solution.py:22
  31.9 4.7 %collective-permute-done.3.after = bf16[34,16,128]{2,1,0:T(8,128)(2,1)S(1)} collective-permute-done((bf16[34,16,128]{2,1,0:T(8,128)(2,1)S(1)}, bf16[34,16,128]{2,1,0:T(8,128)(2,1)S(1)}, u32[]{:S(2)}, u32[]{:S(2)}) %collective-permute-start.3) | collective-permute-done | bytes 139296 | tf_op jit(solution)/shard_map/ppermute | solution.py:23
  36.6 0.0 copy-done.2
  36.6 2.1 %forward.1 = (bf16[16,16,128]{2,1,0:T(8,128)(2,1)S(1)}, bf16[17,16,128]{2,1,0:T(8,128)(2,1)S(1)}, bf16[10,16,128]{2,1,0:T(8,128)(2,1)S(1)}, bf16[7,16,128]{2,1,0:T(8,128)(2,1)S(1)}) custom-call(s32[1]{0:T(128)} %bitcast.at_ref, f32[16]{0:T(128)S(1)} %copy-done.2, bf16[3,96,256]{2,1,0:T(8,128)(2,1)S(1)} %bitcast.29, bf16[16,16,128]{2,1,0:T(8,128)(2,1)S(1)} %bitcast.28, ...), custom_call_target="tpu_custom_call" | custom-call | flops 339738624 | bytes 262144 | tf_op jit(solution)/shard_map/forward/pallas_call | solution.py:271
  38.7 1.9 %collective-permute-start.4 = (bf16[17,16,128]{2,1,0:T(8,128)(2,1)S(1)}, bf16[17,16,128]{2,1,0:T(8,128)(2,1)S(1)}, u32[]{:S(2)}, u32[]{:S(2)}) collective-permute-start(bf16[17,16,128]{2,1,0:T(8,128)(2,1)S(1)} %get-tuple-element.28.face), channel_id=1, source_target_pairs={{0,64},{64,0},{128,192},{192,128},{256,320},{320,256},{384,448},{4... | collective-permute-start | bytes 208904 | tf_op jit(solution)/shard_map/ppermute | solution.py:359
  40.7 1.2 %collective-permute-done.4.other.face_in = bf16[17,16,128]{2,1,0:T(8,128)(2,1)S(1)} collective-permute-done((bf16[17,16,128]{2,1,0:T(8,128)(2,1)S(1)}, bf16[17,16,128]{2,1,0:T(8,128)(2,1)S(1)}, u32[]{:S(2)}, u32[]{:S(2)}) %collective-permute-start.4) | collective-permute-done | bytes 69664 | tf_op jit(solution)/shard_map/ppermute | solution.py:359
  41.9 0.7 pair.1
  42.6 9.3 %all-to-all-start.1 = ((bf16[8,7,16,128]{3,2,1,0:T(8,128)(2,1)}), bf16[8,7,16,128]{3,2,1,0:T(8,128)(2,1)S(1)}, u32[]{:S(2)}, u32[]{:S(2)}) async-start(bf16[8,7,16,128]{3,2,1,0:T(8,128)(2,1)} %pair.1), calls=%async_computation.1 | async-start | bytes 458752 | tf_op jit(solution)/shard_map/all_to_all | solution.py:17
  51.9 0.7 collective-permute-start.5
  52.6 10.8 %all-to-all-done.1.blocks = bf16[8,7,16,128]{3,2,1,0:T(8,128)(2,1)S(1)} async-done(((bf16[8,7,16,128]{3,2,1,0:T(8,128)(2,1)}), bf16[8,7,16,128]{3,2,1,0:T(8,128)(2,1)S(1)}, u32[]{:S(2)}, u32[]{:S(2)}) %all-to-all-start.1) | async-done | bytes 229408 | tf_op jit(solution)/shard_map/all_to_all | solution.py:17
  63.4 0.7 sums.2
  64.1 4.4 %all-to-all-start.2 = ((bf16[4,7,16,128]{3,2,1,0:T(8,128)(2,1)}), bf16[4,7,16,128]{3,2,1,0:T(8,128)(2,1)S(1)}, u32[]{:S(2)}, u32[]{:S(2)}) async-start(bf16[4,7,16,128]{3,2,1,0:T(8,128)(2,1)} %sums.2), calls=%async_computation.2 | async-start | bytes 229376 | tf_op jit(solution)/shard_map/all_to_all | solution.py:17
  68.5 0.0 collective-permute-done.5.far_in
  68.5 1.3 %backward.1 = bf16[8,8,16,128]{3,2,1,0:T(8,128)(2,1)} custom-call(s32[1]{0:T(128)} %bitcast.at_ref, bf16[432,64]{1,0:T(8,128)(2,1)S(1)} %bitcast.33, bf16[17,16,128]{2,1,0:T(8,128)(2,1)S(1)} %get-tuple-element.28.face, bf16[10,16,128]{2,1,0:T(8,128)(2,1)S(1)} %get-tuple-element.29.far, bf16[17,16,128]{2,1,0:T(8,128)(2,1)S(1)} %collective-permute-done.4.other.face_in, ...), custom_call_target="tpu_custom_call" | custom-call | flops 7247757312 | bytes 262144 | tf_op jit(solution)/shard_map/backward/pallas_call | solution.py:271
  69.8 7.0 %all-to-all-done.2.blocks = bf16[4,7,16,128]{3,2,1,0:T(8,128)(2,1)S(1)} async-done(((bf16[4,7,16,128]{3,2,1,0:T(8,128)(2,1)}), bf16[4,7,16,128]{3,2,1,0:T(8,128)(2,1)S(1)}, u32[]{:S(2)}, u32[]{:S(2)}) %all-to-all-start.2) | async-done | bytes 114720 | tf_op jit(solution)/shard_map/all_to_all | solution.py:17
  76.8 4.5 %all-to-all-start.3 = ((bf16[8,8,16,128]{3,2,1,0:T(8,128)(2,1)}), bf16[8,8,16,128]{3,2,1,0:T(8,128)(2,1)S(1)}, u32[]{:S(2)}, u32[]{:S(2)}) async-start(bf16[8,8,16,128]{3,2,1,0:T(8,128)(2,1)} %backward.1), calls=%async_computation.3 | async-start | bytes 524288 | tf_op jit(solution)/shard_map/all_to_all | solution.py:17
  81.3 1.9 %collective-permute-start.6 = (bf16[7,16,128]{2,1,0:T(8,128)(2,1)S(1)}, bf16[7,16,128]{2,1,0:T(8,128)(2,1)S(1)}, u32[]{:S(2)}, u32[]{:S(2)}) collective-permute-start(bf16[7,16,128]{2,1,0:T(8,128)(2,1)S(1)} %bitcast.30), channel_id=1, source_target_pairs={{0,64},{64,0},{128,192},{192,128},{256,320},{320,256},{384,448},{4... | collective-permute-start | bytes 86024 | tf_op jit(solution)/shard_map/ppermute | solution.py:389
  83.2 0.6 copy.21
  83.9 0.5 collective-permute-done.6.other
  84.4 0.8 weights.1
  85.2 2.3 %all-to-all-done.3.parts = bf16[8,8,16,128]{3,2,1,0:T(8,128)(2,1)S(1)} async-done(((bf16[8,8,16,128]{3,2,1,0:T(8,128)(2,1)}), bf16[8,8,16,128]{3,2,1,0:T(8,128)(2,1)S(1)}, u32[]{:S(2)}, u32[]{:S(2)}) %all-to-all-start.3) | async-done | bytes 262176 | tf_op jit(solution)/shard_map/all_to_all | solution.py:17
  87.4 0.7 unpack.1
  (6 shorter events, 0.1 us)
Async XLA Ops:
  0.6 0.8 copy-start.1
  1.4 6.5 %collective-permute-start.1 = (bf16[4,16,128]{2,1,0:T(8,128)(2,1)S(1)}, bf16[4,16,128]{2,1,0:T(8,128)(2,1)S(1)}, u32[]{:S(2)}, u32[]{:S(2)}) collective-permute-start(bf16[4,16,128]{2,1,0:T(8,128)(2,1)S(1)} %far.1), channel_id=1, source_target_pairs={{64,128},{128,64},{192,256},{256,192},{320,384},{384,320},{65,129}... | collective-permute-start | bytes 49160 | tf_op jit(solution)/shard_map/ppermute | solution.py:306
  2.1 6.7 %collective-permute-start = (bf16[4,16,128]{2,1,0:T(8,128)(2,1)S(1)}, bf16[4,16,128]{2,1,0:T(8,128)(2,1)S(1)}, u32[]{:S(2)}, u32[]{:S(2)}) collective-permute-start(bf16[4,16,128]{2,1,0:T(8,128)(2,1)S(1)} %get-tuple-element.20), channel_id=1, source_target_pairs={{0,64},{64,0},{128,192},{192,128},{256,320},{320,256},{384,448},{4... | collective-permute-start | bytes 49160 | tf_op jit(solution)/shard_map/ppermute | solution.py:304
  9.7 5.9 %copy-start.4 = (bf16[16,2,8,128]{3,2,1,0:T(8,128)(2,1)S(1)}, bf16[16,2,8,128]{3,2,1,0:T(8,128)(2,1)}, u32[]{:S(2)}) copy-start(bf16[16,2,8,128]{3,2,1,0:T(8,128)(2,1)} %param.8) | copy-start | bytes 196612
  9.7 15.3 %all-to-all-start = ((bf16[8,4,4,16,128]{4,3,2,1,0:T(8,128)(2,1)}), bf16[8,4,4,16,128]{4,3,2,1,0:T(8,128)(2,1)S(1)}, u32[]{:S(2)}, u32[]{:S(2)}) async-start(bf16[8,4,4,16,128]{4,3,2,1,0:T(8,128)(2,1)} %grid.1), calls=%async_computation | async-start | bytes 1048576 | tf_op jit(solution)/shard_map/all_to_all | solution.py:17
  15.6 0.9 %copy-start = (bf16[27,64,16]{1,2,0:T(8,128)(2,1)S(1)}, bf16[27,64,16]{1,2,0:T(8,128)(2,1)}, u32[]{:S(2)}) copy-start(bf16[27,64,16]{1,2,0:T(8,128)(2,1)} %param.6) | copy-start | bytes 165892
  16.5 0.9 %copy-start.3 = (bf16[2,192,256,1]{2,1,3,0:T(8,128)(2,1)S(1)}, bf16[2,192,256,1]{2,1,3,0:T(8,128)(2,1)}, u32[]{:S(2)}) copy-start(bf16[2,192,256,1]{2,1,3,0:T(8,128)(2,1)} %constant.24) | copy-start | bytes 589828
  25.0 11.6 %copy-start.2 = (f32[16]{0:T(128)S(1)}, f32[16]{0:T(128)}, u32[]{:S(2)}) copy-start(f32[16]{0:T(128)} %bias_ref.1) | copy-start | bytes 196
  25.0 6.9 %collective-permute-start.2 = (bf16[34,16,128]{2,1,0:T(8,128)(2,1)S(1)}, bf16[34,16,128]{2,1,0:T(8,128)(2,1)S(1)}, u32[]{:S(2)}, u32[]{:S(2)}) collective-permute-start(bf16[34,16,128]{2,1,0:T(8,128)(2,1)S(1)} %get-tuple-element.24), channel_id=1, source_target_pairs={{0,8},{8,16},{16,24},{24,32},{32,40},{40,48},{48,56},{1,9},{9,17},... | collective-permute-start | bytes 417800 | tf_op jit(solution)/shard_map/ppermute | solution.py:22
  29.3 7.3 %collective-permute-start.3 = (bf16[34,16,128]{2,1,0:T(8,128)(2,1)S(1)}, bf16[34,16,128]{2,1,0:T(8,128)(2,1)S(1)}, u32[]{:S(2)}, u32[]{:S(2)}) collective-permute-start(bf16[34,16,128]{2,1,0:T(8,128)(2,1)S(1)} %get-tuple-element.25), channel_id=1, source_target_pairs={{8,0},{16,8},{24,16},{32,24},{40,32},{48,40},{56,48},{9,1},{17,9},... | collective-permute-start | bytes 417800 | tf_op jit(solution)/shard_map/ppermute | solution.py:23
  38.7 3.2 %collective-permute-start.4 = (bf16[17,16,128]{2,1,0:T(8,128)(2,1)S(1)}, bf16[17,16,128]{2,1,0:T(8,128)(2,1)S(1)}, u32[]{:S(2)}, u32[]{:S(2)}) collective-permute-start(bf16[17,16,128]{2,1,0:T(8,128)(2,1)S(1)} %get-tuple-element.28.face), channel_id=1, source_target_pairs={{0,64},{64,0},{128,192},{192,128},{256,320},{320,256},{384,448},{4... | collective-permute-start | bytes 208904 | tf_op jit(solution)/shard_map/ppermute | solution.py:359
  42.6 20.8 %all-to-all-start.1 = ((bf16[8,7,16,128]{3,2,1,0:T(8,128)(2,1)}), bf16[8,7,16,128]{3,2,1,0:T(8,128)(2,1)S(1)}, u32[]{:S(2)}, u32[]{:S(2)}) async-start(bf16[8,7,16,128]{3,2,1,0:T(8,128)(2,1)} %pair.1), calls=%async_computation.1 | async-start | bytes 458752 | tf_op jit(solution)/shard_map/all_to_all | solution.py:17
  51.9 16.6 %collective-permute-start.5 = (bf16[10,16,128]{2,1,0:T(8,128)(2,1)S(1)}, bf16[10,16,128]{2,1,0:T(8,128)(2,1)S(1)}, u32[]{:S(2)}, u32[]{:S(2)}) collective-permute-start(bf16[10,16,128]{2,1,0:T(8,128)(2,1)S(1)} %get-tuple-element.29.far), channel_id=1, source_target_pairs={{64,128},{128,64},{192,256},{256,192},{320,384},{384,320},{65,129}... | collective-permute-start | bytes 122888 | tf_op jit(solution)/shard_map/ppermute | solution.py:360
  64.1 12.7 %all-to-all-start.2 = ((bf16[4,7,16,128]{3,2,1,0:T(8,128)(2,1)}), bf16[4,7,16,128]{3,2,1,0:T(8,128)(2,1)S(1)}, u32[]{:S(2)}, u32[]{:S(2)}) async-start(bf16[4,7,16,128]{3,2,1,0:T(8,128)(2,1)} %sums.2), calls=%async_computation.2 | async-start | bytes 229376 | tf_op jit(solution)/shard_map/all_to_all | solution.py:17
  76.8 10.6 %all-to-all-start.3 = ((bf16[8,8,16,128]{3,2,1,0:T(8,128)(2,1)}), bf16[8,8,16,128]{3,2,1,0:T(8,128)(2,1)S(1)}, u32[]{:S(2)}, u32[]{:S(2)}) async-start(bf16[8,8,16,128]{3,2,1,0:T(8,128)(2,1)} %backward.1), calls=%async_computation.3 | async-start | bytes 524288 | tf_op jit(solution)/shard_map/all_to_all | solution.py:17
  81.3 3.1 %collective-permute-start.6 = (bf16[7,16,128]{2,1,0:T(8,128)(2,1)S(1)}, bf16[7,16,128]{2,1,0:T(8,128)(2,1)S(1)}, u32[]{:S(2)}, u32[]{:S(2)}) collective-permute-start(bf16[7,16,128]{2,1,0:T(8,128)(2,1)S(1)} %bitcast.30), channel_id=1, source_target_pairs={{0,64},{64,0},{128,192},{192,128},{256,320},{320,256},{384,448},{4... | collective-permute-start | bytes 86024 | tf_op jit(solution)/shard_map/ppermute | solution.py:389

commit v17 on v16

--- a/solution.py
+++ b/solution.py
@@ -358,7 +358,9 @@
     size = kept_sums.shape
     face_in = lax.ppermute(face, "depth", swap)
     far_in = lax.ppermute(far, "depth", cross)
-    sums = swapped(call(pair_kernel, "pair", kept_sums, face_in, out=[(height,) + size]), "height")
+    groups = [[(i + height - 2) % height for i in range(height)]]
+    sums = call(pair_kernel, "pair", kept_sums, face_in, out=[(height,) + size])
+    sums = swapped(sums, "height", groups)
     parts = call(
         functools.partial(backward_kernel, planes, rows),
         "backward",
@@ -373,7 +375,7 @@
         flops=64 * work,
         scalars=1,
     )
-    groups = [[i for i in range(depth) if i % 2 == k] for k in range(2)]
+    groups = [[(i + depth // 2) % depth for i in range(k, depth, 2)] for k in range(2)]
     sums = swapped(call(sum_kernel, "sums", sums, out=[(depth // 2,) + size]), "depth", groups)
     sums, parts = lax.optimization_barrier((sums, parts))
     parts = swapped(parts, "filt")

time: 88.9 us -> 85.8 us (0.965)
  the two profiles are of different devices: /device:TPU:8 before, /device:TPU:40 now
where the time goes in v17:
time: 85.8 us; the launch traced here: 85 us
  starting transfers between devices  45.4 us (53%)
  waiting for transfers between devices  28.2 us (33%)
  Pallas kernels  7.21 us (8%)
  local copies, waits for them, and re-layouts  3.22 us (4%)
    all_to_all x4, starting transfers between devices, swapped(): lax.all_to_all(blocks, axis, 0, 0, tiled=True, axis_index_groups=groups)  26.8 us
    all_to_all x4, waiting for transfers between devices, swapped(): lax.all_to_all(blocks, axis, 0, 0, tiled=True, axis_index_groups=groups)  18 us
    pallas_call x11, Pallas kernels, call(): pl.pallas_call(body, out_shape=outs, in_specs=[smem] * scalars + [vmem] *...  7.21 us
    ppermute x1, waiting for transfers between devices, neighbours(): after = lax.ppermute(first, axis, [(i + 1, i) for i in range(ends)])  4.73 us
    ppermute x1, starting transfers between devices, per_device(): far_in = lax.ppermute(far, 'depth', cross)  4.44 us
    ppermute x1, starting transfers between devices, neighbours(): before = lax.ppermute(last, axis, [(i, i + 1) for i in range(ends)])  4.28 us
    ppermute x1, starting transfers between devices, per_device(): beyond = lax.ppermute(far, 'depth', cross)  2.58 us
    ppermute x1, waiting for transfers between devices, per_device(): beyond = lax.ppermute(far, 'depth', cross)  2.43 us
  transfers between devices with their start and end apart: 11, of which 9 were waited for; matrix products, arithmetic and copies ran while one was open for 1% of the time, Pallas kernels for 3%

profile of v17, /device:TPU:40, one launch (start us, length us, event | category | flops | bytes accessed | tf_op | source)
XLA Modules:
  0.0 85.0 jit_solution(3104404365257374706)
XLA Ops:
  0.6 0.0 copy-start.1
  0.7 0.7 copy-done.1
  1.4 2.6 %collective-permute-start.1 = (bf16[4,16,128]{2,1,0:T(8,128)(2,1)S(1)}, bf16[4,16,128]{2,1,0:T(8,128)(2,1)S(1)}, u32[]{:S(2)}, u32[]{:S(2)}) collective-permute-start(bf16[4,16,128]{2,1,0:T(8,128)(2,1)S(1)} %far.1), channel_id=1, source_target_pairs={{64,128},{128,64},{192,256},{256,192},{320,384},{384,320},{65,129}... | collective-permute-start | bytes 49160 | tf_op jit(solution)/shard_map/ppermute | solution.py:306
  4.0 2.1 %collective-permute-start = (bf16[4,16,128]{2,1,0:T(8,128)(2,1)S(1)}, bf16[4,16,128]{2,1,0:T(8,128)(2,1)S(1)}, u32[]{:S(2)}, u32[]{:S(2)}) collective-permute-start(bf16[4,16,128]{2,1,0:T(8,128)(2,1)S(1)} %get-tuple-element.20), channel_id=1, source_target_pairs={{0,64},{64,0},{128,192},{192,128},{256,320},{320,256},{384,448},{4... | collective-permute-start | bytes 49160 | tf_op jit(solution)/shard_map/ppermute | solution.py:304
  6.2 2.4 %collective-permute-done.1.beyond = bf16[4,16,128]{2,1,0:T(8,128)(2,1)S(1)} collective-permute-done((bf16[4,16,128]{2,1,0:T(8,128)(2,1)S(1)}, bf16[4,16,128]{2,1,0:T(8,128)(2,1)S(1)}, u32[]{:S(2)}, u32[]{:S(2)}) %collective-permute-start.1) | collective-permute-done | bytes 16416 | tf_op jit(solution)/shard_map/ppermute | solution.py:306
  8.6 0.0 collective-permute-done.facing
  8.6 0.9 %grid.1 = bf16[8,4,4,16,128]{4,3,2,1,0:T(8,128)(2,1)} custom-call(s32[1]{0:T(128)} %bitcast.at_ref, bf16[2,4,16,128]{3,2,1,0:T(8,128)(2,1)S(1)} %get-tuple-element.19.own, bf16[4,16,128]{2,1,0:T(8,128)(2,1)S(1)} %collective-permute-done.facing, bf16[4,16,128]{2,1,0:T(8,128)(2,1)S(1)} %collective-permute-done.1.beyond), custom_call_target="tpu_custom_call" | custom-call | bytes 262144 | tf_op jit(solution)/shard_map/grid/pallas_call | solution.py:271
  9.5 0.0 copy-start.4
  9.5 5.9 %all-to-all-start = ((bf16[8,4,4,16,128]{4,3,2,1,0:T(8,128)(2,1)}), bf16[8,4,4,16,128]{4,3,2,1,0:T(8,128)(2,1)S(1)}, u32[]{:S(2)}, u32[]{:S(2)}) async-start(bf16[8,4,4,16,128]{4,3,2,1,0:T(8,128)(2,1)} %grid.1), calls=%async_computation | async-start | bytes 1048576 | tf_op jit(solution)/shard_map/all_to_all | solution.py:17
  15.4 0.0 copy-start
  15.4 0.0 copy-done.4
  15.4 0.9 %copy-done = bf16[27,64,16]{1,2,0:T(8,128)(2,1)S(1)} copy-done((bf16[27,64,16]{1,2,0:T(8,128)(2,1)S(1)}, bf16[27,64,16]{1,2,0:T(8,128)(2,1)}, u32[]{:S(2)}) %copy-start) | copy-done | bytes 55320
  16.3 0.0 copy-start.3
  16.3 0.1 copy.20
  16.3 0.1 reshape.49
  16.5 0.7 copy-done.3
  17.2 0.2 fusion
  17.4 5.8 %all-to-all-done.tiles = bf16[8,4,4,16,128]{4,3,2,1,0:T(8,128)(2,1)S(1)} async-done(((bf16[8,4,4,16,128]{4,3,2,1,0:T(8,128)(2,1)}), bf16[8,4,4,16,128]{4,3,2,1,0:T(8,128)(2,1)S(1)}, u32[]{:S(2)}, u32[]{:S(2)}) %all-to-all-start) | async-done | bytes 524320 | tf_op jit(solution)/shard_map/all_to_all | solution.py:17
  23.2 0.0 copy-start.2
  23.2 4.3 %collective-permute-start.2 = (bf16[34,16,128]{2,1,0:T(8,128)(2,1)S(1)}, bf16[34,16,128]{2,1,0:T(8,128)(2,1)S(1)}, u32[]{:S(2)}, u32[]{:S(2)}) collective-permute-start(bf16[34,16,128]{2,1,0:T(8,128)(2,1)S(1)} %get-tuple-element.24), channel_id=1, source_target_pairs={{0,8},{8,16},{16,24},{24,32},{32,40},{40,48},{48,56},{1,9},{9,17},... | collective-permute-start | bytes 417800 | tf_op jit(solution)/shard_map/ppermute | solution.py:22
  27.5 1.3 %collective-permute-start.3 = (bf16[34,16,128]{2,1,0:T(8,128)(2,1)S(1)}, bf16[34,16,128]{2,1,0:T(8,128)(2,1)S(1)}, u32[]{:S(2)}, u32[]{:S(2)}) collective-permute-start(bf16[34,16,128]{2,1,0:T(8,128)(2,1)S(1)} %get-tuple-element.25), channel_id=1, source_target_pairs={{8,0},{16,8},{24,16},{32,24},{40,32},{48,40},{56,48},{9,1},{17,9},... | collective-permute-start | bytes 417800 | tf_op jit(solution)/shard_map/ppermute | solution.py:23
  28.8 1.3 %collective-permute-done.2.before = bf16[34,16,128]{2,1,0:T(8,128)(2,1)S(1)} collective-permute-done((bf16[34,16,128]{2,1,0:T(8,128)(2,1)S(1)}, bf16[34,16,128]{2,1,0:T(8,128)(2,1)S(1)}, u32[]{:S(2)}, u32[]{:S(2)}) %collective-permute-start.2) | collective-permute-done | bytes 139296 | tf_op jit(solution)/shard_map/ppermute | solution.py:22
  30.1 4.7 %collective-permute-done.3.after = bf16[34,16,128]{2,1,0:T(8,128)(2,1)S(1)} collective-permute-done((bf16[34,16,128]{2,1,0:T(8,128)(2,1)S(1)}, bf16[34,16,128]{2,1,0:T(8,128)(2,1)S(1)}, u32[]{:S(2)}, u32[]{:S(2)}) %collective-permute-start.3) | collective-permute-done | bytes 139296 | tf_op jit(solution)/shard_map/ppermute | solution.py:23
  34.8 0.0 copy-done.2
  34.8 2.1 %forward.1 = (bf16[16,16,128]{2,1,0:T(8,128)(2,1)S(1)}, bf16[17,16,128]{2,1,0:T(8,128)(2,1)S(1)}, bf16[10,16,128]{2,1,0:T(8,128)(2,1)S(1)}, bf16[7,16,128]{2,1,0:T(8,128)(2,1)S(1)}) custom-call(s32[1]{0:T(128)} %bitcast.at_ref, f32[16]{0:T(128)S(1)} %copy-done.2, bf16[3,96,256]{2,1,0:T(8,128)(2,1)S(1)} %bitcast.29, bf16[16,16,128]{2,1,0:T(8,128)(2,1)S(1)} %bitcast.28, ...), custom_call_target="tpu_custom_call" | custom-call | flops 339738624 | bytes 262144 | tf_op jit(solution)/shard_map/forward/pallas_call | solution.py:271
  36.9 1.9 %collective-permute-start.4 = (bf16[17,16,128]{2,1,0:T(8,128)(2,1)S(1)}, bf16[17,16,128]{2,1,0:T(8,128)(2,1)S(1)}, u32[]{:S(2)}, u32[]{:S(2)}) collective-permute-start(bf16[17,16,128]{2,1,0:T(8,128)(2,1)S(1)} %get-tuple-element.28.face), channel_id=1, source_target_pairs={{0,64},{64,0},{128,192},{192,128},{256,320},{320,256},{384,448},{4... | collective-permute-start | bytes 208904 | tf_op jit(solution)/shard_map/ppermute | solution.py:359
  38.9 1.2 %collective-permute-done.4.other.face_in = bf16[17,16,128]{2,1,0:T(8,128)(2,1)S(1)} collective-permute-done((bf16[17,16,128]{2,1,0:T(8,128)(2,1)S(1)}, bf16[17,16,128]{2,1,0:T(8,128)(2,1)S(1)}, u32[]{:S(2)}, u32[]{:S(2)}) %collective-permute-start.4) | collective-permute-done | bytes 69664 | tf_op jit(solution)/shard_map/ppermute | solution.py:359
  40.1 0.7 pair.1
  40.8 12.0 %all-to-all-start.1 = ((bf16[8,7,16,128]{3,2,1,0:T(8,128)(2,1)}), bf16[8,7,16,128]{3,2,1,0:T(8,128)(2,1)S(1)}, u32[]{:S(2)}, u32[]{:S(2)}) async-start(bf16[8,7,16,128]{3,2,1,0:T(8,128)(2,1)} %pair.1), calls=%async_computation.1 | async-start | bytes 458752 | tf_op jit(solution)/shard_map/all_to_all | solution.py:17
  52.8 4.4 %collective-permute-start.5 = (bf16[10,16,128]{2,1,0:T(8,128)(2,1)S(1)}, bf16[10,16,128]{2,1,0:T(8,128)(2,1)S(1)}, u32[]{:S(2)}, u32[]{:S(2)}) collective-permute-start(bf16[10,16,128]{2,1,0:T(8,128)(2,1)S(1)} %get-tuple-element.29.far), channel_id=1, source_target_pairs={{64,128},{128,64},{192,256},{256,192},{320,384},{384,320},{65,129}... | collective-permute-start | bytes 122888 | tf_op jit(solution)/shard_map/ppermute | solution.py:360
  57.2 2.5 %all-to-all-done.1.blocks = bf16[8,7,16,128]{3,2,1,0:T(8,128)(2,1)S(1)} async-done(((bf16[8,7,16,128]{3,2,1,0:T(8,128)(2,1)}), bf16[8,7,16,128]{3,2,1,0:T(8,128)(2,1)S(1)}, u32[]{:S(2)}, u32[]{:S(2)}) %all-to-all-start.1) | async-done | bytes 229408 | tf_op jit(solution)/shard_map/all_to_all | solution.py:17
  59.8 0.7 sums.2
  60.4 4.6 %all-to-all-start.2 = ((bf16[4,7,16,128]{3,2,1,0:T(8,128)(2,1)}), bf16[4,7,16,128]{3,2,1,0:T(8,128)(2,1)S(1)}, u32[]{:S(2)}, u32[]{:S(2)}) async-start(bf16[4,7,16,128]{3,2,1,0:T(8,128)(2,1)} %sums.2), calls=%async_computation.2 | async-start | bytes 229376 | tf_op jit(solution)/shard_map/all_to_all | solution.py:17
  65.1 0.0 collective-permute-done.5.far_in
  65.1 1.3 %backward.1 = bf16[8,8,16,128]{3,2,1,0:T(8,128)(2,1)} custom-call(s32[1]{0:T(128)} %bitcast.at_ref, bf16[432,64]{1,0:T(8,128)(2,1)S(1)} %bitcast.33, bf16[17,16,128]{2,1,0:T(8,128)(2,1)S(1)} %get-tuple-element.28.face, bf16[10,16,128]{2,1,0:T(8,128)(2,1)S(1)} %get-tuple-element.29.far, bf16[17,16,128]{2,1,0:T(8,128)(2,1)S(1)} %collective-permute-done.4.other.face_in, ...), custom_call_target="tpu_custom_call" | custom-call | flops 7247757312 | bytes 262144 | tf_op jit(solution)/shard_map/backward/pallas_call | solution.py:271
  66.4 7.4 %all-to-all-done.2.blocks = bf16[4,7,16,128]{3,2,1,0:T(8,128)(2,1)S(1)} async-done(((bf16[4,7,16,128]{3,2,1,0:T(8,128)(2,1)}), bf16[4,7,16,128]{3,2,1,0:T(8,128)(2,1)S(1)}, u32[]{:S(2)}, u32[]{:S(2)}) %all-to-all-start.2) | async-done | bytes 114720 | tf_op jit(solution)/shard_map/all_to_all | solution.py:17
  73.8 4.3 %all-to-all-start.3 = ((bf16[8,8,16,128]{3,2,1,0:T(8,128)(2,1)}), bf16[8,8,16,128]{3,2,1,0:T(8,128)(2,1)S(1)}, u32[]{:S(2)}, u32[]{:S(2)}) async-start(bf16[8,8,16,128]{3,2,1,0:T(8,128)(2,1)} %backward.1), calls=%async_computation.3 | async-start | bytes 524288 | tf_op jit(solution)/shard_map/all_to_all | solution.py:17
  78.2 1.9 %collective-permute-start.6 = (bf16[7,16,128]{2,1,0:T(8,128)(2,1)S(1)}, bf16[7,16,128]{2,1,0:T(8,128)(2,1)S(1)}, u32[]{:S(2)}, u32[]{:S(2)}) collective-permute-start(bf16[7,16,128]{2,1,0:T(8,128)(2,1)S(1)} %bitcast.30), channel_id=1, source_target_pairs={{0,64},{64,0},{128,192},{192,128},{256,320},{320,256},{384,448},{4... | collective-permute-start | bytes 86024 | tf_op jit(solution)/shard_map/ppermute | solution.py:391
  80.1 0.6 copy.21
  80.7 0.5 collective-permute-done.6.other
  81.3 0.8 weights.1
  82.0 2.3 %all-to-all-done.3.parts = bf16[8,8,16,128]{3,2,1,0:T(8,128)(2,1)S(1)} async-done(((bf16[8,8,16,128]{3,2,1,0:T(8,128)(2,1)}), bf16[8,8,16,128]{3,2,1,0:T(8,128)(2,1)S(1)}, u32[]{:S(2)}, u32[]{:S(2)}) %all-to-all-start.3) | async-done | bytes 262176 | tf_op jit(solution)/shard_map/all_to_all | solution.py:17
  84.3 0.7 unpack.1
  (6 shorter events, 0.1 us)
Async XLA Ops:
  0.6 0.8 copy-start.1
  1.4 7.2 %collective-permute-start.1 = (bf16[4,16,128]{2,1,0:T(8,128)(2,1)S(1)}, bf16[4,16,128]{2,1,0:T(8,128)(2,1)S(1)}, u32[]{:S(2)}, u32[]{:S(2)}) collective-permute-start(bf16[4,16,128]{2,1,0:T(8,128)(2,1)S(1)} %far.1), channel_id=1, source_target_pairs={{64,128},{128,64},{192,256},{256,192},{320,384},{384,320},{65,129}... | collective-permute-start | bytes 49160 | tf_op jit(solution)/shard_map/ppermute | solution.py:306
  4.0 4.6 %collective-permute-start = (bf16[4,16,128]{2,1,0:T(8,128)(2,1)S(1)}, bf16[4,16,128]{2,1,0:T(8,128)(2,1)S(1)}, u32[]{:S(2)}, u32[]{:S(2)}) collective-permute-start(bf16[4,16,128]{2,1,0:T(8,128)(2,1)S(1)} %get-tuple-element.20), channel_id=1, source_target_pairs={{0,64},{64,0},{128,192},{192,128},{256,320},{320,256},{384,448},{4... | collective-permute-start | bytes 49160 | tf_op jit(solution)/shard_map/ppermute | solution.py:304
  9.5 5.9 %copy-start.4 = (bf16[16,2,8,128]{3,2,1,0:T(8,128)(2,1)S(1)}, bf16[16,2,8,128]{3,2,1,0:T(8,128)(2,1)}, u32[]{:S(2)}) copy-start(bf16[16,2,8,128]{3,2,1,0:T(8,128)(2,1)} %param.8) | copy-start | bytes 196612
  9.5 13.7 %all-to-all-start = ((bf16[8,4,4,16,128]{4,3,2,1,0:T(8,128)(2,1)}), bf16[8,4,4,16,128]{4,3,2,1,0:T(8,128)(2,1)S(1)}, u32[]{:S(2)}, u32[]{:S(2)}) async-start(bf16[8,4,4,16,128]{4,3,2,1,0:T(8,128)(2,1)} %grid.1), calls=%async_computation | async-start | bytes 1048576 | tf_op jit(solution)/shard_map/all_to_all | solution.py:17
  15.4 0.9 %copy-start = (bf16[27,64,16]{1,2,0:T(8,128)(2,1)S(1)}, bf16[27,64,16]{1,2,0:T(8,128)(2,1)}, u32[]{:S(2)}) copy-start(bf16[27,64,16]{1,2,0:T(8,128)(2,1)} %param.6) | copy-start | bytes 165892
  16.3 0.9 %copy-start.3 = (bf16[2,192,256,1]{2,1,3,0:T(8,128)(2,1)S(1)}, bf16[2,192,256,1]{2,1,3,0:T(8,128)(2,1)}, u32[]{:S(2)}) copy-start(bf16[2,192,256,1]{2,1,3,0:T(8,128)(2,1)} %constant.24) | copy-start | bytes 589828
  23.2 11.6 %copy-start.2 = (f32[16]{0:T(128)S(1)}, f32[16]{0:T(128)}, u32[]{:S(2)}) copy-start(f32[16]{0:T(128)} %bias_ref.1) | copy-start | bytes 196
  23.2 6.9 %collective-permute-start.2 = (bf16[34,16,128]{2,1,0:T(8,128)(2,1)S(1)}, bf16[34,16,128]{2,1,0:T(8,128)(2,1)S(1)}, u32[]{:S(2)}, u32[]{:S(2)}) collective-permute-start(bf16[34,16,128]{2,1,0:T(8,128)(2,1)S(1)} %get-tuple-element.24), channel_id=1, source_target_pairs={{0,8},{8,16},{16,24},{24,32},{32,40},{40,48},{48,56},{1,9},{9,17},... | collective-permute-start | bytes 417800 | tf_op jit(solution)/shard_map/ppermute | solution.py:22
  27.5 7.3 %collective-permute-start.3 = (bf16[34,16,128]{2,1,0:T(8,128)(2,1)S(1)}, bf16[34,16,128]{2,1,0:T(8,128)(2,1)S(1)}, u32[]{:S(2)}, u32[]{:S(2)}) collective-permute-start(bf16[34,16,128]{2,1,0:T(8,128)(2,1)S(1)} %get-tuple-element.25), channel_id=1, source_target_pairs={{8,0},{16,8},{24,16},{32,24},{40,32},{48,40},{56,48},{9,1},{17,9},... | collective-permute-start | bytes 417800 | tf_op jit(solution)/shard_map/ppermute | solution.py:23
  36.9 3.2 %collective-permute-start.4 = (bf16[17,16,128]{2,1,0:T(8,128)(2,1)S(1)}, bf16[17,16,128]{2,1,0:T(8,128)(2,1)S(1)}, u32[]{:S(2)}, u32[]{:S(2)}) collective-permute-start(bf16[17,16,128]{2,1,0:T(8,128)(2,1)S(1)} %get-tuple-element.28.face), channel_id=1, source_target_pairs={{0,64},{64,0},{128,192},{192,128},{256,320},{320,256},{384,448},{4... | collective-permute-start | bytes 208904 | tf_op jit(solution)/shard_map/ppermute | solution.py:359
  40.8 19.0 %all-to-all-start.1 = ((bf16[8,7,16,128]{3,2,1,0:T(8,128)(2,1)}), bf16[8,7,16,128]{3,2,1,0:T(8,128)(2,1)S(1)}, u32[]{:S(2)}, u32[]{:S(2)}) async-start(bf16[8,7,16,128]{3,2,1,0:T(8,128)(2,1)} %pair.1), calls=%async_computation.1 | async-start | bytes 458752 | tf_op jit(solution)/shard_map/all_to_all | solution.py:17
  52.8 12.3 %collective-permute-start.5 = (bf16[10,16,128]{2,1,0:T(8,128)(2,1)S(1)}, bf16[10,16,128]{2,1,0:T(8,128)(2,1)S(1)}, u32[]{:S(2)}, u32[]{:S(2)}) collective-permute-start(bf16[10,16,128]{2,1,0:T(8,128)(2,1)S(1)} %get-tuple-element.29.far), channel_id=1, source_target_pairs={{64,128},{128,64},{192,256},{256,192},{320,384},{384,320},{65,129}... | collective-permute-start | bytes 122888 | tf_op jit(solution)/shard_map/ppermute | solution.py:360
  60.4 13.4 %all-to-all-start.2 = ((bf16[4,7,16,128]{3,2,1,0:T(8,128)(2,1)}), bf16[4,7,16,128]{3,2,1,0:T(8,128)(2,1)S(1)}, u32[]{:S(2)}, u32[]{:S(2)}) async-start(bf16[4,7,16,128]{3,2,1,0:T(8,128)(2,1)} %sums.2), calls=%async_computation.2 | async-start | bytes 229376 | tf_op jit(solution)/shard_map/all_to_all | solution.py:17
  73.8 10.5 %all-to-all-start.3 = ((bf16[8,8,16,128]{3,2,1,0:T(8,128)(2,1)}), bf16[8,8,16,128]{3,2,1,0:T(8,128)(2,1)S(1)}, u32[]{:S(2)}, u32[]{:S(2)}) async-start(bf16[8,8,16,128]{3,2,1,0:T(8,128)(2,1)} %backward.1), calls=%async_computation.3 | async-start | bytes 524288 | tf_op jit(solution)/shard_map/all_to_all | solution.py:17
  78.2 3.1 %collective-permute-start.6 = (bf16[7,16,128]{2,1,0:T(8,128)(2,1)S(1)}, bf16[7,16,128]{2,1,0:T(8,128)(2,1)S(1)}, u32[]{:S(2)}, u32[]{:S(2)}) collective-permute-start(bf16[7,16,128]{2,1,0:T(8,128)(2,1)S(1)} %bitcast.30), channel_id=1, source_target_pairs={{0,64},{64,0},{128,192},{192,128},{256,320},{320,256},{384,448},{4... | collective-permute-start | bytes 86024 | tf_op jit(solution)/shard_map/ppermute | solution.py:391

commit v18 on v17

--- a/solution.py
+++ b/solution.py
@@ -358,7 +358,7 @@
     size = kept_sums.shape
     face_in = lax.ppermute(face, "depth", swap)
     far_in = lax.ppermute(far, "depth", cross)
-    groups = [[(i + height - 2) % height for i in range(height)]]
+    groups = [list(range(height))[::-1]]
     sums = call(pair_kernel, "pair", kept_sums, face_in, out=[(height,) + size])
     sums = swapped(sums, "height", groups)
     parts = call(

time: 85.8 us -> 86.2 us (level)
  the two profiles are of different devices: /device:TPU:40 before, /device:TPU:64 now
where the time goes in v18:
time: 86.2 us; the launch traced here: 85.4 us
  starting transfers between devices  44.9 us (52%)
  waiting for transfers between devices  29.1 us (34%)
  Pallas kernels  7.21 us (8%)
  local copies, waits for them, and re-layouts  3.2 us (4%)
    all_to_all x4, starting transfers between devices, swapped(): lax.all_to_all(blocks, axis, 0, 0, tiled=True, axis_index_groups=groups)  27.7 us
    all_to_all x4, waiting for transfers between devices, swapped(): lax.all_to_all(blocks, axis, 0, 0, tiled=True, axis_index_groups=groups)  21.2 us
    pallas_call x11, Pallas kernels, call(): pl.pallas_call(body, out_shape=outs, in_specs=[smem] * scalars + [vmem] *...  7.21 us
    ppermute x1, starting transfers between devices, per_device(): facing = lax.ppermute(face, 'depth', swap)  5.86 us
    ppermute x1, waiting for transfers between devices, neighbours(): after = lax.ppermute(first, axis, [(i + 1, i) for i in range(ends)])  4.65 us
    ppermute x1, starting transfers between devices, neighbours(): before = lax.ppermute(last, axis, [(i, i + 1) for i in range(ends)])  4.28 us
    unnamed x10, local copies, waits for them, and re-layouts  2.33 us
    ppermute x1, starting transfers between devices, neighbours(): after = lax.ppermute(first, axis, [(i + 1, i) for i in range(ends)])  1.92 us
  transfers between devices with their start and end apart: 11, of which 9 were waited for; matrix products, arithmetic and copies ran while one was open for 1% of the time, Pallas kernels for 3%

profile of v18, /device:TPU:64, one launch (start us, length us, event | category | flops | bytes accessed | tf_op | source)
XLA Modules:
  0.0 85.4 jit_solution(5271326293034576135)
XLA Ops:
  0.6 0.0 copy-start.1
  0.7 0.7 copy-done.1
  1.4 0.7 collective-permute-start.1
  2.1 5.9 %collective-permute-start = (bf16[4,16,128]{2,1,0:T(8,128)(2,1)S(1)}, bf16[4,16,128]{2,1,0:T(8,128)(2,1)S(1)}, u32[]{:S(2)}, u32[]{:S(2)}) collective-permute-start(bf16[4,16,128]{2,1,0:T(8,128)(2,1)S(1)} %get-tuple-element.20), channel_id=1, source_target_pairs={{0,64},{64,0},{128,192},{192,128},{256,320},{320,256},{384,448},{4... | collective-permute-start | bytes 49160 | tf_op jit(solution)/shard_map/ppermute | solution.py:304
  8.0 0.0 collective-permute-done.1.beyond
  8.0 0.8 collective-permute-done.facing
  8.8 0.9 %grid.1 = bf16[8,4,4,16,128]{4,3,2,1,0:T(8,128)(2,1)} custom-call(s32[1]{0:T(128)} %bitcast.at_ref, bf16[2,4,16,128]{3,2,1,0:T(8,128)(2,1)S(1)} %get-tuple-element.19.own, bf16[4,16,128]{2,1,0:T(8,128)(2,1)S(1)} %collective-permute-done.facing, bf16[4,16,128]{2,1,0:T(8,128)(2,1)S(1)} %collective-permute-done.1.beyond), custom_call_target="tpu_custom_call" | custom-call | bytes 262144 | tf_op jit(solution)/shard_map/grid/pallas_call | solution.py:271
  9.7 0.0 copy-start.4
  9.7 5.4 %all-to-all-start = ((bf16[8,4,4,16,128]{4,3,2,1,0:T(8,128)(2,1)}), bf16[8,4,4,16,128]{4,3,2,1,0:T(8,128)(2,1)S(1)}, u32[]{:S(2)}, u32[]{:S(2)}) async-start(bf16[8,4,4,16,128]{4,3,2,1,0:T(8,128)(2,1)} %grid.1), calls=%async_computation | async-start | bytes 1048576 | tf_op jit(solution)/shard_map/all_to_all | solution.py:17
  15.1 0.0 copy-start
  15.1 0.0 copy-done.4
  15.2 0.9 %copy-done = bf16[27,64,16]{1,2,0:T(8,128)(2,1)S(1)} copy-done((bf16[27,64,16]{1,2,0:T(8,128)(2,1)S(1)}, bf16[27,64,16]{1,2,0:T(8,128)(2,1)}, u32[]{:S(2)}) %copy-start) | copy-done | bytes 55320
  16.0 0.0 copy-start.3
  16.0 0.1 copy.20
  16.1 0.1 reshape.49
  16.2 0.7 copy-done.3
  16.9 0.2 fusion
  17.2 8.6 %all-to-all-done.tiles = bf16[8,4,4,16,128]{4,3,2,1,0:T(8,128)(2,1)S(1)} async-done(((bf16[8,4,4,16,128]{4,3,2,1,0:T(8,128)(2,1)}), bf16[8,4,4,16,128]{4,3,2,1,0:T(8,128)(2,1)S(1)}, u32[]{:S(2)}, u32[]{:S(2)}) %all-to-all-start) | async-done | bytes 524320 | tf_op jit(solution)/shard_map/all_to_all | solution.py:17
  25.7 0.0 copy-start.2
  25.7 4.3 %collective-permute-start.2 = (bf16[34,16,128]{2,1,0:T(8,128)(2,1)S(1)}, bf16[34,16,128]{2,1,0:T(8,128)(2,1)S(1)}, u32[]{:S(2)}, u32[]{:S(2)}) collective-permute-start(bf16[34,16,128]{2,1,0:T(8,128)(2,1)S(1)} %get-tuple-element.24), channel_id=1, source_target_pairs={{0,8},{8,16},{16,24},{24,32},{32,40},{40,48},{48,56},{1,9},{9,17},... | collective-permute-start | bytes 417800 | tf_op jit(solution)/shard_map/ppermute | solution.py:22
  30.0 1.9 %collective-permute-start.3 = (bf16[34,16,128]{2,1,0:T(8,128)(2,1)S(1)}, bf16[34,16,128]{2,1,0:T(8,128)(2,1)S(1)}, u32[]{:S(2)}, u32[]{:S(2)}) collective-permute-start(bf16[34,16,128]{2,1,0:T(8,128)(2,1)S(1)} %get-tuple-element.25), channel_id=1, source_target_pairs={{8,0},{16,8},{24,16},{32,24},{40,32},{48,40},{56,48},{9,1},{17,9},... | collective-permute-start | bytes 417800 | tf_op jit(solution)/shard_map/ppermute | solution.py:23
  32.0 0.7 collective-permute-done.2.before
  32.7 4.6 %collective-permute-done.3.after = bf16[34,16,128]{2,1,0:T(8,128)(2,1)S(1)} collective-permute-done((bf16[34,16,128]{2,1,0:T(8,128)(2,1)S(1)}, bf16[34,16,128]{2,1,0:T(8,128)(2,1)S(1)}, u32[]{:S(2)}, u32[]{:S(2)}) %collective-permute-start.3) | collective-permute-done | bytes 139296 | tf_op jit(solution)/shard_map/ppermute | solution.py:23
  37.3 0.0 copy-done.2
  37.3 2.1 %forward.1 = (bf16[16,16,128]{2,1,0:T(8,128)(2,1)S(1)}, bf16[17,16,128]{2,1,0:T(8,128)(2,1)S(1)}, bf16[10,16,128]{2,1,0:T(8,128)(2,1)S(1)}, bf16[7,16,128]{2,1,0:T(8,128)(2,1)S(1)}) custom-call(s32[1]{0:T(128)} %bitcast.at_ref, f32[16]{0:T(128)S(1)} %copy-done.2, bf16[3,96,256]{2,1,0:T(8,128)(2,1)S(1)} %bitcast.29, bf16[16,16,128]{2,1,0:T(8,128)(2,1)S(1)} %bitcast.28, ...), custom_call_target="tpu_custom_call" | custom-call | flops 339738624 | bytes 262144 | tf_op jit(solution)/shard_map/forward/pallas_call | solution.py:271
  39.4 1.9 %collective-permute-start.4 = (bf16[17,16,128]{2,1,0:T(8,128)(2,1)S(1)}, bf16[17,16,128]{2,1,0:T(8,128)(2,1)S(1)}, u32[]{:S(2)}, u32[]{:S(2)}) collective-permute-start(bf16[17,16,128]{2,1,0:T(8,128)(2,1)S(1)} %get-tuple-element.28.face), channel_id=1, source_target_pairs={{0,64},{64,0},{128,192},{192,128},{256,320},{320,256},{384,448},{4... | collective-permute-start | bytes 208904 | tf_op jit(solution)/shard_map/ppermute | solution.py:359
  41.4 1.2 %collective-permute-done.4.other.face_in = bf16[17,16,128]{2,1,0:T(8,128)(2,1)S(1)} collective-permute-done((bf16[17,16,128]{2,1,0:T(8,128)(2,1)S(1)}, bf16[17,16,128]{2,1,0:T(8,128)(2,1)S(1)}, u32[]{:S(2)}, u32[]{:S(2)}) %collective-permute-start.4) | collective-permute-done | bytes 69664 | tf_op jit(solution)/shard_map/ppermute | solution.py:359
  42.6 0.7 pair.1
  43.3 11.1 %all-to-all-start.1 = ((bf16[8,7,16,128]{3,2,1,0:T(8,128)(2,1)}), bf16[8,7,16,128]{3,2,1,0:T(8,128)(2,1)S(1)}, u32[]{:S(2)}, u32[]{:S(2)}) async-start(bf16[8,7,16,128]{3,2,1,0:T(8,128)(2,1)} %pair.1), calls=%async_computation.1 | async-start | bytes 458752 | tf_op jit(solution)/shard_map/all_to_all | solution.py:17
  54.4 0.7 collective-permute-start.5
  55.1 7.0 %all-to-all-done.1.blocks = bf16[8,7,16,128]{3,2,1,0:T(8,128)(2,1)S(1)} async-done(((bf16[8,7,16,128]{3,2,1,0:T(8,128)(2,1)}), bf16[8,7,16,128]{3,2,1,0:T(8,128)(2,1)S(1)}, u32[]{:S(2)}, u32[]{:S(2)}) %all-to-all-start.1) | async-done | bytes 229408 | tf_op jit(solution)/shard_map/all_to_all | solution.py:17
  62.1 0.7 sums.2
  62.8 7.7 %all-to-all-start.2 = ((bf16[4,7,16,128]{3,2,1,0:T(8,128)(2,1)}), bf16[4,7,16,128]{3,2,1,0:T(8,128)(2,1)S(1)}, u32[]{:S(2)}, u32[]{:S(2)}) async-start(bf16[4,7,16,128]{3,2,1,0:T(8,128)(2,1)} %sums.2), calls=%async_computation.2 | async-start | bytes 229376 | tf_op jit(solution)/shard_map/all_to_all | solution.py:17
  70.5 0.0 collective-permute-done.5.far_in
  70.5 1.3 %backward.1 = bf16[8,8,16,128]{3,2,1,0:T(8,128)(2,1)} custom-call(s32[1]{0:T(128)} %bitcast.at_ref, bf16[432,64]{1,0:T(8,128)(2,1)S(1)} %bitcast.33, bf16[17,16,128]{2,1,0:T(8,128)(2,1)S(1)} %get-tuple-element.28.face, bf16[10,16,128]{2,1,0:T(8,128)(2,1)S(1)} %get-tuple-element.29.far, bf16[17,16,128]{2,1,0:T(8,128)(2,1)S(1)} %collective-permute-done.4.other.face_in, ...), custom_call_target="tpu_custom_call" | custom-call | flops 7247757312 | bytes 262144 | tf_op jit(solution)/shard_map/backward/pallas_call | solution.py:271
  71.8 2.3 %all-to-all-done.2.blocks = bf16[4,7,16,128]{3,2,1,0:T(8,128)(2,1)S(1)} async-done(((bf16[4,7,16,128]{3,2,1,0:T(8,128)(2,1)}), bf16[4,7,16,128]{3,2,1,0:T(8,128)(2,1)S(1)}, u32[]{:S(2)}, u32[]{:S(2)}) %all-to-all-start.2) | async-done | bytes 114720 | tf_op jit(solution)/shard_map/all_to_all | solution.py:17
  74.1 3.4 %all-to-all-start.3 = ((bf16[8,8,16,128]{3,2,1,0:T(8,128)(2,1)}), bf16[8,8,16,128]{3,2,1,0:T(8,128)(2,1)S(1)}, u32[]{:S(2)}, u32[]{:S(2)}) async-start(bf16[8,8,16,128]{3,2,1,0:T(8,128)(2,1)} %backward.1), calls=%async_computation.3 | async-start | bytes 524288 | tf_op jit(solution)/shard_map/all_to_all | solution.py:17
  77.6 1.9 %collective-permute-start.6 = (bf16[7,16,128]{2,1,0:T(8,128)(2,1)S(1)}, bf16[7,16,128]{2,1,0:T(8,128)(2,1)S(1)}, u32[]{:S(2)}, u32[]{:S(2)}) collective-permute-start(bf16[7,16,128]{2,1,0:T(8,128)(2,1)S(1)} %bitcast.30), channel_id=1, source_target_pairs={{0,64},{64,0},{128,192},{192,128},{256,320},{320,256},{384,448},{4... | collective-permute-start | bytes 86024 | tf_op jit(solution)/shard_map/ppermute | solution.py:391
  79.5 0.6 copy.21
  80.1 0.5 collective-permute-done.6.other
  80.7 0.8 weights.1
  81.4 3.3 %all-to-all-done.3.parts = bf16[8,8,16,128]{3,2,1,0:T(8,128)(2,1)S(1)} async-done(((bf16[8,8,16,128]{3,2,1,0:T(8,128)(2,1)}), bf16[8,8,16,128]{3,2,1,0:T(8,128)(2,1)S(1)}, u32[]{:S(2)}, u32[]{:S(2)}) %all-to-all-start.3) | async-done | bytes 262176 | tf_op jit(solution)/shard_map/all_to_all | solution.py:17
  84.8 0.7 unpack.1
  (6 shorter events, 0.1 us)
Async XLA Ops:
  0.6 0.8 copy-start.1
  1.4 6.5 %collective-permute-start.1 = (bf16[4,16,128]{2,1,0:T(8,128)(2,1)S(1)}, bf16[4,16,128]{2,1,0:T(8,128)(2,1)S(1)}, u32[]{:S(2)}, u32[]{:S(2)}) collective-permute-start(bf16[4,16,128]{2,1,0:T(8,128)(2,1)S(1)} %far.1), channel_id=1, source_target_pairs={{64,128},{128,64},{192,256},{256,192},{320,384},{384,320},{65,129}... | collective-permute-start | bytes 49160 | tf_op jit(solution)/shard_map/ppermute | solution.py:306
  2.1 6.7 %collective-permute-start = (bf16[4,16,128]{2,1,0:T(8,128)(2,1)S(1)}, bf16[4,16,128]{2,1,0:T(8,128)(2,1)S(1)}, u32[]{:S(2)}, u32[]{:S(2)}) collective-permute-start(bf16[4,16,128]{2,1,0:T(8,128)(2,1)S(1)} %get-tuple-element.20), channel_id=1, source_target_pairs={{0,64},{64,0},{128,192},{192,128},{256,320},{320,256},{384,448},{4... | collective-permute-start | bytes 49160 | tf_op jit(solution)/shard_map/ppermute | solution.py:304
  9.7 5.5 %copy-start.4 = (bf16[16,2,8,128]{3,2,1,0:T(8,128)(2,1)S(1)}, bf16[16,2,8,128]{3,2,1,0:T(8,128)(2,1)}, u32[]{:S(2)}) copy-start(bf16[16,2,8,128]{3,2,1,0:T(8,128)(2,1)} %param.8) | copy-start | bytes 196612
  9.7 16.0 %all-to-all-start = ((bf16[8,4,4,16,128]{4,3,2,1,0:T(8,128)(2,1)}), bf16[8,4,4,16,128]{4,3,2,1,0:T(8,128)(2,1)S(1)}, u32[]{:S(2)}, u32[]{:S(2)}) async-start(bf16[8,4,4,16,128]{4,3,2,1,0:T(8,128)(2,1)} %grid.1), calls=%async_computation | async-start | bytes 1048576 | tf_op jit(solution)/shard_map/all_to_all | solution.py:17
  15.1 0.9 %copy-start = (bf16[27,64,16]{1,2,0:T(8,128)(2,1)S(1)}, bf16[27,64,16]{1,2,0:T(8,128)(2,1)}, u32[]{:S(2)}) copy-start(bf16[27,64,16]{1,2,0:T(8,128)(2,1)} %param.6) | copy-start | bytes 165892
  16.0 0.9 %copy-start.3 = (bf16[2,192,256,1]{2,1,3,0:T(8,128)(2,1)S(1)}, bf16[2,192,256,1]{2,1,3,0:T(8,128)(2,1)}, u32[]{:S(2)}) copy-start(bf16[2,192,256,1]{2,1,3,0:T(8,128)(2,1)} %constant.24) | copy-start | bytes 589828
  25.7 11.6 %copy-start.2 = (f32[16]{0:T(128)S(1)}, f32[16]{0:T(128)}, u32[]{:S(2)}) copy-start(f32[16]{0:T(128)} %bias_ref.1) | copy-start | bytes 196
  25.7 6.9 %collective-permute-start.2 = (bf16[34,16,128]{2,1,0:T(8,128)(2,1)S(1)}, bf16[34,16,128]{2,1,0:T(8,128)(2,1)S(1)}, u32[]{:S(2)}, u32[]{:S(2)}) collective-permute-start(bf16[34,16,128]{2,1,0:T(8,128)(2,1)S(1)} %get-tuple-element.24), channel_id=1, source_target_pairs={{0,8},{8,16},{16,24},{24,32},{32,40},{40,48},{48,56},{1,9},{9,17},... | collective-permute-start | bytes 417800 | tf_op jit(solution)/shard_map/ppermute | solution.py:22
  30.0 7.3 %collective-permute-start.3 = (bf16[34,16,128]{2,1,0:T(8,128)(2,1)S(1)}, bf16[34,16,128]{2,1,0:T(8,128)(2,1)S(1)}, u32[]{:S(2)}, u32[]{:S(2)}) collective-permute-start(bf16[34,16,128]{2,1,0:T(8,128)(2,1)S(1)} %get-tuple-element.25), channel_id=1, source_target_pairs={{8,0},{16,8},{24,16},{32,24},{40,32},{48,40},{56,48},{9,1},{17,9},... | collective-permute-start | bytes 417800 | tf_op jit(solution)/shard_map/ppermute | solution.py:23
  39.4 3.2 %collective-permute-start.4 = (bf16[17,16,128]{2,1,0:T(8,128)(2,1)S(1)}, bf16[17,16,128]{2,1,0:T(8,128)(2,1)S(1)}, u32[]{:S(2)}, u32[]{:S(2)}) collective-permute-start(bf16[17,16,128]{2,1,0:T(8,128)(2,1)S(1)} %get-tuple-element.28.face), channel_id=1, source_target_pairs={{0,64},{64,0},{128,192},{192,128},{256,320},{320,256},{384,448},{4... | collective-permute-start | bytes 208904 | tf_op jit(solution)/shard_map/ppermute | solution.py:359
  43.3 18.8 %all-to-all-start.1 = ((bf16[8,7,16,128]{3,2,1,0:T(8,128)(2,1)}), bf16[8,7,16,128]{3,2,1,0:T(8,128)(2,1)S(1)}, u32[]{:S(2)}, u32[]{:S(2)}) async-start(bf16[8,7,16,128]{3,2,1,0:T(8,128)(2,1)} %pair.1), calls=%async_computation.1 | async-start | bytes 458752 | tf_op jit(solution)/shard_map/all_to_all | solution.py:17
  54.4 16.1 %collective-permute-start.5 = (bf16[10,16,128]{2,1,0:T(8,128)(2,1)S(1)}, bf16[10,16,128]{2,1,0:T(8,128)(2,1)S(1)}, u32[]{:S(2)}, u32[]{:S(2)}) collective-permute-start(bf16[10,16,128]{2,1,0:T(8,128)(2,1)S(1)} %get-tuple-element.29.far), channel_id=1, source_target_pairs={{64,128},{128,64},{192,256},{256,192},{320,384},{384,320},{65,129}... | collective-permute-start | bytes 122888 | tf_op jit(solution)/shard_map/ppermute | solution.py:360
  62.8 11.4 %all-to-all-start.2 = ((bf16[4,7,16,128]{3,2,1,0:T(8,128)(2,1)}), bf16[4,7,16,128]{3,2,1,0:T(8,128)(2,1)S(1)}, u32[]{:S(2)}, u32[]{:S(2)}) async-start(bf16[4,7,16,128]{3,2,1,0:T(8,128)(2,1)} %sums.2), calls=%async_computation.2 | async-start | bytes 229376 | tf_op jit(solution)/shard_map/all_to_all | solution.py:17
  74.1 10.6 %all-to-all-start.3 = ((bf16[8,8,16,128]{3,2,1,0:T(8,128)(2,1)}), bf16[8,8,16,128]{3,2,1,0:T(8,128)(2,1)S(1)}, u32[]{:S(2)}, u32[]{:S(2)}) async-start(bf16[8,8,16,128]{3,2,1,0:T(8,128)(2,1)} %backward.1), calls=%async_computation.3 | async-start | bytes 524288 | tf_op jit(solution)/shard_map/all_to_all | solution.py:17
  77.6 3.1 %collective-permute-start.6 = (bf16[7,16,128]{2,1,0:T(8,128)(2,1)S(1)}, bf16[7,16,128]{2,1,0:T(8,128)(2,1)S(1)}, u32[]{:S(2)}, u32[]{:S(2)}) collective-permute-start(bf16[7,16,128]{2,1,0:T(8,128)(2,1)S(1)} %bitcast.30), channel_id=1, source_target_pairs={{0,64},{64,0},{128,192},{192,128},{256,320},{320,256},{384,448},{4... | collective-permute-start | bytes 86024 | tf_op jit(solution)/shard_map/ppermute | solution.py:391

commit v19 on v18

--- a/solution.py
+++ b/solution.py
@@ -236,7 +236,7 @@
             for f in range(count):
                 piece = acc[f * part : (f + 1) * part]
                 piece = jnp.concatenate([piece[:, :width], piece[:, width:]], axis=0).astype(BF16)
-                parts[f, pair] = piece
+                parts[count - 1 - f, pair] = piece
 
 
 def placing(cin):
@@ -358,7 +358,7 @@
     size = kept_sums.shape
     face_in = lax.ppermute(face, "depth", swap)
     far_in = lax.ppermute(far, "depth", cross)
-    groups = [list(range(height))[::-1]]
+    groups = [list(range(2, height))[::-1] + [0, 1]]
     sums = call(pair_kernel, "pair", kept_sums, face_in, out=[(height,) + size])
     sums = swapped(sums, "height", groups)
     parts = call(
@@ -378,7 +378,7 @@
     groups = [[(i + depth // 2) % depth for i in range(k, depth, 2)] for k in range(2)]
     sums = swapped(call(sum_kernel, "sums", sums, out=[(depth // 2,) + size]), "depth", groups)
     sums, parts = lax.optimization_barrier((sums, parts))
-    parts = swapped(parts, "filt")
+    parts = swapped(parts, "filt", [list(range(filt))[::-1]])
     summed = call(
         unpack_kernel,
         "unpack",

time: 86.2 us -> 85.9 us (level)
  waiting for transfers between devices: 29.1 us -> 26.8 us
  starting transfers between devices: 44.9 us -> 46.9 us
    all_to_all x4, waiting for transfers between devices: 21.2 us -> 18.9 us  [swapped(): lax.all_to_all(blocks, axis, 0, 0, tiled=True, axis_index_groups=groups)]
    all_to_all x4, starting transfers between devices: 27.7 us -> 29.7 us  [swapped(): lax.all_to_all(blocks, axis, 0, 0, tiled=True, axis_index_groups=groups)]
where the time goes in v19:
time: 85.9 us; the launch traced here: 85.1 us
  starting transfers between devices  46.9 us (55%)
  waiting for transfers between devices  26.8 us (31%)
  Pallas kernels  7.21 us (8%)
  local copies, waits for them, and re-layouts  3.2 us (4%)
    all_to_all x4, starting transfers between devices, swapped(): lax.all_to_all(blocks, axis, 0, 0, tiled=True, axis_index_groups=groups)  29.7 us
    all_to_all x4, waiting for transfers between devices, swapped(): lax.all_to_all(blocks, axis, 0, 0, tiled=True, axis_index_groups=groups)  18.9 us
    pallas_call x11, Pallas kernels, call(): pl.pallas_call(body, out_shape=outs, in_specs=[smem] * scalars + [vmem] *...  7.21 us
    ppermute x1, starting transfers between devices, per_device(): facing = lax.ppermute(face, 'depth', swap)  5.86 us
    ppermute x1, waiting for transfers between devices, neighbours(): after = lax.ppermute(first, axis, [(i + 1, i) for i in range(ends)])  4.65 us
    ppermute x1, starting transfers between devices, neighbours(): before = lax.ppermute(last, axis, [(i, i + 1) for i in range(ends)])  4.28 us
    unnamed x10, local copies, waits for them, and re-layouts  2.33 us
    ppermute x1, starting transfers between devices, neighbours(): after = lax.ppermute(first, axis, [(i + 1, i) for i in range(ends)])  1.92 us
  transfers between devices with their start and end apart: 11, of which 9 were waited for; matrix products, arithmetic and copies ran while one was open for 1% of the time, Pallas kernels for 3%

profile of v19, /device:TPU:64, one launch (start us, length us, event | category | flops | bytes accessed | tf_op | source)
XLA Modules:
  0.0 85.1 jit_solution(13943547853274324532)
XLA Ops:
  0.6 0.0 copy-start.1
  0.7 0.7 copy-done.1
  1.4 0.7 collective-permute-start.1
  2.1 5.9 %collective-permute-start = (bf16[4,16,128]{2,1,0:T(8,128)(2,1)S(1)}, bf16[4,16,128]{2,1,0:T(8,128)(2,1)S(1)}, u32[]{:S(2)}, u32[]{:S(2)}) collective-permute-start(bf16[4,16,128]{2,1,0:T(8,128)(2,1)S(1)} %get-tuple-element.20), channel_id=1, source_target_pairs={{0,64},{64,0},{128,192},{192,128},{256,320},{320,256},{384,448},{4... | collective-permute-start | bytes 49160 | tf_op jit(solution)/shard_map/ppermute | solution.py:304
  8.0 0.0 collective-permute-done.1.beyond
  8.0 0.8 collective-permute-done.facing
  8.8 0.9 %grid.1 = bf16[8,4,4,16,128]{4,3,2,1,0:T(8,128)(2,1)} custom-call(s32[1]{0:T(128)} %bitcast.at_ref, bf16[2,4,16,128]{3,2,1,0:T(8,128)(2,1)S(1)} %get-tuple-element.19.own, bf16[4,16,128]{2,1,0:T(8,128)(2,1)S(1)} %collective-permute-done.facing, bf16[4,16,128]{2,1,0:T(8,128)(2,1)S(1)} %collective-permute-done.1.beyond), custom_call_target="tpu_custom_call" | custom-call | bytes 262144 | tf_op jit(solution)/shard_map/grid/pallas_call | solution.py:271
  9.7 0.0 copy-start.4
  9.7 5.4 %all-to-all-start = ((bf16[8,4,4,16,128]{4,3,2,1,0:T(8,128)(2,1)}), bf16[8,4,4,16,128]{4,3,2,1,0:T(8,128)(2,1)S(1)}, u32[]{:S(2)}, u32[]{:S(2)}) async-start(bf16[8,4,4,16,128]{4,3,2,1,0:T(8,128)(2,1)} %grid.1), calls=%async_computation | async-start | bytes 1048576 | tf_op jit(solution)/shard_map/all_to_all | solution.py:17
  15.1 0.0 copy-start
  15.1 0.0 copy-done.4
  15.2 0.9 %copy-done = bf16[27,64,16]{1,2,0:T(8,128)(2,1)S(1)} copy-done((bf16[27,64,16]{1,2,0:T(8,128)(2,1)S(1)}, bf16[27,64,16]{1,2,0:T(8,128)(2,1)}, u32[]{:S(2)}) %copy-start) | copy-done | bytes 55320
  16.0 0.0 copy-start.3
  16.0 0.1 copy.20
  16.1 0.1 reshape.49
  16.2 0.7 copy-done.3
  16.9 0.2 fusion
  17.2 8.6 %all-to-all-done.tiles = bf16[8,4,4,16,128]{4,3,2,1,0:T(8,128)(2,1)S(1)} async-done(((bf16[8,4,4,16,128]{4,3,2,1,0:T(8,128)(2,1)}), bf16[8,4,4,16,128]{4,3,2,1,0:T(8,128)(2,1)S(1)}, u32[]{:S(2)}, u32[]{:S(2)}) %all-to-all-start) | async-done | bytes 524320 | tf_op jit(solution)/shard_map/all_to_all | solution.py:17
  25.7 0.0 copy-start.2
  25.7 4.3 %collective-permute-start.2 = (bf16[34,16,128]{2,1,0:T(8,128)(2,1)S(1)}, bf16[34,16,128]{2,1,0:T(8,128)(2,1)S(1)}, u32[]{:S(2)}, u32[]{:S(2)}) collective-permute-start(bf16[34,16,128]{2,1,0:T(8,128)(2,1)S(1)} %get-tuple-element.24), channel_id=1, source_target_pairs={{0,8},{8,16},{16,24},{24,32},{32,40},{40,48},{48,56},{1,9},{9,17},... | collective-permute-start | bytes 417800 | tf_op jit(solution)/shard_map/ppermute | solution.py:22
  30.0 1.9 %collective-permute-start.3 = (bf16[34,16,128]{2,1,0:T(8,128)(2,1)S(1)}, bf16[34,16,128]{2,1,0:T(8,128)(2,1)S(1)}, u32[]{:S(2)}, u32[]{:S(2)}) collective-permute-start(bf16[34,16,128]{2,1,0:T(8,128)(2,1)S(1)} %get-tuple-element.25), channel_id=1, source_target_pairs={{8,0},{16,8},{24,16},{32,24},{40,32},{48,40},{56,48},{9,1},{17,9},... | collective-permute-start | bytes 417800 | tf_op jit(solution)/shard_map/ppermute | solution.py:23
  32.0 0.7 collective-permute-done.2.before
  32.7 4.6 %collective-permute-done.3.after = bf16[34,16,128]{2,1,0:T(8,128)(2,1)S(1)} collective-permute-done((bf16[34,16,128]{2,1,0:T(8,128)(2,1)S(1)}, bf16[34,16,128]{2,1,0:T(8,128)(2,1)S(1)}, u32[]{:S(2)}, u32[]{:S(2)}) %collective-permute-start.3) | collective-permute-done | bytes 139296 | tf_op jit(solution)/shard_map/ppermute | solution.py:23
  37.3 0.0 copy-done.2
  37.3 2.1 %forward.1 = (bf16[16,16,128]{2,1,0:T(8,128)(2,1)S(1)}, bf16[17,16,128]{2,1,0:T(8,128)(2,1)S(1)}, bf16[10,16,128]{2,1,0:T(8,128)(2,1)S(1)}, bf16[7,16,128]{2,1,0:T(8,128)(2,1)S(1)}) custom-call(s32[1]{0:T(128)} %bitcast.at_ref, f32[16]{0:T(128)S(1)} %copy-done.2, bf16[3,96,256]{2,1,0:T(8,128)(2,1)S(1)} %bitcast.29, bf16[16,16,128]{2,1,0:T(8,128)(2,1)S(1)} %bitcast.28, ...), custom_call_target="tpu_custom_call" | custom-call | flops 339738624 | bytes 262144 | tf_op jit(solution)/shard_map/forward/pallas_call | solution.py:271
  39.4 1.9 %collective-permute-start.4 = (bf16[17,16,128]{2,1,0:T(8,128)(2,1)S(1)}, bf16[17,16,128]{2,1,0:T(8,128)(2,1)S(1)}, u32[]{:S(2)}, u32[]{:S(2)}) collective-permute-start(bf16[17,16,128]{2,1,0:T(8,128)(2,1)S(1)} %get-tuple-element.28.face), channel_id=1, source_target_pairs={{0,64},{64,0},{128,192},{192,128},{256,320},{320,256},{384,448},{4... | collective-permute-start | bytes 208904 | tf_op jit(solution)/shard_map/ppermute | solution.py:359
  41.4 1.2 %collective-permute-done.4.other.face_in = bf16[17,16,128]{2,1,0:T(8,128)(2,1)S(1)} collective-permute-done((bf16[17,16,128]{2,1,0:T(8,128)(2,1)S(1)}, bf16[17,16,128]{2,1,0:T(8,128)(2,1)S(1)}, u32[]{:S(2)}, u32[]{:S(2)}) %collective-permute-start.4) | collective-permute-done | bytes 69664 | tf_op jit(solution)/shard_map/ppermute | solution.py:359
  42.6 0.7 pair.1
  43.3 11.1 %all-to-all-start.1 = ((bf16[8,7,16,128]{3,2,1,0:T(8,128)(2,1)}), bf16[8,7,16,128]{3,2,1,0:T(8,128)(2,1)S(1)}, u32[]{:S(2)}, u32[]{:S(2)}) async-start(bf16[8,7,16,128]{3,2,1,0:T(8,128)(2,1)} %pair.1), calls=%async_computation.1 | async-start | bytes 458752 | tf_op jit(solution)/shard_map/all_to_all | solution.py:17
  54.4 0.7 collective-permute-start.5
  55.1 7.3 %all-to-all-done.1.blocks = bf16[8,7,16,128]{3,2,1,0:T(8,128)(2,1)S(1)} async-done(((bf16[8,7,16,128]{3,2,1,0:T(8,128)(2,1)}), bf16[8,7,16,128]{3,2,1,0:T(8,128)(2,1)S(1)}, u32[]{:S(2)}, u32[]{:S(2)}) %all-to-all-start.1) | async-done | bytes 229408 | tf_op jit(solution)/shard_map/all_to_all | solution.py:17
  62.3 0.7 sums.2
  63.0 7.7 %all-to-all-start.2 = ((bf16[4,7,16,128]{3,2,1,0:T(8,128)(2,1)}), bf16[4,7,16,128]{3,2,1,0:T(8,128)(2,1)S(1)}, u32[]{:S(2)}, u32[]{:S(2)}) async-start(bf16[4,7,16,128]{3,2,1,0:T(8,128)(2,1)} %sums.2), calls=%async_computation.2 | async-start | bytes 229376 | tf_op jit(solution)/shard_map/all_to_all | solution.py:17
  70.7 0.0 collective-permute-done.5.far_in
  70.7 1.3 %backward.1 = bf16[8,8,16,128]{3,2,1,0:T(8,128)(2,1)} custom-call(s32[1]{0:T(128)} %bitcast.at_ref, bf16[432,64]{1,0:T(8,128)(2,1)S(1)} %bitcast.33, bf16[17,16,128]{2,1,0:T(8,128)(2,1)S(1)} %get-tuple-element.28.face, bf16[10,16,128]{2,1,0:T(8,128)(2,1)S(1)} %get-tuple-element.29.far, bf16[17,16,128]{2,1,0:T(8,128)(2,1)S(1)} %collective-permute-done.4.other.face_in, ...), custom_call_target="tpu_custom_call" | custom-call | flops 7247757312 | bytes 262144 | tf_op jit(solution)/shard_map/backward/pallas_call | solution.py:271
  72.1 2.3 %all-to-all-done.2.blocks = bf16[4,7,16,128]{3,2,1,0:T(8,128)(2,1)S(1)} async-done(((bf16[4,7,16,128]{3,2,1,0:T(8,128)(2,1)}), bf16[4,7,16,128]{3,2,1,0:T(8,128)(2,1)S(1)}, u32[]{:S(2)}, u32[]{:S(2)}) %all-to-all-start.2) | async-done | bytes 114720 | tf_op jit(solution)/shard_map/all_to_all | solution.py:17
  74.4 5.4 %all-to-all-start.3 = ((bf16[8,8,16,128]{3,2,1,0:T(8,128)(2,1)}), bf16[8,8,16,128]{3,2,1,0:T(8,128)(2,1)S(1)}, u32[]{:S(2)}, u32[]{:S(2)}) async-start(bf16[8,8,16,128]{3,2,1,0:T(8,128)(2,1)} %backward.1), calls=%async_computation.3 | async-start | bytes 524288 | tf_op jit(solution)/shard_map/all_to_all | solution.py:17
  79.8 1.9 %collective-permute-start.6 = (bf16[7,16,128]{2,1,0:T(8,128)(2,1)S(1)}, bf16[7,16,128]{2,1,0:T(8,128)(2,1)S(1)}, u32[]{:S(2)}, u32[]{:S(2)}) collective-permute-start(bf16[7,16,128]{2,1,0:T(8,128)(2,1)S(1)} %bitcast.30), channel_id=1, source_target_pairs={{0,64},{64,0},{128,192},{192,128},{256,320},{320,256},{384,448},{4... | collective-permute-start | bytes 86024 | tf_op jit(solution)/shard_map/ppermute | solution.py:391
  81.7 0.6 copy.21
  82.4 0.5 collective-permute-done.6.other
  82.9 0.8 weights.1
  83.7 0.7 all-to-all-done.3.parts
  84.4 0.7 unpack.1
  (6 shorter events, 0.1 us)
Async XLA Ops:
  0.6 0.8 copy-start.1
  1.4 6.5 %collective-permute-start.1 = (bf16[4,16,128]{2,1,0:T(8,128)(2,1)S(1)}, bf16[4,16,128]{2,1,0:T(8,128)(2,1)S(1)}, u32[]{:S(2)}, u32[]{:S(2)}) collective-permute-start(bf16[4,16,128]{2,1,0:T(8,128)(2,1)S(1)} %far.1), channel_id=1, source_target_pairs={{64,128},{128,64},{192,256},{256,192},{320,384},{384,320},{65,129}... | collective-permute-start | bytes 49160 | tf_op jit(solution)/shard_map/ppermute | solution.py:306
  2.1 6.7 %collective-permute-start = (bf16[4,16,128]{2,1,0:T(8,128)(2,1)S(1)}, bf16[4,16,128]{2,1,0:T(8,128)(2,1)S(1)}, u32[]{:S(2)}, u32[]{:S(2)}) collective-permute-start(bf16[4,16,128]{2,1,0:T(8,128)(2,1)S(1)} %get-tuple-element.20), channel_id=1, source_target_pairs={{0,64},{64,0},{128,192},{192,128},{256,320},{320,256},{384,448},{4... | collective-permute-start | bytes 49160 | tf_op jit(solution)/shard_map/ppermute | solution.py:304
  9.7 5.5 %copy-start.4 = (bf16[16,2,8,128]{3,2,1,0:T(8,128)(2,1)S(1)}, bf16[16,2,8,128]{3,2,1,0:T(8,128)(2,1)}, u32[]{:S(2)}) copy-start(bf16[16,2,8,128]{3,2,1,0:T(8,128)(2,1)} %param.8) | copy-start | bytes 196612
  9.7 16.0 %all-to-all-start = ((bf16[8,4,4,16,128]{4,3,2,1,0:T(8,128)(2,1)}), bf16[8,4,4,16,128]{4,3,2,1,0:T(8,128)(2,1)S(1)}, u32[]{:S(2)}, u32[]{:S(2)}) async-start(bf16[8,4,4,16,128]{4,3,2,1,0:T(8,128)(2,1)} %grid.1), calls=%async_computation | async-start | bytes 1048576 | tf_op jit(solution)/shard_map/all_to_all | solution.py:17
  15.1 0.9 %copy-start = (bf16[27,64,16]{1,2,0:T(8,128)(2,1)S(1)}, bf16[27,64,16]{1,2,0:T(8,128)(2,1)}, u32[]{:S(2)}) copy-start(bf16[27,64,16]{1,2,0:T(8,128)(2,1)} %param.6) | copy-start | bytes 165892
  16.0 0.9 %copy-start.3 = (bf16[2,192,256,1]{2,1,3,0:T(8,128)(2,1)S(1)}, bf16[2,192,256,1]{2,1,3,0:T(8,128)(2,1)}, u32[]{:S(2)}) copy-start(bf16[2,192,256,1]{2,1,3,0:T(8,128)(2,1)} %constant.24) | copy-start | bytes 589828
  25.7 11.6 %copy-start.2 = (f32[16]{0:T(128)S(1)}, f32[16]{0:T(128)}, u32[]{:S(2)}) copy-start(f32[16]{0:T(128)} %bias_ref.1) | copy-start | bytes 196
  25.7 6.9 %collective-permute-start.2 = (bf16[34,16,128]{2,1,0:T(8,128)(2,1)S(1)}, bf16[34,16,128]{2,1,0:T(8,128)(2,1)S(1)}, u32[]{:S(2)}, u32[]{:S(2)}) collective-permute-start(bf16[34,16,128]{2,1,0:T(8,128)(2,1)S(1)} %get-tuple-element.24), channel_id=1, source_target_pairs={{0,8},{8,16},{16,24},{24,32},{32,40},{40,48},{48,56},{1,9},{9,17},... | collective-permute-start | bytes 417800 | tf_op jit(solution)/shard_map/ppermute | solution.py:22
  30.0 7.3 %collective-permute-start.3 = (bf16[34,16,128]{2,1,0:T(8,128)(2,1)S(1)}, bf16[34,16,128]{2,1,0:T(8,128)(2,1)S(1)}, u32[]{:S(2)}, u32[]{:S(2)}) collective-permute-start(bf16[34,16,128]{2,1,0:T(8,128)(2,1)S(1)} %get-tuple-element.25), channel_id=1, source_target_pairs={{8,0},{16,8},{24,16},{32,24},{40,32},{48,40},{56,48},{9,1},{17,9},... | collective-permute-start | bytes 417800 | tf_op jit(solution)/shard_map/ppermute | solution.py:23
  39.4 3.2 %collective-permute-start.4 = (bf16[17,16,128]{2,1,0:T(8,128)(2,1)S(1)}, bf16[17,16,128]{2,1,0:T(8,128)(2,1)S(1)}, u32[]{:S(2)}, u32[]{:S(2)}) collective-permute-start(bf16[17,16,128]{2,1,0:T(8,128)(2,1)S(1)} %get-tuple-element.28.face), channel_id=1, source_target_pairs={{0,64},{64,0},{128,192},{192,128},{256,320},{320,256},{384,448},{4... | collective-permute-start | bytes 208904 | tf_op jit(solution)/shard_map/ppermute | solution.py:359
  43.3 19.0 %all-to-all-start.1 = ((bf16[8,7,16,128]{3,2,1,0:T(8,128)(2,1)}), bf16[8,7,16,128]{3,2,1,0:T(8,128)(2,1)S(1)}, u32[]{:S(2)}, u32[]{:S(2)}) async-start(bf16[8,7,16,128]{3,2,1,0:T(8,128)(2,1)} %pair.1), calls=%async_computation.1 | async-start | bytes 458752 | tf_op jit(solution)/shard_map/all_to_all | solution.py:17
  54.4 16.3 %collective-permute-start.5 = (bf16[10,16,128]{2,1,0:T(8,128)(2,1)S(1)}, bf16[10,16,128]{2,1,0:T(8,128)(2,1)S(1)}, u32[]{:S(2)}, u32[]{:S(2)}) collective-permute-start(bf16[10,16,128]{2,1,0:T(8,128)(2,1)S(1)} %get-tuple-element.29.far), channel_id=1, source_target_pairs={{64,128},{128,64},{192,256},{256,192},{320,384},{384,320},{65,129}... | collective-permute-start | bytes 122888 | tf_op jit(solution)/shard_map/ppermute | solution.py:360
  63.0 11.4 %all-to-all-start.2 = ((bf16[4,7,16,128]{3,2,1,0:T(8,128)(2,1)}), bf16[4,7,16,128]{3,2,1,0:T(8,128)(2,1)S(1)}, u32[]{:S(2)}, u32[]{:S(2)}) async-start(bf16[4,7,16,128]{3,2,1,0:T(8,128)(2,1)} %sums.2), calls=%async_computation.2 | async-start | bytes 229376 | tf_op jit(solution)/shard_map/all_to_all | solution.py:17
  74.4 10.0 %all-to-all-start.3 = ((bf16[8,8,16,128]{3,2,1,0:T(8,128)(2,1)}), bf16[8,8,16,128]{3,2,1,0:T(8,128)(2,1)S(1)}, u32[]{:S(2)}, u32[]{:S(2)}) async-start(bf16[8,8,16,128]{3,2,1,0:T(8,128)(2,1)} %backward.1), calls=%async_computation.3 | async-start | bytes 524288 | tf_op jit(solution)/shard_map/all_to_all | solution.py:17
  79.8 3.1 %collective-permute-start.6 = (bf16[7,16,128]{2,1,0:T(8,128)(2,1)S(1)}, bf16[7,16,128]{2,1,0:T(8,128)(2,1)S(1)}, u32[]{:S(2)}, u32[]{:S(2)}) collective-permute-start(bf16[7,16,128]{2,1,0:T(8,128)(2,1)S(1)} %bitcast.30), channel_id=1, source_target_pairs={{0,64},{64,0},{128,192},{192,128},{256,320},{320,256},{384,448},{4... | collective-permute-start | bytes 86024 | tf_op jit(solution)/shard_map/ppermute | solution.py:391

commit v20 on v17

--- a/solution.py
+++ b/solution.py
@@ -298,7 +298,7 @@
         at,
         activations.reshape(cin_dev, cells, width),
         out=[(planes, pairs, double, width), (pairs, double, width)],
-        scratch=[((cin_dev * cells, width), F32)],
+        scratch=[((cin_dev * cells + cells, width), F32)],
         scalars=1,
     )
     facing = lax.ppermute(face, "depth", swap)
@@ -384,7 +384,7 @@
         "unpack",
         parts,
         out=[(cin_dev, cells, width)],
-        scratch=[((cin_dev * cells, width), F32)],
+        scratch=[((cin_dev * cells + cin_dev, width), F32)],
     ).reshape(activations.shape)
 
     mine = call(sum_kernel, "sums", sums, out=[(1,) + size])[0]

time: 85.8 us -> 85.8 us (level)
  no operation moved by 1% of the time
where the time goes in v20:
time: 85.8 us; the launch traced here: 85 us
  starting transfers between devices  45.4 us (53%)
  waiting for transfers between devices  28.2 us (33%)
  Pallas kernels  7.21 us (8%)
  local copies, waits for them, and re-layouts  3.22 us (4%)
    all_to_all x4, starting transfers between devices, swapped(): lax.all_to_all(blocks, axis, 0, 0, tiled=True, axis_index_groups=groups)  26.8 us
    all_to_all x4, waiting for transfers between devices, swapped(): lax.all_to_all(blocks, axis, 0, 0, tiled=True, axis_index_groups=groups)  18 us
    pallas_call x11, Pallas kernels, call(): pl.pallas_call(body, out_shape=outs, in_specs=[smem] * scalars + [vmem] *...  7.21 us
    ppermute x1, waiting for transfers between devices, neighbours(): after = lax.ppermute(first, axis, [(i + 1, i) for i in range(ends)])  4.73 us
    ppermute x1, starting transfers between devices, per_device(): far_in = lax.ppermute(far, 'depth', cross)  4.44 us
    ppermute x1, starting transfers between devices, neighbours(): before = lax.ppermute(last, axis, [(i, i + 1) for i in range(ends)])  4.28 us
    ppermute x1, starting transfers between devices, per_device(): beyond = lax.ppermute(far, 'depth', cross)  2.58 us
    ppermute x1, waiting for transfers between devices, per_device(): beyond = lax.ppermute(far, 'depth', cross)  2.43 us
  transfers between devices with their start and end apart: 11, of which 9 were waited for; matrix products, arithmetic and copies ran while one was open for 1% of the time, Pallas kernels for 3%

profile of v20, /device:TPU:40, one launch (start us, length us, event | category | flops | bytes accessed | tf_op | source)
XLA Modules:
  0.0 85.0 jit_solution(5128113702744609374)
XLA Ops:
  0.6 0.0 copy-start.1
  0.7 0.7 copy-done.1
  1.4 2.6 %collective-permute-start.1 = (bf16[4,16,128]{2,1,0:T(8,128)(2,1)S(1)}, bf16[4,16,128]{2,1,0:T(8,128)(2,1)S(1)}, u32[]{:S(2)}, u32[]{:S(2)}) collective-permute-start(bf16[4,16,128]{2,1,0:T(8,128)(2,1)S(1)} %far.1), channel_id=1, source_target_pairs={{64,128},{128,64},{192,256},{256,192},{320,384},{384,320},{65,129}... | collective-permute-start | bytes 49160 | tf_op jit(solution)/shard_map/ppermute | solution.py:306
  4.0 2.1 %collective-permute-start = (bf16[4,16,128]{2,1,0:T(8,128)(2,1)S(1)}, bf16[4,16,128]{2,1,0:T(8,128)(2,1)S(1)}, u32[]{:S(2)}, u32[]{:S(2)}) collective-permute-start(bf16[4,16,128]{2,1,0:T(8,128)(2,1)S(1)} %get-tuple-element.20), channel_id=1, source_target_pairs={{0,64},{64,0},{128,192},{192,128},{256,320},{320,256},{384,448},{4... | collective-permute-start | bytes 49160 | tf_op jit(solution)/shard_map/ppermute | solution.py:304
  6.2 2.4 %collective-permute-done.1.beyond = bf16[4,16,128]{2,1,0:T(8,128)(2,1)S(1)} collective-permute-done((bf16[4,16,128]{2,1,0:T(8,128)(2,1)S(1)}, bf16[4,16,128]{2,1,0:T(8,128)(2,1)S(1)}, u32[]{:S(2)}, u32[]{:S(2)}) %collective-permute-start.1) | collective-permute-done | bytes 16416 | tf_op jit(solution)/shard_map/ppermute | solution.py:306
  8.6 0.0 collective-permute-done.facing
  8.6 0.9 %grid.1 = bf16[8,4,4,16,128]{4,3,2,1,0:T(8,128)(2,1)} custom-call(s32[1]{0:T(128)} %bitcast.at_ref, bf16[2,4,16,128]{3,2,1,0:T(8,128)(2,1)S(1)} %get-tuple-element.19.own, bf16[4,16,128]{2,1,0:T(8,128)(2,1)S(1)} %collective-permute-done.facing, bf16[4,16,128]{2,1,0:T(8,128)(2,1)S(1)} %collective-permute-done.1.beyond), custom_call_target="tpu_custom_call" | custom-call | bytes 262144 | tf_op jit(solution)/shard_map/grid/pallas_call | solution.py:271
  9.5 0.0 copy-start.4
  9.5 5.9 %all-to-all-start = ((bf16[8,4,4,16,128]{4,3,2,1,0:T(8,128)(2,1)}), bf16[8,4,4,16,128]{4,3,2,1,0:T(8,128)(2,1)S(1)}, u32[]{:S(2)}, u32[]{:S(2)}) async-start(bf16[8,4,4,16,128]{4,3,2,1,0:T(8,128)(2,1)} %grid.1), calls=%async_computation | async-start | bytes 1048576 | tf_op jit(solution)/shard_map/all_to_all | solution.py:17
  15.4 0.0 copy-start
  15.4 0.0 copy-done.4
  15.4 0.9 %copy-done = bf16[27,64,16]{1,2,0:T(8,128)(2,1)S(1)} copy-done((bf16[27,64,16]{1,2,0:T(8,128)(2,1)S(1)}, bf16[27,64,16]{1,2,0:T(8,128)(2,1)}, u32[]{:S(2)}) %copy-start) | copy-done | bytes 55320
  16.3 0.0 copy-start.3
  16.3 0.1 copy.20
  16.3 0.1 reshape.49
  16.5 0.7 copy-done.3
  17.2 0.2 fusion
  17.4 5.8 %all-to-all-done.tiles = bf16[8,4,4,16,128]{4,3,2,1,0:T(8,128)(2,1)S(1)} async-done(((bf16[8,4,4,16,128]{4,3,2,1,0:T(8,128)(2,1)}), bf16[8,4,4,16,128]{4,3,2,1,0:T(8,128)(2,1)S(1)}, u32[]{:S(2)}, u32[]{:S(2)}) %all-to-all-start) | async-done | bytes 524320 | tf_op jit(solution)/shard_map/all_to_all | solution.py:17
  23.2 0.0 copy-start.2
  23.2 4.3 %collective-permute-start.2 = (bf16[34,16,128]{2,1,0:T(8,128)(2,1)S(1)}, bf16[34,16,128]{2,1,0:T(8,128)(2,1)S(1)}, u32[]{:S(2)}, u32[]{:S(2)}) collective-permute-start(bf16[34,16,128]{2,1,0:T(8,128)(2,1)S(1)} %get-tuple-element.24), channel_id=1, source_target_pairs={{0,8},{8,16},{16,24},{24,32},{32,40},{40,48},{48,56},{1,9},{9,17},... | collective-permute-start | bytes 417800 | tf_op jit(solution)/shard_map/ppermute | solution.py:22
  27.5 1.3 %collective-permute-start.3 = (bf16[34,16,128]{2,1,0:T(8,128)(2,1)S(1)}, bf16[34,16,128]{2,1,0:T(8,128)(2,1)S(1)}, u32[]{:S(2)}, u32[]{:S(2)}) collective-permute-start(bf16[34,16,128]{2,1,0:T(8,128)(2,1)S(1)} %get-tuple-element.25), channel_id=1, source_target_pairs={{8,0},{16,8},{24,16},{32,24},{40,32},{48,40},{56,48},{9,1},{17,9},... | collective-permute-start | bytes 417800 | tf_op jit(solution)/shard_map/ppermute | solution.py:23
  28.8 1.3 %collective-permute-done.2.before = bf16[34,16,128]{2,1,0:T(8,128)(2,1)S(1)} collective-permute-done((bf16[34,16,128]{2,1,0:T(8,128)(2,1)S(1)}, bf16[34,16,128]{2,1,0:T(8,128)(2,1)S(1)}, u32[]{:S(2)}, u32[]{:S(2)}) %collective-permute-start.2) | collective-permute-done | bytes 139296 | tf_op jit(solution)/shard_map/ppermute | solution.py:22
  30.1 4.7 %collective-permute-done.3.after = bf16[34,16,128]{2,1,0:T(8,128)(2,1)S(1)} collective-permute-done((bf16[34,16,128]{2,1,0:T(8,128)(2,1)S(1)}, bf16[34,16,128]{2,1,0:T(8,128)(2,1)S(1)}, u32[]{:S(2)}, u32[]{:S(2)}) %collective-permute-start.3) | collective-permute-done | bytes 139296 | tf_op jit(solution)/shard_map/ppermute | solution.py:23
  34.8 0.0 copy-done.2
  34.8 2.1 %forward.1 = (bf16[16,16,128]{2,1,0:T(8,128)(2,1)S(1)}, bf16[17,16,128]{2,1,0:T(8,128)(2,1)S(1)}, bf16[10,16,128]{2,1,0:T(8,128)(2,1)S(1)}, bf16[7,16,128]{2,1,0:T(8,128)(2,1)S(1)}) custom-call(s32[1]{0:T(128)} %bitcast.at_ref, f32[16]{0:T(128)S(1)} %copy-done.2, bf16[3,96,256]{2,1,0:T(8,128)(2,1)S(1)} %bitcast.29, bf16[16,16,128]{2,1,0:T(8,128)(2,1)S(1)} %bitcast.28, ...), custom_call_target="tpu_custom_call" | custom-call | flops 339738624 | bytes 262144 | tf_op jit(solution)/shard_map/forward/pallas_call | solution.py:271
  36.9 1.9 %collective-permute-start.4 = (bf16[17,16,128]{2,1,0:T(8,128)(2,1)S(1)}, bf16[17,16,128]{2,1,0:T(8,128)(2,1)S(1)}, u32[]{:S(2)}, u32[]{:S(2)}) collective-permute-start(bf16[17,16,128]{2,1,0:T(8,128)(2,1)S(1)} %get-tuple-element.28.face), channel_id=1, source_target_pairs={{0,64},{64,0},{128,192},{192,128},{256,320},{320,256},{384,448},{4... | collective-permute-start | bytes 208904 | tf_op jit(solution)/shard_map/ppermute | solution.py:359
  38.9 1.2 %collective-permute-done.4.other.face_in = bf16[17,16,128]{2,1,0:T(8,128)(2,1)S(1)} collective-permute-done((bf16[17,16,128]{2,1,0:T(8,128)(2,1)S(1)}, bf16[17,16,128]{2,1,0:T(8,128)(2,1)S(1)}, u32[]{:S(2)}, u32[]{:S(2)}) %collective-permute-start.4) | collective-permute-done | bytes 69664 | tf_op jit(solution)/shard_map/ppermute | solution.py:359
  40.1 0.7 pair.1
  40.8 12.0 %all-to-all-start.1 = ((bf16[8,7,16,128]{3,2,1,0:T(8,128)(2,1)}), bf16[8,7,16,128]{3,2,1,0:T(8,128)(2,1)S(1)}, u32[]{:S(2)}, u32[]{:S(2)}) async-start(bf16[8,7,16,128]{3,2,1,0:T(8,128)(2,1)} %pair.1), calls=%async_computation.1 | async-start | bytes 458752 | tf_op jit(solution)/shard_map/all_to_all | solution.py:17
  52.8 4.4 %collective-permute-start.5 = (bf16[10,16,128]{2,1,0:T(8,128)(2,1)S(1)}, bf16[10,16,128]{2,1,0:T(8,128)(2,1)S(1)}, u32[]{:S(2)}, u32[]{:S(2)}) collective-permute-start(bf16[10,16,128]{2,1,0:T(8,128)(2,1)S(1)} %get-tuple-element.29.far), channel_id=1, source_target_pairs={{64,128},{128,64},{192,256},{256,192},{320,384},{384,320},{65,129}... | collective-permute-start | bytes 122888 | tf_op jit(solution)/shard_map/ppermute | solution.py:360
  57.2 2.5 %all-to-all-done.1.blocks = bf16[8,7,16,128]{3,2,1,0:T(8,128)(2,1)S(1)} async-done(((bf16[8,7,16,128]{3,2,1,0:T(8,128)(2,1)}), bf16[8,7,16,128]{3,2,1,0:T(8,128)(2,1)S(1)}, u32[]{:S(2)}, u32[]{:S(2)}) %all-to-all-start.1) | async-done | bytes 229408 | tf_op jit(solution)/shard_map/all_to_all | solution.py:17
  59.8 0.7 sums.2
  60.4 4.6 %all-to-all-start.2 = ((bf16[4,7,16,128]{3,2,1,0:T(8,128)(2,1)}), bf16[4,7,16,128]{3,2,1,0:T(8,128)(2,1)S(1)}, u32[]{:S(2)}, u32[]{:S(2)}) async-start(bf16[4,7,16,128]{3,2,1,0:T(8,128)(2,1)} %sums.2), calls=%async_computation.2 | async-start | bytes 229376 | tf_op jit(solution)/shard_map/all_to_all | solution.py:17
  65.1 0.0 collective-permute-done.5.far_in
  65.1 1.3 %backward.1 = bf16[8,8,16,128]{3,2,1,0:T(8,128)(2,1)} custom-call(s32[1]{0:T(128)} %bitcast.at_ref, bf16[432,64]{1,0:T(8,128)(2,1)S(1)} %bitcast.33, bf16[17,16,128]{2,1,0:T(8,128)(2,1)S(1)} %get-tuple-element.28.face, bf16[10,16,128]{2,1,0:T(8,128)(2,1)S(1)} %get-tuple-element.29.far, bf16[17,16,128]{2,1,0:T(8,128)(2,1)S(1)} %collective-permute-done.4.other.face_in, ...), custom_call_target="tpu_custom_call" | custom-call | flops 7247757312 | bytes 262144 | tf_op jit(solution)/shard_map/backward/pallas_call | solution.py:271
  66.4 7.4 %all-to-all-done.2.blocks = bf16[4,7,16,128]{3,2,1,0:T(8,128)(2,1)S(1)} async-done(((bf16[4,7,16,128]{3,2,1,0:T(8,128)(2,1)}), bf16[4,7,16,128]{3,2,1,0:T(8,128)(2,1)S(1)}, u32[]{:S(2)}, u32[]{:S(2)}) %all-to-all-start.2) | async-done | bytes 114720 | tf_op jit(solution)/shard_map/all_to_all | solution.py:17
  73.8 4.3 %all-to-all-start.3 = ((bf16[8,8,16,128]{3,2,1,0:T(8,128)(2,1)}), bf16[8,8,16,128]{3,2,1,0:T(8,128)(2,1)S(1)}, u32[]{:S(2)}, u32[]{:S(2)}) async-start(bf16[8,8,16,128]{3,2,1,0:T(8,128)(2,1)} %backward.1), calls=%async_computation.3 | async-start | bytes 524288 | tf_op jit(solution)/shard_map/all_to_all | solution.py:17
  78.2 1.9 %collective-permute-start.6 = (bf16[7,16,128]{2,1,0:T(8,128)(2,1)S(1)}, bf16[7,16,128]{2,1,0:T(8,128)(2,1)S(1)}, u32[]{:S(2)}, u32[]{:S(2)}) collective-permute-start(bf16[7,16,128]{2,1,0:T(8,128)(2,1)S(1)} %bitcast.30), channel_id=1, source_target_pairs={{0,64},{64,0},{128,192},{192,128},{256,320},{320,256},{384,448},{4... | collective-permute-start | bytes 86024 | tf_op jit(solution)/shard_map/ppermute | solution.py:391
  80.1 0.6 copy.21
  80.7 0.5 collective-permute-done.6.other
  81.3 0.8 weights.1
  82.0 2.3 %all-to-all-done.3.parts = bf16[8,8,16,128]{3,2,1,0:T(8,128)(2,1)S(1)} async-done(((bf16[8,8,16,128]{3,2,1,0:T(8,128)(2,1)}), bf16[8,8,16,128]{3,2,1,0:T(8,128)(2,1)S(1)}, u32[]{:S(2)}, u32[]{:S(2)}) %all-to-all-start.3) | async-done | bytes 262176 | tf_op jit(solution)/shard_map/all_to_all | solution.py:17
  84.3 0.7 unpack.1
  (6 shorter events, 0.1 us)
Async XLA Ops:
  0.6 0.8 copy-start.1
  1.4 7.2 %collective-permute-start.1 = (bf16[4,16,128]{2,1,0:T(8,128)(2,1)S(1)}, bf16[4,16,128]{2,1,0:T(8,128)(2,1)S(1)}, u32[]{:S(2)}, u32[]{:S(2)}) collective-permute-start(bf16[4,16,128]{2,1,0:T(8,128)(2,1)S(1)} %far.1), channel_id=1, source_target_pairs={{64,128},{128,64},{192,256},{256,192},{320,384},{384,320},{65,129}... | collective-permute-start | bytes 49160 | tf_op jit(solution)/shard_map/ppermute | solution.py:306
  4.0 4.6 %collective-permute-start = (bf16[4,16,128]{2,1,0:T(8,128)(2,1)S(1)}, bf16[4,16,128]{2,1,0:T(8,128)(2,1)S(1)}, u32[]{:S(2)}, u32[]{:S(2)}) collective-permute-start(bf16[4,16,128]{2,1,0:T(8,128)(2,1)S(1)} %get-tuple-element.20), channel_id=1, source_target_pairs={{0,64},{64,0},{128,192},{192,128},{256,320},{320,256},{384,448},{4... | collective-permute-start | bytes 49160 | tf_op jit(solution)/shard_map/ppermute | solution.py:304
  9.5 5.9 %copy-start.4 = (bf16[16,2,8,128]{3,2,1,0:T(8,128)(2,1)S(1)}, bf16[16,2,8,128]{3,2,1,0:T(8,128)(2,1)}, u32[]{:S(2)}) copy-start(bf16[16,2,8,128]{3,2,1,0:T(8,128)(2,1)} %param.8) | copy-start | bytes 196612
  9.5 13.7 %all-to-all-start = ((bf16[8,4,4,16,128]{4,3,2,1,0:T(8,128)(2,1)}), bf16[8,4,4,16,128]{4,3,2,1,0:T(8,128)(2,1)S(1)}, u32[]{:S(2)}, u32[]{:S(2)}) async-start(bf16[8,4,4,16,128]{4,3,2,1,0:T(8,128)(2,1)} %grid.1), calls=%async_computation | async-start | bytes 1048576 | tf_op jit(solution)/shard_map/all_to_all | solution.py:17
  15.4 0.9 %copy-start = (bf16[27,64,16]{1,2,0:T(8,128)(2,1)S(1)}, bf16[27,64,16]{1,2,0:T(8,128)(2,1)}, u32[]{:S(2)}) copy-start(bf16[27,64,16]{1,2,0:T(8,128)(2,1)} %param.6) | copy-start | bytes 165892
  16.3 0.9 %copy-start.3 = (bf16[2,192,256,1]{2,1,3,0:T(8,128)(2,1)S(1)}, bf16[2,192,256,1]{2,1,3,0:T(8,128)(2,1)}, u32[]{:S(2)}) copy-start(bf16[2,192,256,1]{2,1,3,0:T(8,128)(2,1)} %constant.24) | copy-start | bytes 589828
  23.2 11.6 %copy-start.2 = (f32[16]{0:T(128)S(1)}, f32[16]{0:T(128)}, u32[]{:S(2)}) copy-start(f32[16]{0:T(128)} %bias_ref.1) | copy-start | bytes 196
  23.2 6.9 %collective-permute-start.2 = (bf16[34,16,128]{2,1,0:T(8,128)(2,1)S(1)}, bf16[34,16,128]{2,1,0:T(8,128)(2,1)S(1)}, u32[]{:S(2)}, u32[]{:S(2)}) collective-permute-start(bf16[34,16,128]{2,1,0:T(8,128)(2,1)S(1)} %get-tuple-element.24), channel_id=1, source_target_pairs={{0,8},{8,16},{16,24},{24,32},{32,40},{40,48},{48,56},{1,9},{9,17},... | collective-permute-start | bytes 417800 | tf_op jit(solution)/shard_map/ppermute | solution.py:22
  27.5 7.3 %collective-permute-start.3 = (bf16[34,16,128]{2,1,0:T(8,128)(2,1)S(1)}, bf16[34,16,128]{2,1,0:T(8,128)(2,1)S(1)}, u32[]{:S(2)}, u32[]{:S(2)}) collective-permute-start(bf16[34,16,128]{2,1,0:T(8,128)(2,1)S(1)} %get-tuple-element.25), channel_id=1, source_target_pairs={{8,0},{16,8},{24,16},{32,24},{40,32},{48,40},{56,48},{9,1},{17,9},... | collective-permute-start | bytes 417800 | tf_op jit(solution)/shard_map/ppermute | solution.py:23
  36.9 3.2 %collective-permute-start.4 = (bf16[17,16,128]{2,1,0:T(8,128)(2,1)S(1)}, bf16[17,16,128]{2,1,0:T(8,128)(2,1)S(1)}, u32[]{:S(2)}, u32[]{:S(2)}) collective-permute-start(bf16[17,16,128]{2,1,0:T(8,128)(2,1)S(1)} %get-tuple-element.28.face), channel_id=1, source_target_pairs={{0,64},{64,0},{128,192},{192,128},{256,320},{320,256},{384,448},{4... | collective-permute-start | bytes 208904 | tf_op jit(solution)/shard_map/ppermute | solution.py:359
  40.8 19.0 %all-to-all-start.1 = ((bf16[8,7,16,128]{3,2,1,0:T(8,128)(2,1)}), bf16[8,7,16,128]{3,2,1,0:T(8,128)(2,1)S(1)}, u32[]{:S(2)}, u32[]{:S(2)}) async-start(bf16[8,7,16,128]{3,2,1,0:T(8,128)(2,1)} %pair.1), calls=%async_computation.1 | async-start | bytes 458752 | tf_op jit(solution)/shard_map/all_to_all | solution.py:17
  52.8 12.3 %collective-permute-start.5 = (bf16[10,16,128]{2,1,0:T(8,128)(2,1)S(1)}, bf16[10,16,128]{2,1,0:T(8,128)(2,1)S(1)}, u32[]{:S(2)}, u32[]{:S(2)}) collective-permute-start(bf16[10,16,128]{2,1,0:T(8,128)(2,1)S(1)} %get-tuple-element.29.far), channel_id=1, source_target_pairs={{64,128},{128,64},{192,256},{256,192},{320,384},{384,320},{65,129}... | collective-permute-start | bytes 122888 | tf_op jit(solution)/shard_map/ppermute | solution.py:360
  60.4 13.4 %all-to-all-start.2 = ((bf16[4,7,16,128]{3,2,1,0:T(8,128)(2,1)}), bf16[4,7,16,128]{3,2,1,0:T(8,128)(2,1)S(1)}, u32[]{:S(2)}, u32[]{:S(2)}) async-start(bf16[4,7,16,128]{3,2,1,0:T(8,128)(2,1)} %sums.2), calls=%async_computation.2 | async-start | bytes 229376 | tf_op jit(solution)/shard_map/all_to_all | solution.py:17
  73.8 10.5 %all-to-all-start.3 = ((bf16[8,8,16,128]{3,2,1,0:T(8,128)(2,1)}), bf16[8,8,16,128]{3,2,1,0:T(8,128)(2,1)S(1)}, u32[]{:S(2)}, u32[]{:S(2)}) async-start(bf16[8,8,16,128]{3,2,1,0:T(8,128)(2,1)} %backward.1), calls=%async_computation.3 | async-start | bytes 524288 | tf_op jit(solution)/shard_map/all_to_all | solution.py:17
  78.2 3.1 %collective-permute-start.6 = (bf16[7,16,128]{2,1,0:T(8,128)(2,1)S(1)}, bf16[7,16,128]{2,1,0:T(8,128)(2,1)S(1)}, u32[]{:S(2)}, u32[]{:S(2)}) collective-permute-start(bf16[7,16,128]{2,1,0:T(8,128)(2,1)S(1)} %bitcast.30), channel_id=1, source_target_pairs={{0,64},{64,0},{128,192},{192,128},{256,320},{320,256},{384,448},{4... | collective-permute-start | bytes 86024 | tf_op jit(solution)/shard_map/ppermute | solution.py:391

commit v21 on v20

--- a/solution.py
+++ b/solution.py
@@ -19,8 +19,8 @@
 
 def neighbours(first, last, axis):
     ends = lax.axis_size(axis) - 1
+    after = lax.ppermute(first, axis, [(i + 1, i) for i in range(ends)])
     before = lax.ppermute(last, axis, [(i, i + 1) for i in range(ends)])
-    after = lax.ppermute(first, axis, [(i + 1, i) for i in range(ends)])
     return before, after
 
 
@@ -97,7 +97,7 @@
         out_ref[c] = wide[pl.ds(c, lines, stride=count), :].astype(BF16)
 
 
-def forward_kernel(planes, rows, at_ref, bias_ref, w_ref, cot, tiles, before, after, *refs):
+def forward_kernel(planes, rows, at_ref, bias_ref, w_ref, cot, tiles, after, before, *refs):
     out_ref, face_ref, far_ref, kept_ref, grads, halves = refs
     cout, width = cot.shape[1:]
     sources = tiles.shape[0]
@@ -345,8 +345,8 @@
         w_forward,
         cot,
         tiles,
+        after,
         before,
-        after,
         out=[(k, cout, width) for k in (cells, rows + 2 + count, rows + 2, count)],
         scratch=[((planes, rows + 2, cout, width), BF16), ((2, count, cout, width), BF16)],
         flops=3 * work,

time: 85.8 us -> 84.3 us (0.983)
  the two profiles are of different devices: /device:TPU:40 before, /device:TPU:16 now
where the time goes in v21:
time: 84.3 us; the launch traced here: 83.5 us
  starting transfers between devices  46 us (55%)
  waiting for transfers between devices  26.1 us (31%)
  Pallas kernels  7.21 us (9%)
  local copies, waits for them, and re-layouts  3.21 us (4%)
    all_to_all x4, starting transfers between devices, swapped(): lax.all_to_all(blocks, axis, 0, 0, tiled=True, axis_index_groups=groups)  26.3 us
    all_to_all x4, waiting for transfers between devices, swapped(): lax.all_to_all(blocks, axis, 0, 0, tiled=True, axis_index_groups=groups)  20.9 us
    pallas_call x11, Pallas kernels, call(): pl.pallas_call(body, out_shape=outs, in_specs=[smem] * scalars + [vmem] *...  7.21 us
    ppermute x1, starting transfers between devices, per_device(): facing = lax.ppermute(face, 'depth', swap)  5.81 us
    ppermute x1, starting transfers between devices, neighbours(): before = lax.ppermute(last, axis, [(i, i + 1) for i in range(ends)])  4.91 us
    unnamed x10, local copies, waits for them, and re-layouts  2.33 us
    ppermute x1, starting transfers between devices, per_device(): beyond = lax.ppermute(far, 'depth', cross)  1.92 us
    ppermute x1, starting transfers between devices, per_device(): other = lax.ppermute(mine, 'depth', swap)  1.92 us
  transfers between devices with their start and end apart: 11, of which 9 were waited for; matrix products, arithmetic and copies ran while one was open for 1% of the time, Pallas kernels for 3%

profile of v21, /device:TPU:16, one launch (start us, length us, event | category | flops | bytes accessed | tf_op | source)
XLA Modules:
  0.0 83.5 jit_solution(17975973888578211937)
XLA Ops:
  0.6 0.0 copy-start.1
  0.7 0.7 copy-done.1
  1.4 1.9 %collective-permute-start.1 = (bf16[4,16,128]{2,1,0:T(8,128)(2,1)S(1)}, bf16[4,16,128]{2,1,0:T(8,128)(2,1)S(1)}, u32[]{:S(2)}, u32[]{:S(2)}) collective-permute-start(bf16[4,16,128]{2,1,0:T(8,128)(2,1)S(1)} %far.1), channel_id=1, source_target_pairs={{64,128},{128,64},{192,256},{256,192},{320,384},{384,320},{65,129}... | collective-permute-start | bytes 49160 | tf_op jit(solution)/shard_map/ppermute | solution.py:306
  3.4 5.8 %collective-permute-start = (bf16[4,16,128]{2,1,0:T(8,128)(2,1)S(1)}, bf16[4,16,128]{2,1,0:T(8,128)(2,1)S(1)}, u32[]{:S(2)}, u32[]{:S(2)}) collective-permute-start(bf16[4,16,128]{2,1,0:T(8,128)(2,1)S(1)} %get-tuple-element.20), channel_id=1, source_target_pairs={{0,64},{64,0},{128,192},{192,128},{256,320},{320,256},{384,448},{4... | collective-permute-start | bytes 49160 | tf_op jit(solution)/shard_map/ppermute | solution.py:304
  9.2 0.0 collective-permute-done.1.beyond
  9.2 0.8 collective-permute-done.facing
  10.0 0.9 %grid.1 = bf16[8,4,4,16,128]{4,3,2,1,0:T(8,128)(2,1)} custom-call(s32[1]{0:T(128)} %bitcast.at_ref, bf16[2,4,16,128]{3,2,1,0:T(8,128)(2,1)S(1)} %get-tuple-element.19.own, bf16[4,16,128]{2,1,0:T(8,128)(2,1)S(1)} %collective-permute-done.facing, bf16[4,16,128]{2,1,0:T(8,128)(2,1)S(1)} %collective-permute-done.1.beyond), custom_call_target="tpu_custom_call" | custom-call | bytes 262144 | tf_op jit(solution)/shard_map/grid/pallas_call | solution.py:271
  10.9 0.0 copy-start.4
  10.9 4.5 %all-to-all-start = ((bf16[8,4,4,16,128]{4,3,2,1,0:T(8,128)(2,1)}), bf16[8,4,4,16,128]{4,3,2,1,0:T(8,128)(2,1)S(1)}, u32[]{:S(2)}, u32[]{:S(2)}) async-start(bf16[8,4,4,16,128]{4,3,2,1,0:T(8,128)(2,1)} %grid.1), calls=%async_computation | async-start | bytes 1048576 | tf_op jit(solution)/shard_map/all_to_all | solution.py:17
  15.4 0.0 copy-start
  15.4 0.0 copy-done.4
  15.5 0.9 %copy-done = bf16[27,64,16]{1,2,0:T(8,128)(2,1)S(1)} copy-done((bf16[27,64,16]{1,2,0:T(8,128)(2,1)S(1)}, bf16[27,64,16]{1,2,0:T(8,128)(2,1)}, u32[]{:S(2)}) %copy-start) | copy-done | bytes 55320
  16.3 0.0 copy-start.3
  16.3 0.1 copy.20
  16.4 0.1 reshape.49
  16.5 0.7 copy-done.3
  17.3 0.2 fusion
  17.5 8.6 %all-to-all-done.tiles = bf16[8,4,4,16,128]{4,3,2,1,0:T(8,128)(2,1)S(1)} async-done(((bf16[8,4,4,16,128]{4,3,2,1,0:T(8,128)(2,1)}), bf16[8,4,4,16,128]{4,3,2,1,0:T(8,128)(2,1)S(1)}, u32[]{:S(2)}, u32[]{:S(2)}) %all-to-all-start) | async-done | bytes 524320 | tf_op jit(solution)/shard_map/all_to_all | solution.py:17
  26.0 0.0 copy-start.2
  26.1 1.3 %collective-permute-start.2 = (bf16[34,16,128]{2,1,0:T(8,128)(2,1)S(1)}, bf16[34,16,128]{2,1,0:T(8,128)(2,1)S(1)}, u32[]{:S(2)}, u32[]{:S(2)}) collective-permute-start(bf16[34,16,128]{2,1,0:T(8,128)(2,1)S(1)} %get-tuple-element.24), channel_id=1, source_target_pairs={{8,0},{16,8},{24,16},{32,24},{40,32},{48,40},{56,48},{9,1},{17,9},... | collective-permute-start | bytes 417800 | tf_op jit(solution)/shard_map/ppermute | solution.py:22
  27.4 4.9 %collective-permute-start.3 = (bf16[34,16,128]{2,1,0:T(8,128)(2,1)S(1)}, bf16[34,16,128]{2,1,0:T(8,128)(2,1)S(1)}, u32[]{:S(2)}, u32[]{:S(2)}) collective-permute-start(bf16[34,16,128]{2,1,0:T(8,128)(2,1)S(1)} %get-tuple-element.25), channel_id=1, source_target_pairs={{0,8},{8,16},{16,24},{24,32},{32,40},{40,48},{48,56},{1,9},{9,17},... | collective-permute-start | bytes 417800 | tf_op jit(solution)/shard_map/ppermute | solution.py:23
  32.3 1.1 %collective-permute-done.2.after = bf16[34,16,128]{2,1,0:T(8,128)(2,1)S(1)} collective-permute-done((bf16[34,16,128]{2,1,0:T(8,128)(2,1)S(1)}, bf16[34,16,128]{2,1,0:T(8,128)(2,1)S(1)}, u32[]{:S(2)}, u32[]{:S(2)}) %collective-permute-start.2) | collective-permute-done | bytes 139296 | tf_op jit(solution)/shard_map/ppermute | solution.py:22
  33.4 1.5 %collective-permute-done.3.before = bf16[34,16,128]{2,1,0:T(8,128)(2,1)S(1)} collective-permute-done((bf16[34,16,128]{2,1,0:T(8,128)(2,1)S(1)}, bf16[34,16,128]{2,1,0:T(8,128)(2,1)S(1)}, u32[]{:S(2)}, u32[]{:S(2)}) %collective-permute-start.3) | collective-permute-done | bytes 139296 | tf_op jit(solution)/shard_map/ppermute | solution.py:23
  34.8 0.0 copy-done.2
  34.9 2.1 %forward.1 = (bf16[16,16,128]{2,1,0:T(8,128)(2,1)S(1)}, bf16[17,16,128]{2,1,0:T(8,128)(2,1)S(1)}, bf16[10,16,128]{2,1,0:T(8,128)(2,1)S(1)}, bf16[7,16,128]{2,1,0:T(8,128)(2,1)S(1)}) custom-call(s32[1]{0:T(128)} %bitcast.at_ref, f32[16]{0:T(128)S(1)} %copy-done.2, bf16[3,96,256]{2,1,0:T(8,128)(2,1)S(1)} %bitcast.29, bf16[16,16,128]{2,1,0:T(8,128)(2,1)S(1)} %bitcast.28, ...), custom_call_target="tpu_custom_call" | custom-call | flops 339738624 | bytes 262144 | tf_op jit(solution)/shard_map/forward/pallas_call | solution.py:271
  37.0 1.9 %collective-permute-start.4 = (bf16[17,16,128]{2,1,0:T(8,128)(2,1)S(1)}, bf16[17,16,128]{2,1,0:T(8,128)(2,1)S(1)}, u32[]{:S(2)}, u32[]{:S(2)}) collective-permute-start(bf16[17,16,128]{2,1,0:T(8,128)(2,1)S(1)} %get-tuple-element.28.face), channel_id=1, source_target_pairs={{0,64},{64,0},{128,192},{192,128},{256,320},{320,256},{384,448},{4... | collective-permute-start | bytes 208904 | tf_op jit(solution)/shard_map/ppermute | solution.py:359
  38.9 1.2 %collective-permute-done.4.other.face_in = bf16[17,16,128]{2,1,0:T(8,128)(2,1)S(1)} collective-permute-done((bf16[17,16,128]{2,1,0:T(8,128)(2,1)S(1)}, bf16[17,16,128]{2,1,0:T(8,128)(2,1)S(1)}, u32[]{:S(2)}, u32[]{:S(2)}) %collective-permute-start.4) | collective-permute-done | bytes 69664 | tf_op jit(solution)/shard_map/ppermute | solution.py:359
  40.1 0.7 pair.1
  40.8 13.0 %all-to-all-start.1 = ((bf16[8,7,16,128]{3,2,1,0:T(8,128)(2,1)}), bf16[8,7,16,128]{3,2,1,0:T(8,128)(2,1)S(1)}, u32[]{:S(2)}, u32[]{:S(2)}) async-start(bf16[8,7,16,128]{3,2,1,0:T(8,128)(2,1)} %pair.1), calls=%async_computation.1 | async-start | bytes 458752 | tf_op jit(solution)/shard_map/all_to_all | solution.py:17
  53.8 1.9 %collective-permute-start.5 = (bf16[10,16,128]{2,1,0:T(8,128)(2,1)S(1)}, bf16[10,16,128]{2,1,0:T(8,128)(2,1)S(1)}, u32[]{:S(2)}, u32[]{:S(2)}) collective-permute-start(bf16[10,16,128]{2,1,0:T(8,128)(2,1)S(1)} %get-tuple-element.29.far), channel_id=1, source_target_pairs={{64,128},{128,64},{192,256},{256,192},{320,384},{384,320},{65,129}... | collective-permute-start | bytes 122888 | tf_op jit(solution)/shard_map/ppermute | solution.py:360
  55.7 5.4 %all-to-all-done.1.blocks = bf16[8,7,16,128]{3,2,1,0:T(8,128)(2,1)S(1)} async-done(((bf16[8,7,16,128]{3,2,1,0:T(8,128)(2,1)}), bf16[8,7,16,128]{3,2,1,0:T(8,128)(2,1)S(1)}, u32[]{:S(2)}, u32[]{:S(2)}) %all-to-all-start.1) | async-done | bytes 229408 | tf_op jit(solution)/shard_map/all_to_all | solution.py:17
  61.0 0.7 sums.2
  61.7 5.4 %all-to-all-start.2 = ((bf16[4,7,16,128]{3,2,1,0:T(8,128)(2,1)}), bf16[4,7,16,128]{3,2,1,0:T(8,128)(2,1)S(1)}, u32[]{:S(2)}, u32[]{:S(2)}) async-start(bf16[4,7,16,128]{3,2,1,0:T(8,128)(2,1)} %sums.2), calls=%async_computation.2 | async-start | bytes 229376 | tf_op jit(solution)/shard_map/all_to_all | solution.py:17
  67.1 0.0 collective-permute-done.5.far_in
  67.1 1.3 %backward.1 = bf16[8,8,16,128]{3,2,1,0:T(8,128)(2,1)} custom-call(s32[1]{0:T(128)} %bitcast.at_ref, bf16[432,64]{1,0:T(8,128)(2,1)S(1)} %bitcast.33, bf16[17,16,128]{2,1,0:T(8,128)(2,1)S(1)} %get-tuple-element.28.face, bf16[10,16,128]{2,1,0:T(8,128)(2,1)S(1)} %get-tuple-element.29.far, bf16[17,16,128]{2,1,0:T(8,128)(2,1)S(1)} %collective-permute-done.4.other.face_in, ...), custom_call_target="tpu_custom_call" | custom-call | flops 7247757312 | bytes 262144 | tf_op jit(solution)/shard_map/backward/pallas_call | solution.py:271
  68.5 3.7 %all-to-all-done.2.blocks = bf16[4,7,16,128]{3,2,1,0:T(8,128)(2,1)S(1)} async-done(((bf16[4,7,16,128]{3,2,1,0:T(8,128)(2,1)}), bf16[4,7,16,128]{3,2,1,0:T(8,128)(2,1)S(1)}, u32[]{:S(2)}, u32[]{:S(2)}) %all-to-all-start.2) | async-done | bytes 114720 | tf_op jit(solution)/shard_map/all_to_all | solution.py:17
  72.2 3.4 %all-to-all-start.3 = ((bf16[8,8,16,128]{3,2,1,0:T(8,128)(2,1)}), bf16[8,8,16,128]{3,2,1,0:T(8,128)(2,1)S(1)}, u32[]{:S(2)}, u32[]{:S(2)}) async-start(bf16[8,8,16,128]{3,2,1,0:T(8,128)(2,1)} %backward.1), calls=%async_computation.3 | async-start | bytes 524288 | tf_op jit(solution)/shard_map/all_to_all | solution.py:17
  75.6 1.9 %collective-permute-start.6 = (bf16[7,16,128]{2,1,0:T(8,128)(2,1)S(1)}, bf16[7,16,128]{2,1,0:T(8,128)(2,1)S(1)}, u32[]{:S(2)}, u32[]{:S(2)}) collective-permute-start(bf16[7,16,128]{2,1,0:T(8,128)(2,1)S(1)} %bitcast.30), channel_id=1, source_target_pairs={{0,64},{64,0},{128,192},{192,128},{256,320},{320,256},{384,448},{4... | collective-permute-start | bytes 86024 | tf_op jit(solution)/shard_map/ppermute | solution.py:391
  77.5 0.6 copy.21
  78.2 0.5 collective-permute-done.6.other
  78.7 0.8 weights.1
  79.5 3.3 %all-to-all-done.3.parts = bf16[8,8,16,128]{3,2,1,0:T(8,128)(2,1)S(1)} async-done(((bf16[8,8,16,128]{3,2,1,0:T(8,128)(2,1)}), bf16[8,8,16,128]{3,2,1,0:T(8,128)(2,1)S(1)}, u32[]{:S(2)}, u32[]{:S(2)}) %all-to-all-start.3) | async-done | bytes 262176 | tf_op jit(solution)/shard_map/all_to_all | solution.py:17
  82.8 0.7 unpack.1
  (6 shorter events, 0.1 us)
Async XLA Ops:
  0.6 0.8 copy-start.1
  1.4 7.8 %collective-permute-start.1 = (bf16[4,16,128]{2,1,0:T(8,128)(2,1)S(1)}, bf16[4,16,128]{2,1,0:T(8,128)(2,1)S(1)}, u32[]{:S(2)}, u32[]{:S(2)}) collective-permute-start(bf16[4,16,128]{2,1,0:T(8,128)(2,1)S(1)} %far.1), channel_id=1, source_target_pairs={{64,128},{128,64},{192,256},{256,192},{320,384},{384,320},{65,129}... | collective-permute-start | bytes 49160 | tf_op jit(solution)/shard_map/ppermute | solution.py:306
  3.4 6.6 %collective-permute-start = (bf16[4,16,128]{2,1,0:T(8,128)(2,1)S(1)}, bf16[4,16,128]{2,1,0:T(8,128)(2,1)S(1)}, u32[]{:S(2)}, u32[]{:S(2)}) collective-permute-start(bf16[4,16,128]{2,1,0:T(8,128)(2,1)S(1)} %get-tuple-element.20), channel_id=1, source_target_pairs={{0,64},{64,0},{128,192},{192,128},{256,320},{320,256},{384,448},{4... | collective-permute-start | bytes 49160 | tf_op jit(solution)/shard_map/ppermute | solution.py:304
  10.9 4.6 %copy-start.4 = (bf16[16,2,8,128]{3,2,1,0:T(8,128)(2,1)S(1)}, bf16[16,2,8,128]{3,2,1,0:T(8,128)(2,1)}, u32[]{:S(2)}) copy-start(bf16[16,2,8,128]{3,2,1,0:T(8,128)(2,1)} %param.8) | copy-start | bytes 196612
  10.9 15.1 %all-to-all-start = ((bf16[8,4,4,16,128]{4,3,2,1,0:T(8,128)(2,1)}), bf16[8,4,4,16,128]{4,3,2,1,0:T(8,128)(2,1)S(1)}, u32[]{:S(2)}, u32[]{:S(2)}) async-start(bf16[8,4,4,16,128]{4,3,2,1,0:T(8,128)(2,1)} %grid.1), calls=%async_computation | async-start | bytes 1048576 | tf_op jit(solution)/shard_map/all_to_all | solution.py:17
  15.4 0.9 %copy-start = (bf16[27,64,16]{1,2,0:T(8,128)(2,1)S(1)}, bf16[27,64,16]{1,2,0:T(8,128)(2,1)}, u32[]{:S(2)}) copy-start(bf16[27,64,16]{1,2,0:T(8,128)(2,1)} %param.6) | copy-start | bytes 165892
  16.3 0.9 %copy-start.3 = (bf16[2,192,256,1]{2,1,3,0:T(8,128)(2,1)S(1)}, bf16[2,192,256,1]{2,1,3,0:T(8,128)(2,1)}, u32[]{:S(2)}) copy-start(bf16[2,192,256,1]{2,1,3,0:T(8,128)(2,1)} %constant.24) | copy-start | bytes 589828
  26.0 8.8 %copy-start.2 = (f32[16]{0:T(128)S(1)}, f32[16]{0:T(128)}, u32[]{:S(2)}) copy-start(f32[16]{0:T(128)} %bias_ref.1) | copy-start | bytes 196
  26.1 7.3 %collective-permute-start.2 = (bf16[34,16,128]{2,1,0:T(8,128)(2,1)S(1)}, bf16[34,16,128]{2,1,0:T(8,128)(2,1)S(1)}, u32[]{:S(2)}, u32[]{:S(2)}) collective-permute-start(bf16[34,16,128]{2,1,0:T(8,128)(2,1)S(1)} %get-tuple-element.24), channel_id=1, source_target_pairs={{8,0},{16,8},{24,16},{32,24},{40,32},{48,40},{56,48},{9,1},{17,9},... | collective-permute-start | bytes 417800 | tf_op jit(solution)/shard_map/ppermute | solution.py:22
  27.4 7.5 %collective-permute-start.3 = (bf16[34,16,128]{2,1,0:T(8,128)(2,1)S(1)}, bf16[34,16,128]{2,1,0:T(8,128)(2,1)S(1)}, u32[]{:S(2)}, u32[]{:S(2)}) collective-permute-start(bf16[34,16,128]{2,1,0:T(8,128)(2,1)S(1)} %get-tuple-element.25), channel_id=1, source_target_pairs={{0,8},{8,16},{16,24},{24,32},{32,40},{40,48},{48,56},{1,9},{9,17},... | collective-permute-start | bytes 417800 | tf_op jit(solution)/shard_map/ppermute | solution.py:23
  37.0 3.2 %collective-permute-start.4 = (bf16[17,16,128]{2,1,0:T(8,128)(2,1)S(1)}, bf16[17,16,128]{2,1,0:T(8,128)(2,1)S(1)}, u32[]{:S(2)}, u32[]{:S(2)}) collective-permute-start(bf16[17,16,128]{2,1,0:T(8,128)(2,1)S(1)} %get-tuple-element.28.face), channel_id=1, source_target_pairs={{0,64},{64,0},{128,192},{192,128},{256,320},{320,256},{384,448},{4... | collective-permute-start | bytes 208904 | tf_op jit(solution)/shard_map/ppermute | solution.py:359
  40.8 20.2 %all-to-all-start.1 = ((bf16[8,7,16,128]{3,2,1,0:T(8,128)(2,1)}), bf16[8,7,16,128]{3,2,1,0:T(8,128)(2,1)S(1)}, u32[]{:S(2)}, u32[]{:S(2)}) async-start(bf16[8,7,16,128]{3,2,1,0:T(8,128)(2,1)} %pair.1), calls=%async_computation.1 | async-start | bytes 458752 | tf_op jit(solution)/shard_map/all_to_all | solution.py:17
  53.8 13.4 %collective-permute-start.5 = (bf16[10,16,128]{2,1,0:T(8,128)(2,1)S(1)}, bf16[10,16,128]{2,1,0:T(8,128)(2,1)S(1)}, u32[]{:S(2)}, u32[]{:S(2)}) collective-permute-start(bf16[10,16,128]{2,1,0:T(8,128)(2,1)S(1)} %get-tuple-element.29.far), channel_id=1, source_target_pairs={{64,128},{128,64},{192,256},{256,192},{320,384},{384,320},{65,129}... | collective-permute-start | bytes 122888 | tf_op jit(solution)/shard_map/ppermute | solution.py:360
  61.7 10.4 %all-to-all-start.2 = ((bf16[4,7,16,128]{3,2,1,0:T(8,128)(2,1)}), bf16[4,7,16,128]{3,2,1,0:T(8,128)(2,1)S(1)}, u32[]{:S(2)}, u32[]{:S(2)}) async-start(bf16[4,7,16,128]{3,2,1,0:T(8,128)(2,1)} %sums.2), calls=%async_computation.2 | async-start | bytes 229376 | tf_op jit(solution)/shard_map/all_to_all | solution.py:17
  72.2 10.6 %all-to-all-start.3 = ((bf16[8,8,16,128]{3,2,1,0:T(8,128)(2,1)}), bf16[8,8,16,128]{3,2,1,0:T(8,128)(2,1)S(1)}, u32[]{:S(2)}, u32[]{:S(2)}) async-start(bf16[8,8,16,128]{3,2,1,0:T(8,128)(2,1)} %backward.1), calls=%async_computation.3 | async-start | bytes 524288 | tf_op jit(solution)/shard_map/all_to_all | solution.py:17
  75.6 3.1 %collective-permute-start.6 = (bf16[7,16,128]{2,1,0:T(8,128)(2,1)S(1)}, bf16[7,16,128]{2,1,0:T(8,128)(2,1)S(1)}, u32[]{:S(2)}, u32[]{:S(2)}) collective-permute-start(bf16[7,16,128]{2,1,0:T(8,128)(2,1)S(1)} %bitcast.30), channel_id=1, source_target_pairs={{0,64},{64,0},{128,192},{192,128},{256,320},{320,256},{384,448},{4... | collective-permute-start | bytes 86024 | tf_op jit(solution)/shard_map/ppermute | solution.py:391

commit v22 on v21

--- a/solution.py
+++ b/solution.py
@@ -358,7 +358,7 @@
     size = kept_sums.shape
     face_in = lax.ppermute(face, "depth", swap)
     far_in = lax.ppermute(far, "depth", cross)
-    groups = [[(i + height - 2) % height for i in range(height)]]
+    groups = [list(range(2, height))[::-1] + [0, 1]]
     sums = call(pair_kernel, "pair", kept_sums, face_in, out=[(height,) + size])
     sums = swapped(sums, "height", groups)
     parts = call(

time: 84.3 us -> 85 us (level)
  the two profiles are of different devices: /device:TPU:16 before, /device:TPU:64 now
where the time goes in v22:
time: 85 us; the launch traced here: 84.2 us
  starting transfers between devices  45.8 us (54%)
  waiting for transfers between devices  26.9 us (32%)
  Pallas kernels  7.21 us (8%)
  local copies, waits for them, and re-layouts  3.2 us (4%)
    all_to_all x4, starting transfers between devices, swapped(): lax.all_to_all(blocks, axis, 0, 0, tiled=True, axis_index_groups=groups)  28.6 us
    all_to_all x4, waiting for transfers between devices, swapped(): lax.all_to_all(blocks, axis, 0, 0, tiled=True, axis_index_groups=groups)  21.7 us
    pallas_call x11, Pallas kernels, call(): pl.pallas_call(body, out_shape=outs, in_specs=[smem] * scalars + [vmem] *...  7.21 us
    ppermute x1, starting transfers between devices, per_device(): facing = lax.ppermute(face, 'depth', swap)  5.86 us
    ppermute x1, starting transfers between devices, neighbours(): before = lax.ppermute(last, axis, [(i, i + 1) for i in range(ends)])  4.28 us
    unnamed x10, local copies, waits for them, and re-layouts  2.33 us
    ppermute x1, starting transfers between devices, neighbours(): after = lax.ppermute(first, axis, [(i + 1, i) for i in range(ends)])  1.92 us
    ppermute x1, starting transfers between devices, per_device(): other = lax.ppermute(mine, 'depth', swap)  1.92 us
  transfers between devices with their start and end apart: 11, of which 9 were waited for; matrix products, arithmetic and copies ran while one was open for 1% of the time, Pallas kernels for 3%

profile of v22, /device:TPU:64, one launch (start us, length us, event | category | flops | bytes accessed | tf_op | source)
XLA Modules:
  0.0 84.2 jit_solution(17599366188882283841)
XLA Ops:
  0.6 0.0 copy-start.1
  0.7 0.7 copy-done.1
  1.4 0.7 collective-permute-start.1
  2.1 5.9 %collective-permute-start = (bf16[4,16,128]{2,1,0:T(8,128)(2,1)S(1)}, bf16[4,16,128]{2,1,0:T(8,128)(2,1)S(1)}, u32[]{:S(2)}, u32[]{:S(2)}) collective-permute-start(bf16[4,16,128]{2,1,0:T(8,128)(2,1)S(1)} %get-tuple-element.20), channel_id=1, source_target_pairs={{0,64},{64,0},{128,192},{192,128},{256,320},{320,256},{384,448},{4... | collective-permute-start | bytes 49160 | tf_op jit(solution)/shard_map/ppermute | solution.py:304
  8.0 0.0 collective-permute-done.1.beyond
  8.0 0.8 collective-permute-done.facing
  8.8 0.9 %grid.1 = bf16[8,4,4,16,128]{4,3,2,1,0:T(8,128)(2,1)} custom-call(s32[1]{0:T(128)} %bitcast.at_ref, bf16[2,4,16,128]{3,2,1,0:T(8,128)(2,1)S(1)} %get-tuple-element.19.own, bf16[4,16,128]{2,1,0:T(8,128)(2,1)S(1)} %collective-permute-done.facing, bf16[4,16,128]{2,1,0:T(8,128)(2,1)S(1)} %collective-permute-done.1.beyond), custom_call_target="tpu_custom_call" | custom-call | bytes 262144 | tf_op jit(solution)/shard_map/grid/pallas_call | solution.py:271
  9.7 0.0 copy-start.4
  9.7 5.4 %all-to-all-start = ((bf16[8,4,4,16,128]{4,3,2,1,0:T(8,128)(2,1)}), bf16[8,4,4,16,128]{4,3,2,1,0:T(8,128)(2,1)S(1)}, u32[]{:S(2)}, u32[]{:S(2)}) async-start(bf16[8,4,4,16,128]{4,3,2,1,0:T(8,128)(2,1)} %grid.1), calls=%async_computation | async-start | bytes 1048576 | tf_op jit(solution)/shard_map/all_to_all | solution.py:17
  15.1 0.0 copy-start
  15.1 0.0 copy-done.4
  15.2 0.9 %copy-done = bf16[27,64,16]{1,2,0:T(8,128)(2,1)S(1)} copy-done((bf16[27,64,16]{1,2,0:T(8,128)(2,1)S(1)}, bf16[27,64,16]{1,2,0:T(8,128)(2,1)}, u32[]{:S(2)}) %copy-start) | copy-done | bytes 55320
  16.0 0.0 copy-start.3
  16.0 0.1 copy.20
  16.1 0.1 reshape.49
  16.2 0.7 copy-done.3
  16.9 0.2 fusion
  17.2 8.6 %all-to-all-done.tiles = bf16[8,4,4,16,128]{4,3,2,1,0:T(8,128)(2,1)S(1)} async-done(((bf16[8,4,4,16,128]{4,3,2,1,0:T(8,128)(2,1)}), bf16[8,4,4,16,128]{4,3,2,1,0:T(8,128)(2,1)S(1)}, u32[]{:S(2)}, u32[]{:S(2)}) %all-to-all-start) | async-done | bytes 524320 | tf_op jit(solution)/shard_map/all_to_all | solution.py:17
  25.7 0.0 copy-start.2
  25.7 1.9 %collective-permute-start.2 = (bf16[34,16,128]{2,1,0:T(8,128)(2,1)S(1)}, bf16[34,16,128]{2,1,0:T(8,128)(2,1)S(1)}, u32[]{:S(2)}, u32[]{:S(2)}) collective-permute-start(bf16[34,16,128]{2,1,0:T(8,128)(2,1)S(1)} %get-tuple-element.24), channel_id=1, source_target_pairs={{8,0},{16,8},{24,16},{32,24},{40,32},{48,40},{56,48},{9,1},{17,9},... | collective-permute-start | bytes 417800 | tf_op jit(solution)/shard_map/ppermute | solution.py:22
  27.7 4.3 %collective-permute-start.3 = (bf16[34,16,128]{2,1,0:T(8,128)(2,1)S(1)}, bf16[34,16,128]{2,1,0:T(8,128)(2,1)S(1)}, u32[]{:S(2)}, u32[]{:S(2)}) collective-permute-start(bf16[34,16,128]{2,1,0:T(8,128)(2,1)S(1)} %get-tuple-element.25), channel_id=1, source_target_pairs={{0,8},{8,16},{16,24},{24,32},{32,40},{40,48},{48,56},{1,9},{9,17},... | collective-permute-start | bytes 417800 | tf_op jit(solution)/shard_map/ppermute | solution.py:23
  32.0 1.1 %collective-permute-done.2.after = bf16[34,16,128]{2,1,0:T(8,128)(2,1)S(1)} collective-permute-done((bf16[34,16,128]{2,1,0:T(8,128)(2,1)S(1)}, bf16[34,16,128]{2,1,0:T(8,128)(2,1)S(1)}, u32[]{:S(2)}, u32[]{:S(2)}) %collective-permute-start.2) | collective-permute-done | bytes 139296 | tf_op jit(solution)/shard_map/ppermute | solution.py:22
  33.1 1.6 %collective-permute-done.3.before = bf16[34,16,128]{2,1,0:T(8,128)(2,1)S(1)} collective-permute-done((bf16[34,16,128]{2,1,0:T(8,128)(2,1)S(1)}, bf16[34,16,128]{2,1,0:T(8,128)(2,1)S(1)}, u32[]{:S(2)}, u32[]{:S(2)}) %collective-permute-start.3) | collective-permute-done | bytes 139296 | tf_op jit(solution)/shard_map/ppermute | solution.py:23
  34.6 0.0 copy-done.2
  34.6 2.1 %forward.1 = (bf16[16,16,128]{2,1,0:T(8,128)(2,1)S(1)}, bf16[17,16,128]{2,1,0:T(8,128)(2,1)S(1)}, bf16[10,16,128]{2,1,0:T(8,128)(2,1)S(1)}, bf16[7,16,128]{2,1,0:T(8,128)(2,1)S(1)}) custom-call(s32[1]{0:T(128)} %bitcast.at_ref, f32[16]{0:T(128)S(1)} %copy-done.2, bf16[3,96,256]{2,1,0:T(8,128)(2,1)S(1)} %bitcast.29, bf16[16,16,128]{2,1,0:T(8,128)(2,1)S(1)} %bitcast.28, ...), custom_call_target="tpu_custom_call" | custom-call | flops 339738624 | bytes 262144 | tf_op jit(solution)/shard_map/forward/pallas_call | solution.py:271
  36.7 1.9 %collective-permute-start.4 = (bf16[17,16,128]{2,1,0:T(8,128)(2,1)S(1)}, bf16[17,16,128]{2,1,0:T(8,128)(2,1)S(1)}, u32[]{:S(2)}, u32[]{:S(2)}) collective-permute-start(bf16[17,16,128]{2,1,0:T(8,128)(2,1)S(1)} %get-tuple-element.28.face), channel_id=1, source_target_pairs={{0,64},{64,0},{128,192},{192,128},{256,320},{320,256},{384,448},{4... | collective-permute-start | bytes 208904 | tf_op jit(solution)/shard_map/ppermute | solution.py:359
  38.7 1.2 %collective-permute-done.4.other.face_in = bf16[17,16,128]{2,1,0:T(8,128)(2,1)S(1)} collective-permute-done((bf16[17,16,128]{2,1,0:T(8,128)(2,1)S(1)}, bf16[17,16,128]{2,1,0:T(8,128)(2,1)S(1)}, u32[]{:S(2)}, u32[]{:S(2)}) %collective-permute-start.4) | collective-permute-done | bytes 69664 | tf_op jit(solution)/shard_map/ppermute | solution.py:359
  39.9 0.7 pair.1
  40.6 12.0 %all-to-all-start.1 = ((bf16[8,7,16,128]{3,2,1,0:T(8,128)(2,1)}), bf16[8,7,16,128]{3,2,1,0:T(8,128)(2,1)S(1)}, u32[]{:S(2)}, u32[]{:S(2)}) async-start(bf16[8,7,16,128]{3,2,1,0:T(8,128)(2,1)} %pair.1), calls=%async_computation.1 | async-start | bytes 458752 | tf_op jit(solution)/shard_map/all_to_all | solution.py:17
  52.6 0.7 collective-permute-start.5
  53.3 7.5 %all-to-all-done.1.blocks = bf16[8,7,16,128]{3,2,1,0:T(8,128)(2,1)S(1)} async-done(((bf16[8,7,16,128]{3,2,1,0:T(8,128)(2,1)}), bf16[8,7,16,128]{3,2,1,0:T(8,128)(2,1)S(1)}, u32[]{:S(2)}, u32[]{:S(2)}) %all-to-all-start.1) | async-done | bytes 229408 | tf_op jit(solution)/shard_map/all_to_all | solution.py:17
  60.8 0.7 sums.2
  61.5 7.7 %all-to-all-start.2 = ((bf16[4,7,16,128]{3,2,1,0:T(8,128)(2,1)}), bf16[4,7,16,128]{3,2,1,0:T(8,128)(2,1)S(1)}, u32[]{:S(2)}, u32[]{:S(2)}) async-start(bf16[4,7,16,128]{3,2,1,0:T(8,128)(2,1)} %sums.2), calls=%async_computation.2 | async-start | bytes 229376 | tf_op jit(solution)/shard_map/all_to_all | solution.py:17
  69.2 0.0 collective-permute-done.5.far_in
  69.2 1.3 %backward.1 = bf16[8,8,16,128]{3,2,1,0:T(8,128)(2,1)} custom-call(s32[1]{0:T(128)} %bitcast.at_ref, bf16[432,64]{1,0:T(8,128)(2,1)S(1)} %bitcast.33, bf16[17,16,128]{2,1,0:T(8,128)(2,1)S(1)} %get-tuple-element.28.face, bf16[10,16,128]{2,1,0:T(8,128)(2,1)S(1)} %get-tuple-element.29.far, bf16[17,16,128]{2,1,0:T(8,128)(2,1)S(1)} %collective-permute-done.4.other.face_in, ...), custom_call_target="tpu_custom_call" | custom-call | flops 7247757312 | bytes 262144 | tf_op jit(solution)/shard_map/backward/pallas_call | solution.py:271
  70.5 2.3 %all-to-all-done.2.blocks = bf16[4,7,16,128]{3,2,1,0:T(8,128)(2,1)S(1)} async-done(((bf16[4,7,16,128]{3,2,1,0:T(8,128)(2,1)}), bf16[4,7,16,128]{3,2,1,0:T(8,128)(2,1)S(1)}, u32[]{:S(2)}, u32[]{:S(2)}) %all-to-all-start.2) | async-done | bytes 114720 | tf_op jit(solution)/shard_map/all_to_all | solution.py:17
  72.9 3.4 %all-to-all-start.3 = ((bf16[8,8,16,128]{3,2,1,0:T(8,128)(2,1)}), bf16[8,8,16,128]{3,2,1,0:T(8,128)(2,1)S(1)}, u32[]{:S(2)}, u32[]{:S(2)}) async-start(bf16[8,8,16,128]{3,2,1,0:T(8,128)(2,1)} %backward.1), calls=%async_computation.3 | async-start | bytes 524288 | tf_op jit(solution)/shard_map/all_to_all | solution.py:17
  76.3 1.9 %collective-permute-start.6 = (bf16[7,16,128]{2,1,0:T(8,128)(2,1)S(1)}, bf16[7,16,128]{2,1,0:T(8,128)(2,1)S(1)}, u32[]{:S(2)}, u32[]{:S(2)}) collective-permute-start(bf16[7,16,128]{2,1,0:T(8,128)(2,1)S(1)} %bitcast.30), channel_id=1, source_target_pairs={{0,64},{64,0},{128,192},{192,128},{256,320},{320,256},{384,448},{4... | collective-permute-start | bytes 86024 | tf_op jit(solution)/shard_map/ppermute | solution.py:391
  78.2 0.6 copy.21
  78.9 0.5 collective-permute-done.6.other
  79.4 0.8 weights.1
  80.2 3.3 %all-to-all-done.3.parts = bf16[8,8,16,128]{3,2,1,0:T(8,128)(2,1)S(1)} async-done(((bf16[8,8,16,128]{3,2,1,0:T(8,128)(2,1)}), bf16[8,8,16,128]{3,2,1,0:T(8,128)(2,1)S(1)}, u32[]{:S(2)}, u32[]{:S(2)}) %all-to-all-start.3) | async-done | bytes 262176 | tf_op jit(solution)/shard_map/all_to_all | solution.py:17
  83.5 0.7 unpack.1
  (6 shorter events, 0.1 us)
Async XLA Ops:
  0.6 0.8 copy-start.1
  1.4 6.5 %collective-permute-start.1 = (bf16[4,16,128]{2,1,0:T(8,128)(2,1)S(1)}, bf16[4,16,128]{2,1,0:T(8,128)(2,1)S(1)}, u32[]{:S(2)}, u32[]{:S(2)}) collective-permute-start(bf16[4,16,128]{2,1,0:T(8,128)(2,1)S(1)} %far.1), channel_id=1, source_target_pairs={{64,128},{128,64},{192,256},{256,192},{320,384},{384,320},{65,129}... | collective-permute-start | bytes 49160 | tf_op jit(solution)/shard_map/ppermute | solution.py:306
  2.1 6.7 %collective-permute-start = (bf16[4,16,128]{2,1,0:T(8,128)(2,1)S(1)}, bf16[4,16,128]{2,1,0:T(8,128)(2,1)S(1)}, u32[]{:S(2)}, u32[]{:S(2)}) collective-permute-start(bf16[4,16,128]{2,1,0:T(8,128)(2,1)S(1)} %get-tuple-element.20), channel_id=1, source_target_pairs={{0,64},{64,0},{128,192},{192,128},{256,320},{320,256},{384,448},{4... | collective-permute-start | bytes 49160 | tf_op jit(solution)/shard_map/ppermute | solution.py:304
  9.7 5.5 %copy-start.4 = (bf16[16,2,8,128]{3,2,1,0:T(8,128)(2,1)S(1)}, bf16[16,2,8,128]{3,2,1,0:T(8,128)(2,1)}, u32[]{:S(2)}) copy-start(bf16[16,2,8,128]{3,2,1,0:T(8,128)(2,1)} %param.8) | copy-start | bytes 196612
  9.7 16.0 %all-to-all-start = ((bf16[8,4,4,16,128]{4,3,2,1,0:T(8,128)(2,1)}), bf16[8,4,4,16,128]{4,3,2,1,0:T(8,128)(2,1)S(1)}, u32[]{:S(2)}, u32[]{:S(2)}) async-start(bf16[8,4,4,16,128]{4,3,2,1,0:T(8,128)(2,1)} %grid.1), calls=%async_computation | async-start | bytes 1048576 | tf_op jit(solution)/shard_map/all_to_all | solution.py:17
  15.1 0.9 %copy-start = (bf16[27,64,16]{1,2,0:T(8,128)(2,1)S(1)}, bf16[27,64,16]{1,2,0:T(8,128)(2,1)}, u32[]{:S(2)}) copy-start(bf16[27,64,16]{1,2,0:T(8,128)(2,1)} %param.6) | copy-start | bytes 165892
  16.0 0.9 %copy-start.3 = (bf16[2,192,256,1]{2,1,3,0:T(8,128)(2,1)S(1)}, bf16[2,192,256,1]{2,1,3,0:T(8,128)(2,1)}, u32[]{:S(2)}) copy-start(bf16[2,192,256,1]{2,1,3,0:T(8,128)(2,1)} %constant.24) | copy-start | bytes 589828
  25.7 8.9 %copy-start.2 = (f32[16]{0:T(128)S(1)}, f32[16]{0:T(128)}, u32[]{:S(2)}) copy-start(f32[16]{0:T(128)} %bias_ref.1) | copy-start | bytes 196
  25.7 7.3 %collective-permute-start.2 = (bf16[34,16,128]{2,1,0:T(8,128)(2,1)S(1)}, bf16[34,16,128]{2,1,0:T(8,128)(2,1)S(1)}, u32[]{:S(2)}, u32[]{:S(2)}) collective-permute-start(bf16[34,16,128]{2,1,0:T(8,128)(2,1)S(1)} %get-tuple-element.24), channel_id=1, source_target_pairs={{8,0},{16,8},{24,16},{32,24},{40,32},{48,40},{56,48},{9,1},{17,9},... | collective-permute-start | bytes 417800 | tf_op jit(solution)/shard_map/ppermute | solution.py:22
  27.7 6.9 %collective-permute-start.3 = (bf16[34,16,128]{2,1,0:T(8,128)(2,1)S(1)}, bf16[34,16,128]{2,1,0:T(8,128)(2,1)S(1)}, u32[]{:S(2)}, u32[]{:S(2)}) collective-permute-start(bf16[34,16,128]{2,1,0:T(8,128)(2,1)S(1)} %get-tuple-element.25), channel_id=1, source_target_pairs={{0,8},{8,16},{16,24},{24,32},{32,40},{40,48},{48,56},{1,9},{9,17},... | collective-permute-start | bytes 417800 | tf_op jit(solution)/shard_map/ppermute | solution.py:23
  36.7 3.2 %collective-permute-start.4 = (bf16[17,16,128]{2,1,0:T(8,128)(2,1)S(1)}, bf16[17,16,128]{2,1,0:T(8,128)(2,1)S(1)}, u32[]{:S(2)}, u32[]{:S(2)}) collective-permute-start(bf16[17,16,128]{2,1,0:T(8,128)(2,1)S(1)} %get-tuple-element.28.face), channel_id=1, source_target_pairs={{0,64},{64,0},{128,192},{192,128},{256,320},{320,256},{384,448},{4... | collective-permute-start | bytes 208904 | tf_op jit(solution)/shard_map/ppermute | solution.py:359
  40.6 20.2 %all-to-all-start.1 = ((bf16[8,7,16,128]{3,2,1,0:T(8,128)(2,1)}), bf16[8,7,16,128]{3,2,1,0:T(8,128)(2,1)S(1)}, u32[]{:S(2)}, u32[]{:S(2)}) async-start(bf16[8,7,16,128]{3,2,1,0:T(8,128)(2,1)} %pair.1), calls=%async_computation.1 | async-start | bytes 458752 | tf_op jit(solution)/shard_map/all_to_all | solution.py:17
  52.6 16.6 %collective-permute-start.5 = (bf16[10,16,128]{2,1,0:T(8,128)(2,1)S(1)}, bf16[10,16,128]{2,1,0:T(8,128)(2,1)S(1)}, u32[]{:S(2)}, u32[]{:S(2)}) collective-permute-start(bf16[10,16,128]{2,1,0:T(8,128)(2,1)S(1)} %get-tuple-element.29.far), channel_id=1, source_target_pairs={{64,128},{128,64},{192,256},{256,192},{320,384},{384,320},{65,129}... | collective-permute-start | bytes 122888 | tf_op jit(solution)/shard_map/ppermute | solution.py:360
  61.5 11.4 %all-to-all-start.2 = ((bf16[4,7,16,128]{3,2,1,0:T(8,128)(2,1)}), bf16[4,7,16,128]{3,2,1,0:T(8,128)(2,1)S(1)}, u32[]{:S(2)}, u32[]{:S(2)}) async-start(bf16[4,7,16,128]{3,2,1,0:T(8,128)(2,1)} %sums.2), calls=%async_computation.2 | async-start | bytes 229376 | tf_op jit(solution)/shard_map/all_to_all | solution.py:17
  72.9 10.6 %all-to-all-start.3 = ((bf16[8,8,16,128]{3,2,1,0:T(8,128)(2,1)}), bf16[8,8,16,128]{3,2,1,0:T(8,128)(2,1)S(1)}, u32[]{:S(2)}, u32[]{:S(2)}) async-start(bf16[8,8,16,128]{3,2,1,0:T(8,128)(2,1)} %backward.1), calls=%async_computation.3 | async-start | bytes 524288 | tf_op jit(solution)/shard_map/all_to_all | solution.py:17
  76.3 3.1 %collective-permute-start.6 = (bf16[7,16,128]{2,1,0:T(8,128)(2,1)S(1)}, bf16[7,16,128]{2,1,0:T(8,128)(2,1)S(1)}, u32[]{:S(2)}, u32[]{:S(2)}) collective-permute-start(bf16[7,16,128]{2,1,0:T(8,128)(2,1)S(1)} %bitcast.30), channel_id=1, source_target_pairs={{0,64},{64,0},{128,192},{192,128},{256,320},{320,256},{384,448},{4... | collective-permute-start | bytes 86024 | tf_op jit(solution)/shard_map/ppermute | solution.py:391
